TPU v7x, 32 devices: a whole 2x2x4 slice. The times are simulated.
32 devices in a mesh: ctx: 8 (over y, x, core), head: 4 (over z).
Axes of the slice: x: 2, y: 2, z: 4, core: 2. Of those that a mesh axis runs over, the one named last changes fastest.
Arguments:
- queries: bfloat16 [1024, 1024], P('ctx', 'head'), may hold values from -6 to 6
- key_vectors: bfloat16 [1024, 1024], P('ctx', 'head'), may hold values from -6 to 6
- value_rows: bfloat16 [1024, 2048], P('ctx', 'head'), may hold values from -6 to 6
- write_rate: float32 [16, 1024], P('head', 'ctx'), may hold values from 0.0078125 to 1
- log_decay: float32 [16, 1024], P('head', 'ctx'), may hold values from -0.9 to 0
- doc_offsets: int32 [5], replicated, may hold values from 0 to 1024, as said below
- out_weight: bfloat16 [2048, 2048], P('head'), may hold values from -0.125 to 0.125
- grad_out: bfloat16 [1024, 2048], P(('ctx', 'head')), may hold values from -6 to 6
Outputs:
- layer_out: float32 [1024, 2048], P(('ctx', 'head'))
- grad_q: float32 [1024, 1024], P('ctx', 'head')
- grad_k: float32 [1024, 1024], P('ctx', 'head')
- grad_v: float32 [1024, 2048], P('ctx', 'head')
- grad_rate: float32 [16, 1024], P('head', 'ctx')
- grad_decay: float32 [16, 1024], P('head', 'ctx')
- weight_grad: float32 [2048, 2048], P('ctx', 'head')
Inputs may be any that keep to these rules, and one draw needn't show every extreme that they name: `doc_offsets`: Increasing; the first entry is 0 and the last is 1024.
All inputs are finite; a program needn't handle non-finite values.
Results may differ from a plain program's by a relative error of at most 0.0029.
Values may be sent and summed in bfloat16 or wider, within the bound.
No kernel may reach another device: no remote copies, remote signals or barrier semaphores. Data moves between devices by JAX's collectives and lax.ppermute only.
A program may use at most 64 MiB of HBM per device.

v0:
```python
from functools import partial

import jax
import jax.numpy as jnp
from jax import lax
from jax.sharding import PartitionSpec as P

DK = 128
DV = 128
STRETCH = 64


full_precision = lax.Precision.HIGHEST


def shifted(value, axis, by):
    length = lax.axis_size(axis)
    pairs = [(i, i + by) for i in range(length) if 0 <= i + by < length]
    return lax.ppermute(value, axis, pairs)


def tri_inverse(strict_lower):
    order_size = strict_lower.shape[-1]
    identity = jnp.eye(order_size, dtype=strict_lower.dtype)
    powers = -strict_lower
    result = identity + powers
    reach_span = 2
    while reach_span < order_size:
        powers = jnp.einsum("hij,hjk->hik", powers, powers, precision=full_precision)
        result = jnp.einsum("hij,hjk->hik", result, identity + powers, precision=full_precision)
        reach_span = reach_span * 2
    return result


def block_step(state, inputs):
    query_blk, key_blk, value_blk, rate_blk, decay_blk, reset_blk = inputs
    dtype_f = decay_blk.dtype
    cumul = jnp.cumsum(decay_blk, axis=-1)
    segment = jnp.cumsum(reset_blk)
    block_len = reset_blk.shape[0]
    row_ids = lax.broadcasted_iota(jnp.int32, (block_len, block_len), 0)
    col_ids = lax.broadcasted_iota(jnp.int32, (block_len, block_len), 1)
    same_seg = segment[:, None] == segment[None, :]
    together = same_seg & (row_ids >= col_ids)
    strict = same_seg & (row_ids > col_ids)
    gaps = cumul[:, :, None] - cumul[:, None, :]
    ratio = jnp.exp(jnp.where(together, gaps, 0.0)) * together.astype(dtype_f)
    from_start = jnp.exp(cumul) * (segment == 0).astype(dtype_f)
    to_end = jnp.exp(cumul[:, -1:] - cumul) * (segment == segment[-1]).astype(dtype_f)
    whole_decay = jnp.exp(cumul[:, -1]) * (segment[-1] == 0).astype(dtype_f)
    key_dots = jnp.einsum("hik,hjk->hij", key_blk, key_blk, precision=full_precision)
    coupling = rate_blk[:, :, None] * key_dots * ratio * strict.astype(dtype_f)
    inverse = tri_inverse(coupling)
    right_side = jnp.concatenate(
        [rate_blk[:, :, None] * value_blk, (rate_blk * from_start)[:, :, None] * key_blk], axis=-1
    )
    solved = jnp.einsum("hij,hjw->hiw", inverse, right_side, precision=full_precision)
    value_width = value_blk.shape[-1]
    pseudo = solved[..., :value_width] - jnp.einsum(
        "hck,hvk->hcv", solved[..., value_width:], state, precision=full_precision
    )
    scores = jnp.einsum("hik,hjk->hij", query_blk, key_blk, precision=full_precision) * ratio
    outputs = from_start[:, :, None] * jnp.einsum(
        "hck,hvk->hcv", query_blk, state, precision=full_precision
    )
    outputs = outputs + jnp.einsum("hij,hjv->hiv", scores, pseudo, precision=full_precision)
    new_state = whole_decay[:, None, None] * state + jnp.einsum(
        "hcv,hck->hvk", pseudo, to_end[:, :, None] * key_blk, precision=full_precision
    )
    return (new_state, outputs)


def run_blocks(state, query_heads, key_heads, value_heads, rates, decays, resets, block_size):
    head_count, length = rates.shape
    blocks = length // block_size

    def split_rows(tensor):
        return jnp.moveaxis(tensor.reshape(head_count, blocks, block_size, tensor.shape[-1]), 1, 0)

    stacked = (
        split_rows(query_heads),
        split_rows(key_heads),
        split_rows(value_heads),
        jnp.moveaxis(rates.reshape(head_count, blocks, block_size), 1, 0),
        jnp.moveaxis(decays.reshape(head_count, blocks, block_size), 1, 0),
        resets.reshape(blocks, block_size),
    )
    final_state, outputs = lax.scan(jax.checkpoint(block_step), state, stacked)
    outputs = jnp.moveaxis(outputs, 0, 1).reshape(head_count, length, outputs.shape[-1])
    return (final_state, outputs)


def to_heads(query_f, key_f, value_f):
    length = query_f.shape[0]

    def heads_first(tensor, width):
        return jnp.transpose(tensor.reshape(length, tensor.shape[1] // width, width), (1, 0, 2))

    def unit_rows(tensor):
        return tensor / jnp.sqrt(jnp.sum(tensor * tensor, axis=-1, keepdims=True) + 1e-06)

    value_heads = heads_first(value_f, DV)
    repeat_by = value_heads.shape[0] // (key_f.shape[1] // DK)
    query_heads = jnp.repeat(unit_rows(heads_first(query_f, DK)), repeat_by, axis=0)
    key_heads = jnp.repeat(unit_rows(heads_first(key_f, DK)), repeat_by, axis=0)
    return (query_heads, key_heads, value_heads)


def local_pass(query_f, key_f, value_f, rates, decays, resets):
    query_heads, key_heads, value_heads = to_heads(query_f, key_f, value_f)
    head_count, length, value_width = value_heads.shape
    key_width = key_heads.shape[-1]
    padded_values = jnp.concatenate(
        [value_heads, jnp.zeros((head_count, length, key_width), value_f.dtype)], axis=-1
    )
    start_state = jnp.concatenate(
        [
            jnp.zeros((head_count, value_width, key_width), value_f.dtype),
            jnp.broadcast_to(
                jnp.eye(key_width, dtype=value_f.dtype), (head_count, key_width, key_width)
            ),
        ],
        axis=1,
    )
    final_state, outputs = run_blocks(
        start_state, query_heads, key_heads, padded_values, rates, decays, resets, STRETCH
    )
    return (
        outputs[..., :value_width],
        outputs[..., value_width:],
        final_state[:, value_width:, :],
        final_state[:, :value_width, :],
    )


def joint_chain(transfer, local_state, adjoint_local):
    steps_total = lax.axis_size("ctx") - 1

    def advance(step_index, carry_four):
        incoming, outgoing, received, sending = carry_four
        incoming = shifted(outgoing, "ctx", 1)
        received = shifted(sending, "ctx", -1)
        outgoing = (
            jnp.einsum("hvk,hkj->hvj", incoming, transfer, precision=full_precision) + local_state
        )
        sending = (
            jnp.einsum("hvk,hjk->hvj", received, transfer, precision=full_precision) + adjoint_local
        )
        return (incoming, outgoing, received, sending)

    start_four = (
        jnp.zeros_like(local_state),
        local_state,
        jnp.zeros_like(adjoint_local),
        adjoint_local,
    )
    incoming, outgoing, received, sending = lax.fori_loop(0, steps_total, advance, start_four)
    return (incoming, received)


def per_device(
    queries, key_vectors, value_rows, write_rate, log_decay, doc_offsets, out_weight, grad_out
):
    tok_count = queries.shape[0]
    shard_start = lax.axis_index("ctx") * tok_count
    positions = shard_start + lax.broadcasted_iota(jnp.int32, (tok_count,), 0)
    resets = jnp.any(positions[:, None] == doc_offsets[None, :-1], axis=1).astype(jnp.int32)
    full_grad = lax.all_gather(grad_out, "head", axis=0, tiled=True)
    d_core = jnp.einsum("td,cd->tc", full_grad, out_weight, preferred_element_type=jnp.float32)
    head_count = write_rate.shape[0]
    d_heads = jnp.transpose(d_core.reshape(tok_count, head_count, DV), (1, 0, 2))
    pass_out, pass_vjp = jax.vjp(
        partial(local_pass, resets=resets),
        queries.astype(jnp.float32),
        key_vectors.astype(jnp.float32),
        value_rows.astype(jnp.float32),
        write_rate,
        log_decay,
    )
    o_local, q_tilde, transfer, local_state = pass_out
    adjoint_local = jnp.einsum("htv,htk->hvk", d_heads, q_tilde, precision=full_precision)
    incoming, adjoint_out = joint_chain(transfer, local_state, adjoint_local)
    core_heads = o_local + jnp.einsum("htk,hvk->htv", q_tilde, incoming, precision=full_precision)
    mixed_in = (
        jnp.transpose(core_heads, (1, 0, 2))
        .reshape(tok_count, head_count * DV)
        .astype(jnp.bfloat16)
    )
    layer_out = lax.psum_scatter(
        jnp.dot(mixed_in, out_weight, preferred_element_type=jnp.float32),
        "head",
        scatter_dimension=0,
        tiled=True,
    )
    weight_grad = lax.psum_scatter(
        jnp.einsum("td,tc->dc", full_grad, mixed_in, preferred_element_type=jnp.float32),
        "ctx",
        scatter_dimension=0,
        tiled=True,
    )
    d_qtilde = jnp.einsum("htv,hvk->htk", d_heads, incoming, precision=full_precision)
    d_transfer = jnp.einsum("hvk,hvj->hkj", incoming, adjoint_out, precision=full_precision)
    all_grads = pass_vjp((d_heads, d_qtilde, d_transfer, adjoint_out))
    grad_q, grad_k, grad_v, grad_rate, grad_decay = all_grads
    return (layer_out, grad_q, grad_k, grad_v, grad_rate, grad_decay, weight_grad)


def solution(mesh):
    placed = (
        P("ctx", "head"),
        P("ctx", "head"),
        P("ctx", "head"),
        P("head", "ctx"),
        P("head", "ctx"),
        P(),
        P("head", None),
        P(("ctx", "head"), None),
    )
    return jax.shard_map(
        per_device,
        mesh=mesh,
        in_specs=placed,
        out_specs=(
            P(("ctx", "head"), None),
            P("ctx", "head"),
            P("ctx", "head"),
            P("ctx", "head"),
            P("head", "ctx"),
            P("head", "ctx"),
            P("ctx", "head"),
        ),
        check_vma=False,
    )
```

profile of v0, /device:TPU:11, one launch (start us, length us, event | category | flops | bytes accessed | tf_op | source)
XLA Modules:
  0.0 301.5 jit_solution(14770646792553870785)
XLA Ops:
  20.4 13.4 %all_gather.3 = bf16[128,2048]{1,0:T(8,128)(2,1)} all-gather(bf16[32,2048]{1,0:T(8,128)(2,1)S(1)} %copy-done.34), channel_id=1, replica_groups=mesh['ctx'=8,'head'=4] {'head'}, dimensions={0}, use_global_device_ids=true | all-gather | bytes 655360 | tf_op jit(solution)/shard_map/all_gather | solution.py:168
  33.9 31.4 %while.60 = (s32[]{:T(128)}, f32[4,256,128]{2,1,0:T(8,128)S(1)}, f32[2,4,64,256]{3,2,1,0:T(8,128)}, f32[2,4,256,128]{3,2,1,0:T(8,128)}, f32[2,4,64]{2,1,0:T(4,12...) while((s32[]{:T(128)}, f32[4,256,128]{2,1,0:T(8,128)S(1)}, ...), condition=%wide.region_6.7_spmd.clone.clone, body=%wide.region_3.6_spmd.clone.clone.sunk | while | flops 605004736 | bytes 24266692 | solution.py:88
  47.2 2.3 convolution_add_fusion.59
  62.9 2.3 convolution_add_fusion.59
  66.4 2.1 convolution_bitcast_fusion.1
  70.6 102.6 %while.58 = (s32[]{:T(128)}, f32[4,128,128]{2,1,0:T(8,128)}, f32[4,128,128]{2,1,0:T(8,128)S(1)}, f32[4,128,128]{2,1,0:T(8,128)}, f32[4,128,128]{2,1,0:T(8,128)},...) while((s32[]{:T(128)}, f32[4,128,128]{2,1,0:T(8,128)}, ...), condition=%wide.region_8.9_spmd, body=%wide.region_7.8_spmd.sunk | while | flops 201457664 | bytes 6291685 | solution.py:157
  70.6 6.4 %collective-permute-start.1 = (f32[4,128,128]{2,1,0:T(8,128)}, f32[4,128,128]{2,1,0:T(8,128)S(1)}, u32[]{:S(2)}, u32[]{:S(2)}) collective-permute-start(f32[4,128,128]{2,1,0:T(8,128)} %get-tuple-element.1153), channel_id=1, source_target_pairs={{4,0},{8,4},{12,8},{16,12},{20,16},{24,20},{28,24},{5,1},{9,5},{13... | collective-permute-start | bytes 786440 | tf_op jit(solution)/shard_map/while/body/eval_jaxpr/ppermute | solution.py:19
  77.0 3.0 %collective-permute-start = (f32[4,128,128]{2,1,0:T(8,128)S(1)}, f32[4,128,128]{2,1,0:T(8,128)S(1)}, u32[]{:S(2)}, u32[]{:S(2)}) collective-permute-start(f32[4,128,128]{2,1,0:T(8,128)S(1)} %get-tuple-element.1151), channel_id=1, source_target_pairs={{0,4},{4,8},{8,12},{12,16},{16,20},{20,24},{24,28},{1,5},{5,9},{9,... | collective-permute-start | bytes 786440 | tf_op jit(solution)/shard_map/while/body/eval_jaxpr/ppermute | solution.py:19
  80.1 2.4 collective-permute-done.1
  82.5 2.4 convolution_add_fusion.43
  88.3 4.5 %collective-permute-start = (f32[4,128,128]{2,1,0:T(8,128)S(1)}, f32[4,128,128]{2,1,0:T(8,128)S(1)}, u32[]{:S(2)}, u32[]{:S(2)}) collective-permute-start(f32[4,128,128]{2,1,0:T(8,128)S(1)} %get-tuple-element.1151), channel_id=1, source_target_pairs={{0,4},{4,8},{8,12},{12,16},{16,20},{20,24},{24,28},{1,5},{5,9},{9,... | collective-permute-start | bytes 786440 | tf_op jit(solution)/shard_map/while/body/eval_jaxpr/ppermute | solution.py:19
  92.9 3.2 %collective-permute-done.1 = f32[4,128,128]{2,1,0:T(8,128)S(1)} collective-permute-done((f32[4,128,128]{2,1,0:T(8,128)}, f32[4,128,128]{2,1,0:T(8,128)S(1)}, u32[]{:S(2)}, u32[]{:S(2)}) %collective-permute-start.1) | collective-permute-done | bytes 262176 | tf_op jit(solution)/shard_map/while/body/eval_jaxpr/ppermute | solution.py:19
  96.0 2.4 convolution_add_fusion.43
  101.9 4.5 %collective-permute-start = (f32[4,128,128]{2,1,0:T(8,128)S(1)}, f32[4,128,128]{2,1,0:T(8,128)S(1)}, u32[]{:S(2)}, u32[]{:S(2)}) collective-permute-start(f32[4,128,128]{2,1,0:T(8,128)S(1)} %get-tuple-element.1151), channel_id=1, source_target_pairs={{0,4},{4,8},{8,12},{12,16},{16,20},{20,24},{24,28},{1,5},{5,9},{9,... | collective-permute-start | bytes 786440 | tf_op jit(solution)/shard_map/while/body/eval_jaxpr/ppermute | solution.py:19
  106.4 4.8 %collective-permute-done.1 = f32[4,128,128]{2,1,0:T(8,128)S(1)} collective-permute-done((f32[4,128,128]{2,1,0:T(8,128)}, f32[4,128,128]{2,1,0:T(8,128)S(1)}, u32[]{:S(2)}, u32[]{:S(2)}) %collective-permute-start.1) | collective-permute-done | bytes 262176 | tf_op jit(solution)/shard_map/while/body/eval_jaxpr/ppermute | solution.py:19
  111.2 2.4 convolution_add_fusion.43
  117.1 4.5 %collective-permute-start = (f32[4,128,128]{2,1,0:T(8,128)S(1)}, f32[4,128,128]{2,1,0:T(8,128)S(1)}, u32[]{:S(2)}, u32[]{:S(2)}) collective-permute-start(f32[4,128,128]{2,1,0:T(8,128)S(1)} %get-tuple-element.1151), channel_id=1, source_target_pairs={{0,4},{4,8},{8,12},{12,16},{16,20},{20,24},{24,28},{1,5},{5,9},{9,... | collective-permute-start | bytes 786440 | tf_op jit(solution)/shard_map/while/body/eval_jaxpr/ppermute | solution.py:19
  121.6 4.0 %collective-permute-done.1 = f32[4,128,128]{2,1,0:T(8,128)S(1)} collective-permute-done((f32[4,128,128]{2,1,0:T(8,128)}, f32[4,128,128]{2,1,0:T(8,128)S(1)}, u32[]{:S(2)}, u32[]{:S(2)}) %collective-permute-start.1) | collective-permute-done | bytes 262176 | tf_op jit(solution)/shard_map/while/body/eval_jaxpr/ppermute | solution.py:19
  125.6 2.4 convolution_add_fusion.43
  131.4 4.5 %collective-permute-start = (f32[4,128,128]{2,1,0:T(8,128)S(1)}, f32[4,128,128]{2,1,0:T(8,128)S(1)}, u32[]{:S(2)}, u32[]{:S(2)}) collective-permute-start(f32[4,128,128]{2,1,0:T(8,128)S(1)} %get-tuple-element.1151), channel_id=1, source_target_pairs={{0,4},{4,8},{8,12},{12,16},{16,20},{20,24},{24,28},{1,5},{5,9},{9,... | collective-permute-start | bytes 786440 | tf_op jit(solution)/shard_map/while/body/eval_jaxpr/ppermute | solution.py:19
  136.0 4.3 %collective-permute-done.1 = f32[4,128,128]{2,1,0:T(8,128)S(1)} collective-permute-done((f32[4,128,128]{2,1,0:T(8,128)}, f32[4,128,128]{2,1,0:T(8,128)S(1)}, u32[]{:S(2)}, u32[]{:S(2)}) %collective-permute-start.1) | collective-permute-done | bytes 262176 | tf_op jit(solution)/shard_map/while/body/eval_jaxpr/ppermute | solution.py:19
  140.3 2.4 convolution_add_fusion.43
  146.1 4.5 %collective-permute-start = (f32[4,128,128]{2,1,0:T(8,128)S(1)}, f32[4,128,128]{2,1,0:T(8,128)S(1)}, u32[]{:S(2)}, u32[]{:S(2)}) collective-permute-start(f32[4,128,128]{2,1,0:T(8,128)S(1)} %get-tuple-element.1151), channel_id=1, source_target_pairs={{0,4},{4,8},{8,12},{12,16},{16,20},{20,24},{24,28},{1,5},{5,9},{9,... | collective-permute-start | bytes 786440 | tf_op jit(solution)/shard_map/while/body/eval_jaxpr/ppermute | solution.py:19
  150.7 4.0 %collective-permute-done.1 = f32[4,128,128]{2,1,0:T(8,128)S(1)} collective-permute-done((f32[4,128,128]{2,1,0:T(8,128)}, f32[4,128,128]{2,1,0:T(8,128)S(1)}, u32[]{:S(2)}, u32[]{:S(2)}) %collective-permute-start.1) | collective-permute-done | bytes 262176 | tf_op jit(solution)/shard_map/while/body/eval_jaxpr/ppermute | solution.py:19
  154.6 2.4 convolution_add_fusion.43
  160.5 4.5 %collective-permute-start = (f32[4,128,128]{2,1,0:T(8,128)S(1)}, f32[4,128,128]{2,1,0:T(8,128)S(1)}, u32[]{:S(2)}, u32[]{:S(2)}) collective-permute-start(f32[4,128,128]{2,1,0:T(8,128)S(1)} %get-tuple-element.1151), channel_id=1, source_target_pairs={{0,4},{4,8},{8,12},{12,16},{16,20},{20,24},{24,28},{1,5},{5,9},{9,... | collective-permute-start | bytes 786440 | tf_op jit(solution)/shard_map/while/body/eval_jaxpr/ppermute | solution.py:19
  165.0 4.3 %collective-permute-done.1 = f32[4,128,128]{2,1,0:T(8,128)S(1)} collective-permute-done((f32[4,128,128]{2,1,0:T(8,128)}, f32[4,128,128]{2,1,0:T(8,128)S(1)}, u32[]{:S(2)}, u32[]{:S(2)}) %collective-permute-start.1) | collective-permute-done | bytes 262176 | tf_op jit(solution)/shard_map/while/body/eval_jaxpr/ppermute | solution.py:19
  169.3 2.4 convolution_add_fusion.43
  175.1 3.7 %convolution_bitcast_fusion = f32[2048,512]{0,1:T(8,128)} fusion(bf16[128,512]{0,1:T(8,128)(2,1)S(1)} %bitcast.602, bf16[128,2048]{1,0:T(8,128)(2,1)} %all_gather.3), kind=kOutput, calls=%fused_computation.226 | convolution fusion | flops 268435456 | bytes 4849664 | tf_op jit(solution)/shard_map/td,tc->dc/dot_general | solution.py:196
  185.8 99.6 %while.59 = (s32[]{:T(128)}, f32[4,256,128]{2,1,0:T(8,128)S(1)}, f32[2,4,64,128]{3,2,0,1:T(8,128)}, f32[2,4,64,128]{3,2,0,1:T(8,128)}, f32[2,4,64,256]{3,2,0,1:T...) while((s32[]{:T(128)}, f32[4,256,128]{2,1,0:T(8,128)S(1)}, ...), condition=%wide.region_23.24_spmd, body=%wide.region_10.0_spmd.sunk | while | flops 1664381440 | bytes 40054656 | solution.py:88
  193.3 2.2 fusion.614
  243.0 2.2 fusion.614
  (470 shorter events, 173.6 us)
Async XLA Ops:
  7.2 59.2 %copy-start = (bf16[512,2048]{1,0:T(8,128)(2,1)S(1)}, bf16[512,2048]{1,0:T(8,128)(2,1)}, u32[]{:S(2)}) copy-start(bf16[512,2048]{1,0:T(8,128)(2,1)} %param.20) | copy-start | bytes 6291460
  7.2 10.2 %copy-start.35 = (bf16[128,512]{1,0:T(8,128)(2,1)S(1)}, bf16[128,512]{1,0:T(8,128)(2,1)}, u32[]{:S(2)}) copy-start(bf16[128,512]{1,0:T(8,128)(2,1)} %param.16) | copy-start | bytes 393220
  7.2 285.5 %reduce-scatter.5.cloned.1.call-start = ((), (), s32[]{:S(2)}) async-start(), calls=%async_computation.3 | async-start | bytes 4718592 | tf_op jit(solution)/shard_map/reduce_scatter | solution.py:195
  9.8 7.8 %copy-start.40 = (f32[2,128]{1,0:T(2,128)}, f32[2,128]{1,0:T(2,128)S(1)}, u32[]{:S(2)}) copy-start(f32[2,128]{1,0:T(2,128)S(1)} %fusion.154) | copy-start | bytes 3076
  70.6 11.9 %collective-permute-start.1 = (f32[4,128,128]{2,1,0:T(8,128)}, f32[4,128,128]{2,1,0:T(8,128)S(1)}, u32[]{:S(2)}, u32[]{:S(2)}) collective-permute-start(f32[4,128,128]{2,1,0:T(8,128)} %get-tuple-element.1153), channel_id=1, source_target_pairs={{4,0},{8,4},{12,8},{16,12},{20,16},{24,20},{28,24},{5,1},{9,5},{13... | collective-permute-start | bytes 786440 | tf_op jit(solution)/shard_map/while/body/eval_jaxpr/ppermute | solution.py:19
  77.0 7.9 %collective-permute-start = (f32[4,128,128]{2,1,0:T(8,128)S(1)}, f32[4,128,128]{2,1,0:T(8,128)S(1)}, u32[]{:S(2)}, u32[]{:S(2)}) collective-permute-start(f32[4,128,128]{2,1,0:T(8,128)S(1)} %get-tuple-element.1151), channel_id=1, source_target_pairs={{0,4},{4,8},{8,12},{12,16},{16,20},{20,24},{24,28},{1,5},{5,9},{9,... | collective-permute-start | bytes 786440 | tf_op jit(solution)/shard_map/while/body/eval_jaxpr/ppermute | solution.py:19
  86.4 9.6 %collective-permute-start.1 = (f32[4,128,128]{2,1,0:T(8,128)}, f32[4,128,128]{2,1,0:T(8,128)S(1)}, u32[]{:S(2)}, u32[]{:S(2)}) collective-permute-start(f32[4,128,128]{2,1,0:T(8,128)} %get-tuple-element.1153), channel_id=1, source_target_pairs={{4,0},{8,4},{12,8},{16,12},{20,16},{24,20},{28,24},{5,1},{9,5},{13... | collective-permute-start | bytes 786440 | tf_op jit(solution)/shard_map/while/body/eval_jaxpr/ppermute | solution.py:19
  88.3 10.1 %collective-permute-start = (f32[4,128,128]{2,1,0:T(8,128)S(1)}, f32[4,128,128]{2,1,0:T(8,128)S(1)}, u32[]{:S(2)}, u32[]{:S(2)}) collective-permute-start(f32[4,128,128]{2,1,0:T(8,128)S(1)} %get-tuple-element.1151), channel_id=1, source_target_pairs={{0,4},{4,8},{8,12},{12,16},{16,20},{20,24},{24,28},{1,5},{5,9},{9,... | collective-permute-start | bytes 786440 | tf_op jit(solution)/shard_map/while/body/eval_jaxpr/ppermute | solution.py:19
  99.9 11.3 %collective-permute-start.1 = (f32[4,128,128]{2,1,0:T(8,128)}, f32[4,128,128]{2,1,0:T(8,128)S(1)}, u32[]{:S(2)}, u32[]{:S(2)}) collective-permute-start(f32[4,128,128]{2,1,0:T(8,128)} %get-tuple-element.1153), channel_id=1, source_target_pairs={{4,0},{8,4},{12,8},{16,12},{20,16},{24,20},{28,24},{5,1},{9,5},{13... | collective-permute-start | bytes 786440 | tf_op jit(solution)/shard_map/while/body/eval_jaxpr/ppermute | solution.py:19
  101.9 11.8 %collective-permute-start = (f32[4,128,128]{2,1,0:T(8,128)S(1)}, f32[4,128,128]{2,1,0:T(8,128)S(1)}, u32[]{:S(2)}, u32[]{:S(2)}) collective-permute-start(f32[4,128,128]{2,1,0:T(8,128)S(1)} %get-tuple-element.1151), channel_id=1, source_target_pairs={{0,4},{4,8},{8,12},{12,16},{16,20},{20,24},{24,28},{1,5},{5,9},{9,... | collective-permute-start | bytes 786440 | tf_op jit(solution)/shard_map/while/body/eval_jaxpr/ppermute | solution.py:19
  115.1 10.5 %collective-permute-start.1 = (f32[4,128,128]{2,1,0:T(8,128)}, f32[4,128,128]{2,1,0:T(8,128)S(1)}, u32[]{:S(2)}, u32[]{:S(2)}) collective-permute-start(f32[4,128,128]{2,1,0:T(8,128)} %get-tuple-element.1153), channel_id=1, source_target_pairs={{4,0},{8,4},{12,8},{16,12},{20,16},{24,20},{28,24},{5,1},{9,5},{13... | collective-permute-start | bytes 786440 | tf_op jit(solution)/shard_map/while/body/eval_jaxpr/ppermute | solution.py:19
  117.1 10.9 %collective-permute-start = (f32[4,128,128]{2,1,0:T(8,128)S(1)}, f32[4,128,128]{2,1,0:T(8,128)S(1)}, u32[]{:S(2)}, u32[]{:S(2)}) collective-permute-start(f32[4,128,128]{2,1,0:T(8,128)S(1)} %get-tuple-element.1151), channel_id=1, source_target_pairs={{0,4},{4,8},{8,12},{12,16},{16,20},{20,24},{24,28},{1,5},{5,9},{9,... | collective-permute-start | bytes 786440 | tf_op jit(solution)/shard_map/while/body/eval_jaxpr/ppermute | solution.py:19
  129.5 10.8 %collective-permute-start.1 = (f32[4,128,128]{2,1,0:T(8,128)}, f32[4,128,128]{2,1,0:T(8,128)S(1)}, u32[]{:S(2)}, u32[]{:S(2)}) collective-permute-start(f32[4,128,128]{2,1,0:T(8,128)} %get-tuple-element.1153), channel_id=1, source_target_pairs={{4,0},{8,4},{12,8},{16,12},{20,16},{24,20},{28,24},{5,1},{9,5},{13... | collective-permute-start | bytes 786440 | tf_op jit(solution)/shard_map/while/body/eval_jaxpr/ppermute | solution.py:19
  131.4 11.3 %collective-permute-start = (f32[4,128,128]{2,1,0:T(8,128)S(1)}, f32[4,128,128]{2,1,0:T(8,128)S(1)}, u32[]{:S(2)}, u32[]{:S(2)}) collective-permute-start(f32[4,128,128]{2,1,0:T(8,128)S(1)} %get-tuple-element.1151), channel_id=1, source_target_pairs={{0,4},{4,8},{8,12},{12,16},{16,20},{20,24},{24,28},{1,5},{5,9},{9,... | collective-permute-start | bytes 786440 | tf_op jit(solution)/shard_map/while/body/eval_jaxpr/ppermute | solution.py:19
  144.2 10.4 %collective-permute-start.1 = (f32[4,128,128]{2,1,0:T(8,128)}, f32[4,128,128]{2,1,0:T(8,128)S(1)}, u32[]{:S(2)}, u32[]{:S(2)}) collective-permute-start(f32[4,128,128]{2,1,0:T(8,128)} %get-tuple-element.1153), channel_id=1, source_target_pairs={{4,0},{8,4},{12,8},{16,12},{20,16},{24,20},{28,24},{5,1},{9,5},{13... | collective-permute-start | bytes 786440 | tf_op jit(solution)/shard_map/while/body/eval_jaxpr/ppermute | solution.py:19
  146.1 10.9 %collective-permute-start = (f32[4,128,128]{2,1,0:T(8,128)S(1)}, f32[4,128,128]{2,1,0:T(8,128)S(1)}, u32[]{:S(2)}, u32[]{:S(2)}) collective-permute-start(f32[4,128,128]{2,1,0:T(8,128)S(1)} %get-tuple-element.1151), channel_id=1, source_target_pairs={{0,4},{4,8},{8,12},{12,16},{16,20},{20,24},{24,28},{1,5},{5,9},{9,... | collective-permute-start | bytes 786440 | tf_op jit(solution)/shard_map/while/body/eval_jaxpr/ppermute | solution.py:19
  158.5 10.8 %collective-permute-start.1 = (f32[4,128,128]{2,1,0:T(8,128)}, f32[4,128,128]{2,1,0:T(8,128)S(1)}, u32[]{:S(2)}, u32[]{:S(2)}) collective-permute-start(f32[4,128,128]{2,1,0:T(8,128)} %get-tuple-element.1153), channel_id=1, source_target_pairs={{4,0},{8,4},{12,8},{16,12},{20,16},{24,20},{28,24},{5,1},{9,5},{13... | collective-permute-start | bytes 786440 | tf_op jit(solution)/shard_map/while/body/eval_jaxpr/ppermute | solution.py:19
  160.5 11.3 %collective-permute-start = (f32[4,128,128]{2,1,0:T(8,128)S(1)}, f32[4,128,128]{2,1,0:T(8,128)S(1)}, u32[]{:S(2)}, u32[]{:S(2)}) collective-permute-start(f32[4,128,128]{2,1,0:T(8,128)S(1)} %get-tuple-element.1151), channel_id=1, source_target_pairs={{0,4},{4,8},{8,12},{12,16},{16,20},{20,24},{24,28},{1,5},{5,9},{9,... | collective-permute-start | bytes 786440 | tf_op jit(solution)/shard_map/while/body/eval_jaxpr/ppermute | solution.py:19
  178.8 115.8 %reduce-scatter.3.cloned.1.call-start = ((), (), s32[]{:S(2)}) async-start(), calls=%async_computation.2 | async-start | bytes 1310720 | tf_op jit(solution)/shard_map/reduce_scatter | solution.py:189
  204.3 22.1 %copy-start.33 = (f32[4]{0:T(128)}, f32[4]{0:T(128)S(1)}, u32[]{:S(2)}) copy-start(f32[4]{0:T(128)S(1)} %get-tuple-element.1056) | copy-start | bytes 52 | tf_op jit(solution)/shard_map/transpose(jvp())/while
  212.2 11.1 %copy-start.3 = (f32[4,64,384]{2,1,0:T(8,128)}, f32[4,64,384]{2,1,0:T(8,128)S(1)}, u32[]{:S(2)}) copy-start(f32[4,64,384]{2,1,0:T(8,128)S(1)} %fusion.595) | copy-start | bytes 1179652 | tf_op jit(solution)/shard_map/transpose(jvp())/while
  213.5 7.1 %copy-start.5 = (f32[4,64,384]{2,1,0:T(8,128)}, f32[4,64,384]{2,1,0:T(8,128)S(1)}, u32[]{:S(2)}) copy-start(f32[4,64,384]{2,1,0:T(8,128)S(1)} %fusion.596) | copy-start | bytes 1179652 | tf_op jit(solution)/shard_map/transpose(jvp())/while
  225.2 10.5 %copy-start.8 = (f32[2,4,64,128]{3,2,1,0:T(8,128)S(1)}, f32[2,4,64,128]{3,2,1,0:T(8,128)}, u32[]{:S(2)}) copy-start(f32[2,4,64,128]{3,2,1,0:T(8,128)} %copy-done.7) | copy-start | bytes 786436 | tf_op jit(solution)/shard_map/transpose(jvp())/while
  254.0 22.1 %copy-start.33 = (f32[4]{0:T(128)}, f32[4]{0:T(128)S(1)}, u32[]{:S(2)}) copy-start(f32[4]{0:T(128)S(1)} %get-tuple-element.1056) | copy-start | bytes 52 | tf_op jit(solution)/shard_map/transpose(jvp())/while
  262.0 11.1 %copy-start.3 = (f32[4,64,384]{2,1,0:T(8,128)}, f32[4,64,384]{2,1,0:T(8,128)S(1)}, u32[]{:S(2)}) copy-start(f32[4,64,384]{2,1,0:T(8,128)S(1)} %fusion.595) | copy-start | bytes 1179652 | tf_op jit(solution)/shard_map/transpose(jvp())/while
  263.2 7.1 %copy-start.5 = (f32[4,64,384]{2,1,0:T(8,128)}, f32[4,64,384]{2,1,0:T(8,128)S(1)}, u32[]{:S(2)}) copy-start(f32[4,64,384]{2,1,0:T(8,128)S(1)} %fusion.596) | copy-start | bytes 1179652 | tf_op jit(solution)/shard_map/transpose(jvp())/while
  274.9 10.5 %copy-start.8 = (f32[2,4,64,128]{3,2,1,0:T(8,128)S(1)}, f32[2,4,64,128]{3,2,1,0:T(8,128)}, u32[]{:S(2)}) copy-start(f32[2,4,64,128]{3,2,1,0:T(8,128)} %copy-done.7) | copy-start | bytes 786436 | tf_op jit(solution)/shard_map/transpose(jvp())/while
  285.5 6.0 %copy-start.21 = (bf16[128,256]{1,0:T(8,128)(2,1)S(1)}, bf16[128,256]{1,0:T(8,128)(2,1)}, u32[]{:S(2)}) copy-start(bf16[128,256]{1,0:T(8,128)(2,1)} %param.15) | copy-start | bytes 196612
  285.5 6.1 %copy-start.41 = (f32[2,128]{1,0:T(2,128)S(1)}, f32[2,128]{1,0:T(2,128)}, u32[]{:S(2)}) copy-start(f32[2,128]{1,0:T(2,128)} %copy-done.40) | copy-start | bytes 3076
  285.5 6.2 %copy-start.39 = (f32[2,128]{1,0:T(2,128)S(1)}, f32[2,128]{1,0:T(2,128)}, u32[]{:S(2)}) copy-start(f32[2,128]{1,0:T(2,128)} %copy-done.38) | copy-start | bytes 3076
  285.5 6.2 %copy-start.42 = (f32[128,2]{0,1:T(2,128)S(1)}, f32[128,2]{0,1:T(2,128)}, u32[]{:S(2)}) copy-start(f32[128,2]{0,1:T(2,128)} %get-tuple-element.804) | copy-start | bytes 3076
  285.5 6.2 %copy-start.43 = (f32[128,2]{0,1:T(2,128)S(1)}, f32[128,2]{0,1:T(2,128)}, u32[]{:S(2)}) copy-start(f32[128,2]{0,1:T(2,128)} %get-tuple-element.807) | copy-start | bytes 3076
  (65 other events, 177.6 us)
Sparse Core Ops, SparseCore 0:
  178.9 50.8 reduce-scatter.4
  232.8 25.1 reduce-scatter.2
where the time goes:
time: 304 us; the launch traced here: 302 us
  matrix products  107 us (35%)
  starting transfers between devices  48.3 us (16%)
  local copies, waits for them, and re-layouts  46 us (15%)
  other arithmetic  40.1 us (13%)
  waiting for transfers between devices  27.1 us (9%)
  between operations  14.6 us (5%)
  blocking collectives  13.4 us (4%)
  loops' own time  4.69 us (2%)
    ppermute x14, starting transfers between devices, shifted(): return lax.ppermute(value, axis, pairs)  48.2 us
    ppermute x14, waiting for transfers between devices, shifted(): return lax.ppermute(value, axis, pairs)  27 us
    dot_general x7, matrix products, advance(): jnp.einsum('hvk,hjk->hvj', received, transfer, precision=full_precision)  16.9 us
    dot_general x40, matrix products, tri_inverse(): jnp.einsum('hij,hjk->hik', powers, powers, precision=full_precision)  13.9 us
    all_gather x1, blocking collectives, per_device(): full_grad = lax.all_gather(grad_out, 'head', axis=0, tiled=True)  13.4 us
    squeeze x12, local copies, waits for them, and re-layouts, run_blocks(): final_state, outputs = lax.scan(jax.checkpoint(block_step), state, stacked)  13 us
    dot_general x40, matrix products, tri_inverse(): jnp.einsum('hij,hjk->hik', result, identity + powers, precision=full_prec...  12.4 us
    dot_general x8, matrix products, block_step(): jnp.einsum('hck,hvk->hcv', query_blk, state, precision=full_precision)  10.7 us
  transfers between devices with their start and end apart: 16, of which 7 were waited for; matrix products, arithmetic and copies ran while one was open for 42% of the time, Pallas kernels for 0%

commit v1 on v0

v1 whole, which is shorter than its diff:
```python
from functools import partial

import jax
import jax.numpy as jnp
from jax import lax
from jax.experimental import pallas as pl
from jax.experimental.pallas import tpu as pltpu
from jax.sharding import PartitionSpec as P

DK = 128
DV = 128
AUX = 16
EPS = 1e-06
F32 = jnp.float32
BF16 = jnp.bfloat16
VMEM_LIMIT = 56 * 1024 * 1024


def dot(a, b, ca, cb):
    return lax.dot_general(a, b, (((ca,), (cb,)), ((), ())), preferred_element_type=F32)


def halves(x):
    high = x.astype(BF16)
    return high, (x - high.astype(F32)).astype(BF16)


def thirds(x):
    high = x.astype(BF16).astype(F32)
    middle = (x - high).astype(BF16).astype(F32)
    return high, middle, x - high - middle


def mm(a, b, ca=1, cb=0):
    left = jnp.concatenate([a[0], a[0], a[1]], axis=ca)
    right = jnp.concatenate([b[0], b[1], b[0]], axis=cb)
    return dot(left, right, ca, cb)


def iotas(rows, columns):
    shape = (rows, columns)
    return lax.broadcasted_iota(jnp.int32, shape, 0), lax.broadcasted_iota(jnp.int32, shape, 1)


def call(kernel, outs, n_in, smem=(), scratch=()):
    spec = lambda i: pl.BlockSpec(memory_space=pltpu.SMEM if i in smem else pltpu.VMEM)
    return pl.pallas_call(
        kernel,
        out_shape=outs,
        in_specs=[spec(i) for i in range(n_in)],
        out_specs=jax.tree.map(lambda _: pl.BlockSpec(memory_space=pltpu.VMEM), outs),
        scratch_shapes=list(scratch),
        compiler_params=pltpu.CompilerParams(vmem_limit_bytes=VMEM_LIMIT),
    )


def arr(dtype, *shape):
    return jax.ShapeDtypeStruct(shape, dtype)


class Plan:
    def __init__(self, n, tok, hv, hk):
        self.n, self.tok, self.hv, self.hk = n, tok, hv, hk
        self.width = hv * DV // n
        self.padded = -(-self.width // 16) * 16
        self.v_at = 2 * tok
        self.aux_at = 2 * tok + self.padded
        self.rows = self.aux_at + AUX
        self.batch = max(b for b in (1, 2, 4) if n % b == 0)

    def value_head(self, g):
        return g * self.width // DV

    def key_head(self, g):
        return self.value_head(g) * self.hk // self.hv


def aux_rows(rows, columns):
    row_ids = lax.broadcasted_iota(jnp.int32, (AUX, columns), 0)
    out = jnp.zeros((AUX, columns), F32)
    for i, part in enumerate(p for r in rows for p in thirds(r)):
        out = jnp.where(row_ids == i, part, out)
    return out.astype(BF16)


def pack_kernel(plan, q_ref, k_ref, v_ref, rate_ref, decay_ref, out_ref):
    tok = plan.tok
    values = [
        jnp.transpose(v_ref[:, h * DV : (h + 1) * DV].astype(F32)) for h in range(plan.hv)
    ]
    for g in range(plan.n):
        h, kh = plan.value_head(g), plan.key_head(g)
        out_ref[g, :tok] = q_ref[:, kh * DK : (kh + 1) * DK]
        out_ref[g, tok : 2 * tok] = k_ref[:, kh * DK : (kh + 1) * DK]
        first = g * plan.width - h * DV
        piece = values[h][first : first + plan.width]
        if plan.padded > plan.width:
            blank = jnp.zeros((plan.padded - plan.width, tok), F32)
            piece = jnp.concatenate([piece, blank], axis=0)
        out_ref[g, plan.v_at : plan.aux_at] = piece.astype(BF16)
        rows = [rate_ref[h : h + 1, :], decay_ref[h : h + 1, :]]
        out_ref[g, plan.aux_at :] = aux_rows(rows, tok)


def unit(x):
    scale = lax.rsqrt(jnp.sum(x * x, axis=1, keepdims=True) + EPS)
    return x * scale, scale


def segments(off_ref, positions):
    total = jnp.zeros(positions.shape, jnp.int32)
    for j in range(off_ref.shape[0] - 1):
        total = total + (off_ref[j] <= positions).astype(jnp.int32)
    return total


def to_columns(rows, tok):
    row_ids = lax.broadcasted_iota(jnp.int32, (tok, tok), 0)
    stacked = jnp.zeros((tok, tok), F32)
    for i, r in enumerate(rows):
        stacked = jnp.where(row_ids == i, r, stacked)
    turned = jnp.transpose(stacked)
    return [turned[:, i : i + 1] for i in range(len(rows))]


def to_rows(columns, tok):
    column_ids = lax.broadcasted_iota(jnp.int32, (tok, tok), 1)
    stacked = jnp.zeros((tok, tok), F32)
    for i, c in enumerate(columns):
        stacked = jnp.where(column_ids == i, c, stacked)
    turned = jnp.transpose(stacked)
    return [turned[i : i + 1, :] for i in range(len(columns))]


def scalings(plan, off_ref, chunks, auxes):
    tok = plan.tok
    rows, columns = iotas(tok, tok)
    upto = (rows <= columns).astype(BF16)
    sums = [dot(a, upto, 1, 0) for a in auxes]
    rates = [jnp.sum(a[0:3].astype(F32), axis=0, keepdims=True) for a in auxes]
    cumuls = [s[3:4] + s[4:5] + s[5:6] for s in sums]
    turned = to_columns(rates + cumuls, tok)
    out = []
    for i, c in enumerate(chunks):
        b_col, c_col = turned[i], turned[len(chunks) + i]
        c_row = cumuls[i]
        start = c * tok
        seg_col = segments(off_ref, start + rows[:, :1])
        seg_row = segments(off_ref, start + columns[:1, :])
        before = jnp.int32(0)
        last = jnp.int32(0)
        for j in range(off_ref.shape[0] - 1):
            before = before + (off_ref[j] <= start - 1).astype(jnp.int32)
            last = last + (off_ref[j] <= start + tok - 1).astype(jnp.int32)
        c_last = c_row[:, tok - 1 : tok]
        together = (seg_col == seg_row) & (rows >= columns)
        ratio = jnp.where(together, jnp.exp(jnp.where(together, c_col - c_row, 0.0)), 0.0)
        start_col = jnp.where(seg_col == before, jnp.exp(c_col), 0.0)
        end_col = jnp.where(seg_col == last, jnp.exp(c_last - c_col), 0.0)
        whole = jnp.where(last == before, jnp.exp(c_last), 0.0)
        out.append((rates[i], b_col, ratio, start_col, end_col, whole))
    return out


def inverses(lowers):
    size = lowers[0].shape[0]
    rows, columns = iotas(size, size)
    identity = (rows == columns).astype(F32)
    block = min(16, size)
    near = (rows // block) == (columns // block)
    powers = [jnp.where(near, -m, 0.0) for m in lowers]
    results = [identity + p for p in powers]
    split = [halves(p) for p in powers]
    powers = [mm(s, s) for s in split]
    reach = 2
    while reach < block:
        split = [halves(p) for p in powers]
        more = reach * 2 < block
        both = []
        for r, s in zip(results, split):
            left = halves(r)
            if more:
                left = tuple(jnp.concatenate([x, y], axis=0) for x, y in zip(left, s))
            both.append(mm(left, s))
        results = [r + b[:size] for r, b in zip(results, both)]
        if more:
            powers = [b[size:] for b in both]
        reach *= 2
    while block < size:
        across = ((rows // (2 * block)) == (columns // (2 * block))) & (
            (rows // block) > (columns // block)
        )
        split = [halves(r) for r in results]
        middle = [mm(halves(jnp.where(across, m, 0.0)), s) for m, s in zip(lowers, split)]
        results = [r - mm(s, halves(m)) for r, s, m in zip(results, split, middle)]
        block *= 2
    return results


def forward_kernel(
    plan, off_ref, in_ref, out_ref, x_ref, a_ref, w_ref, t_ref, q_ref, ratio_ref, u_ref, s_ref, l_ref, ol_ref
):
    n, tok, width = plan.n, plan.tok, plan.width
    rows, columns = iotas(tok, tok)
    identity = (rows == columns).astype(F32)

    def put(ref, c, pair):
        ref[c, 0], ref[c, 1] = pair

    def group(step, carry):
        chunks = [step * plan.batch + i for i in range(plan.batch)]
        scales = scalings(plan, off_ref, chunks, [in_ref[c, plan.aux_at :] for c in chunks])
        qn = [unit(in_ref[c, :tok].astype(F32))[0] for c in chunks]
        kn = [unit(in_ref[c, tok : 2 * tok].astype(F32))[0] for c in chunks]
        kp = [halves(x) for x in kn]
        qp = [halves(x) for x in qn]
        dots = [
            mm(tuple(jnp.concatenate([a, b], axis=0) for a, b in zip(q, k)), k, 1, 1)
            for q, k in zip(qp, kp)
        ]
        strict = rows > columns
        lowers = [
            jnp.where(strict, s[1] * d[tok:] * s[2], 0.0) for s, d in zip(scales, dots)
        ]
        scores = [d[:tok] * s[2] for s, d in zip(scales, dots)]
        inv = inverses(lowers)
        rated = [halves(x * s[0]) for x, s in zip(inv, scales)]
        w = [mm(x, halves(s[3] * k)) for x, s, k in zip(rated, scales, kn)]
        values = [in_ref[c, plan.v_at : plan.aux_at][:width] for c in chunks]
        u = [
            dot(
                jnp.concatenate([v, v], axis=1), jnp.concatenate(x, axis=1), 1, 1
            )
            for v, x in zip(values, rated)
        ]
        wp = [halves(x) for x in w]
        up = [halves(x) for x in u]
        ap = [halves(x) for x in scores]
        ke = [halves(s[4] * k) for s, k in zip(scales, kn)]
        for i, c in enumerate(chunks):
            put(x_ref, c, halves(inv[i]))
            put(a_ref, c, ap[i])
            put(w_ref, c, wp[i])
            put(t_ref, c, halves(scales[i][5] * identity - mm(wp[i], ke[i], 0, 0)))
            put(q_ref, c, halves(scales[i][3] * qn[i] - mm(ap[i], wp[i])))
            ratio_ref[c] = scales[i][2]
            u_ref[c] = u[i]
            l_ref[c] = mm(up[i], ke[i])
            ol_ref[c] = mm(up[i], ap[i], 1, 1)
        return carry

    lax.fori_loop(0, n // plan.batch, group, 0)
    state = jnp.zeros((width, DK), F32)
    for c in range(n):
        s_ref[c] = state
        pair = halves(state)
        out_ref[c] = (ol_ref[c] + mm(pair, (q_ref[c, 0], q_ref[c, 1]), 1, 1)).astype(BF16)
        state = l_ref[c] + mm(pair, (t_ref[c, 0], t_ref[c, 1]))


def backward_kernel(
    plan, off_ref, in_ref, g_ref, x_ref, a_ref, w_ref, t_ref, q_ref, ratio_ref, u_ref, s_ref, out_ref, e_ref
):
    n, tok, width = plan.n, plan.tok, plan.width
    rows, columns = iotas(tok, tok)
    strict = rows > columns
    upto = (rows >= columns).astype(BF16)

    def get(ref, c):
        return ref[c, 0], ref[c, 1]

    def d_out(c):
        return g_ref[c, :width], g_ref[c, plan.padded : plan.padded + width]

    d_state = jnp.zeros((width, DK), F32)
    for c in reversed(range(n)):
        e_ref[c] = d_state
        d_state = mm(halves(d_state), get(t_ref, c), 1, 1) + mm(d_out(c), get(q_ref, c))

    def cat(pairs, axis):
        return tuple(jnp.concatenate(parts, axis=axis) for parts in zip(*pairs))

    def group(step, carry):
        chunks = [step * plan.batch + i for i in range(plan.batch)]
        scales = scalings(plan, off_ref, chunks, [in_ref[c, plan.aux_at :] for c in chunks])
        qu = [unit(in_ref[c, :tok].astype(F32)) for c in chunks]
        ku = [unit(in_ref[c, tok : 2 * tok].astype(F32)) for c in chunks]
        qp = [halves(x[0]) for x in qu]
        kp = [halves(x[0]) for x in ku]
        do = [d_out(c) for c in chunks]
        s0 = [s_ref[c] for c in chunks]
        ds = [e_ref[c] for c in chunks]
        s0p = [halves(x) for x in s0]
        dsp = [halves(x) for x in ds]
        pseudo = [u_ref[c] - mm(s, get(w_ref, c), 1, 1) for c, s in zip(chunks, s0p)]
        pp = [halves(x) for x in pseudo]
        ke = [halves(s[4] * k[0]) for s, k in zip(scales, ku)]
        dp = [
            mm(o, get(a_ref, c)) + mm(d, k, 1, 1) for c, o, d, k in zip(chunks, do, dsp, ke)
        ]
        dr = [mm(halves(d), get(x_ref, c)) for c, d in zip(chunks, dp)]
        drp = [halves(x) for x in dr]
        big = [
            mm(cat([o, r], 1), cat([p, s], 1), 0, 0) for o, r, p, s in zip(do, drp, pp, s0p)
        ]
        pds = [mm(p, d, 0, 0) for p, d in zip(pp, dsp)]
        da = [b[:tok, :tok] * ratio_ref[c] for b, c in zip(big, chunks)]
        dm = [
            jnp.where(strict, -b[tok:, :tok] * ratio_ref[c], 0.0) for b, c in zip(big, chunks)
        ]
        dap = [halves(x) for x in da]
        dmp = [halves(x) for x in dm]
        dbm = [halves(s[1] * x) for s, x in zip(scales, dm)]
        by_row = [mm(cat([x, y], 0), k) for x, y, k in zip(dap, dmp, kp)]
        by_column = [
            mm(cat([x, y], 0), cat([q, k], 0), 0, 0) for x, y, q, k in zip(dap, dbm, qp, kp)
        ]
        sums = []
        for i, c in enumerate(chunks):
            _, b_col, _, start_col, end_col, whole = scales[i]
            (qn, q_scale), (kn, k_scale) = qu[i], ku[i]
            dqn = by_row[i][:tok] + start_col * big[i][:tok, tok:]
            erase = by_row[i][tok:] - start_col * big[i][tok:, tok:]
            ends = end_col * pds[i]
            write = by_column[i] + ends
            dkn = b_col * erase + write
            s_q = jnp.sum(qn * dqn, axis=1, keepdims=True)
            s_e = jnp.sum(kn * erase, axis=1, keepdims=True)
            s_w = jnp.sum(kn * write, axis=1, keepdims=True)
            total = jnp.sum(jnp.sum(kn * ends, axis=1, keepdims=True), axis=0, keepdims=True)
            both = jnp.sum(jnp.sum(s0[i] * ds[i], axis=1, keepdims=True), axis=0, keepdims=True)
            out_ref[c, :tok] = (q_scale * (dqn - qn * s_q)).astype(BF16)
            out_ref[c, tok : 2 * tok] = (k_scale * (dkn - kn * (b_col * s_e + s_w))).astype(BF16)
            dv = scales[i][0] * dr[i]
            if plan.padded > width:
                dv = jnp.concatenate([dv, jnp.zeros((plan.padded - width, tok), F32)], axis=0)
            out_ref[c, plan.v_at : plan.aux_at] = dv.astype(BF16)
            sums.append((s_e, s_q + b_col * s_e - s_w, total + whole * both))
        turned = to_rows([s[0] for s in sums] + [s[1] for s in sums], tok)
        for i, c in enumerate(chunks):
            values = in_ref[c, plan.v_at : plan.aux_at][:width].astype(F32)
            d_rate = turned[i] + jnp.sum(dr[i] * values, axis=0, keepdims=True)
            parts = dot(aux_rows([turned[len(chunks) + i]], tok), upto, 1, 0)
            d_decay = parts[0:1] + parts[1:2] + parts[2:3] + sums[i][2]
            out_ref[c, plan.aux_at :] = aux_rows([d_rate, d_decay], tok)
        return carry

    lax.fori_loop(0, n // plan.batch, group, 0)


def cotangent_kernel(plan, parts, head_ref, *refs):
    pieces, w_ref, out_ref, all_ref = refs[:parts], refs[parts], refs[parts + 1], refs[parts + 2]
    rows = pieces[0].shape[0]
    for d in range(parts):
        at = lax.rem(head_ref[0] + parts - d, parts)
        all_ref[pl.ds(pl.multiple_of(at * rows, rows), rows), :] = pieces[d][...]
    tok, model = all_ref.shape
    share = model // plan.n
    whole = all_ref[...]
    core = dot(w_ref[...], whole, 1, 1)
    high, low = halves(core)
    width, padded = plan.width, plan.padded
    for g in range(plan.n):
        for i, x in enumerate((core, core - high.astype(F32))):
            piece = x[g * width : (g + 1) * width]
            if padded > width:
                piece = jnp.concatenate([piece, jnp.zeros((padded - width, tok), F32)], axis=0)
            out_ref[g, i * padded : (i + 1) * padded] = piece.astype(BF16)
    turned = jnp.transpose(whole.astype(F32)).astype(BF16)
    for g in range(plan.n):
        out_ref[g, 2 * padded :] = turned[g * share : (g + 1) * share]


def finish_kernel(plan, in_ref, q_ref, k_ref, v_ref, rate_ref, decay_ref):
    tok, n = plan.tok, plan.n
    for kh in range(plan.hk):
        mine = [g for g in range(n) if plan.key_head(g) == kh]
        for ref, at in ((q_ref, 0), (k_ref, tok)):
            total = in_ref[mine[0], at : at + tok].astype(F32)
            for g in mine[1:]:
                total = total + in_ref[g, at : at + tok].astype(F32)
            ref[:, kh * DK : (kh + 1) * DK] = total
    for h in range(plan.hv):
        mine = [g for g in range(n) if plan.value_head(g) == h]
        pieces = [in_ref[g, plan.v_at : plan.aux_at].astype(F32)[: plan.width] for g in mine]
        v_ref[:, h * DV : (h + 1) * DV] = jnp.transpose(jnp.concatenate(pieces, axis=0))
        aux = in_ref[mine[0], plan.aux_at :].astype(F32)
        for g in mine[1:]:
            aux = aux + in_ref[g, plan.aux_at :].astype(F32)
        rate_ref[h : h + 1, :] = aux[0:1] + aux[1:2] + aux[2:3]
        decay_ref[h : h + 1, :] = aux[3:4] + aux[4:5] + aux[5:6]


def exchange(x, axis):
    return lax.all_to_all(x, axis, split_axis=0, concat_axis=0, tiled=True)


def per_device(
    queries, key_vectors, value_rows, write_rate, log_decay, doc_offsets, out_weight, grad_out
):
    n, parts = lax.axis_size("ctx"), lax.axis_size("head")
    tok, hv = queries.shape[0], write_rate.shape[0]
    hk, model = queries.shape[1] // DK, grad_out.shape[1]
    plan = Plan(n, tok, hv, hk)
    width, share = plan.width, model // n

    sent = call(partial(pack_kernel, plan), arr(BF16, n, plan.rows, DK), 5)(
        queries, key_vectors, value_rows, write_rate, log_decay
    )
    got = exchange(sent, "ctx")

    pieces = [grad_out] + [
        lax.ppermute(grad_out, "head", [(i, (i + d) % parts) for i in range(parts)])
        for d in range(1, parts)
    ]
    head = lax.axis_index("head").astype(jnp.int32).reshape(1)
    cot_sent = call(
        partial(cotangent_kernel, plan, parts),
        arr(BF16, n, 2 * plan.padded + share, tok),
        parts + 2,
        smem=(0,),
        scratch=[pltpu.VMEM((tok, model), BF16)],
    )(head, *pieces, out_weight)
    cot = exchange(cot_sent, "ctx")

    pair = lambda r, c: arr(BF16, n, 2, r, c)
    out, x, a, w, t, q, ratio, u, s, _, _ = call(
        partial(forward_kernel, plan),
        (
            arr(BF16, n, width, tok),
            pair(tok, tok),
            pair(tok, tok),
            pair(tok, DK),
            pair(DK, DK),
            pair(tok, DK),
            arr(F32, n, tok, tok),
            arr(F32, n, width, tok),
            arr(F32, n, width, DK),
            arr(F32, n, width, DK),
            arr(F32, n, width, tok),
        ),
        2,
        smem=(0,),
    )(doc_offsets, got)

    mixed = exchange(out, "ctx").reshape(hv * DV, tok)
    projected = dot(mixed, out_weight, 0, 0).astype(BF16)
    layer_parts = exchange(projected, "head").reshape(parts, tok // parts, model)
    layer_out = jnp.sum(layer_parts.astype(F32), axis=0)

    all_mixed = lax.all_gather(out, "ctx", axis=0)
    grads = cot[:, 2 * plan.padded :]
    weight_grad = jnp.einsum(
        "cdt,gcvt->dgv", grads, all_mixed, preferred_element_type=F32
    ).reshape(share, hv * DV)

    back_sent = call(
        partial(backward_kernel, plan),
        arr(BF16, n, plan.rows, DK),
        11,
        smem=(0,),
        scratch=[pltpu.VMEM((n, width, DK), F32)],
    )(doc_offsets, got, cot, x, a, w, t, q, ratio, u, s)
    back = exchange(back_sent, "ctx")
    grad_q, grad_k, grad_v, grad_rate, grad_decay = call(
        partial(finish_kernel, plan),
        (
            arr(F32, tok, hk * DK),
            arr(F32, tok, hk * DK),
            arr(F32, tok, hv * DV),
            arr(F32, hv, tok),
            arr(F32, hv, tok),
        ),
        1,
    )(back)
    return (layer_out, grad_q, grad_k, grad_v, grad_rate, grad_decay, weight_grad)


def solution(mesh):
    placed = (
        P("ctx", "head"),
        P("ctx", "head"),
        P("ctx", "head"),
        P("head", "ctx"),
        P("head", "ctx"),
        P(),
        P("head", None),
        P(("ctx", "head"), None),
    )
    return jax.shard_map(
        per_device,
        mesh=mesh,
        in_specs=placed,
        out_specs=(
            P(("ctx", "head"), None),
            P("ctx", "head"),
            P("ctx", "head"),
            P("ctx", "head"),
            P("head", "ctx"),
            P("head", "ctx"),
            P("ctx", "head"),
        ),
        check_vma=False,
    )
```

time: 304 us -> 107 us (0.35)
  the two profiles are of different devices: /device:TPU:11 before, /device:TPU:0 now
where the time goes in v1:
time: 107 us; the launch traced here: 106 us
  waiting for transfers between devices  31.6 us (30%)
  starting transfers between devices  27.7 us (26%)
  Pallas kernels  27 us (25%)
  between operations  14.1 us (13%)
  matrix products  2.97 us (3%)
  local copies, waits for them, and re-layouts  1.68 us (2%)
    all_to_all x5, waiting for transfers between devices, exchange(): return lax.all_to_all(x, axis, split_axis=0, concat_axis=0, tiled=True)  24 us
    all_to_all x5, starting transfers between devices, exchange(): return lax.all_to_all(x, axis, split_axis=0, concat_axis=0, tiled=True)  21.1 us
    pallas_call x1, Pallas kernels, per_device(): call(partial(forward_kernel, plan), (arr(BF16, n, width, tok), pair(tok,...  9.95 us
    pallas_call x1, Pallas kernels, per_device(): call(partial(backward_kernel, plan), arr(BF16, n, plan.rows, DK), 11, sme...  9.57 us
    ppermute x3, waiting for transfers between devices, per_device(): lax.ppermute(grad_out, 'head', [(i, (i + d) % parts) for i in range(parts)])  7.53 us
    ppermute x3, starting transfers between devices, per_device(): lax.ppermute(grad_out, 'head', [(i, (i + d) % parts) for i in range(parts)])  6.48 us
    pallas_call x1, Pallas kernels, per_device(): call(partial(cotangent_kernel, plan, parts), arr(BF16, n, 2 * plan.padded...  3.53 us
  transfers between devices with their start and end apart: 9, of which 5 were waited for; matrix products, arithmetic and copies ran while one was open for 2% of the time, Pallas kernels for 24%

profile of v1, /device:TPU:0, one launch (start us, length us, event | category | flops | bytes accessed | tf_op | source)
XLA Modules:
  0.0 105.8 jit_solution(5544655629816562257)
XLA Ops:
  7.2 0.0 copy-start.4
  7.2 2.0 %shard_map.135 = bf16[8,336,128]{2,1,0:T(8,128)(2,1)} custom-call(bf16[128,256]{1,0:T(8,128)(2,1)} %q_ref.1, bf16[128,256]{1,0:T(8,128)(2,1)} %k_ref.1, bf16[128,512]{1,0:T(8,128)(2,1)} %v_ref.1, f32[4,128]{1,0:T(4,128)} %rate_ref.1, f32[4,128]{1,0:T(4,128)} %decay_ref.1), custom_call_target="tpu_custom_call" | custom-call | tf_op jit(solution)/shard_map/pallas_call | solution.py:407
  9.2 5.2 %all-to-all-start = ((bf16[8,336,128]{2,1,0:T(8,128)(2,1)}), bf16[8,336,128]{2,1,0:T(8,128)(2,1)S(1)}, u32[]{:S(2)}, u32[]{:S(2)}) async-start(bf16[8,336,128]{2,1,0:T(8,128)(2,1)} %shard_map.135), calls=%async_computation | async-start | bytes 1376256 | tf_op jit(solution)/shard_map/all_to_all | solution.py:395
  14.4 0.0 copy-done.4
  14.4 2.7 %collective-permute-start.1 = (bf16[32,2048]{1,0:T(8,128)(2,1)S(1)}, bf16[32,2048]{1,0:T(8,128)(2,1)S(1)}, u32[]{:S(2)}, u32[]{:S(2)}) collective-permute-start(bf16[32,2048]{1,0:T(8,128)(2,1)S(1)} %copy-done.4), channel_id=1, source_target_pairs={{0,2},{1,3},{2,0},{3,1},{4,6},{5,7},{6,4},{7,5},{8,10},{9,11},{10,... | collective-permute-start | bytes 393224 | tf_op jit(solution)/shard_map/ppermute | solution.py:413
  17.0 1.6 %collective-permute-start = (bf16[32,2048]{1,0:T(8,128)(2,1)S(1)}, bf16[32,2048]{1,0:T(8,128)(2,1)S(1)}, u32[]{:S(2)}, u32[]{:S(2)}) collective-permute-start(bf16[32,2048]{1,0:T(8,128)(2,1)S(1)} %copy-done.4), channel_id=1, source_target_pairs={{0,1},{1,2},{2,3},{3,0},{4,5},{5,6},{6,7},{7,4},{8,9},{9,10},{10,1... | collective-permute-start | bytes 393224 | tf_op jit(solution)/shard_map/ppermute | solution.py:413
  18.6 2.2 %collective-permute-start.2 = (bf16[32,2048]{1,0:T(8,128)(2,1)S(1)}, bf16[32,2048]{1,0:T(8,128)(2,1)S(1)}, u32[]{:S(2)}, u32[]{:S(2)}) collective-permute-start(bf16[32,2048]{1,0:T(8,128)(2,1)S(1)} %copy-done.4), channel_id=1, source_target_pairs={{0,3},{1,0},{2,1},{3,2},{4,7},{5,4},{6,5},{7,6},{8,11},{9,8},{10,9... | collective-permute-start | bytes 393224 | tf_op jit(solution)/shard_map/ppermute | solution.py:413
  20.8 6.5 %collective-permute-done.1.refs_2_ = bf16[32,2048]{1,0:T(8,128)(2,1)S(1)} collective-permute-done((bf16[32,2048]{1,0:T(8,128)(2,1)S(1)}, bf16[32,2048]{1,0:T(8,128)(2,1)S(1)}, u32[]{:S(2)}, u32[]{:S(2)}) %collective-permute-start.1) | collective-permute-done | bytes 131104 | tf_op jit(solution)/shard_map/ppermute | solution.py:413
  27.3 0.0 collective-permute-done.refs_1_
  27.3 1.1 %collective-permute-done.2.refs_3_ = bf16[32,2048]{1,0:T(8,128)(2,1)S(1)} collective-permute-done((bf16[32,2048]{1,0:T(8,128)(2,1)S(1)}, bf16[32,2048]{1,0:T(8,128)(2,1)S(1)}, u32[]{:S(2)}, u32[]{:S(2)}) %collective-permute-start.2) | collective-permute-done | bytes 131104 | tf_op jit(solution)/shard_map/ppermute | solution.py:413
  28.4 0.0 copy-done.5
  28.4 0.6 copy-done.7
  29.0 3.5 %shard_map.137 = bf16[8,384,128]{2,1,0:T(8,128)(2,1)} custom-call(s32[1]{0:T(128)} %bitcast.2.head_ref, bf16[32,2048]{1,0:T(8,128)(2,1)} %refs_0_.1, bf16[32,2048]{1,0:T(8,128)(2,1)} %copy-done.6, bf16[32,2048]{1,0:T(8,128)(2,1)} %copy-done.5, bf16[32,2048]{1,0:T(8,128)(2,1)} %copy-done.7, bf16[512,2048]{1,0:T(8,128)(2,1)} %refs_4_.1), custom_call_target="tpu_custom_call" | custom-call | tf_op jit(solution)/shard_map/pallas_call | solution.py:417
  32.6 0.0 all-to-all-done.in_ref
  32.6 3.8 %all-to-all-start.3 = ((bf16[8,384,128]{2,1,0:T(8,128)(2,1)}), bf16[8,384,128]{2,1,0:T(8,128)(2,1)S(1)}, u32[]{:S(2)}, u32[]{:S(2)}) async-start(bf16[8,384,128]{2,1,0:T(8,128)(2,1)} %shard_map.137), calls=%async_computation.3 | async-start | bytes 1572864 | tf_op jit(solution)/shard_map/all_to_all | solution.py:395
  36.4 0.0 all-gather.3.cloned.1.call-start
  36.5 9.9 %shard_map.136 = (bf16[8,64,128]{2,1,0:T(8,128)(2,1)}, bf16[8,2,128,128]{3,2,1,0:T(8,128)(2,1)}, bf16[8,2,128,128]{3,2,1,0:T(8,128)(2,1)}, bf16[8,2,128,128]{3,2...) custom-call(s32[5]{0:T(128)} %off_ref.3, ...), custom_call_target="tpu_custom_call" | custom-call | tf_op jit(solution)/shard_map/pallas_call | solution.py:427
  46.4 0.0 all-gather.3.cloned.1.call-update
  46.4 2.6 %all-to-all-done.3.g_ref = bf16[8,384,128]{2,1,0:T(8,128)(2,1)S(1)} async-done(((bf16[8,384,128]{2,1,0:T(8,128)(2,1)}), bf16[8,384,128]{2,1,0:T(8,128)(2,1)S(1)}, u32[]{:S(2)}, u32[]{:S(2)}) %all-to-all-start.3) | async-done | bytes 786464 | tf_op jit(solution)/shard_map/all_to_all | solution.py:395
  49.0 3.4 %all-to-all-start.1 = ((bf16[8,64,128]{2,1,0:T(8,128)(2,1)}), bf16[8,64,128]{2,1,0:T(8,128)(2,1)S(1)}, u32[]{:S(2)}, u32[]{:S(2)}) async-start(bf16[8,64,128]{2,1,0:T(8,128)(2,1)} %get-tuple-element.21), calls=%async_computation.1 | async-start | bytes 262144 | tf_op jit(solution)/shard_map/all_to_all | solution.py:395
  52.4 0.0 copy-start
  52.4 9.6 %shard_map.138 = bf16[8,336,128]{2,1,0:T(8,128)(2,1)} custom-call(s32[5]{0:T(128)} %off_ref.3, bf16[8,336,128]{2,1,0:T(8,128)(2,1)} %copy-done.1, bf16[8,384,128]{2,1,0:T(8,128)(2,1)} %copy-done.2, bf16[8,2,128,128]{3,2,1,0:T(8,128)(2,1)} %get-tuple-element.22.x_ref, bf16[8,2,128,128]{3,2,1,0:T(8,128)(2,1)} %get-tuple-element.23.a_ref, ...), custom_call_target="tpu_custom_call" | custom-call | tf_op jit(solution)/shard_map/pallas_call | solution.py:457
  62.0 0.0 all-to-all-done.1
  62.0 4.2 %all-to-all-start.4 = ((bf16[8,336,128]{2,1,0:T(8,128)(2,1)}), bf16[8,336,128]{2,1,0:T(8,128)(2,1)}, u32[]{:S(2)}, u32[]{:S(2)}) async-start(bf16[8,336,128]{2,1,0:T(8,128)(2,1)} %shard_map.138), calls=%async_computation.4 | async-start | bytes 1376256 | tf_op jit(solution)/shard_map/all_to_all | solution.py:395
  66.2 1.3 %convolution_convert_fusion = bf16[128,2048]{1,0:T(8,128)(2,1)} fusion(bf16[512,128]{1,0:T(8,128)(2,1)S(1)} %bitcast.15, bf16[512,2048]{1,0:T(8,128)(2,1)S(1)} %copy-done), kind=kOutput, calls=%fused_computation | convolution fusion | flops 268697600 | bytes 2752512 | tf_op jit(solution)/shard_map/dot_general | solution.py:20
  67.5 11.4 %all-to-all-done.4.in_ref = bf16[8,336,128]{2,1,0:T(8,128)(2,1)} async-done(((bf16[8,336,128]{2,1,0:T(8,128)(2,1)}), bf16[8,336,128]{2,1,0:T(8,128)(2,1)}, u32[]{:S(2)}, u32[]{:S(2)}) %all-to-all-start.4) | async-done | bytes 688160 | tf_op jit(solution)/shard_map/all_to_all | solution.py:395
  78.9 4.6 %all-to-all-start.2 = ((bf16[4,32,2048]{2,1,0:T(8,128)(2,1)}), bf16[4,32,2048]{2,1,0:T(8,128)(2,1)S(1)}, u32[]{:S(2)}, u32[]{:S(2)}) async-start(bf16[4,32,2048]{2,1,0:T(8,128)(2,1)} %bitcast.1), calls=%async_computation.2 | async-start | bytes 1048576 | tf_op jit(solution)/shard_map/all_to_all | solution.py:395
  83.5 2.0 %shard_map.139 = (f32[128,256]{1,0:T(8,128)}, f32[128,256]{1,0:T(8,128)}, f32[128,512]{1,0:T(8,128)}, f32[4,128]{1,0:T(4,128)}, f32[4,128]{1,0:T(4,128)}) custom-call(bf16[8,336,128]{2,1,0:T(8,128)(2,1)} %all-to-all-done.4.in_ref), custom_call_target="tpu_custom_call" | custom-call | tf_op jit(solution)/shard_map/pallas_call | solution.py:465
  85.4 10.0 %all-to-all-done.2 = bf16[4,32,2048]{2,1,0:T(8,128)(2,1)S(1)} async-done(((bf16[4,32,2048]{2,1,0:T(8,128)(2,1)}), bf16[4,32,2048]{2,1,0:T(8,128)(2,1)S(1)}, u32[]{:S(2)}, u32[]{:S(2)}) %all-to-all-start.2) | async-done | bytes 524320 | tf_op jit(solution)/shard_map/all_to_all | solution.py:395
  95.5 0.8 convert_reduce_fusion
  96.2 1.7 %fusion = f32[256,8,64,1]{0,2,3,1:T(8,128)S(1)} fusion(bf16[8,8,64,128]{3,2,1,0:T(8,128)(2,1)} %bitcast.16, bf16[8,384,128]{2,1,0:T(8,128)(2,1)S(1)} %copy-done.3), kind=kOutput, calls=%fused_computation.3 | convolution fusion | flops 268435456 | bytes 2097152 | tf_op jit(solution)/shard_map/cdt,gcvt->dgv/dot_general | solution.py:453
  98.0 1.0 copy.16
  (12 shorter events, 0.0 us)
Async XLA Ops:
  7.2 7.2 %copy-start.4 = (bf16[32,2048]{1,0:T(8,128)(2,1)S(1)}, bf16[32,2048]{1,0:T(8,128)(2,1)}, u32[]{:S(2)}) copy-start(bf16[32,2048]{1,0:T(8,128)(2,1)} %refs_0_.1) | copy-start | bytes 393220
  9.2 23.4 %all-to-all-start = ((bf16[8,336,128]{2,1,0:T(8,128)(2,1)}), bf16[8,336,128]{2,1,0:T(8,128)(2,1)S(1)}, u32[]{:S(2)}, u32[]{:S(2)}) async-start(bf16[8,336,128]{2,1,0:T(8,128)(2,1)} %shard_map.135), calls=%async_computation | async-start | bytes 1376256 | tf_op jit(solution)/shard_map/all_to_all | solution.py:395
  14.4 12.9 %collective-permute-start.1 = (bf16[32,2048]{1,0:T(8,128)(2,1)S(1)}, bf16[32,2048]{1,0:T(8,128)(2,1)S(1)}, u32[]{:S(2)}, u32[]{:S(2)}) collective-permute-start(bf16[32,2048]{1,0:T(8,128)(2,1)S(1)} %copy-done.4), channel_id=1, source_target_pairs={{0,2},{1,3},{2,0},{3,1},{4,6},{5,7},{6,4},{7,5},{8,10},{9,11},{10,... | collective-permute-start | bytes 393224 | tf_op jit(solution)/shard_map/ppermute | solution.py:413
  17.0 10.3 %collective-permute-start = (bf16[32,2048]{1,0:T(8,128)(2,1)S(1)}, bf16[32,2048]{1,0:T(8,128)(2,1)S(1)}, u32[]{:S(2)}, u32[]{:S(2)}) collective-permute-start(bf16[32,2048]{1,0:T(8,128)(2,1)S(1)} %copy-done.4), channel_id=1, source_target_pairs={{0,1},{1,2},{2,3},{3,0},{4,5},{5,6},{6,7},{7,4},{8,9},{9,10},{10,1... | collective-permute-start | bytes 393224 | tf_op jit(solution)/shard_map/ppermute | solution.py:413
  18.6 9.8 %collective-permute-start.2 = (bf16[32,2048]{1,0:T(8,128)(2,1)S(1)}, bf16[32,2048]{1,0:T(8,128)(2,1)S(1)}, u32[]{:S(2)}, u32[]{:S(2)}) collective-permute-start(bf16[32,2048]{1,0:T(8,128)(2,1)S(1)} %copy-done.4), channel_id=1, source_target_pairs={{0,3},{1,0},{2,1},{3,2},{4,7},{5,4},{6,5},{7,6},{8,11},{9,8},{10,9... | collective-permute-start | bytes 393224 | tf_op jit(solution)/shard_map/ppermute | solution.py:413
  27.3 1.1 %copy-start.5 = (bf16[32,2048]{1,0:T(8,128)(2,1)}, bf16[32,2048]{1,0:T(8,128)(2,1)S(1)}, u32[]{:S(2)}) copy-start(bf16[32,2048]{1,0:T(8,128)(2,1)S(1)} %collective-permute-done.1.refs_2_) | copy-start | bytes 393220
  27.3 1.1 %copy-start.6 = (bf16[32,2048]{1,0:T(8,128)(2,1)}, bf16[32,2048]{1,0:T(8,128)(2,1)S(1)}, u32[]{:S(2)}) copy-start(bf16[32,2048]{1,0:T(8,128)(2,1)S(1)} %collective-permute-done.refs_1_) | copy-start | bytes 393220
  28.4 0.7 copy-start.7
  32.6 3.9 %copy-start.1 = (bf16[8,336,128]{2,1,0:T(8,128)(2,1)}, bf16[8,336,128]{2,1,0:T(8,128)(2,1)S(1)}, u32[]{:S(2)}) copy-start(bf16[8,336,128]{2,1,0:T(8,128)(2,1)S(1)} %all-to-all-done.in_ref) | copy-start | bytes 2064388
  32.6 16.4 %all-to-all-start.3 = ((bf16[8,384,128]{2,1,0:T(8,128)(2,1)}), bf16[8,384,128]{2,1,0:T(8,128)(2,1)S(1)}, u32[]{:S(2)}, u32[]{:S(2)}) async-start(bf16[8,384,128]{2,1,0:T(8,128)(2,1)} %shard_map.137), calls=%async_computation.3 | async-start | bytes 1572864 | tf_op jit(solution)/shard_map/all_to_all | solution.py:395
  36.4 59.8 %all-gather.3.cloned.1.call-start = ((), (), s32[]{:S(2)}) async-start(), calls=%async_computation.5 | async-start | bytes 1179648 | tf_op jit(solution)/shard_map/all_gather | solution.py:451
  49.0 3.4 %copy-start.2 = (bf16[8,384,128]{2,1,0:T(8,128)(2,1)}, bf16[8,384,128]{2,1,0:T(8,128)(2,1)S(1)}, u32[]{:S(2)}) copy-start(bf16[8,384,128]{2,1,0:T(8,128)(2,1)S(1)} %all-to-all-done.3.g_ref) | copy-start | bytes 2359300
  49.0 13.0 %all-to-all-start.1 = ((bf16[8,64,128]{2,1,0:T(8,128)(2,1)}), bf16[8,64,128]{2,1,0:T(8,128)(2,1)S(1)}, u32[]{:S(2)}, u32[]{:S(2)}) async-start(bf16[8,64,128]{2,1,0:T(8,128)(2,1)} %get-tuple-element.21), calls=%async_computation.1 | async-start | bytes 262144 | tf_op jit(solution)/shard_map/all_to_all | solution.py:395
  52.4 13.8 %copy-start = (bf16[512,2048]{1,0:T(8,128)(2,1)S(1)}, bf16[512,2048]{1,0:T(8,128)(2,1)}, u32[]{:S(2)}) copy-start(bf16[512,2048]{1,0:T(8,128)(2,1)} %refs_4_.1) | copy-start | bytes 6291460
  62.0 16.9 %all-to-all-start.4 = ((bf16[8,336,128]{2,1,0:T(8,128)(2,1)}), bf16[8,336,128]{2,1,0:T(8,128)(2,1)}, u32[]{:S(2)}, u32[]{:S(2)}) async-start(bf16[8,336,128]{2,1,0:T(8,128)(2,1)} %shard_map.138), calls=%async_computation.4 | async-start | bytes 1376256 | tf_op jit(solution)/shard_map/all_to_all | solution.py:395
  66.2 30.0 %copy-start.3 = (bf16[8,384,128]{2,1,0:T(8,128)(2,1)S(1)}, bf16[8,384,128]{2,1,0:T(8,128)(2,1)}, u32[]{:S(2)}) copy-start(bf16[8,384,128]{2,1,0:T(8,128)(2,1)} %copy-done.2) | copy-start | bytes 2359300
  78.9 16.5 %all-to-all-start.2 = ((bf16[4,32,2048]{2,1,0:T(8,128)(2,1)}), bf16[4,32,2048]{2,1,0:T(8,128)(2,1)S(1)}, u32[]{:S(2)}, u32[]{:S(2)}) async-start(bf16[4,32,2048]{2,1,0:T(8,128)(2,1)} %bitcast.1), calls=%async_computation.2 | async-start | bytes 1048576 | tf_op jit(solution)/shard_map/all_to_all | solution.py:395
Sparse Core Ops, SparseCore 0:
  46.6 26.7 all-gather.2

commit v2 on v1

--- a/solution.py
+++ b/solution.py
@@ -254,7 +254,12 @@
     for c in range(n):
         s_ref[c] = state
         pair = halves(state)
-        out_ref[c] = (ol_ref[c] + mm(pair, (q_ref[c, 0], q_ref[c, 1]), 1, 1)).astype(BF16)
+        core = ol_ref[c] + mm(pair, (q_ref[c, 0], q_ref[c, 1]), 1, 1)
+        if plan.padded > width:
+            core = jnp.concatenate([core, jnp.zeros((plan.padded - width, tok), F32)], axis=0)
+        core = core.astype(BF16)
+        for g in range(n):
+            out_ref[g, (c - g) % n] = core
         state = l_ref[c] + mm(pair, (t_ref[c, 0], t_ref[c, 1]))
 
 
@@ -348,15 +353,10 @@
     lax.fori_loop(0, n // plan.batch, group, 0)
 
 
-def cotangent_kernel(plan, parts, head_ref, *refs):
-    pieces, w_ref, out_ref, all_ref = refs[:parts], refs[parts], refs[parts + 1], refs[parts + 2]
-    rows = pieces[0].shape[0]
-    for d in range(parts):
-        at = lax.rem(head_ref[0] + parts - d, parts)
-        all_ref[pl.ds(pl.multiple_of(at * rows, rows), rows), :] = pieces[d][...]
-    tok, model = all_ref.shape
+def cotangent_kernel(plan, grad_ref, w_ref, out_ref):
+    whole = grad_ref[...]
+    tok, model = whole.shape
     share = model // plan.n
-    whole = all_ref[...]
     core = dot(w_ref[...], whole, 1, 1)
     high, low = halves(core)
     width, padded = plan.width, plan.padded
@@ -391,6 +391,27 @@
         decay_ref[h : h + 1, :] = aux[3:4] + aux[4:5] + aux[5:6]
 
 
+def all_columns(plan, pieces):
+    if plan.padded > plan.width:
+        pieces = [p.astype(F32)[: plan.width] for p in pieces]
+    return jnp.concatenate(pieces, axis=0).astype(BF16)
+
+
+def project_kernel(plan, mixed_ref, w_ref, out_ref):
+    mixed = all_columns(plan, [mixed_ref[g, 0] for g in range(plan.n)])
+    out_ref[...] = dot(mixed, w_ref[...], 0, 0).astype(BF16)
+
+
+def weight_kernel(plan, place_ref, cot_ref, mixed_ref, out_ref):
+    total = None
+    for step in range(plan.n):
+        chunk = lax.rem(place_ref[0] + step, plan.n)
+        mixed = all_columns(plan, [mixed_ref[g, step] for g in range(plan.n)])
+        part = dot(cot_ref[chunk, 2 * plan.padded :], mixed, 1, 1)
+        total = part if total is None else total + part
+    out_ref[...] = total
+
+
 def exchange(x, axis):
     return lax.all_to_all(x, axis, split_axis=0, concat_axis=0, tiled=True)
 
@@ -409,25 +430,18 @@
     )
     got = exchange(sent, "ctx")
 
-    pieces = [grad_out] + [
-        lax.ppermute(grad_out, "head", [(i, (i + d) % parts) for i in range(parts)])
-        for d in range(1, parts)
-    ]
-    head = lax.axis_index("head").astype(jnp.int32).reshape(1)
+    copies = jnp.broadcast_to(grad_out[None], (parts,) + grad_out.shape)
+    whole_grad = exchange(copies, "head").reshape(tok, model)
     cot_sent = call(
-        partial(cotangent_kernel, plan, parts),
-        arr(BF16, n, 2 * plan.padded + share, tok),
-        parts + 2,
-        smem=(0,),
-        scratch=[pltpu.VMEM((tok, model), BF16)],
-    )(head, *pieces, out_weight)
+        partial(cotangent_kernel, plan), arr(BF16, n, 2 * plan.padded + share, tok), 2
+    )(whole_grad, out_weight)
     cot = exchange(cot_sent, "ctx")
 
     pair = lambda r, c: arr(BF16, n, 2, r, c)
     out, x, a, w, t, q, ratio, u, s, _, _ = call(
         partial(forward_kernel, plan),
         (
-            arr(BF16, n, width, tok),
+            arr(BF16, n, n, plan.padded, tok),
             pair(tok, tok),
             pair(tok, tok),
             pair(tok, DK),
@@ -443,17 +457,7 @@
         smem=(0,),
     )(doc_offsets, got)
 
-    mixed = exchange(out, "ctx").reshape(hv * DV, tok)
-    projected = dot(mixed, out_weight, 0, 0).astype(BF16)
-    layer_parts = exchange(projected, "head").reshape(parts, tok // parts, model)
-    layer_out = jnp.sum(layer_parts.astype(F32), axis=0)
-
-    all_mixed = lax.all_gather(out, "ctx", axis=0)
-    grads = cot[:, 2 * plan.padded :]
-    weight_grad = jnp.einsum(
-        "cdt,gcvt->dgv", grads, all_mixed, preferred_element_type=F32
-    ).reshape(share, hv * DV)
-
+    mixed = exchange(out, "ctx")
     back_sent = call(
         partial(backward_kernel, plan),
         arr(BF16, n, plan.rows, DK),
@@ -462,6 +466,22 @@
         scratch=[pltpu.VMEM((n, width, DK), F32)],
     )(doc_offsets, got, cot, x, a, w, t, q, ratio, u, s)
     back = exchange(back_sent, "ctx")
+    block = pl.BlockSpec((n, 1, plan.padded, tok), lambda i: (0, 0, 0, 0))
+    projected = pl.pallas_call(
+        partial(project_kernel, plan),
+        out_shape=arr(BF16, tok, model),
+        grid=(1,),
+        in_specs=[block, pl.BlockSpec(out_weight.shape, lambda i: (0, 0))],
+        out_specs=pl.BlockSpec((tok, model), lambda i: (0, 0)),
+        compiler_params=pltpu.CompilerParams(vmem_limit_bytes=VMEM_LIMIT),
+    )(mixed, out_weight)
+    layer_parts = exchange(projected, "head").reshape(parts, tok // parts, model)
+    layer_out = jnp.sum(layer_parts.astype(F32), axis=0)
+    place = lax.axis_index("ctx").astype(jnp.int32).reshape(1)
+    weight_grad = call(
+        partial(weight_kernel, plan), arr(F32, share, hv * DV), 3, smem=(0,)
+    )(place, cot, mixed)
+
     grad_q, grad_k, grad_v, grad_rate, grad_decay = call(
         partial(finish_kernel, plan),
         (

time: 107 us -> 106 us (level)
  between operations: 14.1 us -> 0.71 us
  waiting for transfers between devices: 31.6 us -> 44.2 us
  Pallas kernels: 27 us -> 32.9 us
  starting transfers between devices: 27.7 us -> 24.2 us
  matrix products: 2.97 us -> 0 us
    all_to_all x5 -> x6, waiting for transfers between devices: 24 us -> 44.2 us  [exchange(): return lax.all_to_all(x, axis, split_axis=0, concat_axis=0, tiled=True)]
    ppermute x3 -> x0, waiting for transfers between devices: 7.53 us -> none  [per_device(): lax.ppermute(grad_out, 'head', [(i, (i + d) % parts) for i in range(parts)])]
    ppermute x3 -> x0, starting transfers between devices: 6.48 us -> none  [per_device(): lax.ppermute(grad_out, 'head', [(i, (i + d) % parts) for i in range(parts)])]
    pallas_call x2 -> x4, Pallas kernels: 13.5 us -> 19.6 us  [the longest x1 10.3 us: per_device(): call(partial(forward_kernel, plan), (arr(BF16, n, n, plan.padded, tok), p...]
    all_to_all x5 -> x6, starting transfers between devices: 21.1 us -> 24.2 us  [exchange(): return lax.all_to_all(x, axis, split_axis=0, concat_axis=0, tiled=True)]
    dot_general x2 -> x0, matrix products: 2.97 us -> none  [the longest x1 1.7 us: per_device(): jnp.einsum('cdt,gcvt->dgv', grads, all_mixed, preferred_element_type=F32)]
    broadcast_in_dim x0 -> x1, local copies, waits for them, and re-layouts: none -> 1.75 us  [per_device(): copies = jnp.broadcast_to(grad_out[None], (parts,) + grad_out.shape)]
    unnamed x17 -> x10, local copies, waits for them, and re-layouts: 1.68 us -> 0.02 us
  transfers between devices with their start and end apart: 9 -> 6, of which waited for: 5 -> 6; matrix products, arithmetic and copies ran while one was open for 2% -> 0% of each run, Pallas kernels for 24% -> 31%
where the time goes in v2:
time: 106 us; the launch traced here: 105 us
  waiting for transfers between devices  44.2 us (42%)
  Pallas kernels  32.9 us (31%)
  starting transfers between devices  24.2 us (23%)
  local copies, waits for them, and re-layouts  1.77 us (2%)
    all_to_all x6, waiting for transfers between devices, exchange(): return lax.all_to_all(x, axis, split_axis=0, concat_axis=0, tiled=True)  44.2 us
    all_to_all x6, starting transfers between devices, exchange(): return lax.all_to_all(x, axis, split_axis=0, concat_axis=0, tiled=True)  24.2 us
    pallas_call x1, Pallas kernels, per_device(): call(partial(forward_kernel, plan), (arr(BF16, n, n, plan.padded, tok), p...  10.3 us
    pallas_call x1, Pallas kernels, per_device(): call(partial(backward_kernel, plan), arr(BF16, n, plan.rows, DK), 11, sme...  9.41 us
    pallas_call x1, Pallas kernels, per_device(): call(partial(cotangent_kernel, plan), arr(BF16, n, 2 * plan.padded + shar...  3.41 us
    pallas_call x1, Pallas kernels, per_device(): call(partial(weight_kernel, plan), arr(F32, share, hv * DV), 3, smem=(0,))  2.96 us
    pallas_call x1, Pallas kernels, per_device(): pl.pallas_call(partial(project_kernel, plan), out_shape=arr(BF16, tok, mo...  2.94 us
  transfers between devices with their start and end apart: 6, of which 6 were waited for; matrix products, arithmetic and copies ran while one was open for 0% of the time, Pallas kernels for 31%

profile of v2, /device:TPU:0, one launch (start us, length us, event | category | flops | bytes accessed | tf_op | source)
XLA Modules:
  0.0 104.5 jit_solution(16825800002993935539)
XLA Ops:
  0.6 1.7 %broadcast_in_dim.2 = bf16[4,32,2048]{2,1,0:T(8,128)(2,1)} broadcast(bf16[32,2048]{1,0:T(8,128)(2,1)} %param.15), dimensions={1,2} | broadcast | bytes 655360 | tf_op jit(solution)/shard_map/broadcast_in_dim | solution.py:433
  2.4 6.3 %all-to-all-start.3 = ((bf16[4,32,2048]{2,1,0:T(8,128)(2,1)}), bf16[4,32,2048]{2,1,0:T(8,128)(2,1)S(1)}, u32[]{:S(2)}, u32[]{:S(2)}) async-start(bf16[4,32,2048]{2,1,0:T(8,128)(2,1)} %broadcast_in_dim.2), calls=%async_computation.3 | async-start | bytes 1048576 | tf_op jit(solution)/shard_map/all_to_all | solution.py:416
  8.7 1.9 %shard_map.135 = bf16[8,336,128]{2,1,0:T(8,128)(2,1)} custom-call(bf16[128,256]{1,0:T(8,128)(2,1)} %q_ref.1, bf16[128,256]{1,0:T(8,128)(2,1)} %k_ref.1, bf16[128,512]{1,0:T(8,128)(2,1)} %v_ref.1, f32[4,128]{1,0:T(4,128)} %rate_ref.1, f32[4,128]{1,0:T(4,128)} %decay_ref.1), custom_call_target="tpu_custom_call" | custom-call | tf_op jit(solution)/shard_map/pallas_call | solution.py:428
  10.6 12.5 %all-to-all-done.3 = bf16[4,32,2048]{2,1,0:T(8,128)(2,1)S(1)} async-done(((bf16[4,32,2048]{2,1,0:T(8,128)(2,1)}), bf16[4,32,2048]{2,1,0:T(8,128)(2,1)S(1)}, u32[]{:S(2)}, u32[]{:S(2)}) %all-to-all-start.3) | async-done | bytes 524320 | tf_op jit(solution)/shard_map/all_to_all | solution.py:416
  23.2 0.0 copy-start.4
  23.2 3.7 %all-to-all-start = ((bf16[8,336,128]{2,1,0:T(8,128)(2,1)}), bf16[8,336,128]{2,1,0:T(8,128)(2,1)S(1)}, u32[]{:S(2)}, u32[]{:S(2)}) async-start(bf16[8,336,128]{2,1,0:T(8,128)(2,1)} %shard_map.135), calls=%async_computation | async-start | bytes 1376256 | tf_op jit(solution)/shard_map/all_to_all | solution.py:416
  26.9 0.0 copy-done.4
  26.9 3.4 %shard_map.138 = bf16[8,384,128]{2,1,0:T(8,128)(2,1)} custom-call(bf16[128,2048]{1,0:T(8,128)(2,1)} %bitcast.4, bf16[512,2048]{1,0:T(8,128)(2,1)} %w_ref.3), custom_call_target="tpu_custom_call" | custom-call | tf_op jit(solution)/shard_map/pallas_call | solution.py:435
  30.3 8.1 %all-to-all-done.in_ref = bf16[8,336,128]{2,1,0:T(8,128)(2,1)S(1)} async-done(((bf16[8,336,128]{2,1,0:T(8,128)(2,1)}), bf16[8,336,128]{2,1,0:T(8,128)(2,1)S(1)}, u32[]{:S(2)}, u32[]{:S(2)}) %all-to-all-start) | async-done | bytes 688160 | tf_op jit(solution)/shard_map/all_to_all | solution.py:416
  38.4 0.0 copy-start.2
  38.4 3.5 %all-to-all-start.4 = ((bf16[8,384,128]{2,1,0:T(8,128)(2,1)}), bf16[8,384,128]{2,1,0:T(8,128)(2,1)S(1)}, u32[]{:S(2)}, u32[]{:S(2)}) async-start(bf16[8,384,128]{2,1,0:T(8,128)(2,1)} %shard_map.138), calls=%async_computation.4 | async-start | bytes 1572864 | tf_op jit(solution)/shard_map/all_to_all | solution.py:416
  42.0 0.0 copy-done.2
  42.0 10.3 %shard_map.136 = (bf16[8,8,64,128]{3,2,1,0:T(8,128)(2,1)}, bf16[8,2,128,128]{3,2,1,0:T(8,128)(2,1)}, bf16[8,2,128,128]{3,2,1,0:T(8,128)(2,1)}, bf16[8,2,128,128]...) custom-call(s32[5]{0:T(128)} %off_ref.3, ...), custom_call_target="tpu_custom_call" | custom-call | tf_op jit(solution)/shard_map/pallas_call | solution.py:441
  52.2 2.3 %all-to-all-done.4.g_ref.cot_ref = bf16[8,384,128]{2,1,0:T(8,128)(2,1)S(1)} async-done(((bf16[8,384,128]{2,1,0:T(8,128)(2,1)}), bf16[8,384,128]{2,1,0:T(8,128)(2,1)S(1)}, u32[]{:S(2)}, u32[]{:S(2)}) %all-to-all-start.4) | async-done | bytes 786464 | tf_op jit(solution)/shard_map/all_to_all | solution.py:416
  54.5 0.0 copy-start.1
  54.5 3.6 %all-to-all-start.1 = ((bf16[8,8,64,128]{3,2,1,0:T(8,128)(2,1)}), bf16[8,8,64,128]{3,2,1,0:T(8,128)(2,1)S(1)}, u32[]{:S(2)}, u32[]{:S(2)}) async-start(bf16[8,8,64,128]{3,2,1,0:T(8,128)(2,1)} %get-tuple-element.21), calls=%async_computation.1 | async-start | bytes 2097152 | tf_op jit(solution)/shard_map/all_to_all | solution.py:416
  58.1 0.0 copy-done.1
  58.1 9.4 %shard_map.139 = bf16[8,336,128]{2,1,0:T(8,128)(2,1)} custom-call(s32[5]{0:T(128)} %off_ref.3, bf16[8,336,128]{2,1,0:T(8,128)(2,1)} %copy-done.2, bf16[8,384,128]{2,1,0:T(8,128)(2,1)} %copy-done.1, bf16[8,2,128,128]{3,2,1,0:T(8,128)(2,1)} %get-tuple-element.22.x_ref, bf16[8,2,128,128]{3,2,1,0:T(8,128)(2,1)} %get-tuple-element.23.a_ref, ...), custom_call_target="tpu_custom_call" | custom-call | tf_op jit(solution)/shard_map/pallas_call | solution.py:461
  67.5 5.9 %all-to-all-done.1.mixed_ref = bf16[8,8,64,128]{3,2,1,0:T(8,128)(2,1)S(1)} async-done(((bf16[8,8,64,128]{3,2,1,0:T(8,128)(2,1)}), bf16[8,8,64,128]{3,2,1,0:T(8,128)(2,1)S(1)}, u32[]{:S(2)}, u32[]{:S(2)}) %all-to-all-start.1) | async-done | bytes 1048608 | tf_op jit(solution)/shard_map/all_to_all | solution.py:416
  73.4 0.0 copy-start
  73.4 3.5 %all-to-all-start.5 = ((bf16[8,336,128]{2,1,0:T(8,128)(2,1)}), bf16[8,336,128]{2,1,0:T(8,128)(2,1)S(1)}, u32[]{:S(2)}, u32[]{:S(2)}) async-start(bf16[8,336,128]{2,1,0:T(8,128)(2,1)} %shard_map.139), calls=%async_computation.5 | async-start | bytes 1376256 | tf_op jit(solution)/shard_map/all_to_all | solution.py:416
  77.0 0.0 copy-done
  77.0 2.9 %shard_map.137 = bf16[128,2048]{1,0:T(8,128)(2,1)} custom-call(bf16[8,8,64,128]{3,2,1,0:T(8,128)(2,1)} %copy-done, bf16[512,2048]{1,0:T(8,128)(2,1)} %w_ref.3), custom_call_target="tpu_custom_call" | custom-call | tf_op jit(solution)/shard_map/pallas_call | solution.py:470
  79.9 8.5 %all-to-all-done.5.in_ref = bf16[8,336,128]{2,1,0:T(8,128)(2,1)S(1)} async-done(((bf16[8,336,128]{2,1,0:T(8,128)(2,1)}), bf16[8,336,128]{2,1,0:T(8,128)(2,1)S(1)}, u32[]{:S(2)}, u32[]{:S(2)}) %all-to-all-start.5) | async-done | bytes 688160 | tf_op jit(solution)/shard_map/all_to_all | solution.py:416
  88.4 0.0 copy-start.3
  88.4 3.5 %all-to-all-start.2 = ((bf16[4,32,2048]{2,1,0:T(8,128)(2,1)}), bf16[4,32,2048]{2,1,0:T(8,128)(2,1)S(1)}, u32[]{:S(2)}, u32[]{:S(2)}) async-start(bf16[4,32,2048]{2,1,0:T(8,128)(2,1)} %bitcast.3), calls=%async_computation.2 | async-start | bytes 1048576 | tf_op jit(solution)/shard_map/all_to_all | solution.py:416
  91.9 3.0 %shard_map.141 = f32[256,512]{1,0:T(8,128)} custom-call(s32[1]{0:T(128)} %bitcast.2.place_ref, bf16[8,384,128]{2,1,0:T(8,128)(2,1)} %copy-done.1, bf16[8,8,64,128]{3,2,1,0:T(8,128)(2,1)} %copy-done), custom_call_target="tpu_custom_call" | custom-call | tf_op jit(solution)/shard_map/pallas_call | solution.py:481
  94.8 0.0 copy-done.3
  94.8 2.0 %shard_map.140 = (f32[128,256]{1,0:T(8,128)}, f32[128,256]{1,0:T(8,128)}, f32[128,512]{1,0:T(8,128)}, f32[4,128]{1,0:T(4,128)}, f32[4,128]{1,0:T(4,128)}) custom-call(bf16[8,336,128]{2,1,0:T(8,128)(2,1)} %copy-done.3), custom_call_target="tpu_custom_call" | custom-call | tf_op jit(solution)/shard_map/pallas_call | solution.py:485
  96.8 7.0 %all-to-all-done.2 = bf16[4,32,2048]{2,1,0:T(8,128)(2,1)S(1)} async-done(((bf16[4,32,2048]{2,1,0:T(8,128)(2,1)}), bf16[4,32,2048]{2,1,0:T(8,128)(2,1)S(1)}, u32[]{:S(2)}, u32[]{:S(2)}) %all-to-all-start.2) | async-done | bytes 524320 | tf_op jit(solution)/shard_map/all_to_all | solution.py:416
  103.7 0.8 convert_reduce_fusion
Async XLA Ops:
  2.4 20.8 %all-to-all-start.3 = ((bf16[4,32,2048]{2,1,0:T(8,128)(2,1)}), bf16[4,32,2048]{2,1,0:T(8,128)(2,1)S(1)}, u32[]{:S(2)}, u32[]{:S(2)}) async-start(bf16[4,32,2048]{2,1,0:T(8,128)(2,1)} %broadcast_in_dim.2), calls=%async_computation.3 | async-start | bytes 1048576 | tf_op jit(solution)/shard_map/all_to_all | solution.py:416
  23.2 3.7 %copy-start.4 = (bf16[4,32,2048]{2,1,0:T(8,128)(2,1)}, bf16[4,32,2048]{2,1,0:T(8,128)(2,1)S(1)}, u32[]{:S(2)}) copy-start(bf16[4,32,2048]{2,1,0:T(8,128)(2,1)S(1)} %all-to-all-done.3) | copy-start | bytes 1572868
  23.2 15.2 %all-to-all-start = ((bf16[8,336,128]{2,1,0:T(8,128)(2,1)}), bf16[8,336,128]{2,1,0:T(8,128)(2,1)S(1)}, u32[]{:S(2)}, u32[]{:S(2)}) async-start(bf16[8,336,128]{2,1,0:T(8,128)(2,1)} %shard_map.135), calls=%async_computation | async-start | bytes 1376256 | tf_op jit(solution)/shard_map/all_to_all | solution.py:416
  38.4 3.6 %copy-start.2 = (bf16[8,336,128]{2,1,0:T(8,128)(2,1)}, bf16[8,336,128]{2,1,0:T(8,128)(2,1)S(1)}, u32[]{:S(2)}) copy-start(bf16[8,336,128]{2,1,0:T(8,128)(2,1)S(1)} %all-to-all-done.in_ref) | copy-start | bytes 2064388
  38.4 16.1 %all-to-all-start.4 = ((bf16[8,384,128]{2,1,0:T(8,128)(2,1)}), bf16[8,384,128]{2,1,0:T(8,128)(2,1)S(1)}, u32[]{:S(2)}, u32[]{:S(2)}) async-start(bf16[8,384,128]{2,1,0:T(8,128)(2,1)} %shard_map.138), calls=%async_computation.4 | async-start | bytes 1572864 | tf_op jit(solution)/shard_map/all_to_all | solution.py:416
  54.5 3.6 %copy-start.1 = (bf16[8,384,128]{2,1,0:T(8,128)(2,1)}, bf16[8,384,128]{2,1,0:T(8,128)(2,1)S(1)}, u32[]{:S(2)}) copy-start(bf16[8,384,128]{2,1,0:T(8,128)(2,1)S(1)} %all-to-all-done.4.g_ref.cot_ref) | copy-start | bytes 2359300
  54.5 18.9 %all-to-all-start.1 = ((bf16[8,8,64,128]{3,2,1,0:T(8,128)(2,1)}), bf16[8,8,64,128]{3,2,1,0:T(8,128)(2,1)S(1)}, u32[]{:S(2)}, u32[]{:S(2)}) async-start(bf16[8,8,64,128]{3,2,1,0:T(8,128)(2,1)} %get-tuple-element.21), calls=%async_computation.1 | async-start | bytes 2097152 | tf_op jit(solution)/shard_map/all_to_all | solution.py:416
  73.4 3.6 %copy-start = (bf16[8,8,64,128]{3,2,1,0:T(8,128)(2,1)}, bf16[8,8,64,128]{3,2,1,0:T(8,128)(2,1)S(1)}, u32[]{:S(2)}) copy-start(bf16[8,8,64,128]{3,2,1,0:T(8,128)(2,1)S(1)} %all-to-all-done.1.mixed_ref) | copy-start | bytes 3145732
  73.4 15.0 %all-to-all-start.5 = ((bf16[8,336,128]{2,1,0:T(8,128)(2,1)}), bf16[8,336,128]{2,1,0:T(8,128)(2,1)S(1)}, u32[]{:S(2)}, u32[]{:S(2)}) async-start(bf16[8,336,128]{2,1,0:T(8,128)(2,1)} %shard_map.139), calls=%async_computation.5 | async-start | bytes 1376256 | tf_op jit(solution)/shard_map/all_to_all | solution.py:416
  88.4 6.4 %copy-start.3 = (bf16[8,336,128]{2,1,0:T(8,128)(2,1)}, bf16[8,336,128]{2,1,0:T(8,128)(2,1)S(1)}, u32[]{:S(2)}) copy-start(bf16[8,336,128]{2,1,0:T(8,128)(2,1)S(1)} %all-to-all-done.5.in_ref) | copy-start | bytes 2064388
  88.4 15.4 %all-to-all-start.2 = ((bf16[4,32,2048]{2,1,0:T(8,128)(2,1)}), bf16[4,32,2048]{2,1,0:T(8,128)(2,1)S(1)}, u32[]{:S(2)}, u32[]{:S(2)}) async-start(bf16[4,32,2048]{2,1,0:T(8,128)(2,1)} %bitcast.3), calls=%async_computation.2 | async-start | bytes 1048576 | tf_op jit(solution)/shard_map/all_to_all | solution.py:416

commit v3 on v1

v3 whole, which is shorter than its diff:
```python
from functools import partial

import jax
import jax.numpy as jnp
from jax import lax
from jax.experimental import pallas as pl
from jax.experimental.pallas import tpu as pltpu
from jax.sharding import PartitionSpec as P

DK = 128
DV = 128
AUX = 16
EPS = 1e-06
F32 = jnp.float32
BF16 = jnp.bfloat16
VMEM_LIMIT = 56 * 1024 * 1024


def dot(a, b, ca, cb):
    return lax.dot_general(a, b, (((ca,), (cb,)), ((), ())), preferred_element_type=F32)


def halves(x):
    high = x.astype(BF16)
    return high, (x - high.astype(F32)).astype(BF16)


def thirds(x):
    high = x.astype(BF16).astype(F32)
    middle = (x - high).astype(BF16).astype(F32)
    return high, middle, x - high - middle


def mm(a, b, ca=1, cb=0):
    left = jnp.concatenate([a[0], a[0], a[1]], axis=ca)
    right = jnp.concatenate([b[0], b[1], b[0]], axis=cb)
    return dot(left, right, ca, cb)


def cat(pairs, axis):
    return tuple(jnp.concatenate(parts, axis=axis) for parts in zip(*pairs))


def put(ref, i, pair):
    ref[i, 0], ref[i, 1] = pair


def get(ref, i):
    return ref[i, 0], ref[i, 1]


def iotas(rows, columns):
    shape = (rows, columns)
    return lax.broadcasted_iota(jnp.int32, shape, 0), lax.broadcasted_iota(jnp.int32, shape, 1)


def call(kernel, outs, n_in, smem=(), scratch=()):
    spec = lambda i: pl.BlockSpec(memory_space=pltpu.SMEM if i in smem else pltpu.VMEM)
    return pl.pallas_call(
        kernel,
        out_shape=outs,
        in_specs=[spec(i) for i in range(n_in)],
        out_specs=jax.tree.map(lambda _: pl.BlockSpec(memory_space=pltpu.VMEM), outs),
        scratch_shapes=list(scratch),
        compiler_params=pltpu.CompilerParams(vmem_limit_bytes=VMEM_LIMIT),
    )


def arr(dtype, *shape):
    return jax.ShapeDtypeStruct(shape, dtype)


class Plan:
    def __init__(self, n, tok, hv, hk):
        self.n, self.tok, self.hv, self.hk = n, tok, hv, hk
        self.mates = n // hv
        self.v_at = 2 * tok
        self.aux_at = 2 * tok + DV
        self.rows = self.aux_at + AUX
        self.groups = [[m * self.mates + b for m in range(hv)] for b in range(self.mates)]

    def key_head(self, head):
        return head * self.hk // self.hv

    def exchange(self, x):
        return lax.all_to_all(
            x, "ctx", split_axis=0, concat_axis=0, axis_index_groups=self.groups, tiled=True
        )

    def from_mate(self, x, d):
        s = self.mates
        pairs = [(i // s * s + (i + d) % s, i) for i in range(self.n)]
        return lax.ppermute(x, "ctx", pairs)


def aux_rows(rows, columns):
    row_ids = lax.broadcasted_iota(jnp.int32, (AUX, columns), 0)
    out = jnp.zeros((AUX, columns), F32)
    for i, part in enumerate(p for r in rows for p in thirds(r)):
        out = jnp.where(row_ids == i, part, out)
    return out.astype(BF16)


def pack_kernel(plan, q_ref, k_ref, v_ref, rate_ref, decay_ref, out_ref):
    tok = plan.tok
    for h in range(plan.hv):
        kh = plan.key_head(h)
        out_ref[h, :tok] = q_ref[:, kh * DK : (kh + 1) * DK]
        out_ref[h, tok : 2 * tok] = k_ref[:, kh * DK : (kh + 1) * DK]
        turned = jnp.transpose(v_ref[:, h * DV : (h + 1) * DV].astype(F32))
        out_ref[h, plan.v_at : plan.aux_at] = turned.astype(BF16)
        rows = [rate_ref[h : h + 1, :], decay_ref[h : h + 1, :]]
        out_ref[h, plan.aux_at :] = aux_rows(rows, tok)


def unit(x):
    scale = lax.rsqrt(jnp.sum(x * x, axis=1, keepdims=True) + EPS)
    return x * scale, scale


def segments(off_ref, positions):
    total = jnp.zeros(positions.shape, jnp.int32)
    for j in range(off_ref.shape[0] - 1):
        total = total + (off_ref[j] <= positions).astype(jnp.int32)
    return total


def to_columns(rows, tok):
    row_ids = lax.broadcasted_iota(jnp.int32, (tok, tok), 0)
    stacked = jnp.zeros((tok, tok), F32)
    for i, r in enumerate(rows):
        stacked = jnp.where(row_ids == i, r, stacked)
    turned = jnp.transpose(stacked)
    return [turned[:, i : i + 1] for i in range(len(rows))]


def to_rows(columns, tok):
    column_ids = lax.broadcasted_iota(jnp.int32, (tok, tok), 1)
    stacked = jnp.zeros((tok, tok), F32)
    for i, c in enumerate(columns):
        stacked = jnp.where(column_ids == i, c, stacked)
    turned = jnp.transpose(stacked)
    return [turned[i : i + 1, :] for i in range(len(columns))]


def scalings(plan, off_ref, chunks, auxes):
    tok = plan.tok
    rows, columns = iotas(tok, tok)
    upto = (rows <= columns).astype(BF16)
    sums = [dot(a, upto, 1, 0) for a in auxes]
    rates = [jnp.sum(a[0:3].astype(F32), axis=0, keepdims=True) for a in auxes]
    cumuls = [s[3:4] + s[4:5] + s[5:6] for s in sums]
    turned = to_columns(rates + cumuls, tok)
    out = []
    for i, c in enumerate(chunks):
        b_col, c_col = turned[i], turned[len(chunks) + i]
        c_row = cumuls[i]
        start = c * tok
        seg_col = segments(off_ref, start + rows[:, :1])
        seg_row = segments(off_ref, start + columns[:1, :])
        before = jnp.int32(0)
        last = jnp.int32(0)
        for j in range(off_ref.shape[0] - 1):
            before = before + (off_ref[j] <= start - 1).astype(jnp.int32)
            last = last + (off_ref[j] <= start + tok - 1).astype(jnp.int32)
        c_last = c_row[:, tok - 1 : tok]
        together = (seg_col == seg_row) & (rows >= columns)
        ratio = jnp.where(together, jnp.exp(jnp.where(together, c_col - c_row, 0.0)), 0.0)
        start_col = jnp.where(seg_col == before, jnp.exp(c_col), 0.0)
        end_col = jnp.where(seg_col == last, jnp.exp(c_last - c_col), 0.0)
        whole = jnp.where(last == before, jnp.exp(c_last), 0.0)
        out.append((rates[i], b_col, ratio, start_col, end_col, whole))
    return out


def inverses(lowers):
    size = lowers[0].shape[0]
    rows, columns = iotas(size, size)
    identity = (rows == columns).astype(F32)
    block = min(16, size)
    near = (rows // block) == (columns // block)
    powers = [jnp.where(near, -m, 0.0) for m in lowers]
    results = [identity + p for p in powers]
    split = [halves(p) for p in powers]
    powers = [mm(s, s) for s in split]
    reach = 2
    while reach < block:
        split = [halves(p) for p in powers]
        more = reach * 2 < block
        both = []
        for r, s in zip(results, split):
            left = halves(r)
            if more:
                left = cat([left, s], 0)
            both.append(mm(left, s))
        results = [r + b[:size] for r, b in zip(results, both)]
        if more:
            powers = [b[size:] for b in both]
        reach *= 2
    while block < size:
        across = ((rows // (2 * block)) == (columns // (2 * block))) & (
            (rows // block) > (columns // block)
        )
        split = [halves(r) for r in results]
        middle = [mm(halves(jnp.where(across, m, 0.0)), s) for m, s in zip(lowers, split)]
        results = [r - mm(s, halves(m)) for r, s, m in zip(results, split, middle)]
        block *= 2
    return results


def prepare_kernel(
    plan, off_ref, mate_ref, in_ref, link_ref, x_ref, a_ref, w_ref, q_ref, ratio_ref, u_ref, ol_ref
):
    tok = plan.tok
    rows, columns = iotas(tok, tok)
    identity = (lax.broadcasted_iota(jnp.int32, (DK, DK), 0) == lax.broadcasted_iota(jnp.int32, (DK, DK), 1)).astype(F32)
    mine = range(plan.hv)
    chunks = [mate_ref[0] + plan.mates * m for m in mine]
    scales = scalings(plan, off_ref, chunks, [in_ref[m, plan.aux_at :] for m in mine])
    qn = [unit(in_ref[m, :tok].astype(F32))[0] for m in mine]
    kn = [unit(in_ref[m, tok : 2 * tok].astype(F32))[0] for m in mine]
    kp = [halves(x) for x in kn]
    qp = [halves(x) for x in qn]
    dots = [mm(cat([q, k], 0), k, 1, 1) for q, k in zip(qp, kp)]
    strict = rows > columns
    lowers = [jnp.where(strict, s[1] * d[tok:] * s[2], 0.0) for s, d in zip(scales, dots)]
    scores = [d[:tok] * s[2] for s, d in zip(scales, dots)]
    inv = inverses(lowers)
    rated = [halves(x * s[0]) for x, s in zip(inv, scales)]
    w = [mm(x, halves(s[3] * k)) for x, s, k in zip(rated, scales, kn)]
    values = [in_ref[m, plan.v_at : plan.aux_at] for m in mine]
    u = [
        dot(jnp.concatenate([v, v], axis=1), jnp.concatenate(x, axis=1), 1, 1)
        for v, x in zip(values, rated)
    ]
    wp = [halves(x) for x in w]
    up = [halves(x) for x in u]
    ap = [halves(x) for x in scores]
    ke = [halves(s[4] * k) for s, k in zip(scales, kn)]
    for m in mine:
        link_ref[m, 0] = scales[m][5] * identity - mm(wp[m], ke[m], 0, 0)
        link_ref[m, 1] = mm(up[m], ke[m])
    for m in mine:
        put(x_ref, m, halves(inv[m]))
        put(a_ref, m, ap[m])
        put(w_ref, m, wp[m])
        put(q_ref, m, halves(scales[m][3] * qn[m] - mm(ap[m], wp[m])))
        ratio_ref[m] = scales[m][2]
        u_ref[m] = u[m]
        ol_ref[m] = mm(up[m], ap[m], 1, 1)


def lay_out(plan, mate, refs, all_ref):
    for d, ref in enumerate(refs):
        all_ref[lax.rem(mate + d, plan.mates)] = ref[...]


def scan_kernel(plan, mate_ref, *refs):
    s = plan.mates
    links, (cot_ref, q_ref, ol_ref, out_ref, s_ref, back_ref, all_ref, states_ref) = refs[:s], refs[s:]
    mate = mate_ref[0]
    lay_out(plan, mate, links, all_ref)
    state = jnp.zeros((DV, DK), F32)
    for c in range(plan.n):
        states_ref[c] = state
        if c < plan.n - 1:
            link = all_ref.at[c % s, c // s]
            state = link[1] + mm(halves(state), halves(link[0]))
    for m in range(plan.hv):
        state = states_ref[mate + s * m]
        s_ref[m] = state
        core = (ol_ref[m] + mm(halves(state), get(q_ref, m), 1, 1)).astype(BF16)
        for g in range(plan.hv):
            out_ref[g, (m - g) % plan.hv] = core
        back_ref[m] = mm(d_out(cot_ref, m), get(q_ref, m))


def d_out(cot_ref, m):
    return cot_ref[m, :DV], cot_ref[m, DV : 2 * DV]


def backward_kernel(plan, off_ref, mate_ref, *refs):
    s, n, tok = plan.mates, plan.n, plan.tok
    links, backs, refs = refs[:s], refs[s : 2 * s], refs[2 * s :]
    in_ref, cot_ref, x_ref, a_ref, w_ref, ratio_ref, u_ref, s_ref, out_ref = refs[:9]
    links_ref, backs_ref, cots_ref = refs[9:]
    mate = mate_ref[0]
    lay_out(plan, mate, links, links_ref)
    lay_out(plan, mate, backs, backs_ref)
    d_state = jnp.zeros((DV, DK), F32)
    for c in reversed(range(n)):
        cots_ref[c] = d_state
        if c:
            d_state = backs_ref[c % s, c // s] + mm(
                halves(d_state), halves(links_ref[c % s, c // s, 0]), 1, 1
            )
    rows, columns = iotas(tok, tok)
    strict = rows > columns
    upto = (rows >= columns).astype(BF16)
    mine = range(plan.hv)
    chunks = [mate + s * m for m in mine]
    scales = scalings(plan, off_ref, chunks, [in_ref[m, plan.aux_at :] for m in mine])
    qu = [unit(in_ref[m, :tok].astype(F32)) for m in mine]
    ku = [unit(in_ref[m, tok : 2 * tok].astype(F32)) for m in mine]
    qp = [halves(x[0]) for x in qu]
    kp = [halves(x[0]) for x in ku]
    do = [d_out(cot_ref, m) for m in mine]
    s0 = [s_ref[m] for m in mine]
    ds = [cots_ref[c] for c in chunks]
    s0p = [halves(x) for x in s0]
    dsp = [halves(x) for x in ds]
    pseudo = [u_ref[m] - mm(s0p[m], get(w_ref, m), 1, 1) for m in mine]
    pp = [halves(x) for x in pseudo]
    ke = [halves(s[4] * k[0]) for s, k in zip(scales, ku)]
    dp = [mm(do[m], get(a_ref, m)) + mm(dsp[m], ke[m], 1, 1) for m in mine]
    dr = [mm(halves(dp[m]), get(x_ref, m)) for m in mine]
    drp = [halves(x) for x in dr]
    big = [mm(cat([o, r], 1), cat([p, s], 1), 0, 0) for o, r, p, s in zip(do, drp, pp, s0p)]
    pds = [mm(p, d, 0, 0) for p, d in zip(pp, dsp)]
    da = [big[m][:tok, :tok] * ratio_ref[m] for m in mine]
    dm = [jnp.where(strict, -big[m][tok:, :tok] * ratio_ref[m], 0.0) for m in mine]
    dap = [halves(x) for x in da]
    dmp = [halves(x) for x in dm]
    dbm = [halves(s[1] * x) for s, x in zip(scales, dm)]
    by_row = [mm(cat([x, y], 0), k) for x, y, k in zip(dap, dmp, kp)]
    by_column = [
        mm(cat([x, y], 0), cat([q, k], 0), 0, 0) for x, y, q, k in zip(dap, dbm, qp, kp)
    ]
    sums = []
    for m in mine:
        _, b_col, _, start_col, end_col, whole = scales[m]
        (qn, q_scale), (kn, k_scale) = qu[m], ku[m]
        dqn = by_row[m][:tok] + start_col * big[m][:tok, tok:]
        erase = by_row[m][tok:] - start_col * big[m][tok:, tok:]
        ends = end_col * pds[m]
        write = by_column[m] + ends
        dkn = b_col * erase + write
        s_q = jnp.sum(qn * dqn, axis=1, keepdims=True)
        s_e = jnp.sum(kn * erase, axis=1, keepdims=True)
        s_w = jnp.sum(kn * write, axis=1, keepdims=True)
        total = jnp.sum(jnp.sum(kn * ends, axis=1, keepdims=True), axis=0, keepdims=True)
        both = jnp.sum(jnp.sum(s0[m] * ds[m], axis=1, keepdims=True), axis=0, keepdims=True)
        out_ref[m, :tok] = (q_scale * (dqn - qn * s_q)).astype(BF16)
        out_ref[m, tok : 2 * tok] = (k_scale * (dkn - kn * (b_col * s_e + s_w))).astype(BF16)
        out_ref[m, plan.v_at : plan.aux_at] = (scales[m][0] * dr[m]).astype(BF16)
        sums.append((s_e, s_q + b_col * s_e - s_w, total + whole * both))
    turned = to_rows([s[0] for s in sums] + [s[1] for s in sums], tok)
    for m in mine:
        values = in_ref[m, plan.v_at : plan.aux_at].astype(F32)
        d_rate = turned[m] + jnp.sum(dr[m] * values, axis=0, keepdims=True)
        parts = dot(aux_rows([turned[plan.hv + m]], tok), upto, 1, 0)
        d_decay = parts[0:1] + parts[1:2] + parts[2:3] + sums[m][2]
        out_ref[m, plan.aux_at :] = aux_rows([d_rate, d_decay], tok)


def cotangent_kernel(plan, parts, head_ref, *refs):
    pieces, (w_ref, out_ref, all_ref) = refs[:parts], refs[parts:]
    rows = pieces[0].shape[0]
    for d in range(parts):
        at = lax.rem(head_ref[0] + d, parts)
        all_ref[pl.ds(pl.multiple_of(at * rows, rows), rows), :] = pieces[d][...]
    whole = all_ref[...]
    share = whole.shape[1] // plan.hv
    high, low = halves(dot(w_ref[...], whole, 1, 1))
    for m in range(plan.hv):
        out_ref[m, :DV] = high[m * DV : (m + 1) * DV]
        out_ref[m, DV : 2 * DV] = low[m * DV : (m + 1) * DV]
        turned = jnp.transpose(whole[:, m * share : (m + 1) * share].astype(F32))
        out_ref[m, 2 * DV :] = turned.astype(BF16)


def project_kernel(plan, parts, head_ref, mixed_ref, w_ref, *refs):
    outs, total_ref = refs[:parts], refs[parts]
    mixed = jnp.concatenate([mixed_ref[g, 0] for g in range(plan.hv)], axis=0)
    total_ref[...] = dot(mixed, w_ref[...], 0, 0)
    rows = outs[0].shape[0]
    for d in range(parts):
        at = lax.rem(head_ref[0] + parts - d, parts)
        block = total_ref[pl.ds(pl.multiple_of(at * rows, rows), rows), :]
        outs[d][...] = block.astype(outs[d].dtype)


def weight_kernel(plan, place_ref, mate_ref, cot_ref, mixed_ref, *outs):
    share = outs[0].shape[0]
    mixed = [
        jnp.concatenate([mixed_ref[g, step] for g in range(plan.hv)], axis=0)
        for step in range(plan.hv)
    ]
    for d, out_ref in enumerate(outs):
        at = lax.rem(mate_ref[0] + plan.mates - d, plan.mates)
        at = pl.multiple_of(2 * DV + at * share, share)
        total = None
        for step in range(plan.hv):
            chunk = lax.rem(place_ref[0] + step, plan.hv)
            part = dot(cot_ref[chunk, pl.ds(at, share), :], mixed[step], 1, 1)
            total = part if total is None else total + part
        out_ref[...] = total


def finish_kernel(plan, in_ref, q_ref, k_ref, v_ref, rate_ref, decay_ref):
    tok = plan.tok
    for kh in range(plan.hk):
        mine = [h for h in range(plan.hv) if plan.key_head(h) == kh]
        for ref, at in ((q_ref, 0), (k_ref, tok)):
            total = in_ref[mine[0], at : at + tok].astype(F32)
            for h in mine[1:]:
                total = total + in_ref[h, at : at + tok].astype(F32)
            ref[:, kh * DK : (kh + 1) * DK] = total
    for h in range(plan.hv):
        v_ref[:, h * DV : (h + 1) * DV] = jnp.transpose(
            in_ref[h, plan.v_at : plan.aux_at].astype(F32)
        )
        aux = in_ref[h, plan.aux_at :].astype(F32)
        rate_ref[h : h + 1, :] = aux[0:1] + aux[1:2] + aux[2:3]
        decay_ref[h : h + 1, :] = aux[3:4] + aux[4:5] + aux[5:6]


def per_device(
    queries, key_vectors, value_rows, write_rate, log_decay, doc_offsets, out_weight, grad_out
):
    n, parts = lax.axis_size("ctx"), lax.axis_size("head")
    tok, hv = queries.shape[0], write_rate.shape[0]
    hk, model = queries.shape[1] // DK, grad_out.shape[1]
    plan = Plan(n, tok, hv, hk)
    s = plan.mates
    index = lax.axis_index("ctx").astype(jnp.int32)
    place, mate = (index // s).reshape(1), (index % s).reshape(1)
    head = lax.axis_index("head").astype(jnp.int32).reshape(1)

    def from_head(x, d):
        return lax.ppermute(x, "head", [((i + d) % parts, i) for i in range(parts)])

    pieces = [grad_out] + [from_head(grad_out, d) for d in range(1, parts)]

    sent = call(partial(pack_kernel, plan), arr(BF16, hv, plan.rows, DK), 5)(
        queries, key_vectors, value_rows, write_rate, log_decay
    )
    got = plan.exchange(sent)

    cot_sent = call(
        partial(cotangent_kernel, plan, parts),
        arr(BF16, hv, 2 * DV + model // hv, tok),
        parts + 2,
        smem=(0,),
        scratch=[pltpu.VMEM((tok, model), BF16)],
    )(head, *pieces, out_weight)
    cot = plan.exchange(cot_sent)

    pair = lambda r, c: arr(BF16, hv, 2, r, c)
    link, x, a, w, q, ratio, u, ol = call(
        partial(prepare_kernel, plan),
        (
            arr(F32, hv, 2, DK, DK),
            pair(tok, tok),
            pair(tok, tok),
            pair(tok, DK),
            pair(tok, DK),
            arr(F32, hv, tok, tok),
            arr(F32, hv, DV, tok),
            arr(F32, hv, DV, tok),
        ),
        3,
        smem=(0, 1),
    )(doc_offsets, mate, got)
    links = [link] + [plan.from_mate(link, d) for d in range(1, s)]
    out, states, back = call(
        partial(scan_kernel, plan),
        (arr(BF16, hv, hv, DV, tok), arr(F32, hv, DV, DK), arr(F32, hv, DV, DK)),
        s + 4,
        smem=(0,),
        scratch=[pltpu.VMEM((s, hv, 2, DK, DK), F32), pltpu.VMEM((n, DV, DK), F32)],
    )(mate, *links, cot, q, ol)
    mixed = plan.exchange(out)
    backs = [back] + [plan.from_mate(back, d) for d in range(1, s)]

    grad_sent = call(
        partial(backward_kernel, plan),
        arr(BF16, hv, plan.rows, DK),
        2 * s + 10,
        smem=(0, 1),
        scratch=[
            pltpu.VMEM((s, hv, 2, DK, DK), F32),
            pltpu.VMEM((s, hv, DV, DK), F32),
            pltpu.VMEM((n, DV, DK), F32),
        ],
    )(doc_offsets, mate, *links, *backs, got, cot, x, a, w, ratio, u, states)

    block = pl.BlockSpec((hv, 1, DV, tok), lambda i: (0, 0, 0, 0))
    rows = tok // parts
    projected = pl.pallas_call(
        partial(project_kernel, plan, parts),
        out_shape=[arr(BF16 if d else F32, rows, model) for d in range(parts)],
        grid=(1,),
        in_specs=[
            pl.BlockSpec(memory_space=pltpu.SMEM),
            block,
            pl.BlockSpec(out_weight.shape, lambda i: (0, 0)),
        ],
        out_specs=[pl.BlockSpec((rows, model), lambda i: (0, 0))] * parts,
        scratch_shapes=[pltpu.VMEM((tok, model), F32)],
        compiler_params=pltpu.CompilerParams(vmem_limit_bytes=VMEM_LIMIT),
    )(head, mixed, out_weight)
    layer_out = projected[0]
    for d in range(1, parts):
        layer_out = layer_out + from_head(projected[d], d).astype(F32)

    shares = call(
        partial(weight_kernel, plan), [arr(F32, model // n, hv * DV)] * s, 4, smem=(0, 1)
    )(place, mate, cot, mixed)
    weight_grad = shares[0]
    for d in range(1, s):
        weight_grad = weight_grad + plan.from_mate(shares[d], d)

    grads = plan.exchange(grad_sent)
    grad_q, grad_k, grad_v, grad_rate, grad_decay = call(
        partial(finish_kernel, plan),
        (
            arr(F32, tok, hk * DK),
            arr(F32, tok, hk * DK),
            arr(F32, tok, hv * DV),
            arr(F32, hv, tok),
            arr(F32, hv, tok),
        ),
        1,
    )(grads)
    return (layer_out, grad_q, grad_k, grad_v, grad_rate, grad_decay, weight_grad)


def solution(mesh):
    placed = (
        P("ctx", "head"),
        P("ctx", "head"),
        P("ctx", "head"),
        P("head", "ctx"),
        P("head", "ctx"),
        P(),
        P("head", None),
        P(("ctx", "head"), None),
    )
    return jax.shard_map(
        per_device,
        mesh=mesh,
        in_specs=placed,
        out_specs=(
            P(("ctx", "head"), None),
            P("ctx", "head"),
            P("ctx", "head"),
            P("ctx", "head"),
            P("head", "ctx"),
            P("head", "ctx"),
            P("ctx", "head"),
        ),
        check_vma=False,
    )
```

time: 107 us -> 91.1 us (0.85)
  between operations: 14.1 us -> 0.73 us
  waiting for transfers between devices: 31.6 us -> 26.4 us
  matrix products: 2.97 us -> 0 us
  local copies, waits for them, and re-layouts: 1.68 us -> 4.06 us
  Pallas kernels: 27 us -> 28.7 us
  starting transfers between devices: 27.7 us -> 29 us
    ppermute x3 -> x9, starting transfers between devices: 6.48 us -> 13 us  [the longest x6 12.9 us: from_head(): return lax.ppermute(x, 'head', [((i + d) % parts, i) for i in range(parts)])]
    all_to_all x5 -> x4, waiting for transfers between devices: 24 us -> 18 us  [exchange(): lax.all_to_all(x, 'ctx', split_axis=0, concat_axis=0, axis_index_groups=s...]
    all_to_all x5 -> x4, starting transfers between devices: 21.1 us -> 16 us  [exchange(): lax.all_to_all(x, 'ctx', split_axis=0, concat_axis=0, axis_index_groups=s...]
    dot_general x2 -> x0, matrix products: 2.97 us -> none  [the longest x1 1.7 us: per_device(): jnp.einsum('cdt,gcvt->dgv', grads, all_mixed, preferred_element_type=F32)]
    unnamed x17 -> x22, local copies, waits for them, and re-layouts: 1.68 us -> 4.06 us
    pallas_call x4 -> x7, Pallas kernels: 25.1 us -> 26.9 us  [the longest x1 6.8 us: per_device(): call(partial(backward_kernel, plan), arr(BF16, hv, plan.rows, DK), 2 * s...]
    add x0 -> x2, other arithmetic: none -> 1.63 us  [the longest x1 0.87 us: per_device(): weight_grad = weight_grad + plan.from_mate(shares[d], d)]
    ppermute x3 -> x9, waiting for transfers between devices: 7.53 us -> 8.35 us  [the longest x6 8.34 us: from_head(): return lax.ppermute(x, 'head', [((i + d) % parts, i) for i in range(parts)])]
  transfers between devices with their start and end apart: 9 -> 13, of which waited for: 5 -> 4; matrix products, arithmetic and copies ran while one was open for 2% -> 1% of each run, Pallas kernels for 24% -> 26%
where the time goes in v3:
time: 91.1 us; the launch traced here: 90.5 us
  starting transfers between devices  29 us (32%)
  Pallas kernels  28.7 us (32%)
  waiting for transfers between devices  26.4 us (29%)
  local copies, waits for them, and re-layouts  4.06 us (4%)
  other arithmetic  1.63 us (2%)
    all_to_all x4, waiting for transfers between devices, exchange(): lax.all_to_all(x, 'ctx', split_axis=0, concat_axis=0, axis_index_groups=s...  18 us
    all_to_all x4, starting transfers between devices, exchange(): lax.all_to_all(x, 'ctx', split_axis=0, concat_axis=0, axis_index_groups=s...  16 us
    ppermute x6, starting transfers between devices, from_head(): return lax.ppermute(x, 'head', [((i + d) % parts, i) for i in range(parts)])  12.9 us
    ppermute x6, waiting for transfers between devices, from_head(): return lax.ppermute(x, 'head', [((i + d) % parts, i) for i in range(parts)])  8.34 us
    pallas_call x1, Pallas kernels, per_device(): call(partial(backward_kernel, plan), arr(BF16, hv, plan.rows, DK), 2 * s...  6.8 us
    pallas_call x1, Pallas kernels, per_device(): call(partial(prepare_kernel, plan), (arr(F32, hv, 2, DK, DK), pair(tok, t...  5.17 us
    unnamed x22, local copies, waits for them, and re-layouts  4.06 us
    pallas_call x1, Pallas kernels, per_device(): call(partial(scan_kernel, plan), (arr(BF16, hv, hv, DV, tok), arr(F32, hv...  3.79 us
  transfers between devices with their start and end apart: 13, of which 4 were waited for; matrix products, arithmetic and copies ran while one was open for 1% of the time, Pallas kernels for 26%

profile of v3, /device:TPU:0, one launch (start us, length us, event | category | flops | bytes accessed | tf_op | source)
XLA Modules:
  0.0 90.5 jit_solution(18193790406287059456)
XLA Ops:
  0.6 1.9 %shard_map.135 = bf16[4,400,128]{2,1,0:T(8,128)(2,1)} custom-call(bf16[128,256]{1,0:T(8,128)(2,1)} %q_ref.1, bf16[128,256]{1,0:T(8,128)(2,1)} %k_ref.1, bf16[128,512]{1,0:T(8,128)(2,1)} %v_ref.1, f32[4,128]{1,0:T(4,128)} %rate_ref.1, f32[4,128]{1,0:T(4,128)} %decay_ref.1), custom_call_target="tpu_custom_call" | custom-call | tf_op jit(solution)/shard_map/pallas_call | solution.py:435
  2.5 5.2 %all-to-all-start = ((bf16[4,400,128]{2,1,0:T(8,128)(2,1)}), bf16[4,400,128]{2,1,0:T(8,128)(2,1)S(1)}, u32[]{:S(2)}, u32[]{:S(2)}) async-start(bf16[4,400,128]{2,1,0:T(8,128)(2,1)} %shard_map.135), calls=%async_computation | async-start | bytes 819200 | tf_op jit(solution)/shard_map/all_to_all | solution.py:86
  7.6 2.6 %collective-permute-start.2 = (bf16[32,2048]{1,0:T(8,128)(2,1)}, bf16[32,2048]{1,0:T(8,128)(2,1)S(1)}, u32[]{:S(2)}, u32[]{:S(2)}) collective-permute-start(bf16[32,2048]{1,0:T(8,128)(2,1)} %refs_0_.1), channel_id=1, source_target_pairs={{2,0},{3,1},{0,2},{1,3},{6,4},{7,5},{4,6},{5,7},{10,8},{11,9},{8,1... | collective-permute-start | bytes 393224 | tf_op jit(solution)/shard_map/ppermute | solution.py:431
  10.2 1.3 %collective-permute-start.1 = (bf16[32,2048]{1,0:T(8,128)(2,1)}, bf16[32,2048]{1,0:T(8,128)(2,1)S(1)}, u32[]{:S(2)}, u32[]{:S(2)}) collective-permute-start(bf16[32,2048]{1,0:T(8,128)(2,1)} %refs_0_.1), channel_id=1, source_target_pairs={{1,0},{2,1},{3,2},{0,3},{5,4},{6,5},{7,6},{4,7},{9,8},{10,9},{11,1... | collective-permute-start | bytes 393224 | tf_op jit(solution)/shard_map/ppermute | solution.py:431
  11.6 0.7 collective-permute-start.3
  12.3 8.3 %collective-permute-done.2.refs_2_ = bf16[32,2048]{1,0:T(8,128)(2,1)S(1)} collective-permute-done((bf16[32,2048]{1,0:T(8,128)(2,1)}, bf16[32,2048]{1,0:T(8,128)(2,1)S(1)}, u32[]{:S(2)}, u32[]{:S(2)}) %collective-permute-start.2) | collective-permute-done | bytes 131104 | tf_op jit(solution)/shard_map/ppermute | solution.py:431
  20.6 0.6 copy-done.8
  21.3 0.0 copy-done.10
  21.3 3.5 %shard_map.137 = bf16[4,768,128]{2,1,0:T(8,128)(2,1)} custom-call(s32[1]{0:T(128)} %bitcast.head_ref, bf16[32,2048]{1,0:T(8,128)(2,1)} %refs_0_.1, bf16[32,2048]{1,0:T(8,128)(2,1)} %copy-done.9, bf16[32,2048]{1,0:T(8,128)(2,1)} %copy-done.8, bf16[32,2048]{1,0:T(8,128)(2,1)} %copy-done.10, bf16[512,2048]{1,0:T(8,128)(2,1)} %w_ref.1), custom_call_target="tpu_custom_call" | custom-call | tf_op jit(solution)/shard_map/pallas_call | solution.py:440
  24.8 3.8 %all-to-all-start.1 = ((bf16[4,768,128]{2,1,0:T(8,128)(2,1)}), bf16[4,768,128]{2,1,0:T(8,128)(2,1)S(1)}, u32[]{:S(2)}, u32[]{:S(2)}) async-start(bf16[4,768,128]{2,1,0:T(8,128)(2,1)} %shard_map.137), calls=%async_computation.1 | async-start | bytes 1572864 | tf_op jit(solution)/shard_map/all_to_all | solution.py:86
  28.7 5.2 %shard_map.136 = (f32[4,2,128,128]{3,2,1,0:T(8,128)}, bf16[4,2,128,128]{3,2,1,0:T(8,128)(2,1)}, bf16[4,2,128,128]{3,2,1,0:T(8,128)(2,1)}, bf16[4,2,128,128]{3,2,...) custom-call(s32[5]{0:T(128)} %off_ref.3, ...), custom_call_target="tpu_custom_call" | custom-call | tf_op jit(solution)/shard_map/pallas_call | solution.py:450
  33.8 4.3 %all-to-all-done.1.refs_2_.refs_5_.cot_ref = bf16[4,768,128]{2,1,0:T(8,128)(2,1)S(1)} async-done(((bf16[4,768,128]{2,1,0:T(8,128)(2,1)}), bf16[4,768,128]{2,1,0:T(8,128)(2,1)S(1)}, u32[]{:S(2)}, u32[]{:S(2)}) %all-to-all-start.1) | async-done | bytes 786464 | tf_op jit(solution)/shard_map/all_to_all | solution.py:86
  38.2 0.9 copy-done
  39.1 0.2 copy-done.3
  39.2 3.8 %shard_map.138 = (bf16[4,4,128,128]{3,2,1,0:T(8,128)(2,1)}, f32[4,128,128]{2,1,0:T(8,128)}, f32[4,128,128]{2,1,0:T(8,128)}) custom-call(s32[1]{0:T(128)} %bitcast.1.mate_ref, f32[4,2,128,128]{3,2,1,0:T(8,128)} %get-tuple-element.29.refs_0_, f32[4,2,128,128]{3,2,1,0:T(8,128)} %copy-done.3, bf16[4,768,128]{2,1,0:T(8,128)(2,1)} %copy-done, ...), custom_call_target="tpu_custom_call" | custom-call | tf_op jit(solution)/shard_map/pallas_call | solution.py:466
  43.0 3.5 %all-to-all-start.2 = ((bf16[4,4,128,128]{3,2,1,0:T(8,128)(2,1)}), bf16[4,4,128,128]{3,2,1,0:T(8,128)(2,1)S(1)}, u32[]{:S(2)}, u32[]{:S(2)}) async-start(bf16[4,4,128,128]{3,2,1,0:T(8,128)(2,1)} %get-tuple-element.32), calls=%async_computation.2 | async-start | bytes 1048576 | tf_op jit(solution)/shard_map/all_to_all | solution.py:86
  46.5 0.1 collective-permute-start.7
  46.6 6.8 %all-to-all-done.2.mixed_ref = bf16[4,4,128,128]{3,2,1,0:T(8,128)(2,1)S(1)} async-done(((bf16[4,4,128,128]{3,2,1,0:T(8,128)(2,1)}), bf16[4,4,128,128]{3,2,1,0:T(8,128)(2,1)S(1)}, u32[]{:S(2)}, u32[]{:S(2)}) %all-to-all-start.2) | async-done | bytes 524320 | tf_op jit(solution)/shard_map/all_to_all | solution.py:86
  53.4 0.8 copy-done.1
  54.2 3.0 %shard_map.139 = (f32[32,2048]{1,0:T(8,128)}, bf16[32,2048]{1,0:T(8,128)(2,1)}, bf16[32,2048]{1,0:T(8,128)(2,1)}, bf16[32,2048]{1,0:T(8,128)(2,1)}) custom-call(s32[1]{0:T(128)} %bitcast.head_ref, bf16[4,4,128,128]{3,2,1,0:T(8,128)(2,1)} %copy-done.1, bf16[512,2048]{1,0:T(8,128)(2,1)} %w_ref.1), custom_call_target="tpu_custom_call" | custom-call | tf_op jit(solution)/shard_map/pallas_call | solution.py:490
  57.2 4.4 %collective-permute-start.4 = (bf16[32,2048]{1,0:T(8,128)(2,1)}, bf16[32,2048]{1,0:T(8,128)(2,1)S(1)}, u32[]{:S(2)}, u32[]{:S(2)}) collective-permute-start(bf16[32,2048]{1,0:T(8,128)(2,1)} %get-tuple-element.34), channel_id=1, source_target_pairs={{1,0},{2,1},{3,2},{0,3},{5,4},{6,5},{7,6},{4,7},{9,8},{10,9},{11,1... | collective-permute-start | bytes 393224 | tf_op jit(solution)/shard_map/ppermute | solution.py:431
  61.6 1.9 %collective-permute-start.5 = (bf16[32,2048]{1,0:T(8,128)(2,1)}, bf16[32,2048]{1,0:T(8,128)(2,1)S(1)}, u32[]{:S(2)}, u32[]{:S(2)}) collective-permute-start(bf16[32,2048]{1,0:T(8,128)(2,1)} %get-tuple-element.35), channel_id=1, source_target_pairs={{2,0},{3,1},{0,2},{1,3},{6,4},{7,5},{4,6},{5,7},{10,8},{11,9},{8,1... | collective-permute-start | bytes 393224 | tf_op jit(solution)/shard_map/ppermute | solution.py:431
  63.4 2.0 %collective-permute-start.6 = (bf16[32,2048]{1,0:T(8,128)(2,1)}, bf16[32,2048]{1,0:T(8,128)(2,1)S(1)}, u32[]{:S(2)}, u32[]{:S(2)}) collective-permute-start(bf16[32,2048]{1,0:T(8,128)(2,1)} %get-tuple-element.36), channel_id=1, source_target_pairs={{3,0},{0,1},{1,2},{2,3},{7,4},{4,5},{5,6},{6,7},{11,8},{8,9},{9,10... | collective-permute-start | bytes 393224 | tf_op jit(solution)/shard_map/ppermute | solution.py:431
  65.5 2.8 %shard_map.142 = (f32[256,512]{1,0:T(8,128)}, f32[256,512]{1,0:T(8,128)}) custom-call(s32[1]{0:T(128)} %bitcast.2.place_ref, s32[1]{0:T(128)} %bitcast.1.mate_ref, bf16[4,768,128]{2,1,0:T(8,128)(2,1)} %copy-done, bf16[4,4,128,128]{3,2,1,0:T(8,128)(2,1)} %copy-done.1), custom_call_target="tpu_custom_call" | custom-call | tf_op jit(solution)/shard_map/pallas_call | solution.py:507
  68.2 0.7 copy-done.7
  69.0 6.8 %shard_map.140 = bf16[4,400,128]{2,1,0:T(8,128)(2,1)} custom-call(s32[5]{0:T(128)} %off_ref.3, s32[1]{0:T(128)} %bitcast.1.mate_ref, f32[4,2,128,128]{3,2,1,0:T(8,128)} %get-tuple-element.29.refs_0_, f32[4,2,128,128]{3,2,1,0:T(8,128)} %copy-done.3, f32[4,128,128]{2,1,0:T(8,128)} %get-tuple-element.37.refs_2_, f32[4,128,128]{2,1,0:T(8,128)} %copy-done.7, ...), custom_call_target="tpu_custom_call" | custom-call | tf_op jit(solution)/shard_map/pallas_call | solution.py:476
  75.8 3.6 %all-to-all-start.3 = ((bf16[4,400,128]{2,1,0:T(8,128)(2,1)}), bf16[4,400,128]{2,1,0:T(8,128)(2,1)S(1)}, u32[]{:S(2)}, u32[]{:S(2)}) async-start(bf16[4,400,128]{2,1,0:T(8,128)(2,1)} %shard_map.140), calls=%async_computation.3 | async-start | bytes 819200 | tf_op jit(solution)/shard_map/all_to_all | solution.py:86
  79.4 0.8 convert_add_fusion
  80.2 6.9 %all-to-all-done.3.in_ref = bf16[4,400,128]{2,1,0:T(8,128)(2,1)S(1)} async-done(((bf16[4,400,128]{2,1,0:T(8,128)(2,1)}), bf16[4,400,128]{2,1,0:T(8,128)(2,1)S(1)}, u32[]{:S(2)}, u32[]{:S(2)}) %all-to-all-start.3) | async-done | bytes 409632 | tf_op jit(solution)/shard_map/all_to_all | solution.py:86
  87.1 0.7 copy-done.4
  87.8 1.8 %shard_map.141 = (f32[128,256]{1,0:T(8,128)}, f32[128,256]{1,0:T(8,128)}, f32[128,512]{1,0:T(8,128)}, f32[4,128]{1,0:T(4,128)}, f32[4,128]{1,0:T(4,128)}) custom-call(bf16[4,400,128]{2,1,0:T(8,128)(2,1)} %copy-done.4), custom_call_target="tpu_custom_call" | custom-call | tf_op jit(solution)/shard_map/pallas_call | solution.py:515
  89.7 0.9 add.21
  (26 shorter events, 0.1 us)
Async XLA Ops:
  2.5 22.4 %all-to-all-start = ((bf16[4,400,128]{2,1,0:T(8,128)(2,1)}), bf16[4,400,128]{2,1,0:T(8,128)(2,1)S(1)}, u32[]{:S(2)}, u32[]{:S(2)}) async-start(bf16[4,400,128]{2,1,0:T(8,128)(2,1)} %shard_map.135), calls=%async_computation | async-start | bytes 819200 | tf_op jit(solution)/shard_map/all_to_all | solution.py:86
  7.6 12.9 %collective-permute-start.2 = (bf16[32,2048]{1,0:T(8,128)(2,1)}, bf16[32,2048]{1,0:T(8,128)(2,1)S(1)}, u32[]{:S(2)}, u32[]{:S(2)}) collective-permute-start(bf16[32,2048]{1,0:T(8,128)(2,1)} %refs_0_.1), channel_id=1, source_target_pairs={{2,0},{3,1},{0,2},{1,3},{6,4},{7,5},{4,6},{5,7},{10,8},{11,9},{8,1... | collective-permute-start | bytes 393224 | tf_op jit(solution)/shard_map/ppermute | solution.py:431
  10.2 10.4 %collective-permute-start.1 = (bf16[32,2048]{1,0:T(8,128)(2,1)}, bf16[32,2048]{1,0:T(8,128)(2,1)S(1)}, u32[]{:S(2)}, u32[]{:S(2)}) collective-permute-start(bf16[32,2048]{1,0:T(8,128)(2,1)} %refs_0_.1), channel_id=1, source_target_pairs={{1,0},{2,1},{3,2},{0,3},{5,4},{6,5},{7,6},{4,7},{9,8},{10,9},{11,1... | collective-permute-start | bytes 393224 | tf_op jit(solution)/shard_map/ppermute | solution.py:431
  11.6 9.0 %collective-permute-start.3 = (bf16[32,2048]{1,0:T(8,128)(2,1)}, bf16[32,2048]{1,0:T(8,128)(2,1)S(1)}, u32[]{:S(2)}, u32[]{:S(2)}) collective-permute-start(bf16[32,2048]{1,0:T(8,128)(2,1)} %refs_0_.1), channel_id=1, source_target_pairs={{3,0},{0,1},{1,2},{2,3},{7,4},{4,5},{5,6},{6,7},{11,8},{8,9},{9,10... | collective-permute-start | bytes 393224 | tf_op jit(solution)/shard_map/ppermute | solution.py:431
  20.6 0.7 copy-start.8
  20.6 0.7 copy-start.9
  20.6 0.7 copy-start.10
  24.8 3.8 %copy-start.2 = (bf16[4,400,128]{2,1,0:T(8,128)(2,1)}, bf16[4,400,128]{2,1,0:T(8,128)(2,1)S(1)}, u32[]{:S(2)}) copy-start(bf16[4,400,128]{2,1,0:T(8,128)(2,1)S(1)} %all-to-all-done.in_ref.refs_4_) | copy-start | bytes 1228804
  24.8 13.3 %all-to-all-start.1 = ((bf16[4,768,128]{2,1,0:T(8,128)(2,1)}), bf16[4,768,128]{2,1,0:T(8,128)(2,1)S(1)}, u32[]{:S(2)}, u32[]{:S(2)}) async-start(bf16[4,768,128]{2,1,0:T(8,128)(2,1)} %shard_map.137), calls=%async_computation.1 | async-start | bytes 1572864 | tf_op jit(solution)/shard_map/all_to_all | solution.py:86
  33.8 4.4 %collective-permute-start = (f32[4,2,128,128]{3,2,1,0:T(8,128)}, f32[4,2,128,128]{3,2,1,0:T(8,128)S(1)}, u32[]{:S(2)}, u32[]{:S(2)}) collective-permute-start(f32[4,2,128,128]{3,2,1,0:T(8,128)} %get-tuple-element.29.refs_0_), channel_id=1, source_target_pairs={{4,0},{0,4},{12,8},{8,12},{20,16},{16,20},{28,24},{24,28},{5,1},{1... | collective-permute-start | bytes 1572872 | tf_op jit(solution)/shard_map/ppermute | solution.py:93
  38.2 0.9 copy-start
  38.2 1.1 %copy-start.3 = (f32[4,2,128,128]{3,2,1,0:T(8,128)}, f32[4,2,128,128]{3,2,1,0:T(8,128)S(1)}, u32[]{:S(2)}) copy-start(f32[4,2,128,128]{3,2,1,0:T(8,128)S(1)} %collective-permute-done.refs_1_) | copy-start | bytes 1572868
  43.0 10.3 %all-to-all-start.2 = ((bf16[4,4,128,128]{3,2,1,0:T(8,128)(2,1)}), bf16[4,4,128,128]{3,2,1,0:T(8,128)(2,1)S(1)}, u32[]{:S(2)}, u32[]{:S(2)}) async-start(bf16[4,4,128,128]{3,2,1,0:T(8,128)(2,1)} %get-tuple-element.32), calls=%async_computation.2 | async-start | bytes 1048576 | tf_op jit(solution)/shard_map/all_to_all | solution.py:86
  46.5 21.7 %collective-permute-start.7 = (f32[4,128,128]{2,1,0:T(8,128)}, f32[4,128,128]{2,1,0:T(8,128)S(1)}, u32[]{:S(2)}, u32[]{:S(2)}) collective-permute-start(f32[4,128,128]{2,1,0:T(8,128)} %get-tuple-element.37.refs_2_), channel_id=1, source_target_pairs={{4,0},{0,4},{12,8},{8,12},{20,16},{16,20},{28,24},{24,28},{5,1},{1... | collective-permute-start | bytes 786440 | tf_op jit(solution)/shard_map/ppermute | solution.py:93
  53.4 0.8 copy-start.1
  57.2 22.2 %collective-permute-start.4 = (bf16[32,2048]{1,0:T(8,128)(2,1)}, bf16[32,2048]{1,0:T(8,128)(2,1)S(1)}, u32[]{:S(2)}, u32[]{:S(2)}) collective-permute-start(bf16[32,2048]{1,0:T(8,128)(2,1)} %get-tuple-element.34), channel_id=1, source_target_pairs={{1,0},{2,1},{3,2},{0,3},{5,4},{6,5},{7,6},{4,7},{9,8},{10,9},{11,1... | collective-permute-start | bytes 393224 | tf_op jit(solution)/shard_map/ppermute | solution.py:431
  61.6 17.8 %collective-permute-start.5 = (bf16[32,2048]{1,0:T(8,128)(2,1)}, bf16[32,2048]{1,0:T(8,128)(2,1)S(1)}, u32[]{:S(2)}, u32[]{:S(2)}) collective-permute-start(bf16[32,2048]{1,0:T(8,128)(2,1)} %get-tuple-element.35), channel_id=1, source_target_pairs={{2,0},{3,1},{0,2},{1,3},{6,4},{7,5},{4,6},{5,7},{10,8},{11,9},{8,1... | collective-permute-start | bytes 393224 | tf_op jit(solution)/shard_map/ppermute | solution.py:431
  63.4 15.9 %collective-permute-start.6 = (bf16[32,2048]{1,0:T(8,128)(2,1)}, bf16[32,2048]{1,0:T(8,128)(2,1)S(1)}, u32[]{:S(2)}, u32[]{:S(2)}) collective-permute-start(bf16[32,2048]{1,0:T(8,128)(2,1)} %get-tuple-element.36), channel_id=1, source_target_pairs={{3,0},{0,1},{1,2},{2,3},{7,4},{4,5},{5,6},{6,7},{11,8},{8,9},{9,10... | collective-permute-start | bytes 393224 | tf_op jit(solution)/shard_map/ppermute | solution.py:431
  68.2 21.4 %collective-permute-start.8 = (f32[256,512]{1,0:T(8,128)}, f32[256,512]{1,0:T(8,128)S(1)}, u32[]{:S(2)}, u32[]{:S(2)}) collective-permute-start(f32[256,512]{1,0:T(8,128)} %get-tuple-element.50), channel_id=1, source_target_pairs={{4,0},{0,4},{12,8},{8,12},{20,16},{16,20},{28,24},{24,28},{5,1},{1... | collective-permute-start | bytes 1572872 | tf_op jit(solution)/shard_map/ppermute | solution.py:93
  68.2 0.7 copy-start.7
  69.0 10.4 %copy-start.6 = (f32[32,2048]{1,0:T(8,128)S(1)}, f32[32,2048]{1,0:T(8,128)}, u32[]{:S(2)}) copy-start(f32[32,2048]{1,0:T(8,128)} %get-tuple-element.33) | copy-start | bytes 786436
  75.8 13.9 %copy-start.5 = (f32[256,512]{1,0:T(8,128)S(1)}, f32[256,512]{1,0:T(8,128)}, u32[]{:S(2)}) copy-start(f32[256,512]{1,0:T(8,128)} %get-tuple-element.49) | copy-start | bytes 1572868
  75.8 11.3 %all-to-all-start.3 = ((bf16[4,400,128]{2,1,0:T(8,128)(2,1)}), bf16[4,400,128]{2,1,0:T(8,128)(2,1)S(1)}, u32[]{:S(2)}, u32[]{:S(2)}) async-start(bf16[4,400,128]{2,1,0:T(8,128)(2,1)} %shard_map.140), calls=%async_computation.3 | async-start | bytes 819200 | tf_op jit(solution)/shard_map/all_to_all | solution.py:86
  87.1 0.8 copy-start.4

commit v4 on v3

--- a/solution.py
+++ b/solution.py
@@ -13,7 +13,7 @@
 EPS = 1e-06
 F32 = jnp.float32
 BF16 = jnp.bfloat16
-VMEM_LIMIT = 56 * 1024 * 1024
+VMEM_LIMIT = 24 * 1024 * 1024
 
 
 def dot(a, b, ca, cb):
@@ -54,16 +54,25 @@
     return lax.broadcasted_iota(jnp.int32, shape, 0), lax.broadcasted_iota(jnp.int32, shape, 1)
 
 
-def call(kernel, outs, n_in, smem=(), scratch=()):
+def call(kernel, outs, n_in, smem=(), scratch=(), flops=0, inside=True, fetch=False):
     spec = lambda i: pl.BlockSpec(memory_space=pltpu.SMEM if i in smem else pltpu.VMEM)
-    return pl.pallas_call(
+    if inside:
+        outs = jax.tree.map(lambda o: pltpu.VMEM(o.shape, o.dtype), outs)
+    run = pl.pallas_call(
         kernel,
         out_shape=outs,
         in_specs=[spec(i) for i in range(n_in)],
         out_specs=jax.tree.map(lambda _: pl.BlockSpec(memory_space=pltpu.VMEM), outs),
         scratch_shapes=list(scratch),
         compiler_params=pltpu.CompilerParams(vmem_limit_bytes=VMEM_LIMIT),
+        cost_estimate=pl.CostEstimate(flops=flops, bytes_accessed=0, transcendentals=0),
     )
+
+    def placed(*args):
+        hold = lambda x: pltpu.with_memory_space_constraint(x, pltpu.VMEM)
+        return run(*(x if fetch or i in smem else hold(x) for i, x in enumerate(args)))
+
+    return placed
 
 
 def arr(dtype, *shape):
@@ -432,7 +441,7 @@
 
     pieces = [grad_out] + [from_head(grad_out, d) for d in range(1, parts)]
 
-    sent = call(partial(pack_kernel, plan), arr(BF16, hv, plan.rows, DK), 5)(
+    sent = call(partial(pack_kernel, plan), arr(BF16, hv, plan.rows, DK), 5, flops=20_000_000_000, fetch=True)(
         queries, key_vectors, value_rows, write_rate, log_decay
     )
     got = plan.exchange(sent)
@@ -443,6 +452,7 @@
         parts + 2,
         smem=(0,),
         scratch=[pltpu.VMEM((tok, model), BF16)],
+        flops=4_000_000_000,
     )(head, *pieces, out_weight)
     cot = plan.exchange(cot_sent)
 
@@ -461,6 +471,7 @@
         ),
         3,
         smem=(0, 1),
+        flops=6_000_000_000,
     )(doc_offsets, mate, got)
     links = [link] + [plan.from_mate(link, d) for d in range(1, s)]
     out, states, back = call(
@@ -469,6 +480,7 @@
         s + 4,
         smem=(0,),
         scratch=[pltpu.VMEM((s, hv, 2, DK, DK), F32), pltpu.VMEM((n, DV, DK), F32)],
+        flops=4_000_000_000,
     )(mate, *links, cot, q, ol)
     mixed = plan.exchange(out)
     backs = [back] + [plan.from_mate(back, d) for d in range(1, s)]
@@ -483,29 +495,24 @@
             pltpu.VMEM((s, hv, DV, DK), F32),
             pltpu.VMEM((n, DV, DK), F32),
         ],
+        flops=20_000_000_000,
     )(doc_offsets, mate, *links, *backs, got, cot, x, a, w, ratio, u, states)
 
-    block = pl.BlockSpec((hv, 1, DV, tok), lambda i: (0, 0, 0, 0))
     rows = tok // parts
-    projected = pl.pallas_call(
+    projected = call(
         partial(project_kernel, plan, parts),
-        out_shape=[arr(BF16 if d else F32, rows, model) for d in range(parts)],
-        grid=(1,),
-        in_specs=[
-            pl.BlockSpec(memory_space=pltpu.SMEM),
-            block,
-            pl.BlockSpec(out_weight.shape, lambda i: (0, 0)),
-        ],
-        out_specs=[pl.BlockSpec((rows, model), lambda i: (0, 0))] * parts,
-        scratch_shapes=[pltpu.VMEM((tok, model), F32)],
-        compiler_params=pltpu.CompilerParams(vmem_limit_bytes=VMEM_LIMIT),
+        [arr(BF16 if d else F32, rows, model) for d in range(parts)],
+        3,
+        smem=(0,),
+        scratch=[pltpu.VMEM((tok, model), F32)],
+        flops=3_000_000_000,
     )(head, mixed, out_weight)
     layer_out = projected[0]
     for d in range(1, parts):
         layer_out = layer_out + from_head(projected[d], d).astype(F32)
 
     shares = call(
-        partial(weight_kernel, plan), [arr(F32, model // n, hv * DV)] * s, 4, smem=(0, 1)
+        partial(weight_kernel, plan), [arr(F32, model // n, hv * DV)] * s, 4, smem=(0, 1), flops=3_000_000_000
     )(place, mate, cot, mixed)
     weight_grad = shares[0]
     for d in range(1, s):
@@ -522,6 +529,8 @@
             arr(F32, hv, tok),
         ),
         1,
+        flops=2_000_000_000,
+        inside=False,
     )(grads)
     return (layer_out, grad_q, grad_k, grad_v, grad_rate, grad_decay, weight_grad)
 

time: 91.1 us -> 76.1 us (0.84)
  Pallas kernels: 28.7 us -> 15.7 us
  local copies, waits for them, and re-layouts: 4.06 us -> 15.5 us
  waiting for transfers between devices: 26.4 us -> 16 us
  starting transfers between devices: 29 us -> 25.7 us
    pallas_call x8, Pallas kernels: 28.7 us -> 15.7 us  [placed(): run(*(x if fetch or i in smem else hold(x) for i, x in enumerate(args)))]
    all_to_all x4, waiting for transfers between devices: 18 us -> 5.63 us  [exchange(): lax.all_to_all(x, 'ctx', split_axis=0, concat_axis=0, axis_index_groups=s...]
    unnamed x22 -> x42, local copies, waits for them, and re-layouts: 4.06 us -> 15.5 us
    ppermute x6, starting transfers between devices: 12.9 us -> 9.96 us  [from_head(): return lax.ppermute(x, 'head', [((i + d) % parts, i) for i in range(parts)])]
    ppermute x6, waiting for transfers between devices: 8.34 us -> 9.86 us  [from_head(): return lax.ppermute(x, 'head', [((i + d) % parts, i) for i in range(parts)])]
  transfers between devices with their start and end apart: 13 -> 13, of which waited for: 4 -> 5; matrix products, arithmetic and copies ran while one was open for 1% -> 1% of each run, Pallas kernels for 26% -> 18%
where the time goes in v4:
time: 76.1 us; the launch traced here: 75.4 us
  starting transfers between devices  25.7 us (34%)
  waiting for transfers between devices  16 us (21%)
  Pallas kernels  15.7 us (21%)
  local copies, waits for them, and re-layouts  15.5 us (20%)
  other arithmetic  1.63 us (2%)
  between operations  0.77 us (1%)
    pallas_call x8, Pallas kernels, placed(): run(*(x if fetch or i in smem else hold(x) for i, x in enumerate(args)))  15.7 us
    all_to_all x4, starting transfers between devices, exchange(): lax.all_to_all(x, 'ctx', split_axis=0, concat_axis=0, axis_index_groups=s...  15.6 us
    unnamed x42, local copies, waits for them, and re-layouts  15.5 us
    ppermute x6, starting transfers between devices, from_head(): return lax.ppermute(x, 'head', [((i + d) % parts, i) for i in range(parts)])  9.96 us
    ppermute x6, waiting for transfers between devices, from_head(): return lax.ppermute(x, 'head', [((i + d) % parts, i) for i in range(parts)])  9.86 us
    all_to_all x4, waiting for transfers between devices, exchange(): lax.all_to_all(x, 'ctx', split_axis=0, concat_axis=0, axis_index_groups=s...  5.63 us
  transfers between devices with their start and end apart: 13, of which 5 were waited for; matrix products, arithmetic and copies ran while one was open for 1% of the time, Pallas kernels for 18%

profile of v4, /device:TPU:0, one launch (start us, length us, event | category | flops | bytes accessed | tf_op | source)
XLA Modules:
  0.0 75.4 jit_solution(3929202442920891681)
XLA Ops:
  0.6 4.1 %collective-permute-start.2 = (bf16[32,2048]{1,0:T(8,128)(2,1)}, bf16[32,2048]{1,0:T(8,128)(2,1)S(1)}, u32[]{:S(2)}, u32[]{:S(2)}) collective-permute-start(bf16[32,2048]{1,0:T(8,128)(2,1)} %refs_0_.1), channel_id=1, source_target_pairs={{2,0},{3,1},{0,2},{1,3},{6,4},{7,5},{4,6},{5,7},{10,8},{11,9},{8,1... | collective-permute-start | bytes 393224 | tf_op jit(solution)/shard_map/ppermute | solution.py:440
  4.7 1.3 %collective-permute-start.1 = (bf16[32,2048]{1,0:T(8,128)(2,1)}, bf16[32,2048]{1,0:T(8,128)(2,1)S(1)}, u32[]{:S(2)}, u32[]{:S(2)}) collective-permute-start(bf16[32,2048]{1,0:T(8,128)(2,1)} %refs_0_.1), channel_id=1, source_target_pairs={{1,0},{2,1},{3,2},{0,3},{5,4},{6,5},{7,6},{4,7},{9,8},{10,9},{11,1... | collective-permute-start | bytes 393224 | tf_op jit(solution)/shard_map/ppermute | solution.py:440
  6.8 0.9 %copy-done.2 = bf16[128,512]{1,0:T(8,128)(2,1)S(1)} copy-done((bf16[128,512]{1,0:T(8,128)(2,1)S(1)}, bf16[128,512]{1,0:T(8,128)(2,1)}, u32[]{:S(2)}) %copy-start.2) | copy-done | bytes 131096
  7.7 0.8 %copy-done.4 = bf16[128,256]{1,0:T(8,128)(2,1)S(1)} copy-done((bf16[128,256]{1,0:T(8,128)(2,1)S(1)}, bf16[128,256]{1,0:T(8,128)(2,1)}, u32[]{:S(2)}) %copy-start.4) | copy-done | bytes 65560
  8.5 0.8 %copy-done.5 = bf16[128,256]{1,0:T(8,128)(2,1)S(1)} copy-done((bf16[128,256]{1,0:T(8,128)(2,1)S(1)}, bf16[128,256]{1,0:T(8,128)(2,1)}, u32[]{:S(2)}) %copy-start.5) | copy-done | bytes 65560
  10.7 0.9 %shard_map.135 = bf16[4,400,128]{2,1,0:T(8,128)(2,1)} custom-call(bf16[128,256]{1,0:T(8,128)(2,1)S(1)} %copy-done.4, bf16[128,256]{1,0:T(8,128)(2,1)S(1)} %copy-done.5, bf16[128,512]{1,0:T(8,128)(2,1)S(1)} %copy-done.2, f32[4,128]{1,0:T(4,128)S(1)} %copy-done.6, f32[4,128]{1,0:T(4,128)S(1)} %copy-done.7), custom_call_target="tpu_custom_call" | custom-call | flops 20000000000 | tf_op jit(solution)/shard_map/pallas_call | solution.py:73
  11.6 3.7 %all-to-all-start = ((bf16[4,400,128]{2,1,0:T(8,128)(2,1)}), bf16[4,400,128]{2,1,0:T(8,128)(2,1)S(1)}, u32[]{:S(2)}, u32[]{:S(2)}) async-start(bf16[4,400,128]{2,1,0:T(8,128)(2,1)} %shard_map.135), calls=%async_computation | async-start | bytes 819200 | tf_op jit(solution)/shard_map/all_to_all | solution.py:95
  15.3 1.7 %shard_map.137 = bf16[4,768,128]{2,1,0:T(8,128)(2,1)} custom-call(s32[1]{0:T(128)} %bitcast.head_ref, bf16[32,2048]{1,0:T(8,128)(2,1)S(1)} %copy-done.3, bf16[32,2048]{1,0:T(8,128)(2,1)S(1)} %collective-permute-done.1.refs_1_, bf16[32,2048]{1,0:T(8,128)(2,1)S(1)} %collective-permute-done.2.refs_2_, bf16[32,2048]{1,0:T(8,128)(2,1)S(1)} %collective-permute-done.3.refs_3_, ...), custom_call_target="tpu_custom_call" | custom-call | flops 4000000000 | tf_op jit(solution)/shard_map/pallas_call | solution.py:73
  17.0 4.3 %all-to-all-done.in_ref.refs_4_ = bf16[4,400,128]{2,1,0:T(8,128)(2,1)S(1)} async-done(((bf16[4,400,128]{2,1,0:T(8,128)(2,1)}), bf16[4,400,128]{2,1,0:T(8,128)(2,1)S(1)}, u32[]{:S(2)}, u32[]{:S(2)}) %all-to-all-start) | async-done | bytes 409632 | tf_op jit(solution)/shard_map/all_to_all | solution.py:95
  21.3 3.5 %all-to-all-start.1 = ((bf16[4,768,128]{2,1,0:T(8,128)(2,1)}), bf16[4,768,128]{2,1,0:T(8,128)(2,1)S(1)}, u32[]{:S(2)}, u32[]{:S(2)}) async-start(bf16[4,768,128]{2,1,0:T(8,128)(2,1)} %shard_map.137), calls=%async_computation.1 | async-start | bytes 1572864 | tf_op jit(solution)/shard_map/all_to_all | solution.py:95
  24.8 3.9 %shard_map.136 = (f32[4,2,128,128]{3,2,1,0:T(8,128)S(1)}, bf16[4,2,128,128]{3,2,1,0:T(8,128)(2,1)S(1)}, bf16[4,2,128,128]{3,2,1,0:T(8,128)(2,1)S(1)}, bf16[4,2,1...) custom-call(s32[5]{0:T(128)S(1)} %copy-done.8, ...), custom_call_target="tpu_custom_call" | custom-call | flops 6000000000 | tf_op jit(solution)/shard_map/pallas_call | solution.py:73
  30.1 0.7 copy-done.15
  30.8 0.7 copy-done.17
  31.5 0.7 copy-done.19
  32.2 1.4 %all-to-all-done.1.refs_2_.refs_5_.cot_ref = bf16[4,768,128]{2,1,0:T(8,128)(2,1)S(1)} async-done(((bf16[4,768,128]{2,1,0:T(8,128)(2,1)}), bf16[4,768,128]{2,1,0:T(8,128)(2,1)S(1)}, u32[]{:S(2)}, u32[]{:S(2)}) %all-to-all-start.1) | async-done | bytes 786464 | tf_op jit(solution)/shard_map/all_to_all | solution.py:95
  34.1 2.1 %shard_map.138 = (bf16[4,4,128,128]{3,2,1,0:T(8,128)(2,1)}, f32[4,128,128]{2,1,0:T(8,128)S(1)}, f32[4,128,128]{2,1,0:T(8,128)S(1)}) custom-call(s32[1]{0:T(128)} %bitcast.1.mate_ref, f32[4,2,128,128]{3,2,1,0:T(8,128)S(1)} %get-tuple-element.29.refs_0_, f32[4,2,128,128]{3,2,1,0:T(8,128)S(1)} %collective-permute-done.refs_1_, ...), custom_call_target="tpu_custom_call" | custom-call | flops 4000000000 | tf_op jit(solution)/shard_map/pallas_call | solution.py:73
  37.1 4.2 %all-to-all-start.2 = ((bf16[4,4,128,128]{3,2,1,0:T(8,128)(2,1)}), bf16[4,4,128,128]{3,2,1,0:T(8,128)(2,1)S(1)}, u32[]{:S(2)}, u32[]{:S(2)}) async-start(bf16[4,4,128,128]{3,2,1,0:T(8,128)(2,1)} %get-tuple-element.32), calls=%async_computation.2 | async-start | bytes 1048576 | tf_op jit(solution)/shard_map/all_to_all | solution.py:95
  41.3 0.9 %copy-done.10 = f32[4,128,128]{2,1,0:T(8,128)S(1)} copy-done((f32[4,128,128]{2,1,0:T(8,128)S(1)}, f32[4,128,128]{2,1,0:T(8,128)}, u32[]{:S(2)}) %copy-start.10) | copy-done | bytes 262168
  42.2 0.9 %copy-done.12 = bf16[4,2,128,128]{3,2,1,0:T(8,128)(2,1)S(1)} copy-done((bf16[4,2,128,128]{3,2,1,0:T(8,128)(2,1)S(1)}, bf16[4,2,128,128]{3,2,1,0:T(8,128)(2,1)}, u32[]{:S(2)}) %copy-start.12) | copy-done | bytes 262168
  43.2 0.9 %copy-done.14 = bf16[4,2,128,128]{3,2,1,0:T(8,128)(2,1)S(1)} copy-done((bf16[4,2,128,128]{3,2,1,0:T(8,128)(2,1)S(1)}, bf16[4,2,128,128]{3,2,1,0:T(8,128)(2,1)}, u32[]{:S(2)}) %copy-start.14) | copy-done | bytes 262168
  44.1 0.9 %copy-done.16 = bf16[4,2,128,128]{3,2,1,0:T(8,128)(2,1)S(1)} copy-done((bf16[4,2,128,128]{3,2,1,0:T(8,128)(2,1)S(1)}, bf16[4,2,128,128]{3,2,1,0:T(8,128)(2,1)}, u32[]{:S(2)}) %copy-start.16) | copy-done | bytes 262168
  45.1 0.9 %copy-done.18 = f32[4,128,128]{2,1,0:T(8,128)S(1)} copy-done((f32[4,128,128]{2,1,0:T(8,128)S(1)}, f32[4,128,128]{2,1,0:T(8,128)}, u32[]{:S(2)}) %copy-start.18) | copy-done | bytes 262168
  46.0 0.9 %copy-done.20 = f32[4,128,128]{2,1,0:T(8,128)S(1)} copy-done((f32[4,128,128]{2,1,0:T(8,128)S(1)}, f32[4,128,128]{2,1,0:T(8,128)}, u32[]{:S(2)}) %copy-start.20) | copy-done | bytes 262168
  47.0 5.1 %shard_map.140 = bf16[4,400,128]{2,1,0:T(8,128)(2,1)} custom-call(s32[5]{0:T(128)S(1)} %copy-done.8, s32[1]{0:T(128)} %bitcast.1.mate_ref, f32[4,2,128,128]{3,2,1,0:T(8,128)S(1)} %get-tuple-element.29.refs_0_, f32[4,2,128,128]{3,2,1,0:T(8,128)S(1)} %collective-permute-done.refs_1_, f32[4,128,128]{2,1,0:T(8,128)S(1)} %get-tuple-element.37.refs_2_, ...), custom_call_target="tpu_custom_call" | custom-call | flops 20000000000 | tf_op jit(solution)/shard_map/pallas_call | solution.py:73
  52.1 4.2 %all-to-all-start.3 = ((bf16[4,400,128]{2,1,0:T(8,128)(2,1)}), bf16[4,400,128]{2,1,0:T(8,128)(2,1)S(1)}, u32[]{:S(2)}, u32[]{:S(2)}) async-start(bf16[4,400,128]{2,1,0:T(8,128)(2,1)} %shard_map.140), calls=%async_computation.3 | async-start | bytes 819200 | tf_op jit(solution)/shard_map/all_to_all | solution.py:95
  56.3 1.6 %copy-done.1 = bf16[512,2048]{1,0:T(8,128)(2,1)S(1)} copy-done((bf16[512,2048]{1,0:T(8,128)(2,1)S(1)}, bf16[512,2048]{1,0:T(8,128)(2,1)}, u32[]{:S(2)}) %copy-start.1) | copy-done | bytes 2097176
  58.4 3.2 %collective-permute-start.4 = (bf16[32,2048]{1,0:T(8,128)(2,1)S(1)}, bf16[32,2048]{1,0:T(8,128)(2,1)S(1)}, u32[]{:S(2)}, u32[]{:S(2)}) collective-permute-start(bf16[32,2048]{1,0:T(8,128)(2,1)S(1)} %get-tuple-element.34), channel_id=1, source_target_pairs={{1,0},{2,1},{3,2},{0,3},{5,4},{6,5},{7,6},{4,7},{9,8},{10,9},{11,1... | collective-permute-start | bytes 393224 | tf_op jit(solution)/shard_map/ppermute | solution.py:440
  63.0 2.5 %collective-permute-done.4 = bf16[32,2048]{1,0:T(8,128)(2,1)S(1)} collective-permute-done((bf16[32,2048]{1,0:T(8,128)(2,1)S(1)}, bf16[32,2048]{1,0:T(8,128)(2,1)S(1)}, u32[]{:S(2)}, u32[]{:S(2)}) %collective-permute-start.4) | collective-permute-done | bytes 131104 | tf_op jit(solution)/shard_map/ppermute | solution.py:440
  65.6 7.3 %collective-permute-done.5 = bf16[32,2048]{1,0:T(8,128)(2,1)S(1)} collective-permute-done((bf16[32,2048]{1,0:T(8,128)(2,1)S(1)}, bf16[32,2048]{1,0:T(8,128)(2,1)S(1)}, u32[]{:S(2)}, u32[]{:S(2)}) %collective-permute-start.5) | collective-permute-done | bytes 131104 | tf_op jit(solution)/shard_map/ppermute | solution.py:440
  72.9 0.8 %convert_add_fusion = f32[32,2048]{1,0:T(8,128)} fusion(bf16[32,2048]{1,0:T(8,128)(2,1)S(1)} %collective-permute-done.6, bf16[32,2048]{1,0:T(8,128)(2,1)S(1)} %collective-permute-done.5, f32[32,2048]{1,0:T(8,128)S(1)} %get-tuple-element.33, bf16[32,2048]{1,0:T(8,128)(2,1)S(1)} %collective-permute-done.4), kind=kLoop, calls=%fused_computation | loop fusion | flops 393216 | bytes 917504 | tf_op jit(solution)/shard_map/add | solution.py:512
  73.7 0.8 %shard_map.141 = (f32[128,256]{1,0:T(8,128)}, f32[128,256]{1,0:T(8,128)}, f32[128,512]{1,0:T(8,128)}, f32[4,128]{1,0:T(4,128)}, f32[4,128]{1,0:T(4,128)}) custom-call(bf16[4,400,128]{2,1,0:T(8,128)(2,1)S(1)} %all-to-all-done.3.in_ref), custom_call_target="tpu_custom_call" | custom-call | flops 2000000000 | tf_op jit(solution)/shard_map/pallas_call | solution.py:73
  74.5 0.9 %add.21 = f32[256,512]{1,0:T(8,128)} add(f32[256,512]{1,0:T(8,128)S(1)} %get-tuple-element.49, f32[256,512]{1,0:T(8,128)S(1)} %collective-permute-done.8) | non-fusion elementwise | flops 131072 | bytes 1572864 | tf_op jit(solution)/shard_map/add | solution.py:519
  (46 shorter events, 6.8 us)
Async XLA Ops:
  0.6 14.7 %copy-start = (bf16[512,2048]{1,0:T(8,128)(2,1)S(1)}, bf16[512,2048]{1,0:T(8,128)(2,1)}, u32[]{:S(2)}) copy-start(bf16[512,2048]{1,0:T(8,128)(2,1)} %w_ref.1) | copy-start | bytes 6291460
  0.6 14.7 %collective-permute-start.2 = (bf16[32,2048]{1,0:T(8,128)(2,1)}, bf16[32,2048]{1,0:T(8,128)(2,1)S(1)}, u32[]{:S(2)}, u32[]{:S(2)}) collective-permute-start(bf16[32,2048]{1,0:T(8,128)(2,1)} %refs_0_.1), channel_id=1, source_target_pairs={{2,0},{3,1},{0,2},{1,3},{6,4},{7,5},{4,6},{5,7},{10,8},{11,9},{8,1... | collective-permute-start | bytes 393224 | tf_op jit(solution)/shard_map/ppermute | solution.py:440
  4.7 10.6 %collective-permute-start.1 = (bf16[32,2048]{1,0:T(8,128)(2,1)}, bf16[32,2048]{1,0:T(8,128)(2,1)S(1)}, u32[]{:S(2)}, u32[]{:S(2)}) collective-permute-start(bf16[32,2048]{1,0:T(8,128)(2,1)} %refs_0_.1), channel_id=1, source_target_pairs={{1,0},{2,1},{3,2},{0,3},{5,4},{6,5},{7,6},{4,7},{9,8},{10,9},{11,1... | collective-permute-start | bytes 393224 | tf_op jit(solution)/shard_map/ppermute | solution.py:440
  6.1 9.2 %collective-permute-start.3 = (bf16[32,2048]{1,0:T(8,128)(2,1)}, bf16[32,2048]{1,0:T(8,128)(2,1)S(1)}, u32[]{:S(2)}, u32[]{:S(2)}) collective-permute-start(bf16[32,2048]{1,0:T(8,128)(2,1)} %refs_0_.1), channel_id=1, source_target_pairs={{3,0},{0,1},{1,2},{2,3},{7,4},{4,5},{5,6},{6,7},{11,8},{8,9},{9,10... | collective-permute-start | bytes 393224 | tf_op jit(solution)/shard_map/ppermute | solution.py:440
  6.8 0.9 %copy-start.2 = (bf16[128,512]{1,0:T(8,128)(2,1)S(1)}, bf16[128,512]{1,0:T(8,128)(2,1)}, u32[]{:S(2)}) copy-start(bf16[128,512]{1,0:T(8,128)(2,1)} %v_ref.1) | copy-start | bytes 393220
  7.7 0.8 %copy-start.4 = (bf16[128,256]{1,0:T(8,128)(2,1)S(1)}, bf16[128,256]{1,0:T(8,128)(2,1)}, u32[]{:S(2)}) copy-start(bf16[128,256]{1,0:T(8,128)(2,1)} %q_ref.1) | copy-start | bytes 196612
  8.5 0.8 %copy-start.5 = (bf16[128,256]{1,0:T(8,128)(2,1)S(1)}, bf16[128,256]{1,0:T(8,128)(2,1)}, u32[]{:S(2)}) copy-start(bf16[128,256]{1,0:T(8,128)(2,1)} %k_ref.1) | copy-start | bytes 196612
  10.7 4.6 %copy-start.3 = (bf16[32,2048]{1,0:T(8,128)(2,1)S(1)}, bf16[32,2048]{1,0:T(8,128)(2,1)}, u32[]{:S(2)}) copy-start(bf16[32,2048]{1,0:T(8,128)(2,1)} %refs_0_.1) | copy-start | bytes 393220
  11.6 9.7 %all-to-all-start = ((bf16[4,400,128]{2,1,0:T(8,128)(2,1)}), bf16[4,400,128]{2,1,0:T(8,128)(2,1)S(1)}, u32[]{:S(2)}, u32[]{:S(2)}) async-start(bf16[4,400,128]{2,1,0:T(8,128)(2,1)} %shard_map.135), calls=%async_computation | async-start | bytes 819200 | tf_op jit(solution)/shard_map/all_to_all | solution.py:95
  15.3 9.4 %copy-start.8 = (s32[5]{0:T(128)S(1)}, s32[5]{0:T(128)}, u32[]{:S(2)}) copy-start(s32[5]{0:T(128)} %off_ref.3) | copy-start | bytes 64
  21.3 12.3 %all-to-all-start.1 = ((bf16[4,768,128]{2,1,0:T(8,128)(2,1)}), bf16[4,768,128]{2,1,0:T(8,128)(2,1)S(1)}, u32[]{:S(2)}, u32[]{:S(2)}) async-start(bf16[4,768,128]{2,1,0:T(8,128)(2,1)} %shard_map.137), calls=%async_computation.1 | async-start | bytes 1572864 | tf_op jit(solution)/shard_map/all_to_all | solution.py:95
  28.7 0.7 copy-start.11
  29.4 0.7 copy-start.13
  30.1 0.7 copy-start.15
  30.8 0.7 copy-start.17
  31.5 0.7 copy-start.19
  32.2 1.9 %collective-permute-start = (f32[4,2,128,128]{3,2,1,0:T(8,128)S(1)}, f32[4,2,128,128]{3,2,1,0:T(8,128)S(1)}, u32[]{:S(2)}, u32[]{:S(2)}) collective-permute-start(f32[4,2,128,128]{3,2,1,0:T(8,128)S(1)} %get-tuple-element.29.refs_0_), channel_id=1, source_target_pairs={{4,0},{0,4},{12,8},{8,12},{20,16},{16,20},{28,24},{24,28},{5,1},{1... | collective-permute-start | bytes 1572872 | tf_op jit(solution)/shard_map/ppermute | solution.py:102
  36.3 0.7 copy-start.9
  37.0 4.3 %collective-permute-start.7 = (f32[4,128,128]{2,1,0:T(8,128)S(1)}, f32[4,128,128]{2,1,0:T(8,128)S(1)}, u32[]{:S(2)}, u32[]{:S(2)}) collective-permute-start(f32[4,128,128]{2,1,0:T(8,128)S(1)} %get-tuple-element.37.refs_2_), channel_id=1, source_target_pairs={{4,0},{0,4},{12,8},{8,12},{20,16},{16,20},{28,24},{24,28},{5,1},{1... | collective-permute-start | bytes 786440 | tf_op jit(solution)/shard_map/ppermute | solution.py:102
  37.1 15.0 %all-to-all-start.2 = ((bf16[4,4,128,128]{3,2,1,0:T(8,128)(2,1)}), bf16[4,4,128,128]{3,2,1,0:T(8,128)(2,1)S(1)}, u32[]{:S(2)}, u32[]{:S(2)}) async-start(bf16[4,4,128,128]{3,2,1,0:T(8,128)(2,1)} %get-tuple-element.32), calls=%async_computation.2 | async-start | bytes 1048576 | tf_op jit(solution)/shard_map/all_to_all | solution.py:95
  41.3 1.0 %copy-start.10 = (f32[4,128,128]{2,1,0:T(8,128)S(1)}, f32[4,128,128]{2,1,0:T(8,128)}, u32[]{:S(2)}) copy-start(f32[4,128,128]{2,1,0:T(8,128)} %copy-done.9) | copy-start | bytes 786436
  42.2 0.9 %copy-start.12 = (bf16[4,2,128,128]{3,2,1,0:T(8,128)(2,1)S(1)}, bf16[4,2,128,128]{3,2,1,0:T(8,128)(2,1)}, u32[]{:S(2)}) copy-start(bf16[4,2,128,128]{3,2,1,0:T(8,128)(2,1)} %copy-done.11) | copy-start | bytes 786436
  43.2 0.9 %copy-start.14 = (bf16[4,2,128,128]{3,2,1,0:T(8,128)(2,1)S(1)}, bf16[4,2,128,128]{3,2,1,0:T(8,128)(2,1)}, u32[]{:S(2)}) copy-start(bf16[4,2,128,128]{3,2,1,0:T(8,128)(2,1)} %copy-done.13) | copy-start | bytes 786436
  44.1 0.9 %copy-start.16 = (bf16[4,2,128,128]{3,2,1,0:T(8,128)(2,1)S(1)}, bf16[4,2,128,128]{3,2,1,0:T(8,128)(2,1)}, u32[]{:S(2)}) copy-start(bf16[4,2,128,128]{3,2,1,0:T(8,128)(2,1)} %copy-done.15) | copy-start | bytes 786436
  45.1 0.9 %copy-start.18 = (f32[4,128,128]{2,1,0:T(8,128)S(1)}, f32[4,128,128]{2,1,0:T(8,128)}, u32[]{:S(2)}) copy-start(f32[4,128,128]{2,1,0:T(8,128)} %copy-done.17) | copy-start | bytes 786436
  46.0 0.9 %copy-start.20 = (f32[4,128,128]{2,1,0:T(8,128)S(1)}, f32[4,128,128]{2,1,0:T(8,128)}, u32[]{:S(2)}) copy-start(f32[4,128,128]{2,1,0:T(8,128)} %copy-done.19) | copy-start | bytes 786436
  52.1 21.6 %all-to-all-start.3 = ((bf16[4,400,128]{2,1,0:T(8,128)(2,1)}), bf16[4,400,128]{2,1,0:T(8,128)(2,1)S(1)}, u32[]{:S(2)}, u32[]{:S(2)}) async-start(bf16[4,400,128]{2,1,0:T(8,128)(2,1)} %shard_map.140), calls=%async_computation.3 | async-start | bytes 819200 | tf_op jit(solution)/shard_map/all_to_all | solution.py:95
  56.3 1.6 %copy-start.1 = (bf16[512,2048]{1,0:T(8,128)(2,1)S(1)}, bf16[512,2048]{1,0:T(8,128)(2,1)}, u32[]{:S(2)}) copy-start(bf16[512,2048]{1,0:T(8,128)(2,1)} %w_ref.1) | copy-start | bytes 6291460
  58.4 7.1 %collective-permute-start.4 = (bf16[32,2048]{1,0:T(8,128)(2,1)S(1)}, bf16[32,2048]{1,0:T(8,128)(2,1)S(1)}, u32[]{:S(2)}, u32[]{:S(2)}) collective-permute-start(bf16[32,2048]{1,0:T(8,128)(2,1)S(1)} %get-tuple-element.34), channel_id=1, source_target_pairs={{1,0},{2,1},{3,2},{0,3},{5,4},{6,5},{7,6},{4,7},{9,8},{10,9},{11,1... | collective-permute-start | bytes 393224 | tf_op jit(solution)/shard_map/ppermute | solution.py:440
  61.6 11.3 %collective-permute-start.5 = (bf16[32,2048]{1,0:T(8,128)(2,1)S(1)}, bf16[32,2048]{1,0:T(8,128)(2,1)S(1)}, u32[]{:S(2)}, u32[]{:S(2)}) collective-permute-start(bf16[32,2048]{1,0:T(8,128)(2,1)S(1)} %get-tuple-element.35), channel_id=1, source_target_pairs={{2,0},{3,1},{0,2},{1,3},{6,4},{7,5},{4,6},{5,7},{10,8},{11,9},{8,1... | collective-permute-start | bytes 393224 | tf_op jit(solution)/shard_map/ppermute | solution.py:440
  61.6 11.3 %collective-permute-start.6 = (bf16[32,2048]{1,0:T(8,128)(2,1)S(1)}, bf16[32,2048]{1,0:T(8,128)(2,1)S(1)}, u32[]{:S(2)}, u32[]{:S(2)}) collective-permute-start(bf16[32,2048]{1,0:T(8,128)(2,1)S(1)} %get-tuple-element.36), channel_id=1, source_target_pairs={{3,0},{0,1},{1,2},{2,3},{7,4},{4,5},{5,6},{6,7},{11,8},{8,9},{9,10... | collective-permute-start | bytes 393224 | tf_op jit(solution)/shard_map/ppermute | solution.py:440
  63.0 11.5 %collective-permute-start.8 = (f32[256,512]{1,0:T(8,128)S(1)}, f32[256,512]{1,0:T(8,128)S(1)}, u32[]{:S(2)}, u32[]{:S(2)}) collective-permute-start(f32[256,512]{1,0:T(8,128)S(1)} %get-tuple-element.50), channel_id=1, source_target_pairs={{4,0},{0,4},{12,8},{8,12},{20,16},{16,20},{28,24},{24,28},{5,1},{1... | collective-permute-start | bytes 1572872 | tf_op jit(solution)/shard_map/ppermute | solution.py:102
  (2 other events, 1.4 us)

commit v5 on v4

--- a/solution.py
+++ b/solution.py
@@ -1,3 +1,4 @@
+import math
 from functools import partial
 
 import jax
@@ -13,7 +14,7 @@
 EPS = 1e-06
 F32 = jnp.float32
 BF16 = jnp.bfloat16
-VMEM_LIMIT = 24 * 1024 * 1024
+SPARE_VMEM = 8 * 1024 * 1024
 
 
 def dot(a, b, ca, cb):
@@ -64,13 +65,16 @@
         in_specs=[spec(i) for i in range(n_in)],
         out_specs=jax.tree.map(lambda _: pl.BlockSpec(memory_space=pltpu.VMEM), outs),
         scratch_shapes=list(scratch),
-        compiler_params=pltpu.CompilerParams(vmem_limit_bytes=VMEM_LIMIT),
+        compiler_params=pltpu.CompilerParams(
+            vmem_limit_bytes=SPARE_VMEM + sum(x.dtype.itemsize * math.prod(x.shape) for x in scratch)
+        ),
         cost_estimate=pl.CostEstimate(flops=flops, bytes_accessed=0, transcendentals=0),
     )
 
     def placed(*args):
-        hold = lambda x: pltpu.with_memory_space_constraint(x, pltpu.VMEM)
-        return run(*(x if fetch or i in smem else hold(x) for i, x in enumerate(args)))
+        space = pltpu.HBM if fetch else pltpu.VMEM
+        hold = lambda x: pltpu.with_memory_space_constraint(x, space)
+        return run(*(x if i in smem else hold(x) for i, x in enumerate(args)))
 
     return placed
 
@@ -507,10 +511,6 @@
         scratch=[pltpu.VMEM((tok, model), F32)],
         flops=3_000_000_000,
     )(head, mixed, out_weight)
-    layer_out = projected[0]
-    for d in range(1, parts):
-        layer_out = layer_out + from_head(projected[d], d).astype(F32)
-
     shares = call(
         partial(weight_kernel, plan), [arr(F32, model // n, hv * DV)] * s, 4, smem=(0, 1), flops=3_000_000_000
     )(place, mate, cot, mixed)
@@ -518,7 +518,11 @@
     for d in range(1, s):
         weight_grad = weight_grad + plan.from_mate(shares[d], d)
 
+    grad_sent, _ = lax.optimization_barrier((grad_sent, projected[1]))
     grads = plan.exchange(grad_sent)
+    layer_out = projected[0]
+    for d in range(1, parts):
+        layer_out = layer_out + from_head(projected[d], d).astype(F32)
     grad_q, grad_k, grad_v, grad_rate, grad_decay = call(
         partial(finish_kernel, plan),
         (

time: 76.1 us -> 72.9 us (0.958)
  local copies, waits for them, and re-layouts: 15.5 us -> 11.5 us
  starting transfers between devices: 25.7 us -> 28 us
  waiting for transfers between devices: 16 us -> 13.8 us
  Pallas kernels: 15.7 us -> 16.7 us
    unnamed x42 -> x32, local copies, waits for them, and re-layouts: 15.5 us -> 11.5 us
    all_to_all x4, waiting for transfers between devices: 5.63 us -> 2.8 us  [exchange(): lax.all_to_all(x, 'ctx', split_axis=0, concat_axis=0, axis_index_groups=s...]
    ppermute x6, starting transfers between devices: 9.96 us -> 12.2 us  [from_head(): return lax.ppermute(x, 'head', [((i + d) % parts, i) for i in range(parts)])]
    pallas_call x8, Pallas kernels: 15.7 us -> 16.7 us  [placed(): return run(*(x if i in smem else hold(x) for i, x in enumerate(args)))]
  transfers between devices with their start and end apart: 13 -> 13, of which waited for: 5 -> 6; matrix products, arithmetic and copies ran while one was open for 1% -> 1% of each run, Pallas kernels for 18% -> 19%
where the time goes in v5:
time: 72.9 us; the launch traced here: 72.3 us
  starting transfers between devices  28 us (38%)
  Pallas kernels  16.7 us (23%)
  waiting for transfers between devices  13.8 us (19%)
  local copies, waits for them, and re-layouts  11.5 us (16%)
  other arithmetic  1.64 us (2%)
  between operations  0.74 us (1%)
    pallas_call x8, Pallas kernels, placed(): return run(*(x if i in smem else hold(x) for i, x in enumerate(args)))  16.7 us
    all_to_all x4, starting transfers between devices, exchange(): lax.all_to_all(x, 'ctx', split_axis=0, concat_axis=0, axis_index_groups=s...  15.6 us
    ppermute x6, starting transfers between devices, from_head(): return lax.ppermute(x, 'head', [((i + d) % parts, i) for i in range(parts)])  12.2 us
    unnamed x32, local copies, waits for them, and re-layouts  11.5 us
    ppermute x6, waiting for transfers between devices, from_head(): return lax.ppermute(x, 'head', [((i + d) % parts, i) for i in range(parts)])  10.5 us
    all_to_all x4, waiting for transfers between devices, exchange(): lax.all_to_all(x, 'ctx', split_axis=0, concat_axis=0, axis_index_groups=s...  2.8 us
  transfers between devices with their start and end apart: 13, of which 6 were waited for; matrix products, arithmetic and copies ran while one was open for 1% of the time, Pallas kernels for 19%

profile of v5, /device:TPU:0, one launch (start us, length us, event | category | flops | bytes accessed | tf_op | source)
XLA Modules:
  0.0 72.3 jit_solution(2795326783523879336)
XLA Ops:
  0.7 4.1 %collective-permute-start.2 = (bf16[32,2048]{1,0:T(8,128)(2,1)}, bf16[32,2048]{1,0:T(8,128)(2,1)S(1)}, u32[]{:S(2)}, u32[]{:S(2)}) collective-permute-start(bf16[32,2048]{1,0:T(8,128)(2,1)} %refs_0_.1), channel_id=1, source_target_pairs={{2,0},{3,1},{0,2},{1,3},{6,4},{7,5},{4,6},{5,7},{10,8},{11,9},{8,1... | collective-permute-start | bytes 393224 | tf_op jit(solution)/shard_map/ppermute | solution.py:444
  4.8 1.3 %collective-permute-start.1 = (bf16[32,2048]{1,0:T(8,128)(2,1)}, bf16[32,2048]{1,0:T(8,128)(2,1)S(1)}, u32[]{:S(2)}, u32[]{:S(2)}) collective-permute-start(bf16[32,2048]{1,0:T(8,128)(2,1)} %refs_0_.1), channel_id=1, source_target_pairs={{1,0},{2,1},{3,2},{0,3},{5,4},{6,5},{7,6},{4,7},{9,8},{10,9},{11,1... | collective-permute-start | bytes 393224 | tf_op jit(solution)/shard_map/ppermute | solution.py:444
  6.8 1.8 %shard_map.135 = bf16[4,400,128]{2,1,0:T(8,128)(2,1)} custom-call(bf16[128,256]{1,0:T(8,128)(2,1)} %q_ref.1, bf16[128,256]{1,0:T(8,128)(2,1)} %k_ref.1, bf16[128,512]{1,0:T(8,128)(2,1)} %v_ref.1, f32[4,128]{1,0:T(4,128)} %rate_ref.1, f32[4,128]{1,0:T(4,128)} %decay_ref.1), custom_call_target="tpu_custom_call" | custom-call | flops 20000000000 | tf_op jit(solution)/shard_map/pallas_call | solution.py:77
  8.6 3.7 %all-to-all-start = ((bf16[4,400,128]{2,1,0:T(8,128)(2,1)}), bf16[4,400,128]{2,1,0:T(8,128)(2,1)S(1)}, u32[]{:S(2)}, u32[]{:S(2)}) async-start(bf16[4,400,128]{2,1,0:T(8,128)(2,1)} %shard_map.135), calls=%async_computation | async-start | bytes 819200 | tf_op jit(solution)/shard_map/all_to_all | solution.py:99
  12.9 2.4 %collective-permute-done.3.refs_3_ = bf16[32,2048]{1,0:T(8,128)(2,1)S(1)} collective-permute-done((bf16[32,2048]{1,0:T(8,128)(2,1)}, bf16[32,2048]{1,0:T(8,128)(2,1)S(1)}, u32[]{:S(2)}, u32[]{:S(2)}) %collective-permute-start.3) | collective-permute-done | bytes 131104 | tf_op jit(solution)/shard_map/ppermute | solution.py:444
  15.3 1.6 %shard_map.137 = bf16[4,768,128]{2,1,0:T(8,128)(2,1)} custom-call(s32[1]{0:T(128)} %bitcast.head_ref, bf16[32,2048]{1,0:T(8,128)(2,1)S(1)} %copy-done.2, bf16[32,2048]{1,0:T(8,128)(2,1)S(1)} %collective-permute-done.1.refs_1_, bf16[32,2048]{1,0:T(8,128)(2,1)S(1)} %collective-permute-done.2.refs_2_, bf16[32,2048]{1,0:T(8,128)(2,1)S(1)} %collective-permute-done.3.refs_3_, ...), custom_call_target="tpu_custom_call" | custom-call | flops 4000000000 | tf_op jit(solution)/shard_map/pallas_call | solution.py:77
  16.9 1.4 %all-to-all-done.in_ref.refs_4_ = bf16[4,400,128]{2,1,0:T(8,128)(2,1)S(1)} async-done(((bf16[4,400,128]{2,1,0:T(8,128)(2,1)}), bf16[4,400,128]{2,1,0:T(8,128)(2,1)S(1)}, u32[]{:S(2)}, u32[]{:S(2)}) %all-to-all-start) | async-done | bytes 409632 | tf_op jit(solution)/shard_map/all_to_all | solution.py:99
  18.3 3.5 %all-to-all-start.1 = ((bf16[4,768,128]{2,1,0:T(8,128)(2,1)}), bf16[4,768,128]{2,1,0:T(8,128)(2,1)S(1)}, u32[]{:S(2)}, u32[]{:S(2)}) async-start(bf16[4,768,128]{2,1,0:T(8,128)(2,1)} %shard_map.137), calls=%async_computation.1 | async-start | bytes 1572864 | tf_op jit(solution)/shard_map/all_to_all | solution.py:99
  21.8 3.9 %shard_map.136 = (f32[4,2,128,128]{3,2,1,0:T(8,128)S(1)}, bf16[4,2,128,128]{3,2,1,0:T(8,128)(2,1)S(1)}, bf16[4,2,128,128]{3,2,1,0:T(8,128)(2,1)S(1)}, bf16[4,2,1...) custom-call(s32[5]{0:T(128)S(1)} %copy-done.3, ...), custom_call_target="tpu_custom_call" | custom-call | flops 6000000000 | tf_op jit(solution)/shard_map/pallas_call | solution.py:77
  26.5 0.7 copy-done.8
  27.2 0.7 copy-done.10
  27.9 0.7 copy-done.12
  29.2 1.4 %all-to-all-done.1.refs_2_.refs_5_.cot_ref = bf16[4,768,128]{2,1,0:T(8,128)(2,1)S(1)} async-done(((bf16[4,768,128]{2,1,0:T(8,128)(2,1)}), bf16[4,768,128]{2,1,0:T(8,128)(2,1)S(1)}, u32[]{:S(2)}, u32[]{:S(2)}) %all-to-all-start.1) | async-done | bytes 786464 | tf_op jit(solution)/shard_map/all_to_all | solution.py:99
  31.2 2.1 %shard_map.138 = (bf16[4,4,128,128]{3,2,1,0:T(8,128)(2,1)}, f32[4,128,128]{2,1,0:T(8,128)S(1)}, f32[4,128,128]{2,1,0:T(8,128)S(1)}) custom-call(s32[1]{0:T(128)} %bitcast.1.mate_ref, f32[4,2,128,128]{3,2,1,0:T(8,128)S(1)} %get-tuple-element.30.refs_0_, f32[4,2,128,128]{3,2,1,0:T(8,128)S(1)} %collective-permute-done.refs_1_, ...), custom_call_target="tpu_custom_call" | custom-call | flops 4000000000 | tf_op jit(solution)/shard_map/pallas_call | solution.py:77
  34.1 4.2 %all-to-all-start.2 = ((bf16[4,4,128,128]{3,2,1,0:T(8,128)(2,1)}), bf16[4,4,128,128]{3,2,1,0:T(8,128)(2,1)S(1)}, u32[]{:S(2)}, u32[]{:S(2)}) async-start(bf16[4,4,128,128]{3,2,1,0:T(8,128)(2,1)} %get-tuple-element.33), calls=%async_computation.2 | async-start | bytes 1048576 | tf_op jit(solution)/shard_map/all_to_all | solution.py:99
  38.3 0.9 %copy-done.5 = f32[4,128,128]{2,1,0:T(8,128)S(1)} copy-done((f32[4,128,128]{2,1,0:T(8,128)S(1)}, f32[4,128,128]{2,1,0:T(8,128)}, u32[]{:S(2)}) %copy-start.5) | copy-done | bytes 262168
  39.2 0.9 %copy-done.7 = bf16[4,2,128,128]{3,2,1,0:T(8,128)(2,1)S(1)} copy-done((bf16[4,2,128,128]{3,2,1,0:T(8,128)(2,1)S(1)}, bf16[4,2,128,128]{3,2,1,0:T(8,128)(2,1)}, u32[]{:S(2)}) %copy-start.7) | copy-done | bytes 262168
  40.2 0.9 %copy-done.9 = bf16[4,2,128,128]{3,2,1,0:T(8,128)(2,1)S(1)} copy-done((bf16[4,2,128,128]{3,2,1,0:T(8,128)(2,1)S(1)}, bf16[4,2,128,128]{3,2,1,0:T(8,128)(2,1)}, u32[]{:S(2)}) %copy-start.9) | copy-done | bytes 262168
  41.1 0.9 %copy-done.11 = bf16[4,2,128,128]{3,2,1,0:T(8,128)(2,1)S(1)} copy-done((bf16[4,2,128,128]{3,2,1,0:T(8,128)(2,1)S(1)}, bf16[4,2,128,128]{3,2,1,0:T(8,128)(2,1)}, u32[]{:S(2)}) %copy-start.11) | copy-done | bytes 262168
  42.1 0.9 %copy-done.13 = f32[4,128,128]{2,1,0:T(8,128)S(1)} copy-done((f32[4,128,128]{2,1,0:T(8,128)S(1)}, f32[4,128,128]{2,1,0:T(8,128)}, u32[]{:S(2)}) %copy-start.13) | copy-done | bytes 262168
  43.0 0.9 %copy-done.15 = f32[4,128,128]{2,1,0:T(8,128)S(1)} copy-done((f32[4,128,128]{2,1,0:T(8,128)S(1)}, f32[4,128,128]{2,1,0:T(8,128)}, u32[]{:S(2)}) %copy-start.15) | copy-done | bytes 262168
  44.0 5.1 %shard_map.140 = bf16[4,400,128]{2,1,0:T(8,128)(2,1)} custom-call(s32[5]{0:T(128)S(1)} %copy-done.3, s32[1]{0:T(128)} %bitcast.1.mate_ref, f32[4,2,128,128]{3,2,1,0:T(8,128)S(1)} %get-tuple-element.30.refs_0_, f32[4,2,128,128]{3,2,1,0:T(8,128)S(1)} %collective-permute-done.refs_1_, f32[4,128,128]{2,1,0:T(8,128)S(1)} %get-tuple-element.38.refs_2_, ...), custom_call_target="tpu_custom_call" | custom-call | flops 20000000000 | tf_op jit(solution)/shard_map/pallas_call | solution.py:77
  49.1 1.6 %copy-done.1 = bf16[512,2048]{1,0:T(8,128)(2,1)S(1)} copy-done((bf16[512,2048]{1,0:T(8,128)(2,1)S(1)}, bf16[512,2048]{1,0:T(8,128)(2,1)}, u32[]{:S(2)}) %copy-start.1) | copy-done | bytes 2097176
  51.3 3.2 %collective-permute-start.4 = (bf16[32,2048]{1,0:T(8,128)(2,1)S(1)}, bf16[32,2048]{1,0:T(8,128)(2,1)S(1)}, u32[]{:S(2)}, u32[]{:S(2)}) collective-permute-start(bf16[32,2048]{1,0:T(8,128)(2,1)S(1)} %get-tuple-element.35), channel_id=1, source_target_pairs={{1,0},{2,1},{3,2},{0,3},{5,4},{6,5},{7,6},{4,7},{9,8},{10,9},{11,1... | collective-permute-start | bytes 393224 | tf_op jit(solution)/shard_map/ppermute | solution.py:444
  54.4 4.2 %all-to-all-start.3 = ((bf16[4,400,128]{2,1,0:T(8,128)(2,1)}), bf16[4,400,128]{2,1,0:T(8,128)(2,1)S(1)}, u32[]{:S(2)}, u32[]{:S(2)}) async-start(bf16[4,400,128]{2,1,0:T(8,128)(2,1)} %shard_map.140), calls=%async_computation.3 | async-start | bytes 819200 | tf_op jit(solution)/shard_map/all_to_all | solution.py:99
  58.6 0.9 %collective-permute-start.5 = (bf16[32,2048]{1,0:T(8,128)(2,1)S(1)}, bf16[32,2048]{1,0:T(8,128)(2,1)S(1)}, u32[]{:S(2)}, u32[]{:S(2)}) collective-permute-start(bf16[32,2048]{1,0:T(8,128)(2,1)S(1)} %get-tuple-element.36), channel_id=1, source_target_pairs={{2,0},{3,1},{0,2},{1,3},{6,4},{7,5},{4,6},{5,7},{10,8},{11,9},{8,1... | collective-permute-start | bytes 393224 | tf_op jit(solution)/shard_map/ppermute | solution.py:444
  59.5 2.0 %collective-permute-start.6 = (bf16[32,2048]{1,0:T(8,128)(2,1)S(1)}, bf16[32,2048]{1,0:T(8,128)(2,1)S(1)}, u32[]{:S(2)}, u32[]{:S(2)}) collective-permute-start(bf16[32,2048]{1,0:T(8,128)(2,1)S(1)} %get-tuple-element.37), channel_id=1, source_target_pairs={{3,0},{0,1},{1,2},{2,3},{7,4},{4,5},{5,6},{6,7},{11,8},{8,9},{9,10... | collective-permute-start | bytes 393224 | tf_op jit(solution)/shard_map/ppermute | solution.py:444
  61.5 0.7 shard_map.142
  62.3 7.5 %collective-permute-done.5 = bf16[32,2048]{1,0:T(8,128)(2,1)S(1)} collective-permute-done((bf16[32,2048]{1,0:T(8,128)(2,1)S(1)}, bf16[32,2048]{1,0:T(8,128)(2,1)S(1)}, u32[]{:S(2)}, u32[]{:S(2)}) %collective-permute-start.5) | collective-permute-done | bytes 131104 | tf_op jit(solution)/shard_map/ppermute | solution.py:444
  69.8 0.8 %convert_add_fusion = f32[32,2048]{1,0:T(8,128)} fusion(bf16[32,2048]{1,0:T(8,128)(2,1)S(1)} %collective-permute-done.6, bf16[32,2048]{1,0:T(8,128)(2,1)S(1)} %collective-permute-done.5, f32[32,2048]{1,0:T(8,128)S(1)} %get-tuple-element.34, bf16[32,2048]{1,0:T(8,128)(2,1)S(1)} %collective-permute-done.4), kind=kLoop, calls=%fused_computation | loop fusion | flops 393216 | bytes 917504 | tf_op jit(solution)/shard_map/add | solution.py:525
  70.6 0.8 %shard_map.141 = (f32[128,256]{1,0:T(8,128)}, f32[128,256]{1,0:T(8,128)}, f32[128,512]{1,0:T(8,128)}, f32[4,128]{1,0:T(4,128)}, f32[4,128]{1,0:T(4,128)}) custom-call(bf16[4,400,128]{2,1,0:T(8,128)(2,1)S(1)} %all-to-all-done.3.in_ref), custom_call_target="tpu_custom_call" | custom-call | flops 2000000000 | tf_op jit(solution)/shard_map/pallas_call | solution.py:77
  71.4 0.9 %add.21 = f32[256,512]{1,0:T(8,128)} add(f32[256,512]{1,0:T(8,128)S(1)} %get-tuple-element.51, f32[256,512]{1,0:T(8,128)S(1)} %collective-permute-done.8) | non-fusion elementwise | flops 131072 | bytes 1572864 | tf_op jit(solution)/shard_map/add | solution.py:519
  (36 shorter events, 4.6 us)
Async XLA Ops:
  0.6 14.7 %copy-start.2 = (bf16[32,2048]{1,0:T(8,128)(2,1)S(1)}, bf16[32,2048]{1,0:T(8,128)(2,1)}, u32[]{:S(2)}) copy-start(bf16[32,2048]{1,0:T(8,128)(2,1)} %refs_0_.1) | copy-start | bytes 393220
  0.6 14.7 %copy-start = (bf16[512,2048]{1,0:T(8,128)(2,1)S(1)}, bf16[512,2048]{1,0:T(8,128)(2,1)}, u32[]{:S(2)}) copy-start(bf16[512,2048]{1,0:T(8,128)(2,1)} %w_ref.1) | copy-start | bytes 6291460
  0.7 12.3 %collective-permute-start.2 = (bf16[32,2048]{1,0:T(8,128)(2,1)}, bf16[32,2048]{1,0:T(8,128)(2,1)S(1)}, u32[]{:S(2)}, u32[]{:S(2)}) collective-permute-start(bf16[32,2048]{1,0:T(8,128)(2,1)} %refs_0_.1), channel_id=1, source_target_pairs={{2,0},{3,1},{0,2},{1,3},{6,4},{7,5},{4,6},{5,7},{10,8},{11,9},{8,1... | collective-permute-start | bytes 393224 | tf_op jit(solution)/shard_map/ppermute | solution.py:444
  4.8 8.2 %collective-permute-start.1 = (bf16[32,2048]{1,0:T(8,128)(2,1)}, bf16[32,2048]{1,0:T(8,128)(2,1)S(1)}, u32[]{:S(2)}, u32[]{:S(2)}) collective-permute-start(bf16[32,2048]{1,0:T(8,128)(2,1)} %refs_0_.1), channel_id=1, source_target_pairs={{1,0},{2,1},{3,2},{0,3},{5,4},{6,5},{7,6},{4,7},{9,8},{10,9},{11,1... | collective-permute-start | bytes 393224 | tf_op jit(solution)/shard_map/ppermute | solution.py:444
  6.1 9.2 %collective-permute-start.3 = (bf16[32,2048]{1,0:T(8,128)(2,1)}, bf16[32,2048]{1,0:T(8,128)(2,1)S(1)}, u32[]{:S(2)}, u32[]{:S(2)}) collective-permute-start(bf16[32,2048]{1,0:T(8,128)(2,1)} %refs_0_.1), channel_id=1, source_target_pairs={{3,0},{0,1},{1,2},{2,3},{7,4},{4,5},{5,6},{6,7},{11,8},{8,9},{9,10... | collective-permute-start | bytes 393224 | tf_op jit(solution)/shard_map/ppermute | solution.py:444
  8.6 9.7 %all-to-all-start = ((bf16[4,400,128]{2,1,0:T(8,128)(2,1)}), bf16[4,400,128]{2,1,0:T(8,128)(2,1)S(1)}, u32[]{:S(2)}, u32[]{:S(2)}) async-start(bf16[4,400,128]{2,1,0:T(8,128)(2,1)} %shard_map.135), calls=%async_computation | async-start | bytes 819200 | tf_op jit(solution)/shard_map/all_to_all | solution.py:99
  15.3 6.5 %copy-start.3 = (s32[5]{0:T(128)S(1)}, s32[5]{0:T(128)}, u32[]{:S(2)}) copy-start(s32[5]{0:T(128)} %off_ref.3) | copy-start | bytes 64
  18.3 12.3 %all-to-all-start.1 = ((bf16[4,768,128]{2,1,0:T(8,128)(2,1)}), bf16[4,768,128]{2,1,0:T(8,128)(2,1)S(1)}, u32[]{:S(2)}, u32[]{:S(2)}) async-start(bf16[4,768,128]{2,1,0:T(8,128)(2,1)} %shard_map.137), calls=%async_computation.1 | async-start | bytes 1572864 | tf_op jit(solution)/shard_map/all_to_all | solution.py:99
  25.7 0.7 copy-start.6
  26.5 0.7 copy-start.8
  27.2 0.7 copy-start.10
  27.9 0.7 copy-start.12
  28.6 0.7 copy-start.14
  29.2 1.9 %collective-permute-start = (f32[4,2,128,128]{3,2,1,0:T(8,128)S(1)}, f32[4,2,128,128]{3,2,1,0:T(8,128)S(1)}, u32[]{:S(2)}, u32[]{:S(2)}) collective-permute-start(f32[4,2,128,128]{3,2,1,0:T(8,128)S(1)} %get-tuple-element.30.refs_0_), channel_id=1, source_target_pairs={{4,0},{0,4},{12,8},{8,12},{20,16},{16,20},{28,24},{24,28},{5,1},{1... | collective-permute-start | bytes 1572872 | tf_op jit(solution)/shard_map/ppermute | solution.py:106
  33.3 0.7 copy-start.4
  34.0 4.3 %collective-permute-start.7 = (f32[4,128,128]{2,1,0:T(8,128)S(1)}, f32[4,128,128]{2,1,0:T(8,128)S(1)}, u32[]{:S(2)}, u32[]{:S(2)}) collective-permute-start(f32[4,128,128]{2,1,0:T(8,128)S(1)} %get-tuple-element.38.refs_2_), channel_id=1, source_target_pairs={{4,0},{0,4},{12,8},{8,12},{20,16},{16,20},{28,24},{24,28},{5,1},{1... | collective-permute-start | bytes 786440 | tf_op jit(solution)/shard_map/ppermute | solution.py:106
  34.1 15.0 %all-to-all-start.2 = ((bf16[4,4,128,128]{3,2,1,0:T(8,128)(2,1)}), bf16[4,4,128,128]{3,2,1,0:T(8,128)(2,1)S(1)}, u32[]{:S(2)}, u32[]{:S(2)}) async-start(bf16[4,4,128,128]{3,2,1,0:T(8,128)(2,1)} %get-tuple-element.33), calls=%async_computation.2 | async-start | bytes 1048576 | tf_op jit(solution)/shard_map/all_to_all | solution.py:99
  38.3 1.0 %copy-start.5 = (f32[4,128,128]{2,1,0:T(8,128)S(1)}, f32[4,128,128]{2,1,0:T(8,128)}, u32[]{:S(2)}) copy-start(f32[4,128,128]{2,1,0:T(8,128)} %copy-done.4) | copy-start | bytes 786436
  39.2 0.9 %copy-start.7 = (bf16[4,2,128,128]{3,2,1,0:T(8,128)(2,1)S(1)}, bf16[4,2,128,128]{3,2,1,0:T(8,128)(2,1)}, u32[]{:S(2)}) copy-start(bf16[4,2,128,128]{3,2,1,0:T(8,128)(2,1)} %copy-done.6) | copy-start | bytes 786436
  40.2 0.9 %copy-start.9 = (bf16[4,2,128,128]{3,2,1,0:T(8,128)(2,1)S(1)}, bf16[4,2,128,128]{3,2,1,0:T(8,128)(2,1)}, u32[]{:S(2)}) copy-start(bf16[4,2,128,128]{3,2,1,0:T(8,128)(2,1)} %copy-done.8) | copy-start | bytes 786436
  41.1 0.9 %copy-start.11 = (bf16[4,2,128,128]{3,2,1,0:T(8,128)(2,1)S(1)}, bf16[4,2,128,128]{3,2,1,0:T(8,128)(2,1)}, u32[]{:S(2)}) copy-start(bf16[4,2,128,128]{3,2,1,0:T(8,128)(2,1)} %copy-done.10) | copy-start | bytes 786436
  42.1 0.9 %copy-start.13 = (f32[4,128,128]{2,1,0:T(8,128)S(1)}, f32[4,128,128]{2,1,0:T(8,128)}, u32[]{:S(2)}) copy-start(f32[4,128,128]{2,1,0:T(8,128)} %copy-done.12) | copy-start | bytes 786436
  43.0 0.9 %copy-start.15 = (f32[4,128,128]{2,1,0:T(8,128)S(1)}, f32[4,128,128]{2,1,0:T(8,128)}, u32[]{:S(2)}) copy-start(f32[4,128,128]{2,1,0:T(8,128)} %copy-done.14) | copy-start | bytes 786436
  49.1 1.6 %copy-start.1 = (bf16[512,2048]{1,0:T(8,128)(2,1)S(1)}, bf16[512,2048]{1,0:T(8,128)(2,1)}, u32[]{:S(2)}) copy-start(bf16[512,2048]{1,0:T(8,128)(2,1)} %w_ref.1) | copy-start | bytes 6291460
  51.3 18.5 %collective-permute-start.4 = (bf16[32,2048]{1,0:T(8,128)(2,1)S(1)}, bf16[32,2048]{1,0:T(8,128)(2,1)S(1)}, u32[]{:S(2)}, u32[]{:S(2)}) collective-permute-start(bf16[32,2048]{1,0:T(8,128)(2,1)S(1)} %get-tuple-element.35), channel_id=1, source_target_pairs={{1,0},{2,1},{3,2},{0,3},{5,4},{6,5},{7,6},{4,7},{9,8},{10,9},{11,1... | collective-permute-start | bytes 393224 | tf_op jit(solution)/shard_map/ppermute | solution.py:444
  54.4 16.1 %all-to-all-start.3 = ((bf16[4,400,128]{2,1,0:T(8,128)(2,1)}), bf16[4,400,128]{2,1,0:T(8,128)(2,1)S(1)}, u32[]{:S(2)}, u32[]{:S(2)}) async-start(bf16[4,400,128]{2,1,0:T(8,128)(2,1)} %shard_map.140), calls=%async_computation.3 | async-start | bytes 819200 | tf_op jit(solution)/shard_map/all_to_all | solution.py:99
  58.6 11.2 %collective-permute-start.5 = (bf16[32,2048]{1,0:T(8,128)(2,1)S(1)}, bf16[32,2048]{1,0:T(8,128)(2,1)S(1)}, u32[]{:S(2)}, u32[]{:S(2)}) collective-permute-start(bf16[32,2048]{1,0:T(8,128)(2,1)S(1)} %get-tuple-element.36), channel_id=1, source_target_pairs={{2,0},{3,1},{0,2},{1,3},{6,4},{7,5},{4,6},{5,7},{10,8},{11,9},{8,1... | collective-permute-start | bytes 393224 | tf_op jit(solution)/shard_map/ppermute | solution.py:444
  59.5 10.3 %collective-permute-start.6 = (bf16[32,2048]{1,0:T(8,128)(2,1)S(1)}, bf16[32,2048]{1,0:T(8,128)(2,1)S(1)}, u32[]{:S(2)}, u32[]{:S(2)}) collective-permute-start(bf16[32,2048]{1,0:T(8,128)(2,1)S(1)} %get-tuple-element.37), channel_id=1, source_target_pairs={{3,0},{0,1},{1,2},{2,3},{7,4},{4,5},{5,6},{6,7},{11,8},{8,9},{9,10... | collective-permute-start | bytes 393224 | tf_op jit(solution)/shard_map/ppermute | solution.py:444
  62.2 9.2 %collective-permute-start.8 = (f32[256,512]{1,0:T(8,128)S(1)}, f32[256,512]{1,0:T(8,128)S(1)}, u32[]{:S(2)}, u32[]{:S(2)}) collective-permute-start(f32[256,512]{1,0:T(8,128)S(1)} %get-tuple-element.52), channel_id=1, source_target_pairs={{4,0},{0,4},{12,8},{8,12},{20,16},{16,20},{28,24},{24,28},{5,1},{1... | collective-permute-start | bytes 1572872 | tf_op jit(solution)/shard_map/ppermute | solution.py:106

commit v6 on v5

--- a/solution.py
+++ b/solution.py
@@ -11,6 +11,7 @@
 DK = 128
 DV = 128
 AUX = 16
+INVERSE, SCORES, FROM_STATE, READS, RATIO, WRITES, STATE, KEPT = range(8)
 EPS = 1e-06
 F32 = jnp.float32
 BF16 = jnp.bfloat16
@@ -42,20 +43,12 @@
     return tuple(jnp.concatenate(parts, axis=axis) for parts in zip(*pairs))
 
 
-def put(ref, i, pair):
-    ref[i, 0], ref[i, 1] = pair
-
-
-def get(ref, i):
-    return ref[i, 0], ref[i, 1]
-
-
 def iotas(rows, columns):
     shape = (rows, columns)
     return lax.broadcasted_iota(jnp.int32, shape, 0), lax.broadcasted_iota(jnp.int32, shape, 1)
 
 
-def call(kernel, outs, n_in, smem=(), scratch=(), flops=0, inside=True, fetch=False):
+def call(kernel, outs, n_in, smem=(), scratch=(), flops=0, inside=True, fetch=()):
     spec = lambda i: pl.BlockSpec(memory_space=pltpu.SMEM if i in smem else pltpu.VMEM)
     if inside:
         outs = jax.tree.map(lambda o: pltpu.VMEM(o.shape, o.dtype), outs)
@@ -72,9 +65,9 @@
     )
 
     def placed(*args):
-        space = pltpu.HBM if fetch else pltpu.VMEM
-        hold = lambda x: pltpu.with_memory_space_constraint(x, space)
-        return run(*(x if i in smem else hold(x) for i, x in enumerate(args)))
+        hold = pltpu.with_memory_space_constraint
+        space = lambda i: pltpu.HBM if i in fetch else pltpu.VMEM
+        return run(*(x if i in smem else hold(x, space(i)) for i, x in enumerate(args)))
 
     return placed
 
@@ -222,7 +215,7 @@
 
 
 def prepare_kernel(
-    plan, off_ref, mate_ref, in_ref, link_ref, x_ref, a_ref, w_ref, q_ref, ratio_ref, u_ref, ol_ref
+    plan, off_ref, mate_ref, in_ref, link_ref, kept_ref
 ):
     tok = plan.tok
     rows, columns = iotas(tok, tok)
@@ -254,13 +247,13 @@
         link_ref[m, 0] = scales[m][5] * identity - mm(wp[m], ke[m], 0, 0)
         link_ref[m, 1] = mm(up[m], ke[m])
     for m in mine:
-        put(x_ref, m, halves(inv[m]))
-        put(a_ref, m, ap[m])
-        put(w_ref, m, wp[m])
-        put(q_ref, m, halves(scales[m][3] * qn[m] - mm(ap[m], wp[m])))
-        ratio_ref[m] = scales[m][2]
-        u_ref[m] = u[m]
-        ol_ref[m] = mm(up[m], ap[m], 1, 1)
+        kept_ref[m, INVERSE] = inv[m]
+        kept_ref[m, SCORES] = scores[m]
+        kept_ref[m, FROM_STATE] = w[m]
+        kept_ref[m, READS] = scales[m][3] * qn[m] - mm(ap[m], wp[m])
+        kept_ref[m, RATIO] = scales[m][2]
+        kept_ref[m, WRITES] = u[m]
+        kept_ref[m, STATE] = mm(up[m], ap[m], 1, 1)
 
 
 def lay_out(plan, mate, refs, all_ref):
@@ -270,7 +263,7 @@
 
 def scan_kernel(plan, mate_ref, *refs):
     s = plan.mates
-    links, (cot_ref, q_ref, ol_ref, out_ref, s_ref, back_ref, all_ref, states_ref) = refs[:s], refs[s:]
+    links, (cot_ref, kept_ref, out_ref, all_kept_ref, back_ref, all_ref, states_ref) = refs[:s], refs[s:]
     mate = mate_ref[0]
     lay_out(plan, mate, links, all_ref)
     state = jnp.zeros((DV, DK), F32)
@@ -281,11 +274,14 @@
             state = link[1] + mm(halves(state), halves(link[0]))
     for m in range(plan.hv):
         state = states_ref[mate + s * m]
-        s_ref[m] = state
-        core = (ol_ref[m] + mm(halves(state), get(q_ref, m), 1, 1)).astype(BF16)
+        reads = halves(kept_ref[m, READS])
+        core = (kept_ref[m, STATE] + mm(halves(state), reads, 1, 1)).astype(BF16)
         for g in range(plan.hv):
             out_ref[g, (m - g) % plan.hv] = core
-        back_ref[m] = mm(d_out(cot_ref, m), get(q_ref, m))
+        back_ref[m] = mm(d_out(cot_ref, m), reads)
+        all_kept_ref[m, STATE] = state
+        for i in range(STATE):
+            all_kept_ref[m, i] = kept_ref[m, i]
 
 
 def d_out(cot_ref, m):
@@ -295,8 +291,7 @@
 def backward_kernel(plan, off_ref, mate_ref, *refs):
     s, n, tok = plan.mates, plan.n, plan.tok
     links, backs, refs = refs[:s], refs[s : 2 * s], refs[2 * s :]
-    in_ref, cot_ref, x_ref, a_ref, w_ref, ratio_ref, u_ref, s_ref, out_ref = refs[:9]
-    links_ref, backs_ref, cots_ref = refs[9:]
+    in_ref, cot_ref, kept_ref, out_ref, links_ref, backs_ref, cots_ref = refs
     mate = mate_ref[0]
     lay_out(plan, mate, links, links_ref)
     lay_out(plan, mate, backs, backs_ref)
@@ -318,20 +313,20 @@
     qp = [halves(x[0]) for x in qu]
     kp = [halves(x[0]) for x in ku]
     do = [d_out(cot_ref, m) for m in mine]
-    s0 = [s_ref[m] for m in mine]
+    s0 = [kept_ref[m, STATE] for m in mine]
     ds = [cots_ref[c] for c in chunks]
     s0p = [halves(x) for x in s0]
     dsp = [halves(x) for x in ds]
-    pseudo = [u_ref[m] - mm(s0p[m], get(w_ref, m), 1, 1) for m in mine]
+    pseudo = [kept_ref[m, WRITES] - mm(s0p[m], halves(kept_ref[m, FROM_STATE]), 1, 1) for m in mine]
     pp = [halves(x) for x in pseudo]
     ke = [halves(s[4] * k[0]) for s, k in zip(scales, ku)]
-    dp = [mm(do[m], get(a_ref, m)) + mm(dsp[m], ke[m], 1, 1) for m in mine]
-    dr = [mm(halves(dp[m]), get(x_ref, m)) for m in mine]
+    dp = [mm(do[m], halves(kept_ref[m, SCORES])) + mm(dsp[m], ke[m], 1, 1) for m in mine]
+    dr = [mm(halves(dp[m]), halves(kept_ref[m, INVERSE])) for m in mine]
     drp = [halves(x) for x in dr]
     big = [mm(cat([o, r], 1), cat([p, s], 1), 0, 0) for o, r, p, s in zip(do, drp, pp, s0p)]
     pds = [mm(p, d, 0, 0) for p, d in zip(pp, dsp)]
-    da = [big[m][:tok, :tok] * ratio_ref[m] for m in mine]
-    dm = [jnp.where(strict, -big[m][tok:, :tok] * ratio_ref[m], 0.0) for m in mine]
+    da = [big[m][:tok, :tok] * kept_ref[m, RATIO] for m in mine]
+    dm = [jnp.where(strict, -big[m][tok:, :tok] * kept_ref[m, RATIO], 0.0) for m in mine]
     dap = [halves(x) for x in da]
     dmp = [halves(x) for x in dm]
     dbm = [halves(s[1] * x) for s, x in zip(scales, dm)]
@@ -445,7 +440,7 @@
 
     pieces = [grad_out] + [from_head(grad_out, d) for d in range(1, parts)]
 
-    sent = call(partial(pack_kernel, plan), arr(BF16, hv, plan.rows, DK), 5, flops=20_000_000_000, fetch=True)(
+    sent = call(partial(pack_kernel, plan), arr(BF16, hv, plan.rows, DK), 5, flops=20_000_000_000, fetch=range(5))(
         queries, key_vectors, value_rows, write_rate, log_decay
     )
     got = plan.exchange(sent)
@@ -460,39 +455,30 @@
     )(head, *pieces, out_weight)
     cot = plan.exchange(cot_sent)
 
-    pair = lambda r, c: arr(BF16, hv, 2, r, c)
-    link, x, a, w, q, ratio, u, ol = call(
+    kept_shape = arr(F32, hv, KEPT, tok, DK)
+    link, kept = call(
         partial(prepare_kernel, plan),
-        (
-            arr(F32, hv, 2, DK, DK),
-            pair(tok, tok),
-            pair(tok, tok),
-            pair(tok, DK),
-            pair(tok, DK),
-            arr(F32, hv, tok, tok),
-            arr(F32, hv, DV, tok),
-            arr(F32, hv, DV, tok),
-        ),
+        (arr(F32, hv, 2, DK, DK), kept_shape),
         3,
         smem=(0, 1),
         flops=6_000_000_000,
     )(doc_offsets, mate, got)
     links = [link] + [plan.from_mate(link, d) for d in range(1, s)]
-    out, states, back = call(
+    out, kept, back = call(
         partial(scan_kernel, plan),
-        (arr(BF16, hv, hv, DV, tok), arr(F32, hv, DV, DK), arr(F32, hv, DV, DK)),
-        s + 4,
+        (arr(BF16, hv, hv, DV, tok), kept_shape, arr(F32, hv, DV, DK)),
+        s + 3,
         smem=(0,),
         scratch=[pltpu.VMEM((s, hv, 2, DK, DK), F32), pltpu.VMEM((n, DV, DK), F32)],
         flops=4_000_000_000,
-    )(mate, *links, cot, q, ol)
+    )(mate, *links, cot, kept)
     mixed = plan.exchange(out)
     backs = [back] + [plan.from_mate(back, d) for d in range(1, s)]
 
     grad_sent = call(
         partial(backward_kernel, plan),
         arr(BF16, hv, plan.rows, DK),
-        2 * s + 10,
+        2 * s + 5,
         smem=(0, 1),
         scratch=[
             pltpu.VMEM((s, hv, 2, DK, DK), F32),
@@ -500,7 +486,7 @@
             pltpu.VMEM((n, DV, DK), F32),
         ],
         flops=20_000_000_000,
-    )(doc_offsets, mate, *links, *backs, got, cot, x, a, w, ratio, u, states)
+    )(doc_offsets, mate, *links, *backs, got, cot, kept)
 
     rows = tok // parts
     projected = call(
@@ -510,6 +496,7 @@
         smem=(0,),
         scratch=[pltpu.VMEM((tok, model), F32)],
         flops=3_000_000_000,
+        fetch=(2,),
     )(head, mixed, out_weight)
     shares = call(
         partial(weight_kernel, plan), [arr(F32, model // n, hv * DV)] * s, 4, smem=(0, 1), flops=3_000_000_000
@@ -520,9 +507,6 @@
 
     grad_sent, _ = lax.optimization_barrier((grad_sent, projected[1]))
     grads = plan.exchange(grad_sent)
-    layer_out = projected[0]
-    for d in range(1, parts):
-        layer_out = layer_out + from_head(projected[d], d).astype(F32)
     grad_q, grad_k, grad_v, grad_rate, grad_decay = call(
         partial(finish_kernel, plan),
         (
@@ -536,6 +520,10 @@
         flops=2_000_000_000,
         inside=False,
     )(grads)
+    pieces = [from_head(projected[d], d) for d in range(1, parts)]
+    layer_out, _, _ = lax.optimization_barrier((projected[0], grad_q, weight_grad))
+    for piece in pieces:
+        layer_out = layer_out + piece.astype(F32)
     return (layer_out, grad_q, grad_k, grad_v, grad_rate, grad_decay, weight_grad)
 
 

time: 72.9 us -> 73.6 us (level)
  local copies, waits for them, and re-layouts: 11.5 us -> 5.51 us
  waiting for transfers between devices: 13.8 us -> 19.1 us
  Pallas kernels: 16.7 us -> 18.3 us
    unnamed x32 -> x14, local copies, waits for them, and re-layouts: 11.5 us -> 5.51 us
    all_to_all x4, waiting for transfers between devices: 2.8 us -> 7.63 us  [exchange(): lax.all_to_all(x, 'ctx', split_axis=0, concat_axis=0, axis_index_groups=s...]
    pallas_call x8, Pallas kernels: 16.7 us -> 18.3 us  [placed(): run(*(x if i in smem else hold(x, space(i)) for i, x in enumerate(args)))]
    all_to_all x4, starting transfers between devices: 15.6 us -> 14.2 us  [exchange(): lax.all_to_all(x, 'ctx', split_axis=0, concat_axis=0, axis_index_groups=s...]
    ppermute x6, starting transfers between devices: 12.2 us -> 13.5 us  [from_head(): return lax.ppermute(x, 'head', [((i + d) % parts, i) for i in range(parts)])]
    ppermute x6, waiting for transfers between devices: 10.5 us -> 11.5 us  [from_head(): return lax.ppermute(x, 'head', [((i + d) % parts, i) for i in range(parts)])]
  transfers between devices with their start and end apart: 13 -> 13, of which waited for: 6 -> 7; matrix products, arithmetic and copies ran while one was open for 1% -> 1% of each run, Pallas kernels for 19% -> 21%
where the time goes in v6:
time: 73.6 us; the launch traced here: 73.1 us
  starting transfers between devices  27.8 us (38%)
  waiting for transfers between devices  19.1 us (26%)
  Pallas kernels  18.3 us (25%)
  local copies, waits for them, and re-layouts  5.51 us (7%)
  other arithmetic  1.63 us (2%)
  between operations  0.76 us (1%)
    pallas_call x8, Pallas kernels, placed(): run(*(x if i in smem else hold(x, space(i)) for i, x in enumerate(args)))  18.3 us
    all_to_all x4, starting transfers between devices, exchange(): lax.all_to_all(x, 'ctx', split_axis=0, concat_axis=0, axis_index_groups=s...  14.2 us
    ppermute x6, starting transfers between devices, from_head(): return lax.ppermute(x, 'head', [((i + d) % parts, i) for i in range(parts)])  13.5 us
    ppermute x6, waiting for transfers between devices, from_head(): return lax.ppermute(x, 'head', [((i + d) % parts, i) for i in range(parts)])  11.5 us
    all_to_all x4, waiting for transfers between devices, exchange(): lax.all_to_all(x, 'ctx', split_axis=0, concat_axis=0, axis_index_groups=s...  7.63 us
    unnamed x14, local copies, waits for them, and re-layouts  5.51 us
  transfers between devices with their start and end apart: 13, of which 7 were waited for; matrix products, arithmetic and copies ran while one was open for 1% of the time, Pallas kernels for 21%

profile of v6, /device:TPU:0, one launch (start us, length us, event | category | flops | bytes accessed | tf_op | source)
XLA Modules:
  0.0 73.1 jit_solution(348146512385293192)
XLA Ops:
  0.7 4.1 %collective-permute-start.2 = (bf16[32,2048]{1,0:T(8,128)(2,1)}, bf16[32,2048]{1,0:T(8,128)(2,1)S(1)}, u32[]{:S(2)}, u32[]{:S(2)}) collective-permute-start(bf16[32,2048]{1,0:T(8,128)(2,1)} %refs_0_.1), channel_id=1, source_target_pairs={{2,0},{3,1},{0,2},{1,3},{6,4},{7,5},{4,6},{5,7},{10,8},{11,9},{8,1... | collective-permute-start | bytes 393224 | tf_op jit(solution)/shard_map/ppermute | solution.py:439
  4.8 1.3 %collective-permute-start.1 = (bf16[32,2048]{1,0:T(8,128)(2,1)}, bf16[32,2048]{1,0:T(8,128)(2,1)S(1)}, u32[]{:S(2)}, u32[]{:S(2)}) collective-permute-start(bf16[32,2048]{1,0:T(8,128)(2,1)} %refs_0_.1), channel_id=1, source_target_pairs={{1,0},{2,1},{3,2},{0,3},{5,4},{6,5},{7,6},{4,7},{9,8},{10,9},{11,1... | collective-permute-start | bytes 393224 | tf_op jit(solution)/shard_map/ppermute | solution.py:439
  6.1 0.7 collective-permute-start.3
  6.8 1.8 %shard_map.135 = bf16[4,400,128]{2,1,0:T(8,128)(2,1)} custom-call(bf16[128,256]{1,0:T(8,128)(2,1)} %q_ref.1, bf16[128,256]{1,0:T(8,128)(2,1)} %k_ref.1, bf16[128,512]{1,0:T(8,128)(2,1)} %v_ref.1, f32[4,128]{1,0:T(4,128)} %rate_ref.1, f32[4,128]{1,0:T(4,128)} %decay_ref.1), custom_call_target="tpu_custom_call" | custom-call | flops 20000000000 | tf_op jit(solution)/shard_map/pallas_call | solution.py:70
  8.6 3.7 %all-to-all-start = ((bf16[4,400,128]{2,1,0:T(8,128)(2,1)}), bf16[4,400,128]{2,1,0:T(8,128)(2,1)S(1)}, u32[]{:S(2)}, u32[]{:S(2)}) async-start(bf16[4,400,128]{2,1,0:T(8,128)(2,1)} %shard_map.135), calls=%async_computation | async-start | bytes 819200 | tf_op jit(solution)/shard_map/all_to_all | solution.py:92
  12.3 0.6 collective-permute-done.2.refs_2_
  12.9 2.4 %collective-permute-done.3.refs_3_ = bf16[32,2048]{1,0:T(8,128)(2,1)S(1)} collective-permute-done((bf16[32,2048]{1,0:T(8,128)(2,1)}, bf16[32,2048]{1,0:T(8,128)(2,1)S(1)}, u32[]{:S(2)}, u32[]{:S(2)}) %collective-permute-start.3) | collective-permute-done | bytes 131104 | tf_op jit(solution)/shard_map/ppermute | solution.py:439
  15.3 1.6 %shard_map.137 = bf16[4,768,128]{2,1,0:T(8,128)(2,1)} custom-call(s32[1]{0:T(128)} %bitcast.head_ref, bf16[32,2048]{1,0:T(8,128)(2,1)S(1)} %copy-done.1, bf16[32,2048]{1,0:T(8,128)(2,1)S(1)} %collective-permute-done.1.refs_1_, bf16[32,2048]{1,0:T(8,128)(2,1)S(1)} %collective-permute-done.2.refs_2_, bf16[32,2048]{1,0:T(8,128)(2,1)S(1)} %collective-permute-done.3.refs_3_, ...), custom_call_target="tpu_custom_call" | custom-call | flops 4000000000 | tf_op jit(solution)/shard_map/pallas_call | solution.py:70
  16.9 1.4 %all-to-all-done.in_ref.refs_4_ = bf16[4,400,128]{2,1,0:T(8,128)(2,1)S(1)} async-done(((bf16[4,400,128]{2,1,0:T(8,128)(2,1)}), bf16[4,400,128]{2,1,0:T(8,128)(2,1)S(1)}, u32[]{:S(2)}, u32[]{:S(2)}) %all-to-all-start) | async-done | bytes 409632 | tf_op jit(solution)/shard_map/all_to_all | solution.py:92
  18.3 3.5 %all-to-all-start.1 = ((bf16[4,768,128]{2,1,0:T(8,128)(2,1)}), bf16[4,768,128]{2,1,0:T(8,128)(2,1)S(1)}, u32[]{:S(2)}, u32[]{:S(2)}) async-start(bf16[4,768,128]{2,1,0:T(8,128)(2,1)} %shard_map.137), calls=%async_computation.1 | async-start | bytes 1572864 | tf_op jit(solution)/shard_map/all_to_all | solution.py:92
  21.8 3.9 %shard_map.136 = (f32[4,2,128,128]{3,2,1,0:T(8,128)S(1)}, f32[4,7,128,128]{3,2,1,0:T(8,128)S(1)}) custom-call(s32[5]{0:T(128)S(1)} %copy-done.2, s32[1]{0:T(128)} %bitcast.1.mate_ref, bf16[4,400,128]{2,1,0:T(8,128)(2,1)S(1)} %all-to-all-done.in_ref.refs_4_), custom_call_target="tpu_custom_call" | custom-call | flops 6000000000 | tf_op jit(solution)/shard_map/pallas_call | solution.py:70
  25.7 1.2 %copy-done.5 = f32[4,7,128,128]{3,2,1,0:T(8,128)} copy-done((f32[4,7,128,128]{3,2,1,0:T(8,128)}, f32[4,7,128,128]{3,2,1,0:T(8,128)S(1)}, u32[]{:S(2)}) %copy-start.5) | copy-done | bytes 1835032
  27.0 3.7 %all-to-all-done.1.refs_2_.refs_5_.cot_ref = bf16[4,768,128]{2,1,0:T(8,128)(2,1)S(1)} async-done(((bf16[4,768,128]{2,1,0:T(8,128)(2,1)}), bf16[4,768,128]{2,1,0:T(8,128)(2,1)S(1)}, u32[]{:S(2)}, u32[]{:S(2)}) %all-to-all-start.1) | async-done | bytes 786464 | tf_op jit(solution)/shard_map/all_to_all | solution.py:92
  30.7 1.5 %copy-done.6 = f32[4,7,128,128]{3,2,1,0:T(8,128)S(1)} copy-done((f32[4,7,128,128]{3,2,1,0:T(8,128)S(1)}, f32[4,7,128,128]{3,2,1,0:T(8,128)}, u32[]{:S(2)}) %copy-start.6) | copy-done | bytes 1835032
  32.2 2.1 %shard_map.138 = (bf16[4,4,128,128]{3,2,1,0:T(8,128)(2,1)}, f32[4,7,128,128]{3,2,1,0:T(8,128)S(1)}, f32[4,128,128]{2,1,0:T(8,128)S(1)}) custom-call(s32[1]{0:T(128)} %bitcast.1.mate_ref, f32[4,2,128,128]{3,2,1,0:T(8,128)S(1)} %get-tuple-element.25.refs_0_, f32[4,2,128,128]{3,2,1,0:T(8,128)S(1)} %collective-permute-done.refs_1_, ...), custom_call_target="tpu_custom_call" | custom-call | flops 4000000000 | tf_op jit(solution)/shard_map/pallas_call | solution.py:70
  34.3 1.3 %copy-done.3 = f32[4,7,128,128]{3,2,1,0:T(8,128)} copy-done((f32[4,7,128,128]{3,2,1,0:T(8,128)}, f32[4,7,128,128]{3,2,1,0:T(8,128)S(1)}, u32[]{:S(2)}) %copy-start.3) | copy-done | bytes 1835032
  35.6 3.5 %all-to-all-start.2 = ((bf16[4,4,128,128]{3,2,1,0:T(8,128)(2,1)}), bf16[4,4,128,128]{3,2,1,0:T(8,128)(2,1)S(1)}, u32[]{:S(2)}, u32[]{:S(2)}) async-start(bf16[4,4,128,128]{3,2,1,0:T(8,128)(2,1)} %get-tuple-element.27), calls=%async_computation.2 | async-start | bytes 1048576 | tf_op jit(solution)/shard_map/all_to_all | solution.py:92
  39.1 1.5 %copy-done.4 = f32[4,7,128,128]{3,2,1,0:T(8,128)S(1)} copy-done((f32[4,7,128,128]{3,2,1,0:T(8,128)S(1)}, f32[4,7,128,128]{3,2,1,0:T(8,128)}, u32[]{:S(2)}) %copy-start.4) | copy-done | bytes 1835032
  40.6 5.1 %shard_map.140 = bf16[4,400,128]{2,1,0:T(8,128)(2,1)} custom-call(s32[5]{0:T(128)S(1)} %copy-done.2, s32[1]{0:T(128)} %bitcast.1.mate_ref, f32[4,2,128,128]{3,2,1,0:T(8,128)S(1)} %get-tuple-element.25.refs_0_, f32[4,2,128,128]{3,2,1,0:T(8,128)S(1)} %collective-permute-done.refs_1_, f32[4,128,128]{2,1,0:T(8,128)S(1)} %get-tuple-element.29.refs_2_, ...), custom_call_target="tpu_custom_call" | custom-call | flops 20000000000 | tf_op jit(solution)/shard_map/pallas_call | solution.py:70
  45.7 2.3 %all-to-all-done.2.mixed_ref = bf16[4,4,128,128]{3,2,1,0:T(8,128)(2,1)S(1)} async-done(((bf16[4,4,128,128]{3,2,1,0:T(8,128)(2,1)}), bf16[4,4,128,128]{3,2,1,0:T(8,128)(2,1)S(1)}, u32[]{:S(2)}, u32[]{:S(2)}) %all-to-all-start.2) | async-done | bytes 524320 | tf_op jit(solution)/shard_map/all_to_all | solution.py:92
  48.0 0.7 shard_map.142
  48.7 0.1 collective-permute-start.5
  48.8 2.1 %shard_map.139 = (f32[32,2048]{1,0:T(8,128)S(1)}, bf16[32,2048]{1,0:T(8,128)(2,1)S(1)}, bf16[32,2048]{1,0:T(8,128)(2,1)S(1)}, bf16[32,2048]{1,0:T(8,128)(2,1)S(1)}) custom-call(s32[1]{0:T(128)} %bitcast.head_ref, bf16[4,4,128,128]{3,2,1,0:T(8,128)(2,1)S(1)} %all-to-all-done.2.mixed_ref, bf16[512,2048]{1,0:T(8,128)(2,1)} %w_ref.1), custom_call_target="tpu_custom_call" | custom-call | flops 3000000000 | tf_op jit(solution)/shard_map/pallas_call | solution.py:70
  50.9 3.5 %all-to-all-start.3 = ((bf16[4,400,128]{2,1,0:T(8,128)(2,1)}), bf16[4,400,128]{2,1,0:T(8,128)(2,1)S(1)}, u32[]{:S(2)}, u32[]{:S(2)}) async-start(bf16[4,400,128]{2,1,0:T(8,128)(2,1)} %shard_map.140), calls=%async_computation.3 | async-start | bytes 819200 | tf_op jit(solution)/shard_map/all_to_all | solution.py:92
  54.4 3.5 %collective-permute-start.6 = (bf16[32,2048]{1,0:T(8,128)(2,1)S(1)}, bf16[32,2048]{1,0:T(8,128)(2,1)S(1)}, u32[]{:S(2)}, u32[]{:S(2)}) collective-permute-start(bf16[32,2048]{1,0:T(8,128)(2,1)S(1)} %get-tuple-element.31), channel_id=1, source_target_pairs={{1,0},{2,1},{3,2},{0,3},{5,4},{6,5},{7,6},{4,7},{9,8},{10,9},{11,1... | collective-permute-start | bytes 393224 | tf_op jit(solution)/shard_map/ppermute | solution.py:439
  57.9 1.9 %collective-permute-start.7 = (bf16[32,2048]{1,0:T(8,128)(2,1)S(1)}, bf16[32,2048]{1,0:T(8,128)(2,1)S(1)}, u32[]{:S(2)}, u32[]{:S(2)}) collective-permute-start(bf16[32,2048]{1,0:T(8,128)(2,1)S(1)} %get-tuple-element.37), channel_id=1, source_target_pairs={{2,0},{3,1},{0,2},{1,3},{6,4},{7,5},{4,6},{5,7},{10,8},{11,9},{8,1... | collective-permute-start | bytes 393224 | tf_op jit(solution)/shard_map/ppermute | solution.py:439
  59.8 1.9 %collective-permute-start.8 = (bf16[32,2048]{1,0:T(8,128)(2,1)S(1)}, bf16[32,2048]{1,0:T(8,128)(2,1)S(1)}, u32[]{:S(2)}, u32[]{:S(2)}) collective-permute-start(bf16[32,2048]{1,0:T(8,128)(2,1)S(1)} %get-tuple-element.38), channel_id=1, source_target_pairs={{3,0},{0,1},{1,2},{2,3},{7,4},{4,5},{5,6},{6,7},{11,8},{8,9},{9,10... | collective-permute-start | bytes 393224 | tf_op jit(solution)/shard_map/ppermute | solution.py:439
  61.8 0.3 all-to-all-done.3.in_ref
  62.1 0.8 %shard_map.141 = (f32[128,256]{1,0:T(8,128)}, f32[128,256]{1,0:T(8,128)}, f32[128,512]{1,0:T(8,128)}, f32[4,128]{1,0:T(4,128)}, f32[4,128]{1,0:T(4,128)}) custom-call(bf16[4,400,128]{2,1,0:T(8,128)(2,1)S(1)} %all-to-all-done.3.in_ref), custom_call_target="tpu_custom_call" | custom-call | flops 2000000000 | tf_op jit(solution)/shard_map/pallas_call | solution.py:70
  62.9 0.9 %add.18 = f32[256,512]{1,0:T(8,128)} add(f32[256,512]{1,0:T(8,128)S(1)} %get-tuple-element.34, f32[256,512]{1,0:T(8,128)S(1)} %collective-permute-done.5) | non-fusion elementwise | flops 131072 | bytes 1572864 | tf_op jit(solution)/shard_map/add | solution.py:506
  63.8 8.6 %collective-permute-done.7 = bf16[32,2048]{1,0:T(8,128)(2,1)S(1)} collective-permute-done((bf16[32,2048]{1,0:T(8,128)(2,1)S(1)}, bf16[32,2048]{1,0:T(8,128)(2,1)S(1)}, u32[]{:S(2)}, u32[]{:S(2)}) %collective-permute-start.7) | collective-permute-done | bytes 131104 | tf_op jit(solution)/shard_map/ppermute | solution.py:439
  72.3 0.8 %convert_add_fusion = f32[32,2048]{1,0:T(8,128)} fusion(bf16[32,2048]{1,0:T(8,128)(2,1)S(1)} %collective-permute-done.8, bf16[32,2048]{1,0:T(8,128)(2,1)S(1)} %collective-permute-done.7, f32[32,2048]{1,0:T(8,128)S(1)} %get-tuple-element.36, bf16[32,2048]{1,0:T(8,128)(2,1)S(1)} %collective-permute-done.6), kind=kLoop, calls=%fused_computation | loop fusion | flops 393216 | bytes 917504 | tf_op jit(solution)/shard_map/add | solution.py:526
  (18 shorter events, 0.0 us)
Async XLA Ops:
  0.6 14.7 %copy-start.1 = (bf16[32,2048]{1,0:T(8,128)(2,1)S(1)}, bf16[32,2048]{1,0:T(8,128)(2,1)}, u32[]{:S(2)}) copy-start(bf16[32,2048]{1,0:T(8,128)(2,1)} %refs_0_.1) | copy-start | bytes 393220
  0.6 14.7 %copy-start = (bf16[512,2048]{1,0:T(8,128)(2,1)S(1)}, bf16[512,2048]{1,0:T(8,128)(2,1)}, u32[]{:S(2)}) copy-start(bf16[512,2048]{1,0:T(8,128)(2,1)} %w_ref.1) | copy-start | bytes 6291460
  0.7 12.3 %collective-permute-start.2 = (bf16[32,2048]{1,0:T(8,128)(2,1)}, bf16[32,2048]{1,0:T(8,128)(2,1)S(1)}, u32[]{:S(2)}, u32[]{:S(2)}) collective-permute-start(bf16[32,2048]{1,0:T(8,128)(2,1)} %refs_0_.1), channel_id=1, source_target_pairs={{2,0},{3,1},{0,2},{1,3},{6,4},{7,5},{4,6},{5,7},{10,8},{11,9},{8,1... | collective-permute-start | bytes 393224 | tf_op jit(solution)/shard_map/ppermute | solution.py:439
  4.8 8.2 %collective-permute-start.1 = (bf16[32,2048]{1,0:T(8,128)(2,1)}, bf16[32,2048]{1,0:T(8,128)(2,1)S(1)}, u32[]{:S(2)}, u32[]{:S(2)}) collective-permute-start(bf16[32,2048]{1,0:T(8,128)(2,1)} %refs_0_.1), channel_id=1, source_target_pairs={{1,0},{2,1},{3,2},{0,3},{5,4},{6,5},{7,6},{4,7},{9,8},{10,9},{11,1... | collective-permute-start | bytes 393224 | tf_op jit(solution)/shard_map/ppermute | solution.py:439
  6.1 9.2 %collective-permute-start.3 = (bf16[32,2048]{1,0:T(8,128)(2,1)}, bf16[32,2048]{1,0:T(8,128)(2,1)S(1)}, u32[]{:S(2)}, u32[]{:S(2)}) collective-permute-start(bf16[32,2048]{1,0:T(8,128)(2,1)} %refs_0_.1), channel_id=1, source_target_pairs={{3,0},{0,1},{1,2},{2,3},{7,4},{4,5},{5,6},{6,7},{11,8},{8,9},{9,10... | collective-permute-start | bytes 393224 | tf_op jit(solution)/shard_map/ppermute | solution.py:439
  8.6 9.7 %all-to-all-start = ((bf16[4,400,128]{2,1,0:T(8,128)(2,1)}), bf16[4,400,128]{2,1,0:T(8,128)(2,1)S(1)}, u32[]{:S(2)}, u32[]{:S(2)}) async-start(bf16[4,400,128]{2,1,0:T(8,128)(2,1)} %shard_map.135), calls=%async_computation | async-start | bytes 819200 | tf_op jit(solution)/shard_map/all_to_all | solution.py:92
  15.3 6.5 %copy-start.2 = (s32[5]{0:T(128)S(1)}, s32[5]{0:T(128)}, u32[]{:S(2)}) copy-start(s32[5]{0:T(128)} %off_ref.3) | copy-start | bytes 64
  18.3 12.3 %all-to-all-start.1 = ((bf16[4,768,128]{2,1,0:T(8,128)(2,1)}), bf16[4,768,128]{2,1,0:T(8,128)(2,1)S(1)}, u32[]{:S(2)}, u32[]{:S(2)}) async-start(bf16[4,768,128]{2,1,0:T(8,128)(2,1)} %shard_map.137), calls=%async_computation.1 | async-start | bytes 1572864 | tf_op jit(solution)/shard_map/all_to_all | solution.py:92
  25.7 1.3 %copy-start.5 = (f32[4,7,128,128]{3,2,1,0:T(8,128)}, f32[4,7,128,128]{3,2,1,0:T(8,128)S(1)}, u32[]{:S(2)}) copy-start(f32[4,7,128,128]{3,2,1,0:T(8,128)S(1)} %get-tuple-element.26.refs_3_) | copy-start | bytes 5505028
  27.0 3.7 %collective-permute-start = (f32[4,2,128,128]{3,2,1,0:T(8,128)S(1)}, f32[4,2,128,128]{3,2,1,0:T(8,128)S(1)}, u32[]{:S(2)}, u32[]{:S(2)}) collective-permute-start(f32[4,2,128,128]{3,2,1,0:T(8,128)S(1)} %get-tuple-element.25.refs_0_), channel_id=1, source_target_pairs={{4,0},{0,4},{12,8},{8,12},{20,16},{16,20},{28,24},{24,28},{5,1},{1... | collective-permute-start | bytes 1572872 | tf_op jit(solution)/shard_map/ppermute | solution.py:99
  30.7 1.5 %copy-start.6 = (f32[4,7,128,128]{3,2,1,0:T(8,128)S(1)}, f32[4,7,128,128]{3,2,1,0:T(8,128)}, u32[]{:S(2)}) copy-start(f32[4,7,128,128]{3,2,1,0:T(8,128)} %copy-done.5) | copy-start | bytes 5505028
  34.3 1.3 %copy-start.3 = (f32[4,7,128,128]{3,2,1,0:T(8,128)}, f32[4,7,128,128]{3,2,1,0:T(8,128)S(1)}, u32[]{:S(2)}) copy-start(f32[4,7,128,128]{3,2,1,0:T(8,128)S(1)} %get-tuple-element.30.refs_6_) | copy-start | bytes 5505028
  35.6 3.5 %collective-permute-start.4 = (f32[4,128,128]{2,1,0:T(8,128)S(1)}, f32[4,128,128]{2,1,0:T(8,128)S(1)}, u32[]{:S(2)}, u32[]{:S(2)}) collective-permute-start(f32[4,128,128]{2,1,0:T(8,128)S(1)} %get-tuple-element.29.refs_2_), channel_id=1, source_target_pairs={{4,0},{0,4},{12,8},{8,12},{20,16},{16,20},{28,24},{24,28},{5,1},{1... | collective-permute-start | bytes 786440 | tf_op jit(solution)/shard_map/ppermute | solution.py:99
  35.6 12.4 %all-to-all-start.2 = ((bf16[4,4,128,128]{3,2,1,0:T(8,128)(2,1)}), bf16[4,4,128,128]{3,2,1,0:T(8,128)(2,1)S(1)}, u32[]{:S(2)}, u32[]{:S(2)}) async-start(bf16[4,4,128,128]{3,2,1,0:T(8,128)(2,1)} %get-tuple-element.27), calls=%async_computation.2 | async-start | bytes 1048576 | tf_op jit(solution)/shard_map/all_to_all | solution.py:92
  39.1 1.5 %copy-start.4 = (f32[4,7,128,128]{3,2,1,0:T(8,128)S(1)}, f32[4,7,128,128]{3,2,1,0:T(8,128)}, u32[]{:S(2)}) copy-start(f32[4,7,128,128]{3,2,1,0:T(8,128)} %copy-done.3) | copy-start | bytes 5505028
  48.7 14.2 %collective-permute-start.5 = (f32[256,512]{1,0:T(8,128)S(1)}, f32[256,512]{1,0:T(8,128)S(1)}, u32[]{:S(2)}, u32[]{:S(2)}) collective-permute-start(f32[256,512]{1,0:T(8,128)S(1)} %get-tuple-element.35), channel_id=1, source_target_pairs={{4,0},{0,4},{12,8},{8,12},{20,16},{16,20},{28,24},{24,28},{5,1},{1... | collective-permute-start | bytes 1572872 | tf_op jit(solution)/shard_map/ppermute | solution.py:99
  50.9 11.2 %all-to-all-start.3 = ((bf16[4,400,128]{2,1,0:T(8,128)(2,1)}), bf16[4,400,128]{2,1,0:T(8,128)(2,1)S(1)}, u32[]{:S(2)}, u32[]{:S(2)}) async-start(bf16[4,400,128]{2,1,0:T(8,128)(2,1)} %shard_map.140), calls=%async_computation.3 | async-start | bytes 819200 | tf_op jit(solution)/shard_map/all_to_all | solution.py:92
  54.4 18.0 %collective-permute-start.6 = (bf16[32,2048]{1,0:T(8,128)(2,1)S(1)}, bf16[32,2048]{1,0:T(8,128)(2,1)S(1)}, u32[]{:S(2)}, u32[]{:S(2)}) collective-permute-start(bf16[32,2048]{1,0:T(8,128)(2,1)S(1)} %get-tuple-element.31), channel_id=1, source_target_pairs={{1,0},{2,1},{3,2},{0,3},{5,4},{6,5},{7,6},{4,7},{9,8},{10,9},{11,1... | collective-permute-start | bytes 393224 | tf_op jit(solution)/shard_map/ppermute | solution.py:439
  57.9 14.4 %collective-permute-start.7 = (bf16[32,2048]{1,0:T(8,128)(2,1)S(1)}, bf16[32,2048]{1,0:T(8,128)(2,1)S(1)}, u32[]{:S(2)}, u32[]{:S(2)}) collective-permute-start(bf16[32,2048]{1,0:T(8,128)(2,1)S(1)} %get-tuple-element.37), channel_id=1, source_target_pairs={{2,0},{3,1},{0,2},{1,3},{6,4},{7,5},{4,6},{5,7},{10,8},{11,9},{8,1... | collective-permute-start | bytes 393224 | tf_op jit(solution)/shard_map/ppermute | solution.py:439
  59.8 12.5 %collective-permute-start.8 = (bf16[32,2048]{1,0:T(8,128)(2,1)S(1)}, bf16[32,2048]{1,0:T(8,128)(2,1)S(1)}, u32[]{:S(2)}, u32[]{:S(2)}) collective-permute-start(bf16[32,2048]{1,0:T(8,128)(2,1)S(1)} %get-tuple-element.38), channel_id=1, source_target_pairs={{3,0},{0,1},{1,2},{2,3},{7,4},{4,5},{5,6},{6,7},{11,8},{8,9},{9,10... | collective-permute-start | bytes 393224 | tf_op jit(solution)/shard_map/ppermute | solution.py:439

commit v7 on v6

--- a/solution.py
+++ b/solution.py
@@ -11,7 +11,7 @@
 DK = 128
 DV = 128
 AUX = 16
-INVERSE, SCORES, FROM_STATE, READS, RATIO, WRITES, STATE, KEPT = range(8)
+INVERSE, SCORES, FROM_STATE, READS, RATIO, WRITES, LOCAL, KEPT = range(8)
 EPS = 1e-06
 F32 = jnp.float32
 BF16 = jnp.bfloat16
@@ -48,32 +48,48 @@
     return lax.broadcasted_iota(jnp.int32, shape, 0), lax.broadcasted_iota(jnp.int32, shape, 1)
 
 
-def call(kernel, outs, n_in, smem=(), scratch=(), flops=0, inside=True, fetch=()):
-    spec = lambda i: pl.BlockSpec(memory_space=pltpu.SMEM if i in smem else pltpu.VMEM)
+def call(kernel, outs, smem=(), scratch=(), flops=0, inside=True, fetch=()):
     if inside:
         outs = jax.tree.map(lambda o: pltpu.VMEM(o.shape, o.dtype), outs)
-    run = pl.pallas_call(
-        kernel,
-        out_shape=outs,
-        in_specs=[spec(i) for i in range(n_in)],
-        out_specs=jax.tree.map(lambda _: pl.BlockSpec(memory_space=pltpu.VMEM), outs),
-        scratch_shapes=list(scratch),
-        compiler_params=pltpu.CompilerParams(
-            vmem_limit_bytes=SPARE_VMEM + sum(x.dtype.itemsize * math.prod(x.shape) for x in scratch)
-        ),
-        cost_estimate=pl.CostEstimate(flops=flops, bytes_accessed=0, transcendentals=0),
-    )
-
-    def placed(*args):
+    scoped = SPARE_VMEM + sum(x.dtype.itemsize * math.prod(x.shape) for x in scratch)
+
+    def run(*args):
+        spec = lambda i: pl.BlockSpec(memory_space=pltpu.SMEM if i in smem else pltpu.VMEM)
+        space = lambda i: pltpu.HBM if i in fetch else pltpu.VMEM
         hold = pltpu.with_memory_space_constraint
-        space = lambda i: pltpu.HBM if i in fetch else pltpu.VMEM
-        return run(*(x if i in smem else hold(x, space(i)) for i, x in enumerate(args)))
-
-    return placed
+        return pl.pallas_call(
+            kernel,
+            out_shape=outs,
+            in_specs=[spec(i) for i in range(len(args))],
+            out_specs=jax.tree.map(lambda _: pl.BlockSpec(memory_space=pltpu.VMEM), outs),
+            scratch_shapes=list(scratch),
+            compiler_params=pltpu.CompilerParams(vmem_limit_bytes=scoped),
+            cost_estimate=pl.CostEstimate(flops=flops, bytes_accessed=0, transcendentals=0),
+        )(*(x if i in smem else hold(x, space(i)) for i, x in enumerate(args)))
+
+    return run
 
 
 def arr(dtype, *shape):
     return jax.ShapeDtypeStruct(shape, dtype)
+
+
+class Ring:
+    def __init__(self, size):
+        self.size = size
+        self.paired = size & (size - 1) == 0
+
+    def source(self, i, d):
+        return i ^ d if self.paired else (i + d) % self.size
+
+    def target(self, i, d):
+        return i ^ d if self.paired else (i + self.size - d) % self.size
+
+    def seen(self, d, k):
+        return d ^ k if self.paired else (k - d) % self.size
+
+    def pairs(self, d):
+        return [(self.source(i, d), i) for i in range(self.size)]
 
 
 class Plan:
@@ -83,15 +99,18 @@
         self.v_at = 2 * tok
         self.aux_at = 2 * tok + DV
         self.rows = self.aux_at + AUX
-        self.groups = [[m * self.mates + b for m in range(hv)] for b in range(self.mates)]
+        self.ring = Ring(hv)
 
     def key_head(self, head):
         return head * self.hk // self.hv
 
-    def exchange(self, x):
-        return lax.all_to_all(
-            x, "ctx", split_axis=0, concat_axis=0, axis_index_groups=self.groups, tiled=True
-        )
+    def exchange(self, pieces):
+        s = self.mates
+        moved = [pieces[0]]
+        for d in range(1, self.hv):
+            pairs = [(i * s + b, j * s + b) for i, j in self.ring.pairs(d) for b in range(s)]
+            moved.append(lax.ppermute(pieces[d], "ctx", pairs))
+        return moved
 
     def from_mate(self, x, d):
         s = self.mates
@@ -107,7 +126,8 @@
     return out.astype(BF16)
 
 
-def pack_kernel(plan, q_ref, k_ref, v_ref, rate_ref, decay_ref, out_ref):
+def pack_kernel(plan, place_ref, q_ref, k_ref, v_ref, rate_ref, decay_ref, *refs):
+    outs, out_ref = refs[:-1], refs[-1]
     tok = plan.tok
     for h in range(plan.hv):
         kh = plan.key_head(h)
@@ -117,6 +137,12 @@
         out_ref[h, plan.v_at : plan.aux_at] = turned.astype(BF16)
         rows = [rate_ref[h : h + 1, :], decay_ref[h : h + 1, :]]
         out_ref[h, plan.aux_at :] = aux_rows(rows, tok)
+    hand_out(plan, place_ref[0], out_ref, outs)
+
+
+def hand_out(plan, place, all_ref, outs):
+    for d, ref in enumerate(outs):
+        ref[...] = all_ref[plan.ring.target(place, d)]
 
 
 def unit(x):
@@ -214,17 +240,21 @@
     return results
 
 
-def prepare_kernel(
-    plan, off_ref, mate_ref, in_ref, link_ref, kept_ref
-):
+def chunks_of(plan, place, mate):
+    return [mate + plan.mates * plan.ring.source(place, d) for d in range(plan.hv)]
+
+
+def prepare_kernel(plan, off_ref, place_ref, mate_ref, *refs):
+    in_refs, (link_ref, kept_ref) = refs[: plan.hv], refs[plan.hv :]
     tok = plan.tok
     rows, columns = iotas(tok, tok)
-    identity = (lax.broadcasted_iota(jnp.int32, (DK, DK), 0) == lax.broadcasted_iota(jnp.int32, (DK, DK), 1)).astype(F32)
+    key_rows, key_columns = iotas(DK, DK)
+    identity = (key_rows == key_columns).astype(F32)
     mine = range(plan.hv)
-    chunks = [mate_ref[0] + plan.mates * m for m in mine]
-    scales = scalings(plan, off_ref, chunks, [in_ref[m, plan.aux_at :] for m in mine])
-    qn = [unit(in_ref[m, :tok].astype(F32))[0] for m in mine]
-    kn = [unit(in_ref[m, tok : 2 * tok].astype(F32))[0] for m in mine]
+    chunks = chunks_of(plan, place_ref[0], mate_ref[0])
+    scales = scalings(plan, off_ref, chunks, [r[plan.aux_at :] for r in in_refs])
+    qn = [unit(in_refs[m][:tok].astype(F32))[0] for m in mine]
+    kn = [unit(in_refs[m][tok : 2 * tok].astype(F32))[0] for m in mine]
     kp = [halves(x) for x in kn]
     qp = [halves(x) for x in qn]
     dots = [mm(cat([q, k], 0), k, 1, 1) for q, k in zip(qp, kp)]
@@ -234,7 +264,7 @@
     inv = inverses(lowers)
     rated = [halves(x * s[0]) for x, s in zip(inv, scales)]
     w = [mm(x, halves(s[3] * k)) for x, s, k in zip(rated, scales, kn)]
-    values = [in_ref[m, plan.v_at : plan.aux_at] for m in mine]
+    values = [in_refs[m][plan.v_at : plan.aux_at] for m in mine]
     u = [
         dot(jnp.concatenate([v, v], axis=1), jnp.concatenate(x, axis=1), 1, 1)
         for v, x in zip(values, rated)
@@ -253,48 +283,55 @@
         kept_ref[m, READS] = scales[m][3] * qn[m] - mm(ap[m], wp[m])
         kept_ref[m, RATIO] = scales[m][2]
         kept_ref[m, WRITES] = u[m]
-        kept_ref[m, STATE] = mm(up[m], ap[m], 1, 1)
-
-
-def lay_out(plan, mate, refs, all_ref):
+        kept_ref[m, LOCAL] = mm(up[m], ap[m], 1, 1)
+
+
+def lay_out(plan, place, mate, refs, all_ref):
     for d, ref in enumerate(refs):
-        all_ref[lax.rem(mate + d, plan.mates)] = ref[...]
-
-
-def scan_kernel(plan, mate_ref, *refs):
-    s = plan.mates
-    links, (cot_ref, kept_ref, out_ref, all_kept_ref, back_ref, all_ref, states_ref) = refs[:s], refs[s:]
-    mate = mate_ref[0]
-    lay_out(plan, mate, links, all_ref)
+        for m in range(plan.hv):
+            all_ref[lax.rem(mate + d, plan.mates), plan.ring.source(place, m)] = ref[m]
+
+
+def scan_kernel(plan, place_ref, mate_ref, *refs):
+    s, hv = plan.mates, plan.hv
+    links, kept_ref, state_ref = refs[:s], refs[s], refs[s + 1]
+    outs, (all_ref, states_ref) = refs[s + 2 : -2], refs[-2:]
+    place, mate = place_ref[0], mate_ref[0]
+    lay_out(plan, place, mate, links, all_ref)
     state = jnp.zeros((DV, DK), F32)
     for c in range(plan.n):
         states_ref[c] = state
         if c < plan.n - 1:
             link = all_ref.at[c % s, c // s]
             state = link[1] + mm(halves(state), halves(link[0]))
+    cores = []
+    for m, c in enumerate(chunks_of(plan, place, mate)):
+        state = states_ref[c]
+        state_ref[m] = state
+        core = kept_ref[m, LOCAL] + mm(halves(state), halves(kept_ref[m, READS]), 1, 1)
+        cores.append(core.astype(BF16))
+    for d in range(hv):
+        for k in range(hv):
+            outs[d][k] = cores[plan.ring.seen(d, k)]
+
+
+def state_cotangent_kernel(plan, kept_ref, *refs):
     for m in range(plan.hv):
-        state = states_ref[mate + s * m]
-        reads = halves(kept_ref[m, READS])
-        core = (kept_ref[m, STATE] + mm(halves(state), reads, 1, 1)).astype(BF16)
-        for g in range(plan.hv):
-            out_ref[g, (m - g) % plan.hv] = core
-        back_ref[m] = mm(d_out(cot_ref, m), reads)
-        all_kept_ref[m, STATE] = state
-        for i in range(STATE):
-            all_kept_ref[m, i] = kept_ref[m, i]
-
-
-def d_out(cot_ref, m):
-    return cot_ref[m, :DV], cot_ref[m, DV : 2 * DV]
-
-
-def backward_kernel(plan, off_ref, mate_ref, *refs):
-    s, n, tok = plan.mates, plan.n, plan.tok
+        refs[-1][m] = mm(d_out(refs[m]), halves(kept_ref[m, READS]))
+
+
+def d_out(ref):
+    return ref[:DV], ref[DV:]
+
+
+def backward_kernel(plan, off_ref, place_ref, mate_ref, *refs):
+    s, n, tok, hv = plan.mates, plan.n, plan.tok, plan.hv
     links, backs, refs = refs[:s], refs[s : 2 * s], refs[2 * s :]
-    in_ref, cot_ref, kept_ref, out_ref, links_ref, backs_ref, cots_ref = refs
-    mate = mate_ref[0]
-    lay_out(plan, mate, links, links_ref)
-    lay_out(plan, mate, backs, backs_ref)
+    in_refs, d_refs, kept_ref, state_ref = refs[:hv], refs[hv : 2 * hv], refs[2 * hv], refs[2 * hv + 1]
+    outs, (links_ref, backs_ref, cots_ref) = refs[2 * hv + 2 : -3], refs[-3:]
+    place, mate = place_ref[0], mate_ref[0]
+    lay_out(plan, place, mate, links, links_ref)
+    lay_out(plan, place, mate, backs, backs_ref)
     d_state = jnp.zeros((DV, DK), F32)
     for c in reversed(range(n)):
         cots_ref[c] = d_state
@@ -305,15 +342,15 @@
     rows, columns = iotas(tok, tok)
     strict = rows > columns
     upto = (rows >= columns).astype(BF16)
-    mine = range(plan.hv)
-    chunks = [mate + s * m for m in mine]
-    scales = scalings(plan, off_ref, chunks, [in_ref[m, plan.aux_at :] for m in mine])
-    qu = [unit(in_ref[m, :tok].astype(F32)) for m in mine]
-    ku = [unit(in_ref[m, tok : 2 * tok].astype(F32)) for m in mine]
+    mine = range(hv)
+    chunks = chunks_of(plan, place, mate)
+    scales = scalings(plan, off_ref, chunks, [r[plan.aux_at :] for r in in_refs])
+    qu = [unit(in_refs[m][:tok].astype(F32)) for m in mine]
+    ku = [unit(in_refs[m][tok : 2 * tok].astype(F32)) for m in mine]
     qp = [halves(x[0]) for x in qu]
     kp = [halves(x[0]) for x in ku]
-    do = [d_out(cot_ref, m) for m in mine]
-    s0 = [kept_ref[m, STATE] for m in mine]
+    do = [d_out(r) for r in d_refs]
+    s0 = [state_ref[m] for m in mine]
     ds = [cots_ref[c] for c in chunks]
     s0p = [halves(x) for x in s0]
     dsp = [halves(x) for x in ds]
@@ -338,6 +375,7 @@
     for m in mine:
         _, b_col, _, start_col, end_col, whole = scales[m]
         (qn, q_scale), (kn, k_scale) = qu[m], ku[m]
+        out_ref = outs[plan.ring.seen(m, 0)]
         dqn = by_row[m][:tok] + start_col * big[m][:tok, tok:]
         erase = by_row[m][tok:] - start_col * big[m][tok:, tok:]
         ends = end_col * pds[m]
@@ -348,65 +386,88 @@
         s_w = jnp.sum(kn * write, axis=1, keepdims=True)
         total = jnp.sum(jnp.sum(kn * ends, axis=1, keepdims=True), axis=0, keepdims=True)
         both = jnp.sum(jnp.sum(s0[m] * ds[m], axis=1, keepdims=True), axis=0, keepdims=True)
-        out_ref[m, :tok] = (q_scale * (dqn - qn * s_q)).astype(BF16)
-        out_ref[m, tok : 2 * tok] = (k_scale * (dkn - kn * (b_col * s_e + s_w))).astype(BF16)
-        out_ref[m, plan.v_at : plan.aux_at] = (scales[m][0] * dr[m]).astype(BF16)
+        out_ref[:tok] = (q_scale * (dqn - qn * s_q)).astype(BF16)
+        out_ref[tok : 2 * tok] = (k_scale * (dkn - kn * (b_col * s_e + s_w))).astype(BF16)
+        out_ref[plan.v_at : plan.aux_at] = (scales[m][0] * dr[m]).astype(BF16)
         sums.append((s_e, s_q + b_col * s_e - s_w, total + whole * both))
     turned = to_rows([s[0] for s in sums] + [s[1] for s in sums], tok)
     for m in mine:
-        values = in_ref[m, plan.v_at : plan.aux_at].astype(F32)
+        values = in_refs[m][plan.v_at : plan.aux_at].astype(F32)
         d_rate = turned[m] + jnp.sum(dr[m] * values, axis=0, keepdims=True)
         parts = dot(aux_rows([turned[plan.hv + m]], tok), upto, 1, 0)
         d_decay = parts[0:1] + parts[1:2] + parts[2:3] + sums[m][2]
-        out_ref[m, plan.aux_at :] = aux_rows([d_rate, d_decay], tok)
-
-
-def cotangent_kernel(plan, parts, head_ref, *refs):
-    pieces, (w_ref, out_ref, all_ref) = refs[:parts], refs[parts:]
-    rows = pieces[0].shape[0]
+        outs[plan.ring.seen(m, 0)][plan.aux_at :] = aux_rows([d_rate, d_decay], tok)
+
+
+def gather_rows(head, pieces, all_ref):
+    rows, ring = pieces[0].shape[0], Ring(len(pieces))
+    for d, piece in enumerate(pieces):
+        at = ring.source(head, d) * rows
+        all_ref[pl.ds(pl.multiple_of(at, rows), rows), :] = piece[...]
+
+
+def cotangent_kernel(plan, parts, head_ref, place_ref, *refs):
+    pieces, w_ref, outs, (all_ref, core_ref) = refs[:parts], refs[parts], refs[parts + 1 : -2], refs[-2:]
+    gather_rows(head_ref[0], pieces, all_ref)
+    high, low = halves(dot(w_ref[...], all_ref[...], 1, 1))
+    for m in range(plan.hv):
+        core_ref[m, :DV] = high[m * DV : (m + 1) * DV]
+        core_ref[m, DV:] = low[m * DV : (m + 1) * DV]
+    hand_out(plan, place_ref[0], core_ref, outs)
+
+
+def turn_kernel(plan, parts, head_ref, place_ref, *refs):
+    pieces, outs, (all_ref, turned_ref) = refs[:parts], refs[parts:-2], refs[-2:]
+    gather_rows(head_ref[0], pieces, all_ref)
+    share = turned_ref.shape[1]
+    for m in range(plan.hv):
+        part = all_ref[:, m * share : (m + 1) * share].astype(F32)
+        turned_ref[m] = jnp.transpose(part).astype(BF16)
+    hand_out(plan, place_ref[0], turned_ref, outs)
+
+
+def project_kernel(plan, parts, head_ref, place_ref, *refs):
+    mixed_refs, w_ref, outs, (all_ref, total_ref) = (
+        refs[: plan.hv],
+        refs[plan.hv],
+        refs[plan.hv + 1 : -2],
+        refs[-2:],
+    )
+    for d, ref in enumerate(mixed_refs):
+        all_ref[plan.ring.source(place_ref[0], d)] = ref[0]
+    mixed = all_ref[...].reshape(plan.hv * DV, plan.tok)
+    total_ref[...] = dot(mixed, w_ref[...], 0, 0)
+    rows, ring = outs[0].shape[0], Ring(parts)
     for d in range(parts):
-        at = lax.rem(head_ref[0] + d, parts)
-        all_ref[pl.ds(pl.multiple_of(at * rows, rows), rows), :] = pieces[d][...]
-    whole = all_ref[...]
-    share = whole.shape[1] // plan.hv
-    high, low = halves(dot(w_ref[...], whole, 1, 1))
-    for m in range(plan.hv):
-        out_ref[m, :DV] = high[m * DV : (m + 1) * DV]
-        out_ref[m, DV : 2 * DV] = low[m * DV : (m + 1) * DV]
-        turned = jnp.transpose(whole[:, m * share : (m + 1) * share].astype(F32))
-        out_ref[m, 2 * DV :] = turned.astype(BF16)
-
-
-def project_kernel(plan, parts, head_ref, mixed_ref, w_ref, *refs):
-    outs, total_ref = refs[:parts], refs[parts]
-    mixed = jnp.concatenate([mixed_ref[g, 0] for g in range(plan.hv)], axis=0)
-    total_ref[...] = dot(mixed, w_ref[...], 0, 0)
-    rows = outs[0].shape[0]
-    for d in range(parts):
-        at = lax.rem(head_ref[0] + parts - d, parts)
-        block = total_ref[pl.ds(pl.multiple_of(at * rows, rows), rows), :]
+        at = ring.target(head_ref[0], d) * rows
+        block = total_ref[pl.ds(pl.multiple_of(at, rows), rows), :]
         outs[d][...] = block.astype(outs[d].dtype)
 
 
-def weight_kernel(plan, place_ref, mate_ref, cot_ref, mixed_ref, *outs):
+def weight_kernel(plan, place_ref, mate_ref, *refs):
+    hv = plan.hv
+    turned, mixed_refs, outs, all_ref = refs[:hv], refs[hv : 2 * hv], refs[2 * hv : -1], refs[-1]
+    for d, ref in enumerate(mixed_refs):
+        head = plan.ring.source(place_ref[0], d)
+        for k in range(hv):
+            all_ref[k, head] = ref[k]
     share = outs[0].shape[0]
-    mixed = [
-        jnp.concatenate([mixed_ref[g, step] for g in range(plan.hv)], axis=0)
-        for step in range(plan.hv)
-    ]
     for d, out_ref in enumerate(outs):
-        at = lax.rem(mate_ref[0] + plan.mates - d, plan.mates)
-        at = pl.multiple_of(2 * DV + at * share, share)
+        at = lax.rem(mate_ref[0] + plan.mates - d, plan.mates) * share
+        at = pl.multiple_of(at, share)
         total = None
-        for step in range(plan.hv):
-            chunk = lax.rem(place_ref[0] + step, plan.hv)
-            part = dot(cot_ref[chunk, pl.ds(at, share), :], mixed[step], 1, 1)
+        for k in range(hv):
+            mixed = all_ref[k].reshape(hv * DV, plan.tok)
+            part = dot(turned[k][pl.ds(at, share), :], mixed, 1, 1)
             total = part if total is None else total + part
         out_ref[...] = total
 
 
-def finish_kernel(plan, in_ref, q_ref, k_ref, v_ref, rate_ref, decay_ref):
+def finish_kernel(plan, place_ref, *refs):
+    pieces, (q_ref, k_ref, v_ref, rate_ref, decay_ref, in_ref) = refs[: plan.hv], refs[plan.hv :]
     tok = plan.tok
+    for d, ref in enumerate(pieces):
+        in_ref[plan.ring.source(place_ref[0], d)] = ref[...]
     for kh in range(plan.hk):
         mine = [h for h in range(plan.hv) if plan.key_head(h) == kh]
         for ref, at in ((q_ref, 0), (k_ref, tok)):
@@ -435,78 +496,94 @@
     place, mate = (index // s).reshape(1), (index % s).reshape(1)
     head = lax.axis_index("head").astype(jnp.int32).reshape(1)
 
-    def from_head(x, d):
-        return lax.ppermute(x, "head", [((i + d) % parts, i) for i in range(parts)])
-
-    pieces = [grad_out] + [from_head(grad_out, d) for d in range(1, parts)]
-
-    sent = call(partial(pack_kernel, plan), arr(BF16, hv, plan.rows, DK), 5, flops=20_000_000_000, fetch=range(5))(
-        queries, key_vectors, value_rows, write_rate, log_decay
-    )
-    got = plan.exchange(sent)
-
-    cot_sent = call(
-        partial(cotangent_kernel, plan, parts),
-        arr(BF16, hv, 2 * DV + model // hv, tok),
-        parts + 2,
+    def across_heads(pieces):
+        moved = [lax.ppermute(pieces[d], "head", Ring(parts).pairs(d)) for d in range(1, parts)]
+        return [pieces[0]] + moved
+
+    vmem = lambda dtype, *shape: pltpu.VMEM(shape, dtype)
+    rows = across_heads([grad_out] * parts)
+
+    packed = call(
+        partial(pack_kernel, plan),
+        [arr(BF16, plan.rows, DK)] * hv,
         smem=(0,),
-        scratch=[pltpu.VMEM((tok, model), BF16)],
-        flops=4_000_000_000,
-    )(head, *pieces, out_weight)
-    cot = plan.exchange(cot_sent)
-
-    kept_shape = arr(F32, hv, KEPT, tok, DK)
+        scratch=[vmem(BF16, hv, plan.rows, DK)],
+        fetch=range(6),
+        flops=2_000_000_000,
+    )(place, queries, key_vectors, value_rows, write_rate, log_decay)
+    got = plan.exchange(packed)
+
     link, kept = call(
         partial(prepare_kernel, plan),
-        (arr(F32, hv, 2, DK, DK), kept_shape),
-        3,
+        (arr(F32, hv, 2, DK, DK), arr(F32, hv, KEPT, tok, DK)),
+        smem=(0, 1, 2),
+        flops=4_500_000_000,
+    )(doc_offsets, place, mate, *got)
+    links = [link] + [plan.from_mate(link, d) for d in range(1, s)]
+
+    d_core = call(
+        partial(cotangent_kernel, plan, parts),
+        [arr(BF16, 2 * DV, tok)] * hv,
         smem=(0, 1),
-        flops=6_000_000_000,
-    )(doc_offsets, mate, got)
-    links = [link] + [plan.from_mate(link, d) for d in range(1, s)]
-    out, kept, back = call(
+        scratch=[vmem(BF16, tok, model), vmem(BF16, hv, 2 * DV, tok)],
+        flops=1_500_000_000,
+    )(head, place, *rows, out_weight)
+    d_core = plan.exchange(d_core)
+    turned = call(
+        partial(turn_kernel, plan, parts),
+        [arr(BF16, model // hv, tok)] * hv,
+        smem=(0, 1),
+        scratch=[vmem(BF16, tok, model), vmem(BF16, hv, model // hv, tok)],
+        flops=1_000_000_000,
+    )(head, place, *rows)
+    turned = plan.exchange(turned)
+
+    states, *mixed = call(
         partial(scan_kernel, plan),
-        (arr(BF16, hv, hv, DV, tok), kept_shape, arr(F32, hv, DV, DK)),
-        s + 3,
-        smem=(0,),
-        scratch=[pltpu.VMEM((s, hv, 2, DK, DK), F32), pltpu.VMEM((n, DV, DK), F32)],
-        flops=4_000_000_000,
-    )(mate, *links, cot, kept)
-    mixed = plan.exchange(out)
+        [arr(F32, hv, DV, DK)] + [arr(BF16, hv, DV, tok)] * hv,
+        smem=(0, 1),
+        scratch=[vmem(F32, s, hv, 2, DK, DK), vmem(F32, n, DV, DK)],
+        flops=2_500_000_000,
+    )(place, mate, *links, kept)
+    mixed = plan.exchange(mixed)
+    back = call(
+        partial(state_cotangent_kernel, plan), arr(F32, hv, DV, DK), flops=500_000_000
+    )(kept, *d_core)
     backs = [back] + [plan.from_mate(back, d) for d in range(1, s)]
 
-    grad_sent = call(
-        partial(backward_kernel, plan),
-        arr(BF16, hv, plan.rows, DK),
-        2 * s + 5,
-        smem=(0, 1),
-        scratch=[
-            pltpu.VMEM((s, hv, 2, DK, DK), F32),
-            pltpu.VMEM((s, hv, DV, DK), F32),
-            pltpu.VMEM((n, DV, DK), F32),
-        ],
-        flops=20_000_000_000,
-    )(doc_offsets, mate, *links, *backs, got, cot, kept)
-
-    rows = tok // parts
     projected = call(
         partial(project_kernel, plan, parts),
-        [arr(BF16 if d else F32, rows, model) for d in range(parts)],
-        3,
-        smem=(0,),
-        scratch=[pltpu.VMEM((tok, model), F32)],
-        flops=3_000_000_000,
-        fetch=(2,),
-    )(head, mixed, out_weight)
+        [arr(BF16 if d else F32, tok // parts, model) for d in range(parts)],
+        smem=(0, 1),
+        scratch=[vmem(BF16, hv, DV, tok), vmem(F32, tok, model)],
+        flops=1_000_000_000,
+    )(head, place, *mixed, out_weight)
+    layer_parts = across_heads(projected)
+
+    grads = call(
+        partial(backward_kernel, plan),
+        [arr(BF16, plan.rows, DK)] * hv,
+        smem=(0, 1, 2),
+        scratch=[
+            vmem(F32, s, hv, 2, DK, DK),
+            vmem(F32, s, hv, DV, DK),
+            vmem(F32, n, DV, DK),
+        ],
+        flops=6_000_000_000,
+    )(doc_offsets, place, mate, *links, *backs, *got, *d_core, kept, states)
+    grads = plan.exchange(grads)
+
     shares = call(
-        partial(weight_kernel, plan), [arr(F32, model // n, hv * DV)] * s, 4, smem=(0, 1), flops=3_000_000_000
-    )(place, mate, cot, mixed)
+        partial(weight_kernel, plan),
+        [arr(F32, model // n, hv * DV)] * s,
+        smem=(0, 1),
+        scratch=[vmem(BF16, hv, hv, DV, tok)],
+        flops=1_000_000_000,
+    )(place, mate, *turned, *mixed)
     weight_grad = shares[0]
     for d in range(1, s):
         weight_grad = weight_grad + plan.from_mate(shares[d], d)
 
-    grad_sent, _ = lax.optimization_barrier((grad_sent, projected[1]))
-    grads = plan.exchange(grad_sent)
     grad_q, grad_k, grad_v, grad_rate, grad_decay = call(
         partial(finish_kernel, plan),
         (
@@ -516,14 +593,14 @@
             arr(F32, hv, tok),
             arr(F32, hv, tok),
         ),
-        1,
-        flops=2_000_000_000,
+        smem=(0,),
+        scratch=[vmem(BF16, hv, plan.rows, DK)],
+        flops=1_000_000_000,
         inside=False,
-    )(grads)
-    pieces = [from_head(projected[d], d) for d in range(1, parts)]
-    layer_out, _, _ = lax.optimization_barrier((projected[0], grad_q, weight_grad))
-    for piece in pieces:
-        layer_out = layer_out + piece.astype(F32)
+    )(place, *grads)
+    layer_out, _, _ = lax.optimization_barrier((layer_parts[0], grad_q, weight_grad))
+    for part in layer_parts[1:]:
+        layer_out = layer_out + part.astype(F32)
     return (layer_out, grad_q, grad_k, grad_v, grad_rate, grad_decay, weight_grad)
 
 

time: 73.6 us -> 76.6 us (1.041)
  waiting for transfers between devices: 19.1 us -> 30.3 us
  Pallas kernels: 18.3 us -> 14.1 us
  local copies, waits for them, and re-layouts: 5.51 us -> 1.64 us
    ppermute x6 -> x21, waiting for transfers between devices: 11.5 us -> 30.3 us  [the longest x6 16.5 us: across_heads(): lax.ppermute(pieces[d], 'head', Ring(parts).pairs(d))]
    all_to_all x4 -> x0, starting transfers between devices: 14.2 us -> none  [exchange(): lax.all_to_all(x, 'ctx', split_axis=0, concat_axis=0, axis_index_groups=s...]
    ppermute x6 -> x21, starting transfers between devices: 13.5 us -> 27.7 us  [the longest x15 19.1 us: exchange(): moved.append(lax.ppermute(pieces[d], 'ctx', pairs))]
    all_to_all x4 -> x0, waiting for transfers between devices: 7.63 us -> none  [exchange(): lax.all_to_all(x, 'ctx', split_axis=0, concat_axis=0, axis_index_groups=s...]
    pallas_call x8 -> x10, Pallas kernels: 18.3 us -> 14.1 us  [run(): pl.pallas_call(kernel, out_shape=outs, in_specs=[spec(i) for i in range(l...]
    unnamed x14 -> x20, local copies, waits for them, and re-layouts: 5.51 us -> 1.64 us
  transfers between devices with their start and end apart: 13 -> 24, of which waited for: 7 -> 12; matrix products, arithmetic and copies ran while one was open for 1% -> 1% of each run, Pallas kernels for 21% -> 12%
where the time goes in v7:
time: 76.6 us; the launch traced here: 76.4 us
  waiting for transfers between devices  30.3 us (40%)
  starting transfers between devices  27.9 us (36%)
  Pallas kernels  14.1 us (18%)
  local copies, waits for them, and re-layouts  1.64 us (2%)
  other arithmetic  1.64 us (2%)
  between operations  0.89 us (1%)
    ppermute x15, starting transfers between devices, exchange(): moved.append(lax.ppermute(pieces[d], 'ctx', pairs))  19.1 us
    ppermute x6, waiting for transfers between devices, across_heads(): lax.ppermute(pieces[d], 'head', Ring(parts).pairs(d))  16.5 us
    pallas_call x10, Pallas kernels, run(): pl.pallas_call(kernel, out_shape=outs, in_specs=[spec(i) for i in range(l...  14.1 us
    ppermute x15, waiting for transfers between devices, exchange(): moved.append(lax.ppermute(pieces[d], 'ctx', pairs))  13.8 us
    ppermute x6, starting transfers between devices, across_heads(): lax.ppermute(pieces[d], 'head', Ring(parts).pairs(d))  8.55 us
    unnamed x20, local copies, waits for them, and re-layouts  1.64 us
  transfers between devices with their start and end apart: 24, of which 12 were waited for; matrix products, arithmetic and copies ran while one was open for 1% of the time, Pallas kernels for 12%

profile of v7, /device:TPU:0, one launch (start us, length us, event | category | flops | bytes accessed | tf_op | source)
XLA Modules:
  0.0 76.4 jit_solution(11730877397886725717)
XLA Ops:
  0.7 1.2 %shard_map.135 = (bf16[400,128]{1,0:T(8,128)(2,1)S(1)}, bf16[400,128]{1,0:T(8,128)(2,1)S(1)}, bf16[400,128]{1,0:T(8,128)(2,1)S(1)}, bf16[400,128]{1,0:T(8,128)(2,1)S(1)}) custom-call(s32[1]{0:T(128)} %bitcast.1.place_ref, bf16[128,256]{1,0:T(8,128)(2,1)} %q_ref.1, bf16[128,256]{1,0:T(8,128)(2,1)} %k_ref.1, bf16[128,512]{1,0:T(8,128)(2,1)} %v_ref.1, ...), custom_call_target="tpu_custom_call" | custom-call | flops 2000000000 | tf_op jit(solution)/shard_map/pallas_call | solution.py:60
  1.8 3.0 %collective-permute-start = (bf16[400,128]{1,0:T(8,128)(2,1)S(1)}, bf16[400,128]{1,0:T(8,128)(2,1)S(1)}, u32[]{:S(2)}, u32[]{:S(2)}) collective-permute-start(bf16[400,128]{1,0:T(8,128)(2,1)S(1)} %get-tuple-element.43), channel_id=1, source_target_pairs={{8,0},{12,4},{0,8},{4,12},{24,16},{28,20},{16,24},{20,28},{9,1},{1... | collective-permute-start | bytes 307208 | tf_op jit(solution)/shard_map/ppermute | solution.py:112
  4.8 1.5 %collective-permute-start.1 = (bf16[400,128]{1,0:T(8,128)(2,1)S(1)}, bf16[400,128]{1,0:T(8,128)(2,1)S(1)}, u32[]{:S(2)}, u32[]{:S(2)}) collective-permute-start(bf16[400,128]{1,0:T(8,128)(2,1)S(1)} %get-tuple-element.44), channel_id=1, source_target_pairs={{16,0},{20,4},{24,8},{28,12},{0,16},{4,20},{8,24},{12,28},{17,1},{... | collective-permute-start | bytes 307208 | tf_op jit(solution)/shard_map/ppermute | solution.py:112
  6.4 1.6 %collective-permute-done.refs_1_.refs_5_ = bf16[400,128]{1,0:T(8,128)(2,1)S(1)} collective-permute-done((bf16[400,128]{1,0:T(8,128)(2,1)S(1)}, bf16[400,128]{1,0:T(8,128)(2,1)S(1)}, u32[]{:S(2)}, u32[]{:S(2)}) %collective-permute-start) | collective-permute-done | bytes 102432 | tf_op jit(solution)/shard_map/ppermute | solution.py:112
  8.0 2.6 %collective-permute-done.1.refs_2_.refs_6_ = bf16[400,128]{1,0:T(8,128)(2,1)S(1)} collective-permute-done((bf16[400,128]{1,0:T(8,128)(2,1)S(1)}, bf16[400,128]{1,0:T(8,128)(2,1)S(1)}, u32[]{:S(2)}, u32[]{:S(2)}) %collective-permute-start.1) | collective-permute-done | bytes 102432 | tf_op jit(solution)/shard_map/ppermute | solution.py:112
  10.6 1.3 %collective-permute-done.2.refs_3_.refs_7_ = bf16[400,128]{1,0:T(8,128)(2,1)S(1)} collective-permute-done((bf16[400,128]{1,0:T(8,128)(2,1)S(1)}, bf16[400,128]{1,0:T(8,128)(2,1)S(1)}, u32[]{:S(2)}, u32[]{:S(2)}) %collective-permute-start.2) | collective-permute-done | bytes 102432 | tf_op jit(solution)/shard_map/ppermute | solution.py:112
  11.9 3.9 %shard_map.136 = (f32[4,2,128,128]{3,2,1,0:T(8,128)S(1)}, f32[4,7,128,128]{3,2,1,0:T(8,128)S(1)}) custom-call(s32[5]{0:T(128)S(1)} %copy-done.7, s32[1]{0:T(128)} %bitcast.1.place_ref, s32[1]{0:T(128)} %bitcast.2.mate_ref, bf16[400,128]{1,0:T(8,128)(2,1)S(1)} %get-tuple-element.42.refs_0_.refs_4_, bf16[400,128]{1,0:T(8,128)(2,1)S(1)} %collective-permute-done.refs_1_.refs_5_, ...), custom_call_target="tpu_custom_call" | custom-call | flops 4499999744 | tf_op jit(solution)/shard_map/pallas_call | solution.py:60
  15.9 3.7 %collective-permute-start.9 = (bf16[32,2048]{1,0:T(8,128)(2,1)S(1)}, bf16[32,2048]{1,0:T(8,128)(2,1)S(1)}, u32[]{:S(2)}, u32[]{:S(2)}) collective-permute-start(bf16[32,2048]{1,0:T(8,128)(2,1)S(1)} %copy-done.2), channel_id=1, source_target_pairs={{3,0},{2,1},{1,2},{0,3},{7,4},{6,5},{5,6},{4,7},{11,8},{10,9},{9,1... | collective-permute-start | bytes 393224 | tf_op jit(solution)/shard_map/ppermute | solution.py:500
  20.4 3.8 %collective-permute-done.9.refs_3_ = bf16[32,2048]{1,0:T(8,128)(2,1)S(1)} collective-permute-done((bf16[32,2048]{1,0:T(8,128)(2,1)S(1)}, bf16[32,2048]{1,0:T(8,128)(2,1)S(1)}, u32[]{:S(2)}, u32[]{:S(2)}) %collective-permute-start.9) | collective-permute-done | bytes 131104 | tf_op jit(solution)/shard_map/ppermute | solution.py:500
  24.2 7.1 %collective-permute-done.8.refs_2_ = bf16[32,2048]{1,0:T(8,128)(2,1)S(1)} collective-permute-done((bf16[32,2048]{1,0:T(8,128)(2,1)S(1)}, bf16[32,2048]{1,0:T(8,128)(2,1)S(1)}, u32[]{:S(2)}, u32[]{:S(2)}) %collective-permute-start.8) | collective-permute-done | bytes 131104 | tf_op jit(solution)/shard_map/ppermute | solution.py:500
  31.3 1.6 %copy-done = bf16[512,2048]{1,0:T(8,128)(2,1)S(1)} copy-done((bf16[512,2048]{1,0:T(8,128)(2,1)S(1)}, bf16[512,2048]{1,0:T(8,128)(2,1)}, u32[]{:S(2)}) %copy-start) | copy-done | bytes 2097176
  34.5 1.0 %collective-permute-start.11 = (bf16[256,128]{1,0:T(8,128)(2,1)S(1)}, bf16[256,128]{1,0:T(8,128)(2,1)S(1)}, u32[]{:S(2)}, u32[]{:S(2)}) collective-permute-start(bf16[256,128]{1,0:T(8,128)(2,1)S(1)} %get-tuple-element.55), channel_id=1, source_target_pairs={{16,0},{20,4},{24,8},{28,12},{0,16},{4,20},{8,24},{12,28},{17,1},{... | collective-permute-start | bytes 196616 | tf_op jit(solution)/shard_map/ppermute | solution.py:112
  35.4 1.8 %collective-permute-start.12 = (bf16[256,128]{1,0:T(8,128)(2,1)S(1)}, bf16[256,128]{1,0:T(8,128)(2,1)S(1)}, u32[]{:S(2)}, u32[]{:S(2)}) collective-permute-start(bf16[256,128]{1,0:T(8,128)(2,1)S(1)} %get-tuple-element.56), channel_id=1, source_target_pairs={{24,0},{28,4},{16,8},{20,12},{8,16},{12,20},{0,24},{4,28},{25,1},{... | collective-permute-start | bytes 196616 | tf_op jit(solution)/shard_map/ppermute | solution.py:112
  38.4 1.1 %collective-permute-start.18 = (bf16[512,128]{1,0:T(8,128)(2,1)S(1)}, bf16[512,128]{1,0:T(8,128)(2,1)S(1)}, u32[]{:S(2)}, u32[]{:S(2)}) collective-permute-start(bf16[512,128]{1,0:T(8,128)(2,1)S(1)} %get-tuple-element.65), channel_id=1, source_target_pairs={{16,0},{20,4},{24,8},{28,12},{0,16},{4,20},{8,24},{12,28},{17,1},{... | collective-permute-start | bytes 393224 | tf_op jit(solution)/shard_map/ppermute | solution.py:112
  39.5 1.7 %collective-permute-start.19 = (bf16[512,128]{1,0:T(8,128)(2,1)S(1)}, bf16[512,128]{1,0:T(8,128)(2,1)S(1)}, u32[]{:S(2)}, u32[]{:S(2)}) collective-permute-start(bf16[512,128]{1,0:T(8,128)(2,1)S(1)} %get-tuple-element.66), channel_id=1, source_target_pairs={{24,0},{28,4},{16,8},{20,12},{8,16},{12,20},{0,24},{4,28},{25,1},{... | collective-permute-start | bytes 393224 | tf_op jit(solution)/shard_map/ppermute | solution.py:112
  41.6 1.3 %shard_map.137 = (f32[4,128,128]{2,1,0:T(8,128)S(1)}, bf16[4,128,128]{2,1,0:T(8,128)(2,1)S(1)}, bf16[4,128,128]{2,1,0:T(8,128)(2,1)S(1)}, bf16[4,128,128]{2,1,0:T(8,128)(2,1)S(1)}, bf16[4,128,128]{2,1,0:T(8,128)(2,1)S(1)}) custom-call(s32[1]{0:T(128)} %bitcast.1.place_ref, s32[1]{0:T(128)} %bitcast.2.mate_ref, ...), custom_call_target="tpu_custom_call" | custom-call | flops 2500000000 | tf_op jit(solution)/shard_map/pallas_call | solution.py:60
  42.9 1.2 %collective-permute-start.4 = (bf16[4,128,128]{2,1,0:T(8,128)(2,1)S(1)}, bf16[4,128,128]{2,1,0:T(8,128)(2,1)S(1)}, u32[]{:S(2)}, u32[]{:S(2)}) collective-permute-start(bf16[4,128,128]{2,1,0:T(8,128)(2,1)S(1)} %get-tuple-element.49), channel_id=1, source_target_pairs={{8,0},{12,4},{0,8},{4,12},{24,16},{28,20},{16,24},{20,28},{9,1},{1... | collective-permute-start | bytes 393224 | tf_op jit(solution)/shard_map/ppermute | solution.py:112
  44.1 1.1 %collective-permute-start.5 = (bf16[4,128,128]{2,1,0:T(8,128)(2,1)S(1)}, bf16[4,128,128]{2,1,0:T(8,128)(2,1)S(1)}, u32[]{:S(2)}, u32[]{:S(2)}) collective-permute-start(bf16[4,128,128]{2,1,0:T(8,128)(2,1)S(1)} %get-tuple-element.50), channel_id=1, source_target_pairs={{16,0},{20,4},{24,8},{28,12},{0,16},{4,20},{8,24},{12,28},{17,1},{... | collective-permute-start | bytes 393224 | tf_op jit(solution)/shard_map/ppermute | solution.py:112
  45.9 1.6 %collective-permute-start.6 = (bf16[4,128,128]{2,1,0:T(8,128)(2,1)S(1)}, bf16[4,128,128]{2,1,0:T(8,128)(2,1)S(1)}, u32[]{:S(2)}, u32[]{:S(2)}) collective-permute-start(bf16[4,128,128]{2,1,0:T(8,128)(2,1)S(1)} %get-tuple-element.51), channel_id=1, source_target_pairs={{24,0},{28,4},{16,8},{20,12},{8,16},{12,20},{0,24},{4,28},{25,1},{... | collective-permute-start | bytes 393224 | tf_op jit(solution)/shard_map/ppermute | solution.py:112
  47.5 1.8 %collective-permute-done.4.refs_1_.refs_5_ = bf16[4,128,128]{2,1,0:T(8,128)(2,1)S(1)} collective-permute-done((bf16[4,128,128]{2,1,0:T(8,128)(2,1)S(1)}, bf16[4,128,128]{2,1,0:T(8,128)(2,1)S(1)}, u32[]{:S(2)}, u32[]{:S(2)}) %collective-permute-start.4) | collective-permute-done | bytes 131104 | tf_op jit(solution)/shard_map/ppermute | solution.py:112
  49.3 3.2 %collective-permute-done.5.refs_2_.refs_6_ = bf16[4,128,128]{2,1,0:T(8,128)(2,1)S(1)} collective-permute-done((bf16[4,128,128]{2,1,0:T(8,128)(2,1)S(1)}, bf16[4,128,128]{2,1,0:T(8,128)(2,1)S(1)}, u32[]{:S(2)}, u32[]{:S(2)}) %collective-permute-start.5) | collective-permute-done | bytes 131104 | tf_op jit(solution)/shard_map/ppermute | solution.py:112
  53.4 4.3 %shard_map.141 = (bf16[400,128]{1,0:T(8,128)(2,1)S(1)}, bf16[400,128]{1,0:T(8,128)(2,1)S(1)}, bf16[400,128]{1,0:T(8,128)(2,1)S(1)}, bf16[400,128]{1,0:T(8,128)(2,1)S(1)}) custom-call(s32[5]{0:T(128)S(1)} %copy-done.7, s32[1]{0:T(128)} %bitcast.1.place_ref, s32[1]{0:T(128)} %bitcast.2.mate_ref, f32[4,2,128,128]{3,2,1,0:T(8,128)S(1)} %get-tuple-element.46.refs_0_, ...), custom_call_target="tpu_custom_call" | custom-call | flops 6000000000 | tf_op jit(solution)/shard_map/pallas_call | solution.py:60
  57.7 1.0 %collective-permute-start.14 = (bf16[400,128]{1,0:T(8,128)(2,1)S(1)}, bf16[400,128]{1,0:T(8,128)(2,1)S(1)}, u32[]{:S(2)}, u32[]{:S(2)}) collective-permute-start(bf16[400,128]{1,0:T(8,128)(2,1)S(1)} %get-tuple-element.59), channel_id=1, source_target_pairs={{8,0},{12,4},{0,8},{4,12},{24,16},{28,20},{16,24},{20,28},{9,1},{1... | collective-permute-start | bytes 307208 | tf_op jit(solution)/shard_map/ppermute | solution.py:112
  58.7 1.1 %collective-permute-start.15 = (bf16[400,128]{1,0:T(8,128)(2,1)S(1)}, bf16[400,128]{1,0:T(8,128)(2,1)S(1)}, u32[]{:S(2)}, u32[]{:S(2)}) collective-permute-start(bf16[400,128]{1,0:T(8,128)(2,1)S(1)} %get-tuple-element.60), channel_id=1, source_target_pairs={{16,0},{20,4},{24,8},{28,12},{0,16},{4,20},{8,24},{12,28},{17,1},{... | collective-permute-start | bytes 307208 | tf_op jit(solution)/shard_map/ppermute | solution.py:112
  59.8 1.5 %collective-permute-start.16 = (bf16[400,128]{1,0:T(8,128)(2,1)S(1)}, bf16[400,128]{1,0:T(8,128)(2,1)S(1)}, u32[]{:S(2)}, u32[]{:S(2)}) collective-permute-start(bf16[400,128]{1,0:T(8,128)(2,1)S(1)} %get-tuple-element.61), channel_id=1, source_target_pairs={{24,0},{28,4},{16,8},{20,12},{8,16},{12,20},{0,24},{4,28},{25,1},{... | collective-permute-start | bytes 307208 | tf_op jit(solution)/shard_map/ppermute | solution.py:112
  61.9 1.5 %collective-permute-done.14.refs_1_ = bf16[400,128]{1,0:T(8,128)(2,1)S(1)} collective-permute-done((bf16[400,128]{1,0:T(8,128)(2,1)S(1)}, bf16[400,128]{1,0:T(8,128)(2,1)S(1)}, u32[]{:S(2)}, u32[]{:S(2)}) %collective-permute-start.14) | collective-permute-done | bytes 102432 | tf_op jit(solution)/shard_map/ppermute | solution.py:112
  63.3 1.6 %collective-permute-start.22 = (bf16[32,2048]{1,0:T(8,128)(2,1)S(1)}, bf16[32,2048]{1,0:T(8,128)(2,1)S(1)}, u32[]{:S(2)}, u32[]{:S(2)}) collective-permute-start(bf16[32,2048]{1,0:T(8,128)(2,1)S(1)} %get-tuple-element.71), channel_id=1, source_target_pairs={{2,0},{3,1},{0,2},{1,3},{6,4},{7,5},{4,6},{5,7},{10,8},{11,9},{8,1... | collective-permute-start | bytes 393224 | tf_op jit(solution)/shard_map/ppermute | solution.py:500
  64.9 1.0 %collective-permute-done.15.refs_2_ = bf16[400,128]{1,0:T(8,128)(2,1)S(1)} collective-permute-done((bf16[400,128]{1,0:T(8,128)(2,1)S(1)}, bf16[400,128]{1,0:T(8,128)(2,1)S(1)}, u32[]{:S(2)}, u32[]{:S(2)}) %collective-permute-start.15) | collective-permute-done | bytes 102432 | tf_op jit(solution)/shard_map/ppermute | solution.py:112
  65.9 2.5 %collective-permute-start.23 = (bf16[32,2048]{1,0:T(8,128)(2,1)S(1)}, bf16[32,2048]{1,0:T(8,128)(2,1)S(1)}, u32[]{:S(2)}, u32[]{:S(2)}) collective-permute-start(bf16[32,2048]{1,0:T(8,128)(2,1)S(1)} %get-tuple-element.72), channel_id=1, source_target_pairs={{3,0},{2,1},{1,2},{0,3},{7,4},{6,5},{5,6},{4,7},{11,8},{10,9},{9,1... | collective-permute-start | bytes 393224 | tf_op jit(solution)/shard_map/ppermute | solution.py:500
  68.3 0.9 %shard_map.142 = (f32[128,256]{1,0:T(8,128)}, f32[128,256]{1,0:T(8,128)}, f32[128,512]{1,0:T(8,128)}, f32[4,128]{1,0:T(4,128)}, f32[4,128]{1,0:T(4,128)}) custom-call(s32[1]{0:T(128)} %bitcast.1.place_ref, bf16[400,128]{1,0:T(8,128)(2,1)S(1)} %get-tuple-element.58.refs_0_, bf16[400,128]{1,0:T(8,128)(2,1)S(1)} %collective-permute-done.14.refs_1_, ...), custom_call_target="tpu_custom_call" | custom-call | flops 1000000000 | tf_op jit(solution)/shard_map/pallas_call | solution.py:60
  69.2 0.9 %add.18 = f32[256,512]{1,0:T(8,128)} add(f32[256,512]{1,0:T(8,128)S(1)} %get-tuple-element.67, f32[256,512]{1,0:T(8,128)S(1)} %collective-permute-done.20) | non-fusion elementwise | flops 131072 | bytes 1572864 | tf_op jit(solution)/shard_map/add | solution.py:585
  70.1 5.6 %collective-permute-done.22 = bf16[32,2048]{1,0:T(8,128)(2,1)S(1)} collective-permute-done((bf16[32,2048]{1,0:T(8,128)(2,1)S(1)}, bf16[32,2048]{1,0:T(8,128)(2,1)S(1)}, u32[]{:S(2)}, u32[]{:S(2)}) %collective-permute-start.22) | collective-permute-done | bytes 131104 | tf_op jit(solution)/shard_map/ppermute | solution.py:500
  (48 shorter events, 7.0 us)
Async XLA Ops:
  0.6 11.3 %copy-start.7 = (s32[5]{0:T(128)S(1)}, s32[5]{0:T(128)}, u32[]{:S(2)}) copy-start(s32[5]{0:T(128)} %off_ref.3) | copy-start | bytes 64
  1.8 14.0 %copy-start.8 = (bf16[400,128]{1,0:T(8,128)(2,1)}, bf16[400,128]{1,0:T(8,128)(2,1)S(1)}, u32[]{:S(2)}) copy-start(bf16[400,128]{1,0:T(8,128)(2,1)S(1)} %get-tuple-element.42.refs_0_.refs_4_) | copy-start | bytes 307204
  1.8 6.2 %collective-permute-start = (bf16[400,128]{1,0:T(8,128)(2,1)S(1)}, bf16[400,128]{1,0:T(8,128)(2,1)S(1)}, u32[]{:S(2)}, u32[]{:S(2)}) collective-permute-start(bf16[400,128]{1,0:T(8,128)(2,1)S(1)} %get-tuple-element.43), channel_id=1, source_target_pairs={{8,0},{12,4},{0,8},{4,12},{24,16},{28,20},{16,24},{20,28},{9,1},{1... | collective-permute-start | bytes 307208 | tf_op jit(solution)/shard_map/ppermute | solution.py:112
  4.8 5.8 %collective-permute-start.1 = (bf16[400,128]{1,0:T(8,128)(2,1)S(1)}, bf16[400,128]{1,0:T(8,128)(2,1)S(1)}, u32[]{:S(2)}, u32[]{:S(2)}) collective-permute-start(bf16[400,128]{1,0:T(8,128)(2,1)S(1)} %get-tuple-element.44), channel_id=1, source_target_pairs={{16,0},{20,4},{24,8},{28,12},{0,16},{4,20},{8,24},{12,28},{17,1},{... | collective-permute-start | bytes 307208 | tf_op jit(solution)/shard_map/ppermute | solution.py:112
  6.4 5.6 %collective-permute-start.2 = (bf16[400,128]{1,0:T(8,128)(2,1)S(1)}, bf16[400,128]{1,0:T(8,128)(2,1)S(1)}, u32[]{:S(2)}, u32[]{:S(2)}) collective-permute-start(bf16[400,128]{1,0:T(8,128)(2,1)S(1)} %get-tuple-element.45), channel_id=1, source_target_pairs={{24,0},{28,4},{16,8},{20,12},{8,16},{12,20},{0,24},{4,28},{25,1},{... | collective-permute-start | bytes 307208 | tf_op jit(solution)/shard_map/ppermute | solution.py:112
  10.6 5.2 %copy-start.3 = (bf16[400,128]{1,0:T(8,128)(2,1)}, bf16[400,128]{1,0:T(8,128)(2,1)S(1)}, u32[]{:S(2)}) copy-start(bf16[400,128]{1,0:T(8,128)(2,1)S(1)} %collective-permute-done.1.refs_2_.refs_6_) | copy-start | bytes 307204
  11.9 4.0 %copy-start.2 = (bf16[32,2048]{1,0:T(8,128)(2,1)S(1)}, bf16[32,2048]{1,0:T(8,128)(2,1)}, u32[]{:S(2)}) copy-start(bf16[32,2048]{1,0:T(8,128)(2,1)} %refs_0_.3) | copy-start | bytes 393220
  15.9 25.7 %collective-permute-start.3 = (f32[4,2,128,128]{3,2,1,0:T(8,128)S(1)}, f32[4,2,128,128]{3,2,1,0:T(8,128)S(1)}, u32[]{:S(2)}, u32[]{:S(2)}) collective-permute-start(f32[4,2,128,128]{3,2,1,0:T(8,128)S(1)} %get-tuple-element.46.refs_0_), channel_id=1, source_target_pairs={{4,0},{0,4},{12,8},{8,12},{20,16},{16,20},{28,24},{24,28},{5,1},{1... | collective-permute-start | bytes 1572872 | tf_op jit(solution)/shard_map/ppermute | solution.py:118
  15.9 8.3 %collective-permute-start.9 = (bf16[32,2048]{1,0:T(8,128)(2,1)S(1)}, bf16[32,2048]{1,0:T(8,128)(2,1)S(1)}, u32[]{:S(2)}, u32[]{:S(2)}) collective-permute-start(bf16[32,2048]{1,0:T(8,128)(2,1)S(1)} %copy-done.2), channel_id=1, source_target_pairs={{3,0},{2,1},{1,2},{0,3},{7,4},{6,5},{5,6},{4,7},{11,8},{10,9},{9,1... | collective-permute-start | bytes 393224 | tf_op jit(solution)/shard_map/ppermute | solution.py:500
  19.6 11.7 %collective-permute-start.8 = (bf16[32,2048]{1,0:T(8,128)(2,1)S(1)}, bf16[32,2048]{1,0:T(8,128)(2,1)S(1)}, u32[]{:S(2)}, u32[]{:S(2)}) collective-permute-start(bf16[32,2048]{1,0:T(8,128)(2,1)S(1)} %copy-done.2), channel_id=1, source_target_pairs={{2,0},{3,1},{0,2},{1,3},{6,4},{7,5},{4,6},{5,7},{10,8},{11,9},{8,1... | collective-permute-start | bytes 393224 | tf_op jit(solution)/shard_map/ppermute | solution.py:500
  19.6 11.7 %collective-permute-start.7 = (bf16[32,2048]{1,0:T(8,128)(2,1)S(1)}, bf16[32,2048]{1,0:T(8,128)(2,1)S(1)}, u32[]{:S(2)}, u32[]{:S(2)}) collective-permute-start(bf16[32,2048]{1,0:T(8,128)(2,1)S(1)} %copy-done.2), channel_id=1, source_target_pairs={{1,0},{0,1},{3,2},{2,3},{5,4},{4,5},{7,6},{6,7},{9,8},{8,9},{11,10... | collective-permute-start | bytes 393224 | tf_op jit(solution)/shard_map/ppermute | solution.py:500
  33.7 4.7 %collective-permute-start.10 = (bf16[256,128]{1,0:T(8,128)(2,1)S(1)}, bf16[256,128]{1,0:T(8,128)(2,1)S(1)}, u32[]{:S(2)}, u32[]{:S(2)}) collective-permute-start(bf16[256,128]{1,0:T(8,128)(2,1)S(1)} %get-tuple-element.54), channel_id=1, source_target_pairs={{8,0},{12,4},{0,8},{4,12},{24,16},{28,20},{16,24},{20,28},{9,1},{1... | collective-permute-start | bytes 196616 | tf_op jit(solution)/shard_map/ppermute | solution.py:112
  34.5 5.0 %collective-permute-start.11 = (bf16[256,128]{1,0:T(8,128)(2,1)S(1)}, bf16[256,128]{1,0:T(8,128)(2,1)S(1)}, u32[]{:S(2)}, u32[]{:S(2)}) collective-permute-start(bf16[256,128]{1,0:T(8,128)(2,1)S(1)} %get-tuple-element.55), channel_id=1, source_target_pairs={{16,0},{20,4},{24,8},{28,12},{0,16},{4,20},{8,24},{12,28},{17,1},{... | collective-permute-start | bytes 196616 | tf_op jit(solution)/shard_map/ppermute | solution.py:112
  35.4 5.8 %collective-permute-start.12 = (bf16[256,128]{1,0:T(8,128)(2,1)S(1)}, bf16[256,128]{1,0:T(8,128)(2,1)S(1)}, u32[]{:S(2)}, u32[]{:S(2)}) collective-permute-start(bf16[256,128]{1,0:T(8,128)(2,1)S(1)} %get-tuple-element.56), channel_id=1, source_target_pairs={{24,0},{28,4},{16,8},{20,12},{8,16},{12,20},{0,24},{4,28},{25,1},{... | collective-permute-start | bytes 196616 | tf_op jit(solution)/shard_map/ppermute | solution.py:112
  37.5 6.6 %collective-permute-start.17 = (bf16[512,128]{1,0:T(8,128)(2,1)S(1)}, bf16[512,128]{1,0:T(8,128)(2,1)S(1)}, u32[]{:S(2)}, u32[]{:S(2)}) collective-permute-start(bf16[512,128]{1,0:T(8,128)(2,1)S(1)} %get-tuple-element.64), channel_id=1, source_target_pairs={{8,0},{12,4},{0,8},{4,12},{24,16},{28,20},{16,24},{20,28},{9,1},{1... | collective-permute-start | bytes 393224 | tf_op jit(solution)/shard_map/ppermute | solution.py:112
  38.4 7.5 %collective-permute-start.18 = (bf16[512,128]{1,0:T(8,128)(2,1)S(1)}, bf16[512,128]{1,0:T(8,128)(2,1)S(1)}, u32[]{:S(2)}, u32[]{:S(2)}) collective-permute-start(bf16[512,128]{1,0:T(8,128)(2,1)S(1)} %get-tuple-element.65), channel_id=1, source_target_pairs={{16,0},{20,4},{24,8},{28,12},{0,16},{4,20},{8,24},{12,28},{17,1},{... | collective-permute-start | bytes 393224 | tf_op jit(solution)/shard_map/ppermute | solution.py:112
  39.5 8.0 %collective-permute-start.19 = (bf16[512,128]{1,0:T(8,128)(2,1)S(1)}, bf16[512,128]{1,0:T(8,128)(2,1)S(1)}, u32[]{:S(2)}, u32[]{:S(2)}) collective-permute-start(bf16[512,128]{1,0:T(8,128)(2,1)S(1)} %get-tuple-element.66), channel_id=1, source_target_pairs={{24,0},{28,4},{16,8},{20,12},{8,16},{12,20},{0,24},{4,28},{25,1},{... | collective-permute-start | bytes 393224 | tf_op jit(solution)/shard_map/ppermute | solution.py:112
  41.5 11.9 %collective-permute-start.13 = (f32[4,128,128]{2,1,0:T(8,128)S(1)}, f32[4,128,128]{2,1,0:T(8,128)S(1)}, u32[]{:S(2)}, u32[]{:S(2)}) collective-permute-start(f32[4,128,128]{2,1,0:T(8,128)S(1)} %shard_map.140.refs_2_), channel_id=1, source_target_pairs={{4,0},{0,4},{12,8},{8,12},{20,16},{16,20},{28,24},{24,28},{5,1},{1... | collective-permute-start | bytes 786440 | tf_op jit(solution)/shard_map/ppermute | solution.py:118
  42.9 10.5 %copy-start.4 = (bf16[400,128]{1,0:T(8,128)(2,1)S(1)}, bf16[400,128]{1,0:T(8,128)(2,1)}, u32[]{:S(2)}) copy-start(bf16[400,128]{1,0:T(8,128)(2,1)} %copy-done.3) | copy-start | bytes 307204
  42.9 10.5 %copy-start.6 = (bf16[400,128]{1,0:T(8,128)(2,1)S(1)}, bf16[400,128]{1,0:T(8,128)(2,1)}, u32[]{:S(2)}) copy-start(bf16[400,128]{1,0:T(8,128)(2,1)} %copy-done.5) | copy-start | bytes 307204
  42.9 10.5 %copy-start.9 = (bf16[400,128]{1,0:T(8,128)(2,1)S(1)}, bf16[400,128]{1,0:T(8,128)(2,1)}, u32[]{:S(2)}) copy-start(bf16[400,128]{1,0:T(8,128)(2,1)} %copy-done.8) | copy-start | bytes 307204
  42.9 6.4 %collective-permute-start.4 = (bf16[4,128,128]{2,1,0:T(8,128)(2,1)S(1)}, bf16[4,128,128]{2,1,0:T(8,128)(2,1)S(1)}, u32[]{:S(2)}, u32[]{:S(2)}) collective-permute-start(bf16[4,128,128]{2,1,0:T(8,128)(2,1)S(1)} %get-tuple-element.49), channel_id=1, source_target_pairs={{8,0},{12,4},{0,8},{4,12},{24,16},{28,20},{16,24},{20,28},{9,1},{1... | collective-permute-start | bytes 393224 | tf_op jit(solution)/shard_map/ppermute | solution.py:112
  44.1 8.4 %collective-permute-start.5 = (bf16[4,128,128]{2,1,0:T(8,128)(2,1)S(1)}, bf16[4,128,128]{2,1,0:T(8,128)(2,1)S(1)}, u32[]{:S(2)}, u32[]{:S(2)}) collective-permute-start(bf16[4,128,128]{2,1,0:T(8,128)(2,1)S(1)} %get-tuple-element.50), channel_id=1, source_target_pairs={{16,0},{20,4},{24,8},{28,12},{0,16},{4,20},{8,24},{12,28},{17,1},{... | collective-permute-start | bytes 393224 | tf_op jit(solution)/shard_map/ppermute | solution.py:112
  45.9 6.6 %collective-permute-start.6 = (bf16[4,128,128]{2,1,0:T(8,128)(2,1)S(1)}, bf16[4,128,128]{2,1,0:T(8,128)(2,1)S(1)}, u32[]{:S(2)}, u32[]{:S(2)}) collective-permute-start(bf16[4,128,128]{2,1,0:T(8,128)(2,1)S(1)} %get-tuple-element.51), channel_id=1, source_target_pairs={{24,0},{28,4},{16,8},{20,12},{8,16},{12,20},{0,24},{4,28},{25,1},{... | collective-permute-start | bytes 393224 | tf_op jit(solution)/shard_map/ppermute | solution.py:112
  53.3 16.0 %collective-permute-start.20 = (f32[256,512]{1,0:T(8,128)S(1)}, f32[256,512]{1,0:T(8,128)S(1)}, u32[]{:S(2)}, u32[]{:S(2)}) collective-permute-start(f32[256,512]{1,0:T(8,128)S(1)} %get-tuple-element.68), channel_id=1, source_target_pairs={{4,0},{0,4},{12,8},{8,12},{20,16},{16,20},{28,24},{24,28},{5,1},{1... | collective-permute-start | bytes 1572872 | tf_op jit(solution)/shard_map/ppermute | solution.py:118
  53.4 7.9 %copy-start.1 = (bf16[512,2048]{1,0:T(8,128)(2,1)S(1)}, bf16[512,2048]{1,0:T(8,128)(2,1)}, u32[]{:S(2)}) copy-start(bf16[512,2048]{1,0:T(8,128)(2,1)} %refs_4_.3) | copy-start | bytes 6291460
  57.7 5.6 %collective-permute-start.14 = (bf16[400,128]{1,0:T(8,128)(2,1)S(1)}, bf16[400,128]{1,0:T(8,128)(2,1)S(1)}, u32[]{:S(2)}, u32[]{:S(2)}) collective-permute-start(bf16[400,128]{1,0:T(8,128)(2,1)S(1)} %get-tuple-element.59), channel_id=1, source_target_pairs={{8,0},{12,4},{0,8},{4,12},{24,16},{28,20},{16,24},{20,28},{9,1},{1... | collective-permute-start | bytes 307208 | tf_op jit(solution)/shard_map/ppermute | solution.py:112
  58.7 7.2 %collective-permute-start.15 = (bf16[400,128]{1,0:T(8,128)(2,1)S(1)}, bf16[400,128]{1,0:T(8,128)(2,1)S(1)}, u32[]{:S(2)}, u32[]{:S(2)}) collective-permute-start(bf16[400,128]{1,0:T(8,128)(2,1)S(1)} %get-tuple-element.60), channel_id=1, source_target_pairs={{16,0},{20,4},{24,8},{28,12},{0,16},{4,20},{8,24},{12,28},{17,1},{... | collective-permute-start | bytes 307208 | tf_op jit(solution)/shard_map/ppermute | solution.py:112
  59.8 8.6 %collective-permute-start.16 = (bf16[400,128]{1,0:T(8,128)(2,1)S(1)}, bf16[400,128]{1,0:T(8,128)(2,1)S(1)}, u32[]{:S(2)}, u32[]{:S(2)}) collective-permute-start(bf16[400,128]{1,0:T(8,128)(2,1)S(1)} %get-tuple-element.61), channel_id=1, source_target_pairs={{24,0},{28,4},{16,8},{20,12},{8,16},{12,20},{0,24},{4,28},{25,1},{... | collective-permute-start | bytes 307208 | tf_op jit(solution)/shard_map/ppermute | solution.py:112
  61.8 8.3 %collective-permute-start.21 = (bf16[32,2048]{1,0:T(8,128)(2,1)S(1)}, bf16[32,2048]{1,0:T(8,128)(2,1)S(1)}, u32[]{:S(2)}, u32[]{:S(2)}) collective-permute-start(bf16[32,2048]{1,0:T(8,128)(2,1)S(1)} %get-tuple-element.70), channel_id=1, source_target_pairs={{1,0},{0,1},{3,2},{2,3},{5,4},{4,5},{7,6},{6,7},{9,8},{8,9},{11,10... | collective-permute-start | bytes 393224 | tf_op jit(solution)/shard_map/ppermute | solution.py:500
  63.3 12.3 %collective-permute-start.22 = (bf16[32,2048]{1,0:T(8,128)(2,1)S(1)}, bf16[32,2048]{1,0:T(8,128)(2,1)S(1)}, u32[]{:S(2)}, u32[]{:S(2)}) collective-permute-start(bf16[32,2048]{1,0:T(8,128)(2,1)S(1)} %get-tuple-element.71), channel_id=1, source_target_pairs={{2,0},{3,1},{0,2},{1,3},{6,4},{7,5},{4,6},{5,7},{10,8},{11,9},{8,1... | collective-permute-start | bytes 393224 | tf_op jit(solution)/shard_map/ppermute | solution.py:500
  65.9 9.8 %collective-permute-start.23 = (bf16[32,2048]{1,0:T(8,128)(2,1)S(1)}, bf16[32,2048]{1,0:T(8,128)(2,1)S(1)}, u32[]{:S(2)}, u32[]{:S(2)}) collective-permute-start(bf16[32,2048]{1,0:T(8,128)(2,1)S(1)} %get-tuple-element.72), channel_id=1, source_target_pairs={{3,0},{2,1},{1,2},{0,3},{7,4},{6,5},{5,6},{4,7},{11,8},{10,9},{9,1... | collective-permute-start | bytes 393224 | tf_op jit(solution)/shard_map/ppermute | solution.py:500
  (2 other events, 5.5 us)

commit v8 on v7

--- a/solution.py
+++ b/solution.py
@@ -112,6 +112,13 @@
             moved.append(lax.ppermute(pieces[d], "ctx", pairs))
         return moved
 
+    def exchange_at_once(self, pieces):
+        s = self.mates
+        groups = [[m * s + b for m in range(self.hv)] for b in range(s)]
+        return lax.all_to_all(
+            pieces, "ctx", split_axis=0, concat_axis=0, axis_index_groups=groups, tiled=True
+        )
+
     def from_mate(self, x, d):
         s = self.mates
         pairs = [(i // s * s + (i + d) % s, i) for i in range(self.n)]
@@ -126,8 +133,7 @@
     return out.astype(BF16)
 
 
-def pack_kernel(plan, place_ref, q_ref, k_ref, v_ref, rate_ref, decay_ref, *refs):
-    outs, out_ref = refs[:-1], refs[-1]
+def pack_kernel(plan, q_ref, k_ref, v_ref, rate_ref, decay_ref, out_ref):
     tok = plan.tok
     for h in range(plan.hv):
         kh = plan.key_head(h)
@@ -137,7 +143,6 @@
         out_ref[h, plan.v_at : plan.aux_at] = turned.astype(BF16)
         rows = [rate_ref[h : h + 1, :], decay_ref[h : h + 1, :]]
         out_ref[h, plan.aux_at :] = aux_rows(rows, tok)
-    hand_out(plan, place_ref[0], out_ref, outs)
 
 
 def hand_out(plan, place, all_ref, outs):
@@ -244,8 +249,13 @@
     return [mate + plan.mates * plan.ring.source(place, d) for d in range(plan.hv)]
 
 
+def in_place_order(plan, place, ref):
+    return [ref.at[plan.ring.source(place, d)] for d in range(plan.hv)]
+
+
 def prepare_kernel(plan, off_ref, place_ref, mate_ref, *refs):
-    in_refs, (link_ref, kept_ref) = refs[: plan.hv], refs[plan.hv :]
+    in_ref, link_ref, kept_ref = refs
+    in_refs = in_place_order(plan, place_ref[0], in_ref)
     tok = plan.tok
     rows, columns = iotas(tok, tok)
     key_rows, key_columns = iotas(DK, DK)
@@ -321,15 +331,16 @@
 
 
 def d_out(ref):
-    return ref[:DV], ref[DV:]
+    return ref[:DV], ref[DV : 2 * DV]
 
 
 def backward_kernel(plan, off_ref, place_ref, mate_ref, *refs):
     s, n, tok, hv = plan.mates, plan.n, plan.tok, plan.hv
-    links, backs, refs = refs[:s], refs[s : 2 * s], refs[2 * s :]
-    in_refs, d_refs, kept_ref, state_ref = refs[:hv], refs[hv : 2 * hv], refs[2 * hv], refs[2 * hv + 1]
-    outs, (links_ref, backs_ref, cots_ref) = refs[2 * hv + 2 : -3], refs[-3:]
+    links, backs, in_ref, refs = refs[:s], refs[s : 2 * s], refs[2 * s], refs[2 * s + 1 :]
+    d_refs, (kept_ref, state_ref, out_ref, links_ref, backs_ref, cots_ref) = refs[:hv], refs[hv:]
     place, mate = place_ref[0], mate_ref[0]
+    in_refs = in_place_order(plan, place, in_ref)
+    outs = in_place_order(plan, place, out_ref)
     lay_out(plan, place, mate, links, links_ref)
     lay_out(plan, place, mate, backs, backs_ref)
     d_state = jnp.zeros((DV, DK), F32)
@@ -375,7 +386,7 @@
     for m in mine:
         _, b_col, _, start_col, end_col, whole = scales[m]
         (qn, q_scale), (kn, k_scale) = qu[m], ku[m]
-        out_ref = outs[plan.ring.seen(m, 0)]
+        out = outs[m]
         dqn = by_row[m][:tok] + start_col * big[m][:tok, tok:]
         erase = by_row[m][tok:] - start_col * big[m][tok:, tok:]
         ends = end_col * pds[m]
@@ -386,9 +397,9 @@
         s_w = jnp.sum(kn * write, axis=1, keepdims=True)
         total = jnp.sum(jnp.sum(kn * ends, axis=1, keepdims=True), axis=0, keepdims=True)
         both = jnp.sum(jnp.sum(s0[m] * ds[m], axis=1, keepdims=True), axis=0, keepdims=True)
-        out_ref[:tok] = (q_scale * (dqn - qn * s_q)).astype(BF16)
-        out_ref[tok : 2 * tok] = (k_scale * (dkn - kn * (b_col * s_e + s_w))).astype(BF16)
-        out_ref[plan.v_at : plan.aux_at] = (scales[m][0] * dr[m]).astype(BF16)
+        out[:tok] = (q_scale * (dqn - qn * s_q)).astype(BF16)
+        out[tok : 2 * tok] = (k_scale * (dkn - kn * (b_col * s_e + s_w))).astype(BF16)
+        out[plan.v_at : plan.aux_at] = (scales[m][0] * dr[m]).astype(BF16)
         sums.append((s_e, s_q + b_col * s_e - s_w, total + whole * both))
     turned = to_rows([s[0] for s in sums] + [s[1] for s in sums], tok)
     for m in mine:
@@ -396,7 +407,7 @@
         d_rate = turned[m] + jnp.sum(dr[m] * values, axis=0, keepdims=True)
         parts = dot(aux_rows([turned[plan.hv + m]], tok), upto, 1, 0)
         d_decay = parts[0:1] + parts[1:2] + parts[2:3] + sums[m][2]
-        outs[plan.ring.seen(m, 0)][plan.aux_at :] = aux_rows([d_rate, d_decay], tok)
+        outs[m][plan.aux_at :] = aux_rows([d_rate, d_decay], tok)
 
 
 def gather_rows(head, pieces, all_ref):
@@ -407,23 +418,16 @@
 
 
 def cotangent_kernel(plan, parts, head_ref, place_ref, *refs):
-    pieces, w_ref, outs, (all_ref, core_ref) = refs[:parts], refs[parts], refs[parts + 1 : -2], refs[-2:]
+    pieces, w_ref, outs, (all_ref, out_ref) = refs[:parts], refs[parts], refs[parts + 1 : -2], refs[-2:]
     gather_rows(head_ref[0], pieces, all_ref)
     high, low = halves(dot(w_ref[...], all_ref[...], 1, 1))
+    share = all_ref.shape[1] // plan.hv
     for m in range(plan.hv):
-        core_ref[m, :DV] = high[m * DV : (m + 1) * DV]
-        core_ref[m, DV:] = low[m * DV : (m + 1) * DV]
-    hand_out(plan, place_ref[0], core_ref, outs)
-
-
-def turn_kernel(plan, parts, head_ref, place_ref, *refs):
-    pieces, outs, (all_ref, turned_ref) = refs[:parts], refs[parts:-2], refs[-2:]
-    gather_rows(head_ref[0], pieces, all_ref)
-    share = turned_ref.shape[1]
-    for m in range(plan.hv):
+        out_ref[m, :DV] = high[m * DV : (m + 1) * DV]
+        out_ref[m, DV : 2 * DV] = low[m * DV : (m + 1) * DV]
         part = all_ref[:, m * share : (m + 1) * share].astype(F32)
-        turned_ref[m] = jnp.transpose(part).astype(BF16)
-    hand_out(plan, place_ref[0], turned_ref, outs)
+        out_ref[m, 2 * DV :] = jnp.transpose(part).astype(BF16)
+    hand_out(plan, place_ref[0], out_ref, outs)
 
 
 def project_kernel(plan, parts, head_ref, place_ref, *refs):
@@ -446,7 +450,7 @@
 
 def weight_kernel(plan, place_ref, mate_ref, *refs):
     hv = plan.hv
-    turned, mixed_refs, outs, all_ref = refs[:hv], refs[hv : 2 * hv], refs[2 * hv : -1], refs[-1]
+    cot_refs, mixed_refs, outs, all_ref = refs[:hv], refs[hv : 2 * hv], refs[2 * hv : -1], refs[-1]
     for d, ref in enumerate(mixed_refs):
         head = plan.ring.source(place_ref[0], d)
         for k in range(hv):
@@ -454,20 +458,17 @@
     share = outs[0].shape[0]
     for d, out_ref in enumerate(outs):
         at = lax.rem(mate_ref[0] + plan.mates - d, plan.mates) * share
-        at = pl.multiple_of(at, share)
+        at = 2 * DV + pl.multiple_of(at, share)
         total = None
         for k in range(hv):
             mixed = all_ref[k].reshape(hv * DV, plan.tok)
-            part = dot(turned[k][pl.ds(at, share), :], mixed, 1, 1)
+            part = dot(cot_refs[k][pl.ds(at, share), :], mixed, 1, 1)
             total = part if total is None else total + part
         out_ref[...] = total
 
 
-def finish_kernel(plan, place_ref, *refs):
-    pieces, (q_ref, k_ref, v_ref, rate_ref, decay_ref, in_ref) = refs[: plan.hv], refs[plan.hv :]
+def finish_kernel(plan, in_ref, q_ref, k_ref, v_ref, rate_ref, decay_ref):
     tok = plan.tok
-    for d, ref in enumerate(pieces):
-        in_ref[plan.ring.source(place_ref[0], d)] = ref[...]
     for kh in range(plan.hk):
         mine = [h for h in range(plan.hv) if plan.key_head(h) == kh]
         for ref, at in ((q_ref, 0), (k_ref, tok)):
@@ -484,6 +485,10 @@
         decay_ref[h : h + 1, :] = aux[3:4] + aux[4:5] + aux[5:6]
 
 
+def after(x, y):
+    return lax.optimization_barrier((x, y))[0]
+
+
 def per_device(
     queries, key_vectors, value_rows, write_rate, log_decay, doc_offsets, out_weight, grad_out
 ):
@@ -501,42 +506,32 @@
         return [pieces[0]] + moved
 
     vmem = lambda dtype, *shape: pltpu.VMEM(shape, dtype)
-    rows = across_heads([grad_out] * parts)
 
     packed = call(
         partial(pack_kernel, plan),
-        [arr(BF16, plan.rows, DK)] * hv,
-        smem=(0,),
-        scratch=[vmem(BF16, hv, plan.rows, DK)],
-        fetch=range(6),
-        flops=2_000_000_000,
-    )(place, queries, key_vectors, value_rows, write_rate, log_decay)
-    got = plan.exchange(packed)
+        arr(BF16, hv, plan.rows, DK),
+        fetch=range(5),
+    )(queries, key_vectors, value_rows, write_rate, log_decay)
+    got = plan.exchange_at_once(packed)
+    rows = across_heads([after(grad_out, packed)] * parts)
 
     link, kept = call(
         partial(prepare_kernel, plan),
         (arr(F32, hv, 2, DK, DK), arr(F32, hv, KEPT, tok, DK)),
         smem=(0, 1, 2),
-        flops=4_500_000_000,
-    )(doc_offsets, place, mate, *got)
+        flops=20_000_000_000,
+    )(doc_offsets, place, mate, got)
     links = [link] + [plan.from_mate(link, d) for d in range(1, s)]
 
-    d_core = call(
+    cot = call(
         partial(cotangent_kernel, plan, parts),
-        [arr(BF16, 2 * DV, tok)] * hv,
+        [arr(BF16, 2 * DV + model // hv, tok)] * hv,
         smem=(0, 1),
-        scratch=[vmem(BF16, tok, model), vmem(BF16, hv, 2 * DV, tok)],
-        flops=1_500_000_000,
-    )(head, place, *rows, out_weight)
-    d_core = plan.exchange(d_core)
-    turned = call(
-        partial(turn_kernel, plan, parts),
-        [arr(BF16, model // hv, tok)] * hv,
-        smem=(0, 1),
-        scratch=[vmem(BF16, tok, model), vmem(BF16, hv, model // hv, tok)],
-        flops=1_000_000_000,
-    )(head, place, *rows)
-    turned = plan.exchange(turned)
+        scratch=[vmem(BF16, tok, model), vmem(BF16, hv, 2 * DV + model // hv, tok)],
+        flops=30_000_000_000,
+    )(head, place, *after(rows, link), out_weight)
+    kept = after(kept, cot[0])
+    cot = plan.exchange(cot)
 
     states, *mixed = call(
         partial(scan_kernel, plan),
@@ -548,7 +543,7 @@
     mixed = plan.exchange(mixed)
     back = call(
         partial(state_cotangent_kernel, plan), arr(F32, hv, DV, DK), flops=500_000_000
-    )(kept, *d_core)
+    )(kept, *after(cot, states))
     backs = [back] + [plan.from_mate(back, d) for d in range(1, s)]
 
     projected = call(
@@ -562,7 +557,7 @@
 
     grads = call(
         partial(backward_kernel, plan),
-        [arr(BF16, plan.rows, DK)] * hv,
+        arr(BF16, hv, plan.rows, DK),
         smem=(0, 1, 2),
         scratch=[
             vmem(F32, s, hv, 2, DK, DK),
@@ -570,8 +565,8 @@
             vmem(F32, n, DV, DK),
         ],
         flops=6_000_000_000,
-    )(doc_offsets, place, mate, *links, *backs, *got, *d_core, kept, states)
-    grads = plan.exchange(grads)
+    )(doc_offsets, place, mate, *links, *backs, got, *cot, kept, states)
+    grads = plan.exchange_at_once(grads)
 
     shares = call(
         partial(weight_kernel, plan),
@@ -579,7 +574,7 @@
         smem=(0, 1),
         scratch=[vmem(BF16, hv, hv, DV, tok)],
         flops=1_000_000_000,
-    )(place, mate, *turned, *mixed)
+    )(place, mate, *cot, *mixed)
     weight_grad = shares[0]
     for d in range(1, s):
         weight_grad = weight_grad + plan.from_mate(shares[d], d)
@@ -593,12 +588,10 @@
             arr(F32, hv, tok),
             arr(F32, hv, tok),
         ),
-        smem=(0,),
-        scratch=[vmem(BF16, hv, plan.rows, DK)],
         flops=1_000_000_000,
         inside=False,
-    )(place, *grads)
-    layer_out, _, _ = lax.optimization_barrier((layer_parts[0], grad_q, weight_grad))
+    )(grads)
+    layer_out = after(layer_parts[0], (grad_q, weight_grad))
     for part in layer_parts[1:]:
         layer_out = layer_out + part.astype(F32)
     return (layer_out, grad_q, grad_k, grad_v, grad_rate, grad_decay, weight_grad)

time: 76.6 us -> 72.2 us (0.943)
  waiting for transfers between devices: 30.3 us -> 24.4 us
  starting transfers between devices: 27.9 us -> 24.6 us
  Pallas kernels: 14.1 us -> 16.8 us
  other arithmetic: 1.64 us -> 2.67 us
  local copies, waits for them, and re-layouts: 1.64 us -> 2.48 us
    ppermute x15 -> x6, starting transfers between devices: 19.1 us -> 7.11 us  [exchange(): moved.append(lax.ppermute(pieces[d], 'ctx', pairs))]
    all_to_all x0 -> x2, starting transfers between devices: none -> 8.62 us  [exchange_at_once(): lax.all_to_all(pieces, 'ctx', split_axis=0, concat_axis=0, axis_index_gro...]
    ppermute x6, waiting for transfers between devices: 16.5 us -> 8.96 us  [across_heads(): lax.ppermute(pieces[d], 'head', Ring(parts).pairs(d))]
    pallas_call x10 -> x9, Pallas kernels: 14.1 us -> 16.8 us  [run(): pl.pallas_call(kernel, out_shape=outs, in_specs=[spec(i) for i in range(l...]
    all_to_all x0 -> x2, waiting for transfers between devices: none -> 2.65 us  [exchange_at_once(): lax.all_to_all(pieces, 'ctx', split_axis=0, concat_axis=0, axis_index_gro...]
    ppermute x15 -> x6, waiting for transfers between devices: 13.8 us -> 12.7 us  [exchange(): moved.append(lax.ppermute(pieces[d], 'ctx', pairs))]
    add x1, other arithmetic: 0.88 us -> 1.91 us  [per_device(): weight_grad = weight_grad + plan.from_mate(shares[d], d)]
    unnamed x20 -> x16, local copies, waits for them, and re-layouts: 1.64 us -> 2.48 us
  transfers between devices with their start and end apart: 24 -> 17, of which waited for: 12 -> 10; matrix products, arithmetic and copies ran while one was open for 1% -> 3% of each run, Pallas kernels for 12% -> 20%
where the time goes in v8:
time: 72.2 us; the launch traced here: 71.7 us
  starting transfers between devices  24.6 us (34%)
  waiting for transfers between devices  24.4 us (34%)
  Pallas kernels  16.8 us (23%)
  other arithmetic  2.67 us (4%)
  local copies, waits for them, and re-layouts  2.48 us (3%)
  between operations  0.76 us (1%)
    pallas_call x9, Pallas kernels, run(): pl.pallas_call(kernel, out_shape=outs, in_specs=[spec(i) for i in range(l...  16.8 us
    ppermute x6, waiting for transfers between devices, exchange(): moved.append(lax.ppermute(pieces[d], 'ctx', pairs))  12.7 us
    ppermute x6, waiting for transfers between devices, across_heads(): lax.ppermute(pieces[d], 'head', Ring(parts).pairs(d))  8.96 us
    ppermute x6, starting transfers between devices, across_heads(): lax.ppermute(pieces[d], 'head', Ring(parts).pairs(d))  8.77 us
    all_to_all x2, starting transfers between devices, exchange_at_once(): lax.all_to_all(pieces, 'ctx', split_axis=0, concat_axis=0, axis_index_gro...  8.62 us
    ppermute x6, starting transfers between devices, exchange(): moved.append(lax.ppermute(pieces[d], 'ctx', pairs))  7.11 us
    all_to_all x2, waiting for transfers between devices, exchange_at_once(): lax.all_to_all(pieces, 'ctx', split_axis=0, concat_axis=0, axis_index_gro...  2.65 us
    unnamed x16, local copies, waits for them, and re-layouts  2.48 us
  transfers between devices with their start and end apart: 17, of which 10 were waited for; matrix products, arithmetic and copies ran while one was open for 3% of the time, Pallas kernels for 20%

profile of v8, /device:TPU:0, one launch (start us, length us, event | category | flops | bytes accessed | tf_op | source)
XLA Modules:
  0.0 71.7 jit_solution(18292063620816033298)
XLA Ops:
  0.6 1.9 %shard_map.135 = bf16[4,400,128]{2,1,0:T(8,128)(2,1)} custom-call(bf16[128,256]{1,0:T(8,128)(2,1)} %q_ref.1, bf16[128,256]{1,0:T(8,128)(2,1)} %k_ref.1, bf16[128,512]{1,0:T(8,128)(2,1)} %v_ref.1, f32[4,128]{1,0:T(4,128)} %rate_ref.1, f32[4,128]{1,0:T(4,128)} %decay_ref.1), custom_call_target="tpu_custom_call" | custom-call | tf_op jit(solution)/shard_map/pallas_call | solution.py:60
  2.5 5.2 %all-to-all-start = ((bf16[4,400,128]{2,1,0:T(8,128)(2,1)}), bf16[4,400,128]{2,1,0:T(8,128)(2,1)S(1)}, u32[]{:S(2)}, u32[]{:S(2)}) async-start(bf16[4,400,128]{2,1,0:T(8,128)(2,1)} %shard_map.135), calls=%async_computation | async-start | bytes 819200 | tf_op jit(solution)/shard_map/all_to_all | solution.py:118
  7.6 3.6 %collective-permute-start.3 = (bf16[32,2048]{1,0:T(8,128)(2,1)}, bf16[32,2048]{1,0:T(8,128)(2,1)S(1)}, u32[]{:S(2)}, u32[]{:S(2)}) collective-permute-start(bf16[32,2048]{1,0:T(8,128)(2,1)} %refs_0_), channel_id=1, source_target_pairs={{3,0},{2,1},{1,2},{0,3},{7,4},{6,5},{5,6},{4,7},{11,8},{10,9},{9,1... | collective-permute-start | bytes 393224 | tf_op jit(solution)/shard_map/ppermute | solution.py:505
  11.3 0.8 %collective-permute-start.1 = (bf16[32,2048]{1,0:T(8,128)(2,1)}, bf16[32,2048]{1,0:T(8,128)(2,1)S(1)}, u32[]{:S(2)}, u32[]{:S(2)}) collective-permute-start(bf16[32,2048]{1,0:T(8,128)(2,1)} %refs_0_), channel_id=1, source_target_pairs={{1,0},{0,1},{3,2},{2,3},{5,4},{4,5},{7,6},{6,7},{9,8},{8,9},{11,10... | collective-permute-start | bytes 393224 | tf_op jit(solution)/shard_map/ppermute | solution.py:505
  12.0 2.4 %all-to-all-done.refs_0_.refs_4_ = bf16[4,400,128]{2,1,0:T(8,128)(2,1)S(1)} async-done(((bf16[4,400,128]{2,1,0:T(8,128)(2,1)}), bf16[4,400,128]{2,1,0:T(8,128)(2,1)S(1)}, u32[]{:S(2)}, u32[]{:S(2)}) %all-to-all-start) | async-done | bytes 409632 | tf_op jit(solution)/shard_map/all_to_all | solution.py:118
  14.4 0.7 copy-done.4
  15.1 3.9 %shard_map.136 = (f32[4,2,128,128]{3,2,1,0:T(8,128)S(1)}, f32[4,7,128,128]{3,2,1,0:T(8,128)S(1)}) custom-call(s32[5]{0:T(128)S(1)} %copy-done.4, s32[1]{0:T(128)} %bitcast.1.place_ref, s32[1]{0:T(128)} %bitcast.2.mate_ref, bf16[4,400,128]{2,1,0:T(8,128)(2,1)S(1)} %all-to-all-done.refs_0_.refs_4_), custom_call_target="tpu_custom_call" | custom-call | flops 20000000000 | tf_op jit(solution)/shard_map/pallas_call | solution.py:60
  19.1 3.3 %collective-permute-done.2.refs_2_ = bf16[32,2048]{1,0:T(8,128)(2,1)S(1)} collective-permute-done((bf16[32,2048]{1,0:T(8,128)(2,1)}, bf16[32,2048]{1,0:T(8,128)(2,1)S(1)}, u32[]{:S(2)}, u32[]{:S(2)}) %collective-permute-start.2) | collective-permute-done | bytes 131104 | tf_op jit(solution)/shard_map/ppermute | solution.py:505
  22.4 0.8 %shard_map.137 = (bf16[768,128]{1,0:T(8,128)(2,1)S(1)}, bf16[768,128]{1,0:T(8,128)(2,1)S(1)}, bf16[768,128]{1,0:T(8,128)(2,1)S(1)}, bf16[768,128]{1,0:T(8,128)(2,1)S(1)}) custom-call(s32[1]{0:T(128)} %bitcast.head_ref, s32[1]{0:T(128)} %bitcast.1.place_ref, bf16[32,2048]{1,0:T(8,128)(2,1)S(1)} %copy-done.1, ...), custom_call_target="tpu_custom_call" | custom-call | flops 30000001024 | tf_op jit(solution)/shard_map/pallas_call | solution.py:60
  23.2 1.7 %collective-permute-start.7 = (bf16[768,128]{1,0:T(8,128)(2,1)S(1)}, bf16[768,128]{1,0:T(8,128)(2,1)S(1)}, u32[]{:S(2)}, u32[]{:S(2)}) collective-permute-start(bf16[768,128]{1,0:T(8,128)(2,1)S(1)} %get-tuple-element.54), channel_id=1, source_target_pairs={{8,0},{12,4},{0,8},{4,12},{24,16},{28,20},{16,24},{20,28},{9,1},{1... | collective-permute-start | bytes 589832 | tf_op jit(solution)/shard_map/ppermute | solution.py:112
  24.9 1.5 %collective-permute-start.8 = (bf16[768,128]{1,0:T(8,128)(2,1)S(1)}, bf16[768,128]{1,0:T(8,128)(2,1)S(1)}, u32[]{:S(2)}, u32[]{:S(2)}) collective-permute-start(bf16[768,128]{1,0:T(8,128)(2,1)S(1)} %get-tuple-element.55), channel_id=1, source_target_pairs={{16,0},{20,4},{24,8},{28,12},{0,16},{4,20},{8,24},{12,28},{17,1},{... | collective-permute-start | bytes 589832 | tf_op jit(solution)/shard_map/ppermute | solution.py:112
  26.7 1.3 %shard_map.138 = (f32[4,128,128]{2,1,0:T(8,128)S(1)}, bf16[4,128,128]{2,1,0:T(8,128)(2,1)S(1)}, bf16[4,128,128]{2,1,0:T(8,128)(2,1)S(1)}, bf16[4,128,128]{2,1,0:T(8,128)(2,1)S(1)}, bf16[4,128,128]{2,1,0:T(8,128)(2,1)S(1)}) custom-call(s32[1]{0:T(128)} %bitcast.1.place_ref, s32[1]{0:T(128)} %bitcast.2.mate_ref, ...), custom_call_target="tpu_custom_call" | custom-call | flops 2500000000 | tf_op jit(solution)/shard_map/pallas_call | solution.py:60
  28.1 2.8 %collective-permute-done.7.refs_1_.refs_6_ = bf16[768,128]{1,0:T(8,128)(2,1)S(1)} collective-permute-done((bf16[768,128]{1,0:T(8,128)(2,1)S(1)}, bf16[768,128]{1,0:T(8,128)(2,1)S(1)}, u32[]{:S(2)}, u32[]{:S(2)}) %collective-permute-start.7) | collective-permute-done | bytes 196640 | tf_op jit(solution)/shard_map/ppermute | solution.py:112
  30.9 3.8 %collective-permute-done.8.refs_2_.refs_7_ = bf16[768,128]{1,0:T(8,128)(2,1)S(1)} collective-permute-done((bf16[768,128]{1,0:T(8,128)(2,1)S(1)}, bf16[768,128]{1,0:T(8,128)(2,1)S(1)}, u32[]{:S(2)}, u32[]{:S(2)}) %collective-permute-start.8) | collective-permute-done | bytes 196640 | tf_op jit(solution)/shard_map/ppermute | solution.py:112
  35.1 1.2 %collective-permute-start.4 = (bf16[4,128,128]{2,1,0:T(8,128)(2,1)S(1)}, bf16[4,128,128]{2,1,0:T(8,128)(2,1)S(1)}, u32[]{:S(2)}, u32[]{:S(2)}) collective-permute-start(bf16[4,128,128]{2,1,0:T(8,128)(2,1)S(1)} %get-tuple-element.50), channel_id=1, source_target_pairs={{8,0},{12,4},{0,8},{4,12},{24,16},{28,20},{16,24},{20,28},{9,1},{1... | collective-permute-start | bytes 393224 | tf_op jit(solution)/shard_map/ppermute | solution.py:112
  36.3 0.9 %collective-permute-start.5 = (bf16[4,128,128]{2,1,0:T(8,128)(2,1)S(1)}, bf16[4,128,128]{2,1,0:T(8,128)(2,1)S(1)}, u32[]{:S(2)}, u32[]{:S(2)}) collective-permute-start(bf16[4,128,128]{2,1,0:T(8,128)(2,1)S(1)} %get-tuple-element.51), channel_id=1, source_target_pairs={{16,0},{20,4},{24,8},{28,12},{0,16},{4,20},{8,24},{12,28},{17,1},{... | collective-permute-start | bytes 393224 | tf_op jit(solution)/shard_map/ppermute | solution.py:112
  37.2 1.5 %collective-permute-start.6 = (bf16[4,128,128]{2,1,0:T(8,128)(2,1)S(1)}, bf16[4,128,128]{2,1,0:T(8,128)(2,1)S(1)}, u32[]{:S(2)}, u32[]{:S(2)}) collective-permute-start(bf16[4,128,128]{2,1,0:T(8,128)(2,1)S(1)} %get-tuple-element.52), channel_id=1, source_target_pairs={{24,0},{28,4},{16,8},{20,12},{8,16},{12,20},{0,24},{4,28},{25,1},{... | collective-permute-start | bytes 393224 | tf_op jit(solution)/shard_map/ppermute | solution.py:112
  38.6 2.8 %collective-permute-done.4.refs_1_.refs_5_ = bf16[4,128,128]{2,1,0:T(8,128)(2,1)S(1)} collective-permute-done((bf16[4,128,128]{2,1,0:T(8,128)(2,1)S(1)}, bf16[4,128,128]{2,1,0:T(8,128)(2,1)S(1)}, u32[]{:S(2)}, u32[]{:S(2)}) %collective-permute-start.4) | collective-permute-done | bytes 131104 | tf_op jit(solution)/shard_map/ppermute | solution.py:112
  41.5 0.9 %collective-permute-done.5.refs_2_.refs_6_ = bf16[4,128,128]{2,1,0:T(8,128)(2,1)S(1)} collective-permute-done((bf16[4,128,128]{2,1,0:T(8,128)(2,1)S(1)}, bf16[4,128,128]{2,1,0:T(8,128)(2,1)S(1)}, u32[]{:S(2)}, u32[]{:S(2)}) %collective-permute-start.5) | collective-permute-done | bytes 131104 | tf_op jit(solution)/shard_map/ppermute | solution.py:112
  42.3 2.4 %collective-permute-done.6.refs_3_.refs_7_ = bf16[4,128,128]{2,1,0:T(8,128)(2,1)S(1)} collective-permute-done((bf16[4,128,128]{2,1,0:T(8,128)(2,1)S(1)}, bf16[4,128,128]{2,1,0:T(8,128)(2,1)S(1)}, u32[]{:S(2)}, u32[]{:S(2)}) %collective-permute-start.6) | collective-permute-done | bytes 131104 | tf_op jit(solution)/shard_map/ppermute | solution.py:112
  44.7 1.5 %shard_map.143 = (f32[256,512]{1,0:T(8,128)S(1)}, f32[256,512]{1,0:T(8,128)}) custom-call(s32[1]{0:T(128)} %bitcast.1.place_ref, s32[1]{0:T(128)} %bitcast.2.mate_ref, bf16[768,128]{1,0:T(8,128)(2,1)S(1)} %get-tuple-element.58.refs_0_.refs_5_, bf16[768,128]{1,0:T(8,128)(2,1)S(1)} %collective-permute-done.7.refs_1_.refs_6_, ...), custom_call_target="tpu_custom_call" | custom-call | flops 1000000000 | tf_op jit(solution)/shard_map/pallas_call | solution.py:60
  46.3 5.1 %shard_map.141 = bf16[4,400,128]{2,1,0:T(8,128)(2,1)} custom-call(s32[5]{0:T(128)S(1)} %copy-done.5, s32[1]{0:T(128)} %bitcast.1.place_ref, s32[1]{0:T(128)} %bitcast.2.mate_ref, f32[4,2,128,128]{3,2,1,0:T(8,128)S(1)} %get-tuple-element.40.refs_0_, f32[4,2,128,128]{3,2,1,0:T(8,128)S(1)} %collective-permute-done.refs_1_, ...), custom_call_target="tpu_custom_call" | custom-call | flops 6000000000 | tf_op jit(solution)/shard_map/pallas_call | solution.py:60
  51.3 3.5 %all-to-all-start.1 = ((bf16[4,400,128]{2,1,0:T(8,128)(2,1)}), bf16[4,400,128]{2,1,0:T(8,128)(2,1)S(1)}, u32[]{:S(2)}, u32[]{:S(2)}) async-start(bf16[4,400,128]{2,1,0:T(8,128)(2,1)} %shard_map.141), calls=%async_computation.1 | async-start | bytes 819200 | tf_op jit(solution)/shard_map/all_to_all | solution.py:118
  54.8 0.9 %copy-done.3 = bf16[4,128,128]{2,1,0:T(8,128)(2,1)S(1)} copy-done((bf16[4,128,128]{2,1,0:T(8,128)(2,1)S(1)}, bf16[4,128,128]{2,1,0:T(8,128)(2,1)}, u32[]{:S(2)}) %copy-start.3) | copy-done | bytes 131096
  55.7 0.9 %copy-done.7 = bf16[4,128,128]{2,1,0:T(8,128)(2,1)S(1)} copy-done((bf16[4,128,128]{2,1,0:T(8,128)(2,1)S(1)}, bf16[4,128,128]{2,1,0:T(8,128)(2,1)}, u32[]{:S(2)}) %copy-start.7) | copy-done | bytes 131096
  56.6 1.2 %shard_map.139 = (f32[32,2048]{1,0:T(8,128)S(1)}, bf16[32,2048]{1,0:T(8,128)(2,1)}, bf16[32,2048]{1,0:T(8,128)(2,1)}, bf16[32,2048]{1,0:T(8,128)(2,1)}) custom-call(s32[1]{0:T(128)} %bitcast.head_ref, s32[1]{0:T(128)} %bitcast.1.place_ref, bf16[4,128,128]{2,1,0:T(8,128)(2,1)S(1)} %copy-done.7, ...), custom_call_target="tpu_custom_call" | custom-call | flops 1000000000 | tf_op jit(solution)/shard_map/pallas_call | solution.py:60
  57.9 2.1 %collective-permute-start.13 = (bf16[32,2048]{1,0:T(8,128)(2,1)}, bf16[32,2048]{1,0:T(8,128)(2,1)S(1)}, u32[]{:S(2)}, u32[]{:S(2)}) collective-permute-start(bf16[32,2048]{1,0:T(8,128)(2,1)} %get-tuple-element.67), channel_id=1, source_target_pairs={{2,0},{3,1},{0,2},{1,3},{6,4},{7,5},{4,6},{5,7},{10,8},{11,9},{8,1... | collective-permute-start | bytes 393224 | tf_op jit(solution)/shard_map/ppermute | solution.py:505
  60.0 2.3 %collective-permute-start.14 = (bf16[32,2048]{1,0:T(8,128)(2,1)}, bf16[32,2048]{1,0:T(8,128)(2,1)S(1)}, u32[]{:S(2)}, u32[]{:S(2)}) collective-permute-start(bf16[32,2048]{1,0:T(8,128)(2,1)} %get-tuple-element.68), channel_id=1, source_target_pairs={{3,0},{2,1},{1,2},{0,3},{7,4},{6,5},{5,6},{4,7},{11,8},{10,9},{9,1... | collective-permute-start | bytes 393224 | tf_op jit(solution)/shard_map/ppermute | solution.py:505
  62.5 0.8 %shard_map.142 = (f32[128,256]{1,0:T(8,128)}, f32[128,256]{1,0:T(8,128)}, f32[128,512]{1,0:T(8,128)}, f32[4,128]{1,0:T(4,128)}, f32[4,128]{1,0:T(4,128)}) custom-call(bf16[4,400,128]{2,1,0:T(8,128)(2,1)S(1)} %all-to-all-done.1.in_ref), custom_call_target="tpu_custom_call" | custom-call | flops 1000000000 | tf_op jit(solution)/shard_map/pallas_call | solution.py:60
  63.3 1.9 %add.18 = f32[256,512]{1,0:T(8,128)} add(f32[256,512]{1,0:T(8,128)S(1)} %get-tuple-element.63, f32[256,512]{1,0:T(8,128)} %collective-permute-done.11) | non-fusion elementwise | flops 131072 | bytes 1572864 | tf_op jit(solution)/shard_map/add | solution.py:580
  65.7 5.2 %collective-permute-done.13 = bf16[32,2048]{1,0:T(8,128)(2,1)S(1)} collective-permute-done((bf16[32,2048]{1,0:T(8,128)(2,1)}, bf16[32,2048]{1,0:T(8,128)(2,1)S(1)}, u32[]{:S(2)}, u32[]{:S(2)}) %collective-permute-start.13) | collective-permute-done | bytes 131104 | tf_op jit(solution)/shard_map/ppermute | solution.py:505
  70.9 0.8 %convert_add_fusion = f32[32,2048]{1,0:T(8,128)} fusion(bf16[32,2048]{1,0:T(8,128)(2,1)S(1)} %collective-permute-done.14, bf16[32,2048]{1,0:T(8,128)(2,1)S(1)} %collective-permute-done.13, f32[32,2048]{1,0:T(8,128)S(1)} %get-tuple-element.65, bf16[32,2048]{1,0:T(8,128)(2,1)S(1)} %collective-permute-done.12), kind=kLoop, calls=%fused_computation | loop fusion | flops 393216 | bytes 917504 | tf_op jit(solution)/shard_map/add | solution.py:596
  (29 shorter events, 1.6 us)
Async XLA Ops:
  2.5 12.0 %all-to-all-start = ((bf16[4,400,128]{2,1,0:T(8,128)(2,1)}), bf16[4,400,128]{2,1,0:T(8,128)(2,1)S(1)}, u32[]{:S(2)}, u32[]{:S(2)}) async-start(bf16[4,400,128]{2,1,0:T(8,128)(2,1)} %shard_map.135), calls=%async_computation | async-start | bytes 819200 | tf_op jit(solution)/shard_map/all_to_all | solution.py:118
  7.6 11.4 %collective-permute-start.3 = (bf16[32,2048]{1,0:T(8,128)(2,1)}, bf16[32,2048]{1,0:T(8,128)(2,1)S(1)}, u32[]{:S(2)}, u32[]{:S(2)}) collective-permute-start(bf16[32,2048]{1,0:T(8,128)(2,1)} %refs_0_), channel_id=1, source_target_pairs={{3,0},{2,1},{1,2},{0,3},{7,4},{6,5},{5,6},{4,7},{11,8},{10,9},{9,1... | collective-permute-start | bytes 393224 | tf_op jit(solution)/shard_map/ppermute | solution.py:505
  11.2 11.1 %collective-permute-start.2 = (bf16[32,2048]{1,0:T(8,128)(2,1)}, bf16[32,2048]{1,0:T(8,128)(2,1)S(1)}, u32[]{:S(2)}, u32[]{:S(2)}) collective-permute-start(bf16[32,2048]{1,0:T(8,128)(2,1)} %refs_0_), channel_id=1, source_target_pairs={{2,0},{3,1},{0,2},{1,3},{6,4},{7,5},{4,6},{5,7},{10,8},{11,9},{8,1... | collective-permute-start | bytes 393224 | tf_op jit(solution)/shard_map/ppermute | solution.py:505
  11.3 11.1 %collective-permute-start.1 = (bf16[32,2048]{1,0:T(8,128)(2,1)}, bf16[32,2048]{1,0:T(8,128)(2,1)S(1)}, u32[]{:S(2)}, u32[]{:S(2)}) collective-permute-start(bf16[32,2048]{1,0:T(8,128)(2,1)} %refs_0_), channel_id=1, source_target_pairs={{1,0},{0,1},{3,2},{2,3},{5,4},{4,5},{7,6},{6,7},{9,8},{8,9},{11,10... | collective-permute-start | bytes 393224 | tf_op jit(solution)/shard_map/ppermute | solution.py:505
  14.4 0.7 copy-start.4
  15.1 7.3 %copy-start = (bf16[512,2048]{1,0:T(8,128)(2,1)S(1)}, bf16[512,2048]{1,0:T(8,128)(2,1)}, u32[]{:S(2)}) copy-start(bf16[512,2048]{1,0:T(8,128)(2,1)} %refs_4_.3) | copy-start | bytes 6291460
  15.1 7.3 %copy-start.1 = (bf16[32,2048]{1,0:T(8,128)(2,1)S(1)}, bf16[32,2048]{1,0:T(8,128)(2,1)}, u32[]{:S(2)}) copy-start(bf16[32,2048]{1,0:T(8,128)(2,1)} %refs_0_) | copy-start | bytes 393220
  19.0 7.8 %collective-permute-start = (f32[4,2,128,128]{3,2,1,0:T(8,128)S(1)}, f32[4,2,128,128]{3,2,1,0:T(8,128)S(1)}, u32[]{:S(2)}, u32[]{:S(2)}) collective-permute-start(f32[4,2,128,128]{3,2,1,0:T(8,128)S(1)} %get-tuple-element.40.refs_0_), channel_id=1, source_target_pairs={{4,0},{0,4},{12,8},{8,12},{20,16},{16,20},{28,24},{24,28},{5,1},{1... | collective-permute-start | bytes 1572872 | tf_op jit(solution)/shard_map/ppermute | solution.py:125
  23.2 7.7 %collective-permute-start.7 = (bf16[768,128]{1,0:T(8,128)(2,1)S(1)}, bf16[768,128]{1,0:T(8,128)(2,1)S(1)}, u32[]{:S(2)}, u32[]{:S(2)}) collective-permute-start(bf16[768,128]{1,0:T(8,128)(2,1)S(1)} %get-tuple-element.54), channel_id=1, source_target_pairs={{8,0},{12,4},{0,8},{4,12},{24,16},{28,20},{16,24},{20,28},{9,1},{1... | collective-permute-start | bytes 589832 | tf_op jit(solution)/shard_map/ppermute | solution.py:112
  24.9 9.9 %collective-permute-start.8 = (bf16[768,128]{1,0:T(8,128)(2,1)S(1)}, bf16[768,128]{1,0:T(8,128)(2,1)S(1)}, u32[]{:S(2)}, u32[]{:S(2)}) collective-permute-start(bf16[768,128]{1,0:T(8,128)(2,1)S(1)} %get-tuple-element.55), channel_id=1, source_target_pairs={{16,0},{20,4},{24,8},{28,12},{0,16},{4,20},{8,24},{12,28},{17,1},{... | collective-permute-start | bytes 589832 | tf_op jit(solution)/shard_map/ppermute | solution.py:112
  26.4 8.4 %collective-permute-start.9 = (bf16[768,128]{1,0:T(8,128)(2,1)S(1)}, bf16[768,128]{1,0:T(8,128)(2,1)S(1)}, u32[]{:S(2)}, u32[]{:S(2)}) collective-permute-start(bf16[768,128]{1,0:T(8,128)(2,1)S(1)} %get-tuple-element.56), channel_id=1, source_target_pairs={{24,0},{28,4},{16,8},{20,12},{8,16},{12,20},{0,24},{4,28},{25,1},{... | collective-permute-start | bytes 589832 | tf_op jit(solution)/shard_map/ppermute | solution.py:112
  28.1 18.2 %copy-start.6 = (bf16[4,128,128]{2,1,0:T(8,128)(2,1)}, bf16[4,128,128]{2,1,0:T(8,128)(2,1)S(1)}, u32[]{:S(2)}) copy-start(bf16[4,128,128]{2,1,0:T(8,128)(2,1)S(1)} %get-tuple-element.49.refs_0_.refs_4_) | copy-start | bytes 393220
  35.0 11.3 %copy-start.5 = (s32[5]{0:T(128)S(1)}, s32[5]{0:T(128)}, u32[]{:S(2)}) copy-start(s32[5]{0:T(128)} %off_ref.3) | copy-start | bytes 64
  35.0 11.2 %collective-permute-start.10 = (f32[4,128,128]{2,1,0:T(8,128)S(1)}, f32[4,128,128]{2,1,0:T(8,128)S(1)}, u32[]{:S(2)}, u32[]{:S(2)}) collective-permute-start(f32[4,128,128]{2,1,0:T(8,128)S(1)} %shard_map.140.refs_2_), channel_id=1, source_target_pairs={{4,0},{0,4},{12,8},{8,12},{20,16},{16,20},{28,24},{24,28},{5,1},{1... | collective-permute-start | bytes 786440 | tf_op jit(solution)/shard_map/ppermute | solution.py:125
  35.1 6.4 %collective-permute-start.4 = (bf16[4,128,128]{2,1,0:T(8,128)(2,1)S(1)}, bf16[4,128,128]{2,1,0:T(8,128)(2,1)S(1)}, u32[]{:S(2)}, u32[]{:S(2)}) collective-permute-start(bf16[4,128,128]{2,1,0:T(8,128)(2,1)S(1)} %get-tuple-element.50), channel_id=1, source_target_pairs={{8,0},{12,4},{0,8},{4,12},{24,16},{28,20},{16,24},{20,28},{9,1},{1... | collective-permute-start | bytes 393224 | tf_op jit(solution)/shard_map/ppermute | solution.py:112
  36.3 6.0 %collective-permute-start.5 = (bf16[4,128,128]{2,1,0:T(8,128)(2,1)S(1)}, bf16[4,128,128]{2,1,0:T(8,128)(2,1)S(1)}, u32[]{:S(2)}, u32[]{:S(2)}) collective-permute-start(bf16[4,128,128]{2,1,0:T(8,128)(2,1)S(1)} %get-tuple-element.51), channel_id=1, source_target_pairs={{16,0},{20,4},{24,8},{28,12},{0,16},{4,20},{8,24},{12,28},{17,1},{... | collective-permute-start | bytes 393224 | tf_op jit(solution)/shard_map/ppermute | solution.py:112
  37.2 7.5 %collective-permute-start.6 = (bf16[4,128,128]{2,1,0:T(8,128)(2,1)S(1)}, bf16[4,128,128]{2,1,0:T(8,128)(2,1)S(1)}, u32[]{:S(2)}, u32[]{:S(2)}) collective-permute-start(bf16[4,128,128]{2,1,0:T(8,128)(2,1)S(1)} %get-tuple-element.52), channel_id=1, source_target_pairs={{24,0},{28,4},{16,8},{20,12},{8,16},{12,20},{0,24},{4,28},{25,1},{... | collective-permute-start | bytes 393224 | tf_op jit(solution)/shard_map/ppermute | solution.py:112
  44.7 1.6 %copy-start.2 = (bf16[4,128,128]{2,1,0:T(8,128)(2,1)}, bf16[4,128,128]{2,1,0:T(8,128)(2,1)S(1)}, u32[]{:S(2)}) copy-start(bf16[4,128,128]{2,1,0:T(8,128)(2,1)S(1)} %collective-permute-done.6.refs_3_.refs_7_) | copy-start | bytes 393220
  46.3 17.1 %collective-permute-start.11 = (f32[256,512]{1,0:T(8,128)}, f32[256,512]{1,0:T(8,128)}, u32[]{:S(2)}, u32[]{:S(2)}) collective-permute-start(f32[256,512]{1,0:T(8,128)} %get-tuple-element.64), channel_id=1, source_target_pairs={{4,0},{0,4},{12,8},{8,12},{20,16},{16,20},{28,24},{24,28},{5,1},{1... | collective-permute-start | bytes 1572872 | tf_op jit(solution)/shard_map/ppermute | solution.py:125
  51.3 11.2 %all-to-all-start.1 = ((bf16[4,400,128]{2,1,0:T(8,128)(2,1)}), bf16[4,400,128]{2,1,0:T(8,128)(2,1)S(1)}, u32[]{:S(2)}, u32[]{:S(2)}) async-start(bf16[4,400,128]{2,1,0:T(8,128)(2,1)} %shard_map.141), calls=%async_computation.1 | async-start | bytes 819200 | tf_op jit(solution)/shard_map/all_to_all | solution.py:118
  54.8 0.9 %copy-start.3 = (bf16[4,128,128]{2,1,0:T(8,128)(2,1)S(1)}, bf16[4,128,128]{2,1,0:T(8,128)(2,1)}, u32[]{:S(2)}) copy-start(bf16[4,128,128]{2,1,0:T(8,128)(2,1)} %copy-done.2) | copy-start | bytes 393220
  55.7 0.9 %copy-start.7 = (bf16[4,128,128]{2,1,0:T(8,128)(2,1)S(1)}, bf16[4,128,128]{2,1,0:T(8,128)(2,1)}, u32[]{:S(2)}) copy-start(bf16[4,128,128]{2,1,0:T(8,128)(2,1)} %copy-done.6) | copy-start | bytes 393220
  57.9 7.9 %collective-permute-start.12 = (bf16[32,2048]{1,0:T(8,128)(2,1)}, bf16[32,2048]{1,0:T(8,128)(2,1)S(1)}, u32[]{:S(2)}, u32[]{:S(2)}) collective-permute-start(bf16[32,2048]{1,0:T(8,128)(2,1)} %get-tuple-element.66), channel_id=1, source_target_pairs={{1,0},{0,1},{3,2},{2,3},{5,4},{4,5},{7,6},{6,7},{9,8},{8,9},{11,10... | collective-permute-start | bytes 393224 | tf_op jit(solution)/shard_map/ppermute | solution.py:505
  57.9 13.1 %collective-permute-start.13 = (bf16[32,2048]{1,0:T(8,128)(2,1)}, bf16[32,2048]{1,0:T(8,128)(2,1)S(1)}, u32[]{:S(2)}, u32[]{:S(2)}) collective-permute-start(bf16[32,2048]{1,0:T(8,128)(2,1)} %get-tuple-element.67), channel_id=1, source_target_pairs={{2,0},{3,1},{0,2},{1,3},{6,4},{7,5},{4,6},{5,7},{10,8},{11,9},{8,1... | collective-permute-start | bytes 393224 | tf_op jit(solution)/shard_map/ppermute | solution.py:505
  60.0 11.0 %collective-permute-start.14 = (bf16[32,2048]{1,0:T(8,128)(2,1)}, bf16[32,2048]{1,0:T(8,128)(2,1)S(1)}, u32[]{:S(2)}, u32[]{:S(2)}) collective-permute-start(bf16[32,2048]{1,0:T(8,128)(2,1)} %get-tuple-element.68), channel_id=1, source_target_pairs={{3,0},{2,1},{1,2},{0,3},{7,4},{6,5},{5,6},{4,7},{11,8},{10,9},{9,1... | collective-permute-start | bytes 393224 | tf_op jit(solution)/shard_map/ppermute | solution.py:505

commit v9 on v8

--- a/solution.py
+++ b/solution.py
@@ -542,8 +542,8 @@
     )(place, mate, *links, kept)
     mixed = plan.exchange(mixed)
     back = call(
-        partial(state_cotangent_kernel, plan), arr(F32, hv, DV, DK), flops=500_000_000
-    )(kept, *after(cot, states))
+        partial(state_cotangent_kernel, plan), arr(F32, hv, DV, DK), flops=30_000_000_000
+    )(kept, *after(cot, mixed[1]))
     backs = [back] + [plan.from_mate(back, d) for d in range(1, s)]
 
     projected = call(
@@ -565,8 +565,7 @@
             vmem(F32, n, DV, DK),
         ],
         flops=6_000_000_000,
-    )(doc_offsets, place, mate, *links, *backs, got, *cot, kept, states)
-    grads = plan.exchange_at_once(grads)
+    )(doc_offsets, place, mate, *links, *backs, got, *cot, kept, after(states, projected[1]))
 
     shares = call(
         partial(weight_kernel, plan),
@@ -575,6 +574,7 @@
         scratch=[vmem(BF16, hv, hv, DV, tok)],
         flops=1_000_000_000,
     )(place, mate, *cot, *mixed)
+    grads = plan.exchange_at_once(after(grads, shares[0]))
     weight_grad = shares[0]
     for d in range(1, s):
         weight_grad = weight_grad + plan.from_mate(shares[d], d)

time: 72.2 us -> 64.4 us (0.89)
  waiting for transfers between devices: 24.4 us -> 19.8 us
  local copies, waits for them, and re-layouts: 2.48 us -> 0.67 us
  Pallas kernels: 16.8 us -> 15.3 us
  starting transfers between devices: 24.6 us -> 25.9 us
  other arithmetic: 2.67 us -> 1.63 us
    ppermute x6, waiting for transfers between devices: 12.7 us -> 6.39 us  [exchange(): moved.append(lax.ppermute(pieces[d], 'ctx', pairs))]
    all_to_all x2, waiting for transfers between devices: 2.65 us -> 5.64 us  [exchange_at_once(): lax.all_to_all(pieces, 'ctx', split_axis=0, concat_axis=0, axis_index_gro...]
    ppermute x6, starting transfers between devices: 7.11 us -> 9.13 us  [exchange(): moved.append(lax.ppermute(pieces[d], 'ctx', pairs))]
    unnamed x16 -> x8, local copies, waits for them, and re-layouts: 2.48 us -> 0.67 us
    pallas_call x9, Pallas kernels: 16.8 us -> 15.3 us  [run(): pl.pallas_call(kernel, out_shape=outs, in_specs=[spec(i) for i in range(l...]
    ppermute x6, waiting for transfers between devices: 8.96 us -> 7.81 us  [across_heads(): lax.ppermute(pieces[d], 'head', Ring(parts).pairs(d))]
    add x1, other arithmetic: 1.91 us -> 0.87 us  [per_device(): weight_grad = weight_grad + plan.from_mate(shares[d], d)]
    ppermute x6, starting transfers between devices: 8.77 us -> 7.94 us  [across_heads(): lax.ppermute(pieces[d], 'head', Ring(parts).pairs(d))]
  transfers between devices with their start and end apart: 17 -> 17, of which waited for: 10 -> 8; matrix products, arithmetic and copies ran while one was open for 3% -> 1% of each run, Pallas kernels for 20% -> 21%
where the time goes in v9:
time: 64.4 us; the launch traced here: 64.1 us
  starting transfers between devices  25.9 us (40%)
  waiting for transfers between devices  19.8 us (31%)
  Pallas kernels  15.3 us (24%)
  other arithmetic  1.63 us (3%)
  between operations  0.76 us (1%)
  local copies, waits for them, and re-layouts  0.67 us (1%)
    pallas_call x9, Pallas kernels, run(): pl.pallas_call(kernel, out_shape=outs, in_specs=[spec(i) for i in range(l...  15.3 us
    ppermute x6, starting transfers between devices, exchange(): moved.append(lax.ppermute(pieces[d], 'ctx', pairs))  9.13 us
    all_to_all x2, starting transfers between devices, exchange_at_once(): lax.all_to_all(pieces, 'ctx', split_axis=0, concat_axis=0, axis_index_gro...  8.62 us
    ppermute x6, starting transfers between devices, across_heads(): lax.ppermute(pieces[d], 'head', Ring(parts).pairs(d))  7.94 us
    ppermute x6, waiting for transfers between devices, across_heads(): lax.ppermute(pieces[d], 'head', Ring(parts).pairs(d))  7.81 us
    ppermute x6, waiting for transfers between devices, exchange(): moved.append(lax.ppermute(pieces[d], 'ctx', pairs))  6.39 us
    all_to_all x2, waiting for transfers between devices, exchange_at_once(): lax.all_to_all(pieces, 'ctx', split_axis=0, concat_axis=0, axis_index_gro...  5.64 us
  transfers between devices with their start and end apart: 17, of which 8 were waited for; matrix products, arithmetic and copies ran while one was open for 1% of the time, Pallas kernels for 21%

profile of v9, /device:TPU:0, one launch (start us, length us, event | category | flops | bytes accessed | tf_op | source)
XLA Modules:
  0.0 64.1 jit_solution(15905728280959140727)
XLA Ops:
  0.6 1.9 %shard_map.135 = bf16[4,400,128]{2,1,0:T(8,128)(2,1)} custom-call(bf16[128,256]{1,0:T(8,128)(2,1)} %q_ref.1, bf16[128,256]{1,0:T(8,128)(2,1)} %k_ref.1, bf16[128,512]{1,0:T(8,128)(2,1)} %v_ref.1, f32[4,128]{1,0:T(4,128)} %rate_ref.1, f32[4,128]{1,0:T(4,128)} %decay_ref.1), custom_call_target="tpu_custom_call" | custom-call | tf_op jit(solution)/shard_map/pallas_call | solution.py:60
  2.5 5.2 %all-to-all-start = ((bf16[4,400,128]{2,1,0:T(8,128)(2,1)}), bf16[4,400,128]{2,1,0:T(8,128)(2,1)S(1)}, u32[]{:S(2)}, u32[]{:S(2)}) async-start(bf16[4,400,128]{2,1,0:T(8,128)(2,1)} %shard_map.135), calls=%async_computation | async-start | bytes 819200 | tf_op jit(solution)/shard_map/all_to_all | solution.py:118
  7.6 3.6 %collective-permute-start.3 = (bf16[32,2048]{1,0:T(8,128)(2,1)}, bf16[32,2048]{1,0:T(8,128)(2,1)S(1)}, u32[]{:S(2)}, u32[]{:S(2)}) collective-permute-start(bf16[32,2048]{1,0:T(8,128)(2,1)} %refs_0_), channel_id=1, source_target_pairs={{3,0},{2,1},{1,2},{0,3},{7,4},{6,5},{5,6},{4,7},{11,8},{10,9},{9,1... | collective-permute-start | bytes 393224 | tf_op jit(solution)/shard_map/ppermute | solution.py:505
  11.3 0.8 %collective-permute-start.1 = (bf16[32,2048]{1,0:T(8,128)(2,1)}, bf16[32,2048]{1,0:T(8,128)(2,1)S(1)}, u32[]{:S(2)}, u32[]{:S(2)}) collective-permute-start(bf16[32,2048]{1,0:T(8,128)(2,1)} %refs_0_), channel_id=1, source_target_pairs={{1,0},{0,1},{3,2},{2,3},{5,4},{4,5},{7,6},{6,7},{9,8},{8,9},{11,10... | collective-permute-start | bytes 393224 | tf_op jit(solution)/shard_map/ppermute | solution.py:505
  12.0 2.4 %all-to-all-done.refs_0_.refs_4_ = bf16[4,400,128]{2,1,0:T(8,128)(2,1)S(1)} async-done(((bf16[4,400,128]{2,1,0:T(8,128)(2,1)}), bf16[4,400,128]{2,1,0:T(8,128)(2,1)S(1)}, u32[]{:S(2)}, u32[]{:S(2)}) %all-to-all-start) | async-done | bytes 409632 | tf_op jit(solution)/shard_map/all_to_all | solution.py:118
  14.4 0.7 %copy-done.2 = s32[5]{0:T(128)S(1)} copy-done((s32[5]{0:T(128)S(1)}, s32[5]{0:T(128)}, u32[]{:S(2)}) %copy-start.2) | copy-done | bytes 44
  15.1 3.9 %shard_map.136 = (f32[4,2,128,128]{3,2,1,0:T(8,128)S(1)}, f32[4,7,128,128]{3,2,1,0:T(8,128)S(1)}) custom-call(s32[5]{0:T(128)S(1)} %copy-done.2, s32[1]{0:T(128)} %bitcast.1.place_ref, s32[1]{0:T(128)} %bitcast.2.mate_ref, bf16[4,400,128]{2,1,0:T(8,128)(2,1)S(1)} %all-to-all-done.refs_0_.refs_4_), custom_call_target="tpu_custom_call" | custom-call | flops 20000000000 | tf_op jit(solution)/shard_map/pallas_call | solution.py:60
  19.1 3.3 %collective-permute-done.2.refs_2_ = bf16[32,2048]{1,0:T(8,128)(2,1)S(1)} collective-permute-done((bf16[32,2048]{1,0:T(8,128)(2,1)}, bf16[32,2048]{1,0:T(8,128)(2,1)S(1)}, u32[]{:S(2)}, u32[]{:S(2)}) %collective-permute-start.2) | collective-permute-done | bytes 131104 | tf_op jit(solution)/shard_map/ppermute | solution.py:505
  22.4 0.8 %shard_map.137 = (bf16[768,128]{1,0:T(8,128)(2,1)S(1)}, bf16[768,128]{1,0:T(8,128)(2,1)S(1)}, bf16[768,128]{1,0:T(8,128)(2,1)S(1)}, bf16[768,128]{1,0:T(8,128)(2,1)S(1)}) custom-call(s32[1]{0:T(128)} %bitcast.head_ref, s32[1]{0:T(128)} %bitcast.1.place_ref, bf16[32,2048]{1,0:T(8,128)(2,1)S(1)} %copy-done.1, ...), custom_call_target="tpu_custom_call" | custom-call | flops 30000001024 | tf_op jit(solution)/shard_map/pallas_call | solution.py:60
  23.2 1.7 %collective-permute-start.7 = (bf16[768,128]{1,0:T(8,128)(2,1)S(1)}, bf16[768,128]{1,0:T(8,128)(2,1)S(1)}, u32[]{:S(2)}, u32[]{:S(2)}) collective-permute-start(bf16[768,128]{1,0:T(8,128)(2,1)S(1)} %get-tuple-element.56), channel_id=1, source_target_pairs={{8,0},{12,4},{0,8},{4,12},{24,16},{28,20},{16,24},{20,28},{9,1},{1... | collective-permute-start | bytes 589832 | tf_op jit(solution)/shard_map/ppermute | solution.py:112
  24.9 1.5 %collective-permute-start.8 = (bf16[768,128]{1,0:T(8,128)(2,1)S(1)}, bf16[768,128]{1,0:T(8,128)(2,1)S(1)}, u32[]{:S(2)}, u32[]{:S(2)}) collective-permute-start(bf16[768,128]{1,0:T(8,128)(2,1)S(1)} %get-tuple-element.57), channel_id=1, source_target_pairs={{16,0},{20,4},{24,8},{28,12},{0,16},{4,20},{8,24},{12,28},{17,1},{... | collective-permute-start | bytes 589832 | tf_op jit(solution)/shard_map/ppermute | solution.py:112
  26.4 0.4 collective-permute-start.9
  26.7 1.3 %shard_map.138 = (f32[4,128,128]{2,1,0:T(8,128)S(1)}, bf16[4,128,128]{2,1,0:T(8,128)(2,1)S(1)}, bf16[4,128,128]{2,1,0:T(8,128)(2,1)S(1)}, bf16[4,128,128]{2,1,0:T(8,128)(2,1)S(1)}, bf16[4,128,128]{2,1,0:T(8,128)(2,1)S(1)}) custom-call(s32[1]{0:T(128)} %bitcast.1.place_ref, s32[1]{0:T(128)} %bitcast.2.mate_ref, ...), custom_call_target="tpu_custom_call" | custom-call | flops 2500000000 | tf_op jit(solution)/shard_map/pallas_call | solution.py:60
  28.1 1.7 %collective-permute-start.4 = (bf16[4,128,128]{2,1,0:T(8,128)(2,1)S(1)}, bf16[4,128,128]{2,1,0:T(8,128)(2,1)S(1)}, u32[]{:S(2)}, u32[]{:S(2)}) collective-permute-start(bf16[4,128,128]{2,1,0:T(8,128)(2,1)S(1)} %get-tuple-element.52), channel_id=1, source_target_pairs={{8,0},{12,4},{0,8},{4,12},{24,16},{28,20},{16,24},{20,28},{9,1},{1... | collective-permute-start | bytes 393224 | tf_op jit(solution)/shard_map/ppermute | solution.py:112
  29.8 1.5 %collective-permute-start.5 = (bf16[4,128,128]{2,1,0:T(8,128)(2,1)S(1)}, bf16[4,128,128]{2,1,0:T(8,128)(2,1)S(1)}, u32[]{:S(2)}, u32[]{:S(2)}) collective-permute-start(bf16[4,128,128]{2,1,0:T(8,128)(2,1)S(1)} %get-tuple-element.53), channel_id=1, source_target_pairs={{16,0},{20,4},{24,8},{28,12},{0,16},{4,20},{8,24},{12,28},{17,1},{... | collective-permute-start | bytes 393224 | tf_op jit(solution)/shard_map/ppermute | solution.py:112
  31.2 2.4 %collective-permute-start.6 = (bf16[4,128,128]{2,1,0:T(8,128)(2,1)S(1)}, bf16[4,128,128]{2,1,0:T(8,128)(2,1)S(1)}, u32[]{:S(2)}, u32[]{:S(2)}) collective-permute-start(bf16[4,128,128]{2,1,0:T(8,128)(2,1)S(1)} %get-tuple-element.54), channel_id=1, source_target_pairs={{24,0},{28,4},{16,8},{20,12},{8,16},{12,20},{0,24},{4,28},{25,1},{... | collective-permute-start | bytes 393224 | tf_op jit(solution)/shard_map/ppermute | solution.py:112
  33.6 2.9 %collective-permute-done.8.refs_2_.refs_7_ = bf16[768,128]{1,0:T(8,128)(2,1)S(1)} collective-permute-done((bf16[768,128]{1,0:T(8,128)(2,1)S(1)}, bf16[768,128]{1,0:T(8,128)(2,1)S(1)}, u32[]{:S(2)}, u32[]{:S(2)}) %collective-permute-start.8) | collective-permute-done | bytes 196640 | tf_op jit(solution)/shard_map/ppermute | solution.py:112
  36.5 1.1 %collective-permute-done.4.refs_1_.refs_5_ = bf16[4,128,128]{2,1,0:T(8,128)(2,1)S(1)} collective-permute-done((bf16[4,128,128]{2,1,0:T(8,128)(2,1)S(1)}, bf16[4,128,128]{2,1,0:T(8,128)(2,1)S(1)}, u32[]{:S(2)}, u32[]{:S(2)}) %collective-permute-start.4) | collective-permute-done | bytes 131104 | tf_op jit(solution)/shard_map/ppermute | solution.py:112
  37.9 2.4 %collective-permute-done.5.refs_2_.refs_6_ = bf16[4,128,128]{2,1,0:T(8,128)(2,1)S(1)} collective-permute-done((bf16[4,128,128]{2,1,0:T(8,128)(2,1)S(1)}, bf16[4,128,128]{2,1,0:T(8,128)(2,1)S(1)}, u32[]{:S(2)}, u32[]{:S(2)}) %collective-permute-start.5) | collective-permute-done | bytes 131104 | tf_op jit(solution)/shard_map/ppermute | solution.py:112
  40.4 0.5 shard_map.139
  40.9 0.7 %shard_map.142 = (f32[256,512]{1,0:T(8,128)S(1)}, f32[256,512]{1,0:T(8,128)S(1)}) custom-call(s32[1]{0:T(128)} %bitcast.1.place_ref, s32[1]{0:T(128)} %bitcast.2.mate_ref, bf16[768,128]{1,0:T(8,128)(2,1)S(1)} %get-tuple-element.59.refs_0_.refs_5_, bf16[768,128]{1,0:T(8,128)(2,1)S(1)} %collective-permute-done.7.refs_1_.refs_6_, ...), custom_call_target="tpu_custom_call" | custom-call | flops 1000000000 | tf_op jit(solution)/shard_map/pallas_call | solution.py:60
  41.8 5.1 %shard_map.141 = bf16[4,400,128]{2,1,0:T(8,128)(2,1)} custom-call(s32[5]{0:T(128)S(1)} %copy-done.3, s32[1]{0:T(128)} %bitcast.1.place_ref, s32[1]{0:T(128)} %bitcast.2.mate_ref, f32[4,2,128,128]{3,2,1,0:T(8,128)S(1)} %get-tuple-element.42.refs_0_, f32[4,2,128,128]{3,2,1,0:T(8,128)S(1)} %collective-permute-done.refs_1_, ...), custom_call_target="tpu_custom_call" | custom-call | flops 6000000000 | tf_op jit(solution)/shard_map/pallas_call | solution.py:60
  46.8 3.5 %all-to-all-start.1 = ((bf16[4,400,128]{2,1,0:T(8,128)(2,1)}), bf16[4,400,128]{2,1,0:T(8,128)(2,1)S(1)}, u32[]{:S(2)}, u32[]{:S(2)}) async-start(bf16[4,400,128]{2,1,0:T(8,128)(2,1)} %shard_map.141), calls=%async_computation.1 | async-start | bytes 819200 | tf_op jit(solution)/shard_map/all_to_all | solution.py:118
  50.3 0.6 collective-permute-start.13
  50.9 1.4 %collective-permute-start.14 = (bf16[32,2048]{1,0:T(8,128)(2,1)S(1)}, bf16[32,2048]{1,0:T(8,128)(2,1)S(1)}, u32[]{:S(2)}, u32[]{:S(2)}) collective-permute-start(bf16[32,2048]{1,0:T(8,128)(2,1)S(1)} %get-tuple-element.72), channel_id=1, source_target_pairs={{3,0},{2,1},{1,2},{0,3},{7,4},{6,5},{5,6},{4,7},{11,8},{10,9},{9,1... | collective-permute-start | bytes 393224 | tf_op jit(solution)/shard_map/ppermute | solution.py:505
  52.2 1.6 %collective-permute-start.12 = (bf16[32,2048]{1,0:T(8,128)(2,1)S(1)}, bf16[32,2048]{1,0:T(8,128)(2,1)S(1)}, u32[]{:S(2)}, u32[]{:S(2)}) collective-permute-start(bf16[32,2048]{1,0:T(8,128)(2,1)S(1)} %get-tuple-element.64), channel_id=1, source_target_pairs={{1,0},{0,1},{3,2},{2,3},{5,4},{4,5},{7,6},{6,7},{9,8},{8,9},{11,10... | collective-permute-start | bytes 393224 | tf_op jit(solution)/shard_map/ppermute | solution.py:505
  53.9 0.9 %add.18 = f32[256,512]{1,0:T(8,128)} add(f32[256,512]{1,0:T(8,128)S(1)} %get-tuple-element.66, f32[256,512]{1,0:T(8,128)S(1)} %collective-permute-done.11) | non-fusion elementwise | flops 131072 | bytes 1572864 | tf_op jit(solution)/shard_map/add | solution.py:580
  54.7 3.2 %all-to-all-done.1.in_ref = bf16[4,400,128]{2,1,0:T(8,128)(2,1)S(1)} async-done(((bf16[4,400,128]{2,1,0:T(8,128)(2,1)}), bf16[4,400,128]{2,1,0:T(8,128)(2,1)S(1)}, u32[]{:S(2)}, u32[]{:S(2)}) %all-to-all-start.1) | async-done | bytes 409632 | tf_op jit(solution)/shard_map/all_to_all | solution.py:118
  58.0 0.8 %shard_map.143 = (f32[128,256]{1,0:T(8,128)}, f32[128,256]{1,0:T(8,128)}, f32[128,512]{1,0:T(8,128)}, f32[4,128]{1,0:T(4,128)}, f32[4,128]{1,0:T(4,128)}) custom-call(bf16[4,400,128]{2,1,0:T(8,128)(2,1)S(1)} %all-to-all-done.1.in_ref), custom_call_target="tpu_custom_call" | custom-call | flops 1000000000 | tf_op jit(solution)/shard_map/pallas_call | solution.py:60
  58.8 3.1 %collective-permute-done.13 = bf16[32,2048]{1,0:T(8,128)(2,1)S(1)} collective-permute-done((bf16[32,2048]{1,0:T(8,128)(2,1)S(1)}, bf16[32,2048]{1,0:T(8,128)(2,1)S(1)}, u32[]{:S(2)}, u32[]{:S(2)}) %collective-permute-start.13) | collective-permute-done | bytes 131104 | tf_op jit(solution)/shard_map/ppermute | solution.py:505
  62.0 1.4 %collective-permute-done.12 = bf16[32,2048]{1,0:T(8,128)(2,1)S(1)} collective-permute-done((bf16[32,2048]{1,0:T(8,128)(2,1)S(1)}, bf16[32,2048]{1,0:T(8,128)(2,1)S(1)}, u32[]{:S(2)}, u32[]{:S(2)}) %collective-permute-start.12) | collective-permute-done | bytes 131104 | tf_op jit(solution)/shard_map/ppermute | solution.py:505
  63.3 0.8 %convert_add_fusion = f32[32,2048]{1,0:T(8,128)} fusion(bf16[32,2048]{1,0:T(8,128)(2,1)S(1)} %collective-permute-done.14, bf16[32,2048]{1,0:T(8,128)(2,1)S(1)} %collective-permute-done.13, f32[32,2048]{1,0:T(8,128)S(1)} %get-tuple-element.70, bf16[32,2048]{1,0:T(8,128)(2,1)S(1)} %collective-permute-done.12), kind=kLoop, calls=%fused_computation | loop fusion | flops 393216 | bytes 917504 | tf_op jit(solution)/shard_map/add | solution.py:596
  (21 shorter events, 0.5 us)
Async XLA Ops:
  2.5 12.0 %all-to-all-start = ((bf16[4,400,128]{2,1,0:T(8,128)(2,1)}), bf16[4,400,128]{2,1,0:T(8,128)(2,1)S(1)}, u32[]{:S(2)}, u32[]{:S(2)}) async-start(bf16[4,400,128]{2,1,0:T(8,128)(2,1)} %shard_map.135), calls=%async_computation | async-start | bytes 819200 | tf_op jit(solution)/shard_map/all_to_all | solution.py:118
  7.6 11.4 %collective-permute-start.3 = (bf16[32,2048]{1,0:T(8,128)(2,1)}, bf16[32,2048]{1,0:T(8,128)(2,1)S(1)}, u32[]{:S(2)}, u32[]{:S(2)}) collective-permute-start(bf16[32,2048]{1,0:T(8,128)(2,1)} %refs_0_), channel_id=1, source_target_pairs={{3,0},{2,1},{1,2},{0,3},{7,4},{6,5},{5,6},{4,7},{11,8},{10,9},{9,1... | collective-permute-start | bytes 393224 | tf_op jit(solution)/shard_map/ppermute | solution.py:505
  11.2 11.1 %collective-permute-start.2 = (bf16[32,2048]{1,0:T(8,128)(2,1)}, bf16[32,2048]{1,0:T(8,128)(2,1)S(1)}, u32[]{:S(2)}, u32[]{:S(2)}) collective-permute-start(bf16[32,2048]{1,0:T(8,128)(2,1)} %refs_0_), channel_id=1, source_target_pairs={{2,0},{3,1},{0,2},{1,3},{6,4},{7,5},{4,6},{5,7},{10,8},{11,9},{8,1... | collective-permute-start | bytes 393224 | tf_op jit(solution)/shard_map/ppermute | solution.py:505
  11.3 11.1 %collective-permute-start.1 = (bf16[32,2048]{1,0:T(8,128)(2,1)}, bf16[32,2048]{1,0:T(8,128)(2,1)S(1)}, u32[]{:S(2)}, u32[]{:S(2)}) collective-permute-start(bf16[32,2048]{1,0:T(8,128)(2,1)} %refs_0_), channel_id=1, source_target_pairs={{1,0},{0,1},{3,2},{2,3},{5,4},{4,5},{7,6},{6,7},{9,8},{8,9},{11,10... | collective-permute-start | bytes 393224 | tf_op jit(solution)/shard_map/ppermute | solution.py:505
  14.4 0.7 %copy-start.2 = (s32[5]{0:T(128)S(1)}, s32[5]{0:T(128)}, u32[]{:S(2)}) copy-start(s32[5]{0:T(128)} %off_ref.3) | copy-start | bytes 64
  15.1 7.3 %copy-start = (bf16[512,2048]{1,0:T(8,128)(2,1)S(1)}, bf16[512,2048]{1,0:T(8,128)(2,1)}, u32[]{:S(2)}) copy-start(bf16[512,2048]{1,0:T(8,128)(2,1)} %refs_4_.3) | copy-start | bytes 6291460
  15.1 7.3 %copy-start.1 = (bf16[32,2048]{1,0:T(8,128)(2,1)S(1)}, bf16[32,2048]{1,0:T(8,128)(2,1)}, u32[]{:S(2)}) copy-start(bf16[32,2048]{1,0:T(8,128)(2,1)} %refs_0_) | copy-start | bytes 393220
  19.0 7.8 %collective-permute-start = (f32[4,2,128,128]{3,2,1,0:T(8,128)S(1)}, f32[4,2,128,128]{3,2,1,0:T(8,128)S(1)}, u32[]{:S(2)}, u32[]{:S(2)}) collective-permute-start(f32[4,2,128,128]{3,2,1,0:T(8,128)S(1)} %get-tuple-element.42.refs_0_), channel_id=1, source_target_pairs={{4,0},{0,4},{12,8},{8,12},{20,16},{16,20},{28,24},{24,28},{5,1},{1... | collective-permute-start | bytes 1572872 | tf_op jit(solution)/shard_map/ppermute | solution.py:125
  23.2 8.1 %collective-permute-start.7 = (bf16[768,128]{1,0:T(8,128)(2,1)S(1)}, bf16[768,128]{1,0:T(8,128)(2,1)S(1)}, u32[]{:S(2)}, u32[]{:S(2)}) collective-permute-start(bf16[768,128]{1,0:T(8,128)(2,1)S(1)} %get-tuple-element.56), channel_id=1, source_target_pairs={{8,0},{12,4},{0,8},{4,12},{24,16},{28,20},{16,24},{20,28},{9,1},{1... | collective-permute-start | bytes 589832 | tf_op jit(solution)/shard_map/ppermute | solution.py:112
  24.9 11.6 %collective-permute-start.8 = (bf16[768,128]{1,0:T(8,128)(2,1)S(1)}, bf16[768,128]{1,0:T(8,128)(2,1)S(1)}, u32[]{:S(2)}, u32[]{:S(2)}) collective-permute-start(bf16[768,128]{1,0:T(8,128)(2,1)S(1)} %get-tuple-element.57), channel_id=1, source_target_pairs={{16,0},{20,4},{24,8},{28,12},{0,16},{4,20},{8,24},{12,28},{17,1},{... | collective-permute-start | bytes 589832 | tf_op jit(solution)/shard_map/ppermute | solution.py:112
  26.4 10.2 %collective-permute-start.9 = (bf16[768,128]{1,0:T(8,128)(2,1)S(1)}, bf16[768,128]{1,0:T(8,128)(2,1)S(1)}, u32[]{:S(2)}, u32[]{:S(2)}) collective-permute-start(bf16[768,128]{1,0:T(8,128)(2,1)S(1)} %get-tuple-element.58), channel_id=1, source_target_pairs={{24,0},{28,4},{16,8},{20,12},{8,16},{12,20},{0,24},{4,28},{25,1},{... | collective-permute-start | bytes 589832 | tf_op jit(solution)/shard_map/ppermute | solution.py:112
  28.1 9.5 %collective-permute-start.4 = (bf16[4,128,128]{2,1,0:T(8,128)(2,1)S(1)}, bf16[4,128,128]{2,1,0:T(8,128)(2,1)S(1)}, u32[]{:S(2)}, u32[]{:S(2)}) collective-permute-start(bf16[4,128,128]{2,1,0:T(8,128)(2,1)S(1)} %get-tuple-element.52), channel_id=1, source_target_pairs={{8,0},{12,4},{0,8},{4,12},{24,16},{28,20},{16,24},{20,28},{9,1},{1... | collective-permute-start | bytes 393224 | tf_op jit(solution)/shard_map/ppermute | solution.py:112
  29.8 10.6 %collective-permute-start.5 = (bf16[4,128,128]{2,1,0:T(8,128)(2,1)S(1)}, bf16[4,128,128]{2,1,0:T(8,128)(2,1)S(1)}, u32[]{:S(2)}, u32[]{:S(2)}) collective-permute-start(bf16[4,128,128]{2,1,0:T(8,128)(2,1)S(1)} %get-tuple-element.53), channel_id=1, source_target_pairs={{16,0},{20,4},{24,8},{28,12},{0,16},{4,20},{8,24},{12,28},{17,1},{... | collective-permute-start | bytes 393224 | tf_op jit(solution)/shard_map/ppermute | solution.py:112
  31.2 9.1 %collective-permute-start.6 = (bf16[4,128,128]{2,1,0:T(8,128)(2,1)S(1)}, bf16[4,128,128]{2,1,0:T(8,128)(2,1)S(1)}, u32[]{:S(2)}, u32[]{:S(2)}) collective-permute-start(bf16[4,128,128]{2,1,0:T(8,128)(2,1)S(1)} %get-tuple-element.54), channel_id=1, source_target_pairs={{24,0},{28,4},{16,8},{20,12},{8,16},{12,20},{0,24},{4,28},{25,1},{... | collective-permute-start | bytes 393224 | tf_op jit(solution)/shard_map/ppermute | solution.py:112
  37.9 3.9 %collective-permute-start.10 = (f32[4,128,128]{2,1,0:T(8,128)S(1)}, f32[4,128,128]{2,1,0:T(8,128)S(1)}, u32[]{:S(2)}, u32[]{:S(2)}) collective-permute-start(f32[4,128,128]{2,1,0:T(8,128)S(1)} %shard_map.140.refs_2_), channel_id=1, source_target_pairs={{4,0},{0,4},{12,8},{8,12},{20,16},{16,20},{28,24},{24,28},{5,1},{1... | collective-permute-start | bytes 786440 | tf_op jit(solution)/shard_map/ppermute | solution.py:125
  40.9 0.9 %copy-start.3 = (s32[5]{0:T(128)S(1)}, s32[5]{0:T(128)}, u32[]{:S(2)}) copy-start(s32[5]{0:T(128)} %off_ref.3) | copy-start | bytes 64
  41.7 12.2 %collective-permute-start.11 = (f32[256,512]{1,0:T(8,128)S(1)}, f32[256,512]{1,0:T(8,128)S(1)}, u32[]{:S(2)}, u32[]{:S(2)}) collective-permute-start(f32[256,512]{1,0:T(8,128)S(1)} %get-tuple-element.69), channel_id=1, source_target_pairs={{4,0},{0,4},{12,8},{8,12},{20,16},{16,20},{28,24},{24,28},{5,1},{1... | collective-permute-start | bytes 1572872 | tf_op jit(solution)/shard_map/ppermute | solution.py:125
  46.8 11.1 %all-to-all-start.1 = ((bf16[4,400,128]{2,1,0:T(8,128)(2,1)}), bf16[4,400,128]{2,1,0:T(8,128)(2,1)S(1)}, u32[]{:S(2)}, u32[]{:S(2)}) async-start(bf16[4,400,128]{2,1,0:T(8,128)(2,1)} %shard_map.141), calls=%async_computation.1 | async-start | bytes 819200 | tf_op jit(solution)/shard_map/all_to_all | solution.py:118
  50.3 11.6 %collective-permute-start.13 = (bf16[32,2048]{1,0:T(8,128)(2,1)S(1)}, bf16[32,2048]{1,0:T(8,128)(2,1)S(1)}, u32[]{:S(2)}, u32[]{:S(2)}) collective-permute-start(bf16[32,2048]{1,0:T(8,128)(2,1)S(1)} %get-tuple-element.71), channel_id=1, source_target_pairs={{2,0},{3,1},{0,2},{1,3},{6,4},{7,5},{4,6},{5,7},{10,8},{11,9},{8,1... | collective-permute-start | bytes 393224 | tf_op jit(solution)/shard_map/ppermute | solution.py:505
  50.9 11.1 %collective-permute-start.14 = (bf16[32,2048]{1,0:T(8,128)(2,1)S(1)}, bf16[32,2048]{1,0:T(8,128)(2,1)S(1)}, u32[]{:S(2)}, u32[]{:S(2)}) collective-permute-start(bf16[32,2048]{1,0:T(8,128)(2,1)S(1)} %get-tuple-element.72), channel_id=1, source_target_pairs={{3,0},{2,1},{1,2},{0,3},{7,4},{6,5},{5,6},{4,7},{11,8},{10,9},{9,1... | collective-permute-start | bytes 393224 | tf_op jit(solution)/shard_map/ppermute | solution.py:505
  52.2 11.1 %collective-permute-start.12 = (bf16[32,2048]{1,0:T(8,128)(2,1)S(1)}, bf16[32,2048]{1,0:T(8,128)(2,1)S(1)}, u32[]{:S(2)}, u32[]{:S(2)}) collective-permute-start(bf16[32,2048]{1,0:T(8,128)(2,1)S(1)} %get-tuple-element.64), channel_id=1, source_target_pairs={{1,0},{0,1},{3,2},{2,3},{5,4},{4,5},{7,6},{6,7},{9,8},{8,9},{11,10... | collective-permute-start | bytes 393224 | tf_op jit(solution)/shard_map/ppermute | solution.py:505

commit v10 on v9

--- a/solution.py
+++ b/solution.py
@@ -65,7 +65,7 @@
             scratch_shapes=list(scratch),
             compiler_params=pltpu.CompilerParams(vmem_limit_bytes=scoped),
             cost_estimate=pl.CostEstimate(flops=flops, bytes_accessed=0, transcendentals=0),
-        )(*(x if i in smem else hold(x, space(i)) for i, x in enumerate(args)))
+        )(*(hold(x, space(i)) if i in fetch or i not in smem else x for i, x in enumerate(args)))
 
     return run
 
@@ -112,13 +112,6 @@
             moved.append(lax.ppermute(pieces[d], "ctx", pairs))
         return moved
 
-    def exchange_at_once(self, pieces):
-        s = self.mates
-        groups = [[m * s + b for m in range(self.hv)] for b in range(s)]
-        return lax.all_to_all(
-            pieces, "ctx", split_axis=0, concat_axis=0, axis_index_groups=groups, tiled=True
-        )
-
     def from_mate(self, x, d):
         s = self.mates
         pairs = [(i // s * s + (i + d) % s, i) for i in range(self.n)]
@@ -133,7 +126,8 @@
     return out.astype(BF16)
 
 
-def pack_kernel(plan, q_ref, k_ref, v_ref, rate_ref, decay_ref, out_ref):
+def pack_kernel(plan, place_ref, q_ref, k_ref, v_ref, rate_ref, decay_ref, *refs):
+    outs, out_ref = refs[:-1], refs[-1]
     tok = plan.tok
     for h in range(plan.hv):
         kh = plan.key_head(h)
@@ -143,6 +137,7 @@
         out_ref[h, plan.v_at : plan.aux_at] = turned.astype(BF16)
         rows = [rate_ref[h : h + 1, :], decay_ref[h : h + 1, :]]
         out_ref[h, plan.aux_at :] = aux_rows(rows, tok)
+    hand_out(plan, place_ref[0], out_ref, outs)
 
 
 def hand_out(plan, place, all_ref, outs):
@@ -249,13 +244,8 @@
     return [mate + plan.mates * plan.ring.source(place, d) for d in range(plan.hv)]
 
 
-def in_place_order(plan, place, ref):
-    return [ref.at[plan.ring.source(place, d)] for d in range(plan.hv)]
-
-
 def prepare_kernel(plan, off_ref, place_ref, mate_ref, *refs):
-    in_ref, link_ref, kept_ref = refs
-    in_refs = in_place_order(plan, place_ref[0], in_ref)
+    in_refs, (link_ref, kept_ref) = refs[: plan.hv], refs[plan.hv :]
     tok = plan.tok
     rows, columns = iotas(tok, tok)
     key_rows, key_columns = iotas(DK, DK)
@@ -336,11 +326,11 @@
 
 def backward_kernel(plan, off_ref, place_ref, mate_ref, *refs):
     s, n, tok, hv = plan.mates, plan.n, plan.tok, plan.hv
-    links, backs, in_ref, refs = refs[:s], refs[s : 2 * s], refs[2 * s], refs[2 * s + 1 :]
-    d_refs, (kept_ref, state_ref, out_ref, links_ref, backs_ref, cots_ref) = refs[:hv], refs[hv:]
+    links, backs, refs = refs[:s], refs[s : 2 * s], refs[2 * s :]
+    in_refs, d_refs, kept_ref, state_ref = refs[:hv], refs[hv : 2 * hv], refs[2 * hv], refs[2 * hv + 1]
+    outs, (links_ref, backs_ref, cots_ref) = refs[2 * hv + 2 : -3], refs[-3:]
+    outs = [outs[plan.ring.seen(m, 0)] for m in range(hv)]
     place, mate = place_ref[0], mate_ref[0]
-    in_refs = in_place_order(plan, place, in_ref)
-    outs = in_place_order(plan, place, out_ref)
     lay_out(plan, place, mate, links, links_ref)
     lay_out(plan, place, mate, backs, backs_ref)
     d_state = jnp.zeros((DV, DK), F32)
@@ -467,8 +457,11 @@
         out_ref[...] = total
 
 
-def finish_kernel(plan, in_ref, q_ref, k_ref, v_ref, rate_ref, decay_ref):
+def finish_kernel(plan, place_ref, *refs):
+    pieces, (q_ref, k_ref, v_ref, rate_ref, decay_ref, in_ref) = refs[: plan.hv], refs[plan.hv :]
     tok = plan.tok
+    for d, ref in enumerate(pieces):
+        in_ref[plan.ring.source(place_ref[0], d)] = ref[...]
     for kh in range(plan.hk):
         mine = [h for h in range(plan.hv) if plan.key_head(h) == kh]
         for ref, at in ((q_ref, 0), (k_ref, tok)):
@@ -509,18 +502,21 @@
 
     packed = call(
         partial(pack_kernel, plan),
-        arr(BF16, hv, plan.rows, DK),
-        fetch=range(5),
-    )(queries, key_vectors, value_rows, write_rate, log_decay)
-    got = plan.exchange_at_once(packed)
-    rows = across_heads([after(grad_out, packed)] * parts)
+        [arr(BF16, plan.rows, DK)] * hv,
+        smem=(0,),
+        scratch=[vmem(BF16, hv, plan.rows, DK)],
+        fetch=range(1, 6),
+    )(place, queries, key_vectors, value_rows, write_rate, log_decay)
+    got = plan.exchange(packed)
+    rows = across_heads([grad_out] * parts)
 
     link, kept = call(
         partial(prepare_kernel, plan),
         (arr(F32, hv, 2, DK, DK), arr(F32, hv, KEPT, tok, DK)),
         smem=(0, 1, 2),
+        fetch=(0,),
         flops=20_000_000_000,
-    )(doc_offsets, place, mate, got)
+    )(doc_offsets, place, mate, *got)
     links = [link] + [plan.from_mate(link, d) for d in range(1, s)]
 
     cot = call(
@@ -529,7 +525,7 @@
         smem=(0, 1),
         scratch=[vmem(BF16, tok, model), vmem(BF16, hv, 2 * DV + model // hv, tok)],
         flops=30_000_000_000,
-    )(head, place, *after(rows, link), out_weight)
+    )(head, place, *rows, after(out_weight, link))
     kept = after(kept, cot[0])
     cot = plan.exchange(cot)
 
@@ -557,15 +553,16 @@
 
     grads = call(
         partial(backward_kernel, plan),
-        arr(BF16, hv, plan.rows, DK),
+        [arr(BF16, plan.rows, DK)] * hv,
         smem=(0, 1, 2),
+        fetch=(0,),
         scratch=[
             vmem(F32, s, hv, 2, DK, DK),
             vmem(F32, s, hv, DV, DK),
             vmem(F32, n, DV, DK),
         ],
         flops=6_000_000_000,
-    )(doc_offsets, place, mate, *links, *backs, got, *cot, kept, after(states, projected[1]))
+    )(doc_offsets, place, mate, *links, *backs, *got, *cot, kept, after(states, projected[1]))
 
     shares = call(
         partial(weight_kernel, plan),
@@ -574,11 +571,15 @@
         scratch=[vmem(BF16, hv, hv, DV, tok)],
         flops=1_000_000_000,
     )(place, mate, *cot, *mixed)
-    grads = plan.exchange_at_once(after(grads, shares[0]))
+    grads = plan.exchange(after(grads, shares[0]))
     weight_grad = shares[0]
     for d in range(1, s):
         weight_grad = weight_grad + plan.from_mate(shares[d], d)
 
+    layer_out = layer_parts[0]
+    for part in layer_parts[1:]:
+        layer_out = layer_out + part.astype(F32)
+    grads = after(grads, layer_out)
     grad_q, grad_k, grad_v, grad_rate, grad_decay = call(
         partial(finish_kernel, plan),
         (
@@ -588,12 +589,11 @@
             arr(F32, hv, tok),
             arr(F32, hv, tok),
         ),
+        smem=(0,),
+        scratch=[vmem(BF16, hv, plan.rows, DK)],
         flops=1_000_000_000,
         inside=False,
-    )(grads)
-    layer_out = after(layer_parts[0], (grad_q, weight_grad))
-    for part in layer_parts[1:]:
-        layer_out = layer_out + part.astype(F32)
+    )(place, *grads)
     return (layer_out, grad_q, grad_k, grad_v, grad_rate, grad_decay, weight_grad)
 
 

time: 64.4 us -> 58.3 us (0.905)
  waiting for transfers between devices: 19.8 us -> 12.7 us
  starting transfers between devices: 25.9 us -> 28.8 us
  Pallas kernels: 15.3 us -> 14.2 us
  local copies, waits for them, and re-layouts: 0.67 us -> 0.01 us
    all_to_all x2 -> x0, starting transfers between devices: 8.62 us -> none  [exchange_at_once(): lax.all_to_all(pieces, 'ctx', split_axis=0, concat_axis=0, axis_index_gro...]
    ppermute x6 -> x12, starting transfers between devices: 9.13 us -> 17.6 us  [exchange(): moved.append(lax.ppermute(pieces[d], 'ctx', pairs))]
    all_to_all x2 -> x0, waiting for transfers between devices: 5.64 us -> none  [exchange_at_once(): lax.all_to_all(pieces, 'ctx', split_axis=0, concat_axis=0, axis_index_gro...]
    ppermute x6, starting transfers between devices: 7.94 us -> 10.9 us  [across_heads(): lax.ppermute(pieces[d], 'head', Ring(parts).pairs(d))]
    ppermute x6, waiting for transfers between devices: 7.81 us -> 6.09 us  [across_heads(): lax.ppermute(pieces[d], 'head', Ring(parts).pairs(d))]
    pallas_call x9, Pallas kernels: 15.3 us -> 14.2 us  [run(): pl.pallas_call(kernel, out_shape=outs, in_specs=[spec(i) for i in range(l...]
    unnamed x8 -> x4, local copies, waits for them, and re-layouts: 0.67 us -> 0.01 us
    ppermute x6 -> x12, waiting for transfers between devices: 6.39 us -> 6.6 us  [exchange(): moved.append(lax.ppermute(pieces[d], 'ctx', pairs))]
  transfers between devices with their start and end apart: 17 -> 21, of which waited for: 8 -> 9; matrix products, arithmetic and copies ran while one was open for 1% -> 1% of each run, Pallas kernels for 21% -> 23%
where the time goes in v10:
time: 58.3 us; the launch traced here: 58.1 us
  starting transfers between devices  28.8 us (49%)
  Pallas kernels  14.2 us (24%)
  waiting for transfers between devices  12.7 us (22%)
  other arithmetic  1.63 us (3%)
  between operations  0.77 us (1%)
    ppermute x12, starting transfers between devices, exchange(): moved.append(lax.ppermute(pieces[d], 'ctx', pairs))  17.6 us
    pallas_call x9, Pallas kernels, run(): pl.pallas_call(kernel, out_shape=outs, in_specs=[spec(i) for i in range(l...  14.2 us
    ppermute x6, starting transfers between devices, across_heads(): lax.ppermute(pieces[d], 'head', Ring(parts).pairs(d))  10.9 us
    ppermute x12, waiting for transfers between devices, exchange(): moved.append(lax.ppermute(pieces[d], 'ctx', pairs))  6.6 us
    ppermute x6, waiting for transfers between devices, across_heads(): lax.ppermute(pieces[d], 'head', Ring(parts).pairs(d))  6.09 us
  transfers between devices with their start and end apart: 21, of which 9 were waited for; matrix products, arithmetic and copies ran while one was open for 1% of the time, Pallas kernels for 23%

profile of v10, /device:TPU:0, one launch (start us, length us, event | category | flops | bytes accessed | tf_op | source)
XLA Modules:
  0.0 58.1 jit_solution(10875270932183762685)
XLA Ops:
  0.6 1.2 %shard_map.135 = (bf16[400,128]{1,0:T(8,128)(2,1)S(1)}, bf16[400,128]{1,0:T(8,128)(2,1)S(1)}, bf16[400,128]{1,0:T(8,128)(2,1)S(1)}, bf16[400,128]{1,0:T(8,128)(2,1)S(1)}) custom-call(s32[1]{0:T(128)} %bitcast.1.place_ref, bf16[128,256]{1,0:T(8,128)(2,1)} %q_ref.1, bf16[128,256]{1,0:T(8,128)(2,1)} %k_ref.1, bf16[128,512]{1,0:T(8,128)(2,1)} %v_ref.1, ...), custom_call_target="tpu_custom_call" | custom-call | tf_op jit(solution)/shard_map/pallas_call | solution.py:60
  1.8 3.0 %collective-permute-start = (bf16[400,128]{1,0:T(8,128)(2,1)S(1)}, bf16[400,128]{1,0:T(8,128)(2,1)S(1)}, u32[]{:S(2)}, u32[]{:S(2)}) collective-permute-start(bf16[400,128]{1,0:T(8,128)(2,1)S(1)} %get-tuple-element.53), channel_id=1, source_target_pairs={{8,0},{12,4},{0,8},{4,12},{24,16},{28,20},{16,24},{20,28},{9,1},{1... | collective-permute-start | bytes 307208 | tf_op jit(solution)/shard_map/ppermute | solution.py:112
  4.8 1.5 %collective-permute-start.1 = (bf16[400,128]{1,0:T(8,128)(2,1)S(1)}, bf16[400,128]{1,0:T(8,128)(2,1)S(1)}, u32[]{:S(2)}, u32[]{:S(2)}) collective-permute-start(bf16[400,128]{1,0:T(8,128)(2,1)S(1)} %get-tuple-element.54), channel_id=1, source_target_pairs={{16,0},{20,4},{24,8},{28,12},{0,16},{4,20},{8,24},{12,28},{17,1},{... | collective-permute-start | bytes 307208 | tf_op jit(solution)/shard_map/ppermute | solution.py:112
  6.4 2.0 %collective-permute-start.4 = (bf16[32,2048]{1,0:T(8,128)(2,1)}, bf16[32,2048]{1,0:T(8,128)(2,1)S(1)}, u32[]{:S(2)}, u32[]{:S(2)}) collective-permute-start(bf16[32,2048]{1,0:T(8,128)(2,1)} %refs_0_.1), channel_id=1, source_target_pairs={{1,0},{0,1},{3,2},{2,3},{5,4},{4,5},{7,6},{6,7},{9,8},{8,9},{11,10... | collective-permute-start | bytes 393224 | tf_op jit(solution)/shard_map/ppermute | solution.py:498
  8.4 2.6 %collective-permute-start.5 = (bf16[32,2048]{1,0:T(8,128)(2,1)}, bf16[32,2048]{1,0:T(8,128)(2,1)S(1)}, u32[]{:S(2)}, u32[]{:S(2)}) collective-permute-start(bf16[32,2048]{1,0:T(8,128)(2,1)} %refs_0_.1), channel_id=1, source_target_pairs={{2,0},{3,1},{0,2},{1,3},{6,4},{7,5},{4,6},{5,7},{10,8},{11,9},{8,1... | collective-permute-start | bytes 393224 | tf_op jit(solution)/shard_map/ppermute | solution.py:498
  11.0 0.6 %collective-permute-start.6 = (bf16[32,2048]{1,0:T(8,128)(2,1)}, bf16[32,2048]{1,0:T(8,128)(2,1)S(1)}, u32[]{:S(2)}, u32[]{:S(2)}) collective-permute-start(bf16[32,2048]{1,0:T(8,128)(2,1)} %refs_0_.1), channel_id=1, source_target_pairs={{3,0},{2,1},{1,2},{0,3},{7,4},{6,5},{5,6},{4,7},{11,8},{10,9},{9,1... | collective-permute-start | bytes 393224 | tf_op jit(solution)/shard_map/ppermute | solution.py:498
  11.9 4.1 %shard_map.136 = (f32[4,2,128,128]{3,2,1,0:T(8,128)S(1)}, f32[4,7,128,128]{3,2,1,0:T(8,128)S(1)}) custom-call(s32[5]{0:T(128)} %off_ref.3, s32[1]{0:T(128)} %bitcast.1.place_ref, s32[1]{0:T(128)} %bitcast.2.mate_ref, bf16[400,128]{1,0:T(8,128)(2,1)S(1)} %get-tuple-element.52.refs_0_.refs_4_, bf16[400,128]{1,0:T(8,128)(2,1)S(1)} %collective-permute-done.refs_1_.refs_5_, ...), custom_call_target="tpu_custom_call" | custom-call | flops 20000000000 | tf_op jit(solution)/shard_map/pallas_call | solution.py:60
  16.1 4.6 %collective-permute-done.5.refs_2_ = bf16[32,2048]{1,0:T(8,128)(2,1)S(1)} collective-permute-done((bf16[32,2048]{1,0:T(8,128)(2,1)}, bf16[32,2048]{1,0:T(8,128)(2,1)S(1)}, u32[]{:S(2)}, u32[]{:S(2)}) %collective-permute-start.5) | collective-permute-done | bytes 131104 | tf_op jit(solution)/shard_map/ppermute | solution.py:498
  20.7 0.8 %shard_map.137 = (bf16[768,128]{1,0:T(8,128)(2,1)S(1)}, bf16[768,128]{1,0:T(8,128)(2,1)S(1)}, bf16[768,128]{1,0:T(8,128)(2,1)S(1)}, bf16[768,128]{1,0:T(8,128)(2,1)S(1)}) custom-call(s32[1]{0:T(128)} %bitcast.head_ref, s32[1]{0:T(128)} %bitcast.1.place_ref, bf16[32,2048]{1,0:T(8,128)(2,1)S(1)} %copy-done.1, ...), custom_call_target="tpu_custom_call" | custom-call | flops 30000001024 | tf_op jit(solution)/shard_map/pallas_call | solution.py:60
  21.5 1.6 %collective-permute-start.13 = (bf16[768,128]{1,0:T(8,128)(2,1)S(1)}, bf16[768,128]{1,0:T(8,128)(2,1)S(1)}, u32[]{:S(2)}, u32[]{:S(2)}) collective-permute-start(bf16[768,128]{1,0:T(8,128)(2,1)S(1)} %get-tuple-element.69), channel_id=1, source_target_pairs={{8,0},{12,4},{0,8},{4,12},{24,16},{28,20},{16,24},{20,28},{9,1},{1... | collective-permute-start | bytes 589832 | tf_op jit(solution)/shard_map/ppermute | solution.py:112
  23.1 1.5 %collective-permute-start.14 = (bf16[768,128]{1,0:T(8,128)(2,1)S(1)}, bf16[768,128]{1,0:T(8,128)(2,1)S(1)}, u32[]{:S(2)}, u32[]{:S(2)}) collective-permute-start(bf16[768,128]{1,0:T(8,128)(2,1)S(1)} %get-tuple-element.70), channel_id=1, source_target_pairs={{16,0},{20,4},{24,8},{28,12},{0,16},{4,20},{8,24},{12,28},{17,1},{... | collective-permute-start | bytes 589832 | tf_op jit(solution)/shard_map/ppermute | solution.py:112
  24.6 0.5 collective-permute-start.15
  25.1 1.3 %shard_map.138 = (f32[4,128,128]{2,1,0:T(8,128)S(1)}, bf16[4,128,128]{2,1,0:T(8,128)(2,1)S(1)}, bf16[4,128,128]{2,1,0:T(8,128)(2,1)S(1)}, bf16[4,128,128]{2,1,0:T(8,128)(2,1)S(1)}, bf16[4,128,128]{2,1,0:T(8,128)(2,1)S(1)}) custom-call(s32[1]{0:T(128)} %bitcast.1.place_ref, s32[1]{0:T(128)} %bitcast.2.mate_ref, ...), custom_call_target="tpu_custom_call" | custom-call | flops 2500000000 | tf_op jit(solution)/shard_map/pallas_call | solution.py:60
  26.4 1.6 %collective-permute-start.7 = (bf16[4,128,128]{2,1,0:T(8,128)(2,1)S(1)}, bf16[4,128,128]{2,1,0:T(8,128)(2,1)S(1)}, u32[]{:S(2)}, u32[]{:S(2)}) collective-permute-start(bf16[4,128,128]{2,1,0:T(8,128)(2,1)S(1)} %get-tuple-element.62), channel_id=1, source_target_pairs={{8,0},{12,4},{0,8},{4,12},{24,16},{28,20},{16,24},{20,28},{9,1},{1... | collective-permute-start | bytes 393224 | tf_op jit(solution)/shard_map/ppermute | solution.py:112
  28.0 1.5 %collective-permute-start.8 = (bf16[4,128,128]{2,1,0:T(8,128)(2,1)S(1)}, bf16[4,128,128]{2,1,0:T(8,128)(2,1)S(1)}, u32[]{:S(2)}, u32[]{:S(2)}) collective-permute-start(bf16[4,128,128]{2,1,0:T(8,128)(2,1)S(1)} %get-tuple-element.63), channel_id=1, source_target_pairs={{16,0},{20,4},{24,8},{28,12},{0,16},{4,20},{8,24},{12,28},{17,1},{... | collective-permute-start | bytes 393224 | tf_op jit(solution)/shard_map/ppermute | solution.py:112
  29.5 2.4 %collective-permute-start.9 = (bf16[4,128,128]{2,1,0:T(8,128)(2,1)S(1)}, bf16[4,128,128]{2,1,0:T(8,128)(2,1)S(1)}, u32[]{:S(2)}, u32[]{:S(2)}) collective-permute-start(bf16[4,128,128]{2,1,0:T(8,128)(2,1)S(1)} %get-tuple-element.64), channel_id=1, source_target_pairs={{24,0},{28,4},{16,8},{20,12},{8,16},{12,20},{0,24},{4,28},{25,1},{... | collective-permute-start | bytes 393224 | tf_op jit(solution)/shard_map/ppermute | solution.py:112
  32.1 1.1 %collective-permute-done.15.refs_3_.refs_11_ = bf16[768,128]{1,0:T(8,128)(2,1)S(1)} collective-permute-done((bf16[768,128]{1,0:T(8,128)(2,1)S(1)}, bf16[768,128]{1,0:T(8,128)(2,1)S(1)}, u32[]{:S(2)}, u32[]{:S(2)}) %collective-permute-start.15) | collective-permute-done | bytes 196640 | tf_op jit(solution)/shard_map/ppermute | solution.py:112
  34.0 1.0 %collective-permute-done.8.refs_2_.refs_6_ = bf16[4,128,128]{2,1,0:T(8,128)(2,1)S(1)} collective-permute-done((bf16[4,128,128]{2,1,0:T(8,128)(2,1)S(1)}, bf16[4,128,128]{2,1,0:T(8,128)(2,1)S(1)}, u32[]{:S(2)}, u32[]{:S(2)}) %collective-permute-start.8) | collective-permute-done | bytes 131104 | tf_op jit(solution)/shard_map/ppermute | solution.py:112
  35.0 1.0 %collective-permute-done.9.refs_3_.refs_7_ = bf16[4,128,128]{2,1,0:T(8,128)(2,1)S(1)} collective-permute-done((bf16[4,128,128]{2,1,0:T(8,128)(2,1)S(1)}, bf16[4,128,128]{2,1,0:T(8,128)(2,1)S(1)}, u32[]{:S(2)}, u32[]{:S(2)}) %collective-permute-start.9) | collective-permute-done | bytes 131104 | tf_op jit(solution)/shard_map/ppermute | solution.py:112
  35.9 0.5 shard_map.139
  36.5 2.8 %collective-permute-start.12 = (bf16[32,2048]{1,0:T(8,128)(2,1)S(1)}, bf16[32,2048]{1,0:T(8,128)(2,1)S(1)}, u32[]{:S(2)}, u32[]{:S(2)}) collective-permute-start(bf16[32,2048]{1,0:T(8,128)(2,1)S(1)} %get-tuple-element.68), channel_id=1, source_target_pairs={{3,0},{2,1},{1,2},{0,3},{7,4},{6,5},{5,6},{4,7},{11,8},{10,9},{9,1... | collective-permute-start | bytes 393224 | tf_op jit(solution)/shard_map/ppermute | solution.py:498
  39.3 2.9 %collective-permute-start.11 = (bf16[32,2048]{1,0:T(8,128)(2,1)S(1)}, bf16[32,2048]{1,0:T(8,128)(2,1)S(1)}, u32[]{:S(2)}, u32[]{:S(2)}) collective-permute-start(bf16[32,2048]{1,0:T(8,128)(2,1)S(1)} %get-tuple-element.67), channel_id=1, source_target_pairs={{2,0},{3,1},{0,2},{1,3},{6,4},{7,5},{4,6},{5,7},{10,8},{11,9},{8,1... | collective-permute-start | bytes 393224 | tf_op jit(solution)/shard_map/ppermute | solution.py:498
  42.2 0.7 %shard_map.142 = (f32[256,512]{1,0:T(8,128)S(1)}, f32[256,512]{1,0:T(8,128)S(1)}) custom-call(s32[1]{0:T(128)} %bitcast.1.place_ref, s32[1]{0:T(128)} %bitcast.2.mate_ref, bf16[768,128]{1,0:T(8,128)(2,1)S(1)} %get-tuple-element.72.refs_0_.refs_8_, bf16[768,128]{1,0:T(8,128)(2,1)S(1)} %collective-permute-done.13.refs_1_.refs_9_, ...), custom_call_target="tpu_custom_call" | custom-call | flops 1000000000 | tf_op jit(solution)/shard_map/pallas_call | solution.py:60
  43.0 4.4 %shard_map.141 = (bf16[400,128]{1,0:T(8,128)(2,1)S(1)}, bf16[400,128]{1,0:T(8,128)(2,1)S(1)}, bf16[400,128]{1,0:T(8,128)(2,1)S(1)}, bf16[400,128]{1,0:T(8,128)(2,1)S(1)}) custom-call(s32[5]{0:T(128)} %off_ref.3, s32[1]{0:T(128)} %bitcast.1.place_ref, s32[1]{0:T(128)} %bitcast.2.mate_ref, f32[4,2,128,128]{3,2,1,0:T(8,128)S(1)} %get-tuple-element.56.refs_0_, ...), custom_call_target="tpu_custom_call" | custom-call | flops 6000000000 | tf_op jit(solution)/shard_map/pallas_call | solution.py:60
  47.5 1.0 %collective-permute-start.17 = (bf16[400,128]{1,0:T(8,128)(2,1)S(1)}, bf16[400,128]{1,0:T(8,128)(2,1)S(1)}, u32[]{:S(2)}, u32[]{:S(2)}) collective-permute-start(bf16[400,128]{1,0:T(8,128)(2,1)S(1)} %get-tuple-element.84), channel_id=1, source_target_pairs={{8,0},{12,4},{0,8},{4,12},{24,16},{28,20},{16,24},{20,28},{9,1},{1... | collective-permute-start | bytes 307208 | tf_op jit(solution)/shard_map/ppermute | solution.py:112
  48.5 0.8 %collective-permute-start.18 = (bf16[400,128]{1,0:T(8,128)(2,1)S(1)}, bf16[400,128]{1,0:T(8,128)(2,1)S(1)}, u32[]{:S(2)}, u32[]{:S(2)}) collective-permute-start(bf16[400,128]{1,0:T(8,128)(2,1)S(1)} %get-tuple-element.85), channel_id=1, source_target_pairs={{16,0},{20,4},{24,8},{28,12},{0,16},{4,20},{8,24},{12,28},{17,1},{... | collective-permute-start | bytes 307208 | tf_op jit(solution)/shard_map/ppermute | solution.py:112
  49.3 1.5 %collective-permute-done.11 = bf16[32,2048]{1,0:T(8,128)(2,1)S(1)} collective-permute-done((bf16[32,2048]{1,0:T(8,128)(2,1)S(1)}, bf16[32,2048]{1,0:T(8,128)(2,1)S(1)}, u32[]{:S(2)}, u32[]{:S(2)}) %collective-permute-start.11) | collective-permute-done | bytes 131104 | tf_op jit(solution)/shard_map/ppermute | solution.py:498
  50.8 2.2 %collective-permute-start.19 = (bf16[400,128]{1,0:T(8,128)(2,1)S(1)}, bf16[400,128]{1,0:T(8,128)(2,1)S(1)}, u32[]{:S(2)}, u32[]{:S(2)}) collective-permute-start(bf16[400,128]{1,0:T(8,128)(2,1)S(1)} %get-tuple-element.86), channel_id=1, source_target_pairs={{24,0},{28,4},{16,8},{20,12},{8,16},{12,20},{0,24},{4,28},{25,1},{... | collective-permute-start | bytes 307208 | tf_op jit(solution)/shard_map/ppermute | solution.py:112
  53.0 0.8 %convert_add_fusion = f32[32,2048]{1,0:T(8,128)} fusion(bf16[32,2048]{1,0:T(8,128)(2,1)S(1)} %collective-permute-done.12, bf16[32,2048]{1,0:T(8,128)(2,1)S(1)} %collective-permute-done.11, f32[32,2048]{1,0:T(8,128)S(1)} %get-tuple-element.65, bf16[32,2048]{1,0:T(8,128)(2,1)S(1)} %collective-permute-done.10), kind=kLoop, calls=%fused_computation | loop fusion | flops 393216 | bytes 917504 | tf_op jit(solution)/shard_map/add | solution.py:581
  53.8 2.6 %collective-permute-done.19.refs_3_ = bf16[400,128]{1,0:T(8,128)(2,1)S(1)} collective-permute-done((bf16[400,128]{1,0:T(8,128)(2,1)S(1)}, bf16[400,128]{1,0:T(8,128)(2,1)S(1)}, u32[]{:S(2)}, u32[]{:S(2)}) %collective-permute-start.19) | collective-permute-done | bytes 102432 | tf_op jit(solution)/shard_map/ppermute | solution.py:112
  56.4 0.9 %shard_map.143 = (f32[128,256]{1,0:T(8,128)}, f32[128,256]{1,0:T(8,128)}, f32[128,512]{1,0:T(8,128)}, f32[4,128]{1,0:T(4,128)}, f32[4,128]{1,0:T(4,128)}) custom-call(s32[1]{0:T(128)} %bitcast.1.place_ref, bf16[400,128]{1,0:T(8,128)(2,1)S(1)} %get-tuple-element.87.refs_0_, bf16[400,128]{1,0:T(8,128)(2,1)S(1)} %collective-permute-done.17.refs_1_, ...), custom_call_target="tpu_custom_call" | custom-call | flops 1000000000 | tf_op jit(solution)/shard_map/pallas_call | solution.py:60
  57.2 0.9 %add.21 = f32[256,512]{1,0:T(8,128)} add(f32[256,512]{1,0:T(8,128)S(1)} %get-tuple-element.82, f32[256,512]{1,0:T(8,128)S(1)} %collective-permute-done.20) | non-fusion elementwise | flops 131072 | bytes 1572864 | tf_op jit(solution)/shard_map/add | solution.py:577
  (25 shorter events, 1.5 us)
Async XLA Ops:
  1.8 9.2 %collective-permute-start = (bf16[400,128]{1,0:T(8,128)(2,1)S(1)}, bf16[400,128]{1,0:T(8,128)(2,1)S(1)}, u32[]{:S(2)}, u32[]{:S(2)}) collective-permute-start(bf16[400,128]{1,0:T(8,128)(2,1)S(1)} %get-tuple-element.53), channel_id=1, source_target_pairs={{8,0},{12,4},{0,8},{4,12},{24,16},{28,20},{16,24},{20,28},{9,1},{1... | collective-permute-start | bytes 307208 | tf_op jit(solution)/shard_map/ppermute | solution.py:112
  4.8 6.8 %collective-permute-start.1 = (bf16[400,128]{1,0:T(8,128)(2,1)S(1)}, bf16[400,128]{1,0:T(8,128)(2,1)S(1)}, u32[]{:S(2)}, u32[]{:S(2)}) collective-permute-start(bf16[400,128]{1,0:T(8,128)(2,1)S(1)} %get-tuple-element.54), channel_id=1, source_target_pairs={{16,0},{20,4},{24,8},{28,12},{0,16},{4,20},{8,24},{12,28},{17,1},{... | collective-permute-start | bytes 307208 | tf_op jit(solution)/shard_map/ppermute | solution.py:112
  6.3 5.6 %collective-permute-start.2 = (bf16[400,128]{1,0:T(8,128)(2,1)S(1)}, bf16[400,128]{1,0:T(8,128)(2,1)S(1)}, u32[]{:S(2)}, u32[]{:S(2)}) collective-permute-start(bf16[400,128]{1,0:T(8,128)(2,1)S(1)} %get-tuple-element.55), channel_id=1, source_target_pairs={{24,0},{28,4},{16,8},{20,12},{8,16},{12,20},{0,24},{4,28},{25,1},{... | collective-permute-start | bytes 307208 | tf_op jit(solution)/shard_map/ppermute | solution.py:112
  6.4 9.8 %collective-permute-start.4 = (bf16[32,2048]{1,0:T(8,128)(2,1)}, bf16[32,2048]{1,0:T(8,128)(2,1)S(1)}, u32[]{:S(2)}, u32[]{:S(2)}) collective-permute-start(bf16[32,2048]{1,0:T(8,128)(2,1)} %refs_0_.1), channel_id=1, source_target_pairs={{1,0},{0,1},{3,2},{2,3},{5,4},{4,5},{7,6},{6,7},{9,8},{8,9},{11,10... | collective-permute-start | bytes 393224 | tf_op jit(solution)/shard_map/ppermute | solution.py:498
  8.4 12.3 %collective-permute-start.5 = (bf16[32,2048]{1,0:T(8,128)(2,1)}, bf16[32,2048]{1,0:T(8,128)(2,1)S(1)}, u32[]{:S(2)}, u32[]{:S(2)}) collective-permute-start(bf16[32,2048]{1,0:T(8,128)(2,1)} %refs_0_.1), channel_id=1, source_target_pairs={{2,0},{3,1},{0,2},{1,3},{6,4},{7,5},{4,6},{5,7},{10,8},{11,9},{8,1... | collective-permute-start | bytes 393224 | tf_op jit(solution)/shard_map/ppermute | solution.py:498
  11.0 9.7 %collective-permute-start.6 = (bf16[32,2048]{1,0:T(8,128)(2,1)}, bf16[32,2048]{1,0:T(8,128)(2,1)S(1)}, u32[]{:S(2)}, u32[]{:S(2)}) collective-permute-start(bf16[32,2048]{1,0:T(8,128)(2,1)} %refs_0_.1), channel_id=1, source_target_pairs={{3,0},{2,1},{1,2},{0,3},{7,4},{6,5},{5,6},{4,7},{11,8},{10,9},{9,1... | collective-permute-start | bytes 393224 | tf_op jit(solution)/shard_map/ppermute | solution.py:498
  11.9 8.8 %copy-start = (bf16[512,2048]{1,0:T(8,128)(2,1)S(1)}, bf16[512,2048]{1,0:T(8,128)(2,1)}, u32[]{:S(2)}) copy-start(bf16[512,2048]{1,0:T(8,128)(2,1)} %refs_4_.2) | copy-start | bytes 6291460
  11.9 8.8 %copy-start.1 = (bf16[32,2048]{1,0:T(8,128)(2,1)S(1)}, bf16[32,2048]{1,0:T(8,128)(2,1)}, u32[]{:S(2)}) copy-start(bf16[32,2048]{1,0:T(8,128)(2,1)} %refs_0_.1) | copy-start | bytes 393220
  16.0 9.1 %collective-permute-start.3 = (f32[4,2,128,128]{3,2,1,0:T(8,128)S(1)}, f32[4,2,128,128]{3,2,1,0:T(8,128)S(1)}, u32[]{:S(2)}, u32[]{:S(2)}) collective-permute-start(f32[4,2,128,128]{3,2,1,0:T(8,128)S(1)} %get-tuple-element.56.refs_0_), channel_id=1, source_target_pairs={{4,0},{0,4},{12,8},{8,12},{20,16},{16,20},{28,24},{24,28},{5,1},{1... | collective-permute-start | bytes 1572872 | tf_op jit(solution)/shard_map/ppermute | solution.py:118
  21.5 8.0 %collective-permute-start.13 = (bf16[768,128]{1,0:T(8,128)(2,1)S(1)}, bf16[768,128]{1,0:T(8,128)(2,1)S(1)}, u32[]{:S(2)}, u32[]{:S(2)}) collective-permute-start(bf16[768,128]{1,0:T(8,128)(2,1)S(1)} %get-tuple-element.69), channel_id=1, source_target_pairs={{8,0},{12,4},{0,8},{4,12},{24,16},{28,20},{16,24},{20,28},{9,1},{1... | collective-permute-start | bytes 589832 | tf_op jit(solution)/shard_map/ppermute | solution.py:112
  23.1 9.0 %collective-permute-start.14 = (bf16[768,128]{1,0:T(8,128)(2,1)S(1)}, bf16[768,128]{1,0:T(8,128)(2,1)S(1)}, u32[]{:S(2)}, u32[]{:S(2)}) collective-permute-start(bf16[768,128]{1,0:T(8,128)(2,1)S(1)} %get-tuple-element.70), channel_id=1, source_target_pairs={{16,0},{20,4},{24,8},{28,12},{0,16},{4,20},{8,24},{12,28},{17,1},{... | collective-permute-start | bytes 589832 | tf_op jit(solution)/shard_map/ppermute | solution.py:112
  24.6 8.6 %collective-permute-start.15 = (bf16[768,128]{1,0:T(8,128)(2,1)S(1)}, bf16[768,128]{1,0:T(8,128)(2,1)S(1)}, u32[]{:S(2)}, u32[]{:S(2)}) collective-permute-start(bf16[768,128]{1,0:T(8,128)(2,1)S(1)} %get-tuple-element.71), channel_id=1, source_target_pairs={{24,0},{28,4},{16,8},{20,12},{8,16},{12,20},{0,24},{4,28},{25,1},{... | collective-permute-start | bytes 589832 | tf_op jit(solution)/shard_map/ppermute | solution.py:112
  26.4 7.2 %collective-permute-start.7 = (bf16[4,128,128]{2,1,0:T(8,128)(2,1)S(1)}, bf16[4,128,128]{2,1,0:T(8,128)(2,1)S(1)}, u32[]{:S(2)}, u32[]{:S(2)}) collective-permute-start(bf16[4,128,128]{2,1,0:T(8,128)(2,1)S(1)} %get-tuple-element.62), channel_id=1, source_target_pairs={{8,0},{12,4},{0,8},{4,12},{24,16},{28,20},{16,24},{20,28},{9,1},{1... | collective-permute-start | bytes 393224 | tf_op jit(solution)/shard_map/ppermute | solution.py:112
  28.0 7.0 %collective-permute-start.8 = (bf16[4,128,128]{2,1,0:T(8,128)(2,1)S(1)}, bf16[4,128,128]{2,1,0:T(8,128)(2,1)S(1)}, u32[]{:S(2)}, u32[]{:S(2)}) collective-permute-start(bf16[4,128,128]{2,1,0:T(8,128)(2,1)S(1)} %get-tuple-element.63), channel_id=1, source_target_pairs={{16,0},{20,4},{24,8},{28,12},{0,16},{4,20},{8,24},{12,28},{17,1},{... | collective-permute-start | bytes 393224 | tf_op jit(solution)/shard_map/ppermute | solution.py:112
  29.5 6.4 %collective-permute-start.9 = (bf16[4,128,128]{2,1,0:T(8,128)(2,1)S(1)}, bf16[4,128,128]{2,1,0:T(8,128)(2,1)S(1)}, u32[]{:S(2)}, u32[]{:S(2)}) collective-permute-start(bf16[4,128,128]{2,1,0:T(8,128)(2,1)S(1)} %get-tuple-element.64), channel_id=1, source_target_pairs={{24,0},{28,4},{16,8},{20,12},{8,16},{12,20},{0,24},{4,28},{25,1},{... | collective-permute-start | bytes 393224 | tf_op jit(solution)/shard_map/ppermute | solution.py:112
  33.9 9.1 %collective-permute-start.16 = (f32[4,128,128]{2,1,0:T(8,128)S(1)}, f32[4,128,128]{2,1,0:T(8,128)S(1)}, u32[]{:S(2)}, u32[]{:S(2)}) collective-permute-start(f32[4,128,128]{2,1,0:T(8,128)S(1)} %shard_map.140.refs_2_), channel_id=1, source_target_pairs={{4,0},{0,4},{12,8},{8,12},{20,16},{16,20},{28,24},{24,28},{5,1},{1... | collective-permute-start | bytes 786440 | tf_op jit(solution)/shard_map/ppermute | solution.py:118
  36.5 12.0 %collective-permute-start.12 = (bf16[32,2048]{1,0:T(8,128)(2,1)S(1)}, bf16[32,2048]{1,0:T(8,128)(2,1)S(1)}, u32[]{:S(2)}, u32[]{:S(2)}) collective-permute-start(bf16[32,2048]{1,0:T(8,128)(2,1)S(1)} %get-tuple-element.68), channel_id=1, source_target_pairs={{3,0},{2,1},{1,2},{0,3},{7,4},{6,5},{5,6},{4,7},{11,8},{10,9},{9,1... | collective-permute-start | bytes 393224 | tf_op jit(solution)/shard_map/ppermute | solution.py:498
  39.3 11.5 %collective-permute-start.11 = (bf16[32,2048]{1,0:T(8,128)(2,1)S(1)}, bf16[32,2048]{1,0:T(8,128)(2,1)S(1)}, u32[]{:S(2)}, u32[]{:S(2)}) collective-permute-start(bf16[32,2048]{1,0:T(8,128)(2,1)S(1)} %get-tuple-element.67), channel_id=1, source_target_pairs={{2,0},{3,1},{0,2},{1,3},{6,4},{7,5},{4,6},{5,7},{10,8},{11,9},{8,1... | collective-permute-start | bytes 393224 | tf_op jit(solution)/shard_map/ppermute | solution.py:498
  42.2 10.8 %collective-permute-start.10 = (bf16[32,2048]{1,0:T(8,128)(2,1)S(1)}, bf16[32,2048]{1,0:T(8,128)(2,1)S(1)}, u32[]{:S(2)}, u32[]{:S(2)}) collective-permute-start(bf16[32,2048]{1,0:T(8,128)(2,1)S(1)} %get-tuple-element.66), channel_id=1, source_target_pairs={{1,0},{0,1},{3,2},{2,3},{5,4},{4,5},{7,6},{6,7},{9,8},{8,9},{11,10... | collective-permute-start | bytes 393224 | tf_op jit(solution)/shard_map/ppermute | solution.py:498
  42.9 14.3 %collective-permute-start.20 = (f32[256,512]{1,0:T(8,128)S(1)}, f32[256,512]{1,0:T(8,128)S(1)}, u32[]{:S(2)}, u32[]{:S(2)}) collective-permute-start(f32[256,512]{1,0:T(8,128)S(1)} %get-tuple-element.96), channel_id=1, source_target_pairs={{4,0},{0,4},{12,8},{8,12},{20,16},{16,20},{28,24},{24,28},{5,1},{1... | collective-permute-start | bytes 1572872 | tf_op jit(solution)/shard_map/ppermute | solution.py:118
  47.5 6.3 %collective-permute-start.17 = (bf16[400,128]{1,0:T(8,128)(2,1)S(1)}, bf16[400,128]{1,0:T(8,128)(2,1)S(1)}, u32[]{:S(2)}, u32[]{:S(2)}) collective-permute-start(bf16[400,128]{1,0:T(8,128)(2,1)S(1)} %get-tuple-element.84), channel_id=1, source_target_pairs={{8,0},{12,4},{0,8},{4,12},{24,16},{28,20},{16,24},{20,28},{9,1},{1... | collective-permute-start | bytes 307208 | tf_op jit(solution)/shard_map/ppermute | solution.py:112
  48.5 5.3 %collective-permute-start.18 = (bf16[400,128]{1,0:T(8,128)(2,1)S(1)}, bf16[400,128]{1,0:T(8,128)(2,1)S(1)}, u32[]{:S(2)}, u32[]{:S(2)}) collective-permute-start(bf16[400,128]{1,0:T(8,128)(2,1)S(1)} %get-tuple-element.85), channel_id=1, source_target_pairs={{16,0},{20,4},{24,8},{28,12},{0,16},{4,20},{8,24},{12,28},{17,1},{... | collective-permute-start | bytes 307208 | tf_op jit(solution)/shard_map/ppermute | solution.py:112
  50.8 5.6 %collective-permute-start.19 = (bf16[400,128]{1,0:T(8,128)(2,1)S(1)}, bf16[400,128]{1,0:T(8,128)(2,1)S(1)}, u32[]{:S(2)}, u32[]{:S(2)}) collective-permute-start(bf16[400,128]{1,0:T(8,128)(2,1)S(1)} %get-tuple-element.86), channel_id=1, source_target_pairs={{24,0},{28,4},{16,8},{20,12},{8,16},{12,20},{0,24},{4,28},{25,1},{... | collective-permute-start | bytes 307208 | tf_op jit(solution)/shard_map/ppermute | solution.py:112

commit v11 on v10

--- a/solution.py
+++ b/solution.py
@@ -527,8 +527,6 @@
         flops=30_000_000_000,
     )(head, place, *rows, after(out_weight, link))
     kept = after(kept, cot[0])
-    cot = plan.exchange(cot)
-
     states, *mixed = call(
         partial(scan_kernel, plan),
         [arr(F32, hv, DV, DK)] + [arr(BF16, hv, DV, tok)] * hv,
@@ -537,11 +535,7 @@
         flops=2_500_000_000,
     )(place, mate, *links, kept)
     mixed = plan.exchange(mixed)
-    back = call(
-        partial(state_cotangent_kernel, plan), arr(F32, hv, DV, DK), flops=30_000_000_000
-    )(kept, *after(cot, mixed[1]))
-    backs = [back] + [plan.from_mate(back, d) for d in range(1, s)]
-
+    cot = plan.exchange(after(cot, states))
     projected = call(
         partial(project_kernel, plan, parts),
         [arr(BF16 if d else F32, tok // parts, model) for d in range(parts)],
@@ -550,6 +544,11 @@
         flops=1_000_000_000,
     )(head, place, *mixed, out_weight)
     layer_parts = across_heads(projected)
+    back = call(
+        partial(state_cotangent_kernel, plan), arr(F32, hv, DV, DK), flops=30_000_000_000
+    )(after(kept, layer_parts[1]), *cot)
+    backs = [back] + [plan.from_mate(back, d) for d in range(1, s)]
+
 
     grads = call(
         partial(backward_kernel, plan),
@@ -564,14 +563,15 @@
         flops=6_000_000_000,
     )(doc_offsets, place, mate, *links, *backs, *got, *cot, kept, after(states, projected[1]))
 
+    shares_of = after(cot, grads[0])
+    grads = plan.exchange(grads)
     shares = call(
         partial(weight_kernel, plan),
         [arr(F32, model // n, hv * DV)] * s,
         smem=(0, 1),
         scratch=[vmem(BF16, hv, hv, DV, tok)],
         flops=1_000_000_000,
-    )(place, mate, *cot, *mixed)
-    grads = plan.exchange(after(grads, shares[0]))
+    )(place, mate, *shares_of, *mixed)
     weight_grad = shares[0]
     for d in range(1, s):
         weight_grad = weight_grad + plan.from_mate(shares[d], d)
@@ -579,7 +579,7 @@
     layer_out = layer_parts[0]
     for part in layer_parts[1:]:
         layer_out = layer_out + part.astype(F32)
-    grads = after(grads, layer_out)
+    grads = after(grads, (layer_out, weight_grad))
     grad_q, grad_k, grad_v, grad_rate, grad_decay = call(
         partial(finish_kernel, plan),
         (

time: 58.3 us -> 60.2 us (1.033)
  waiting for transfers between devices: 12.7 us -> 14.4 us
    ppermute x6, waiting for transfers between devices: 6.09 us -> 8.48 us  [across_heads(): lax.ppermute(pieces[d], 'head', Ring(parts).pairs(d))]
    ppermute x6, starting transfers between devices: 10.9 us -> 12.6 us  [across_heads(): lax.ppermute(pieces[d], 'head', Ring(parts).pairs(d))]
    ppermute x12, starting transfers between devices: 17.6 us -> 16.2 us  [exchange(): moved.append(lax.ppermute(pieces[d], 'ctx', pairs))]
    ppermute x12, waiting for transfers between devices: 6.6 us -> 5.91 us  [exchange(): moved.append(lax.ppermute(pieces[d], 'ctx', pairs))]
  transfers between devices with their start and end apart: 21 -> 21, of which waited for: 9 -> 8; matrix products, arithmetic and copies ran while one was open for 1% -> 3% of each run, Pallas kernels for 23% -> 18%
where the time goes in v11:
time: 60.2 us; the launch traced here: 60.1 us
  starting transfers between devices  29 us (48%)
  waiting for transfers between devices  14.4 us (24%)
  Pallas kernels  14.2 us (24%)
  other arithmetic  1.64 us (3%)
  between operations  0.76 us (1%)
    ppermute x12, starting transfers between devices, exchange(): moved.append(lax.ppermute(pieces[d], 'ctx', pairs))  16.2 us
    pallas_call x9, Pallas kernels, run(): pl.pallas_call(kernel, out_shape=outs, in_specs=[spec(i) for i in range(l...  14.2 us
    ppermute x6, starting transfers between devices, across_heads(): lax.ppermute(pieces[d], 'head', Ring(parts).pairs(d))  12.6 us
    ppermute x6, waiting for transfers between devices, across_heads(): lax.ppermute(pieces[d], 'head', Ring(parts).pairs(d))  8.48 us
    ppermute x12, waiting for transfers between devices, exchange(): moved.append(lax.ppermute(pieces[d], 'ctx', pairs))  5.91 us
  transfers between devices with their start and end apart: 21, of which 8 were waited for; matrix products, arithmetic and copies ran while one was open for 3% of the time, Pallas kernels for 18%

profile of v11, /device:TPU:0, one launch (start us, length us, event | category | flops | bytes accessed | tf_op | source)
XLA Modules:
  0.0 60.1 jit_solution(5692617466475902396)
XLA Ops:
  0.6 1.2 %shard_map.135 = (bf16[400,128]{1,0:T(8,128)(2,1)S(1)}, bf16[400,128]{1,0:T(8,128)(2,1)S(1)}, bf16[400,128]{1,0:T(8,128)(2,1)S(1)}, bf16[400,128]{1,0:T(8,128)(2,1)S(1)}) custom-call(s32[1]{0:T(128)} %bitcast.1.place_ref, bf16[128,256]{1,0:T(8,128)(2,1)} %q_ref.1, bf16[128,256]{1,0:T(8,128)(2,1)} %k_ref.1, bf16[128,512]{1,0:T(8,128)(2,1)} %v_ref.1, ...), custom_call_target="tpu_custom_call" | custom-call | tf_op jit(solution)/shard_map/pallas_call | solution.py:60
  1.8 3.0 %collective-permute-start = (bf16[400,128]{1,0:T(8,128)(2,1)S(1)}, bf16[400,128]{1,0:T(8,128)(2,1)S(1)}, u32[]{:S(2)}, u32[]{:S(2)}) collective-permute-start(bf16[400,128]{1,0:T(8,128)(2,1)S(1)} %get-tuple-element.54), channel_id=1, source_target_pairs={{8,0},{12,4},{0,8},{4,12},{24,16},{28,20},{16,24},{20,28},{9,1},{1... | collective-permute-start | bytes 307208 | tf_op jit(solution)/shard_map/ppermute | solution.py:112
  4.8 1.5 %collective-permute-start.1 = (bf16[400,128]{1,0:T(8,128)(2,1)S(1)}, bf16[400,128]{1,0:T(8,128)(2,1)S(1)}, u32[]{:S(2)}, u32[]{:S(2)}) collective-permute-start(bf16[400,128]{1,0:T(8,128)(2,1)S(1)} %get-tuple-element.55), channel_id=1, source_target_pairs={{16,0},{20,4},{24,8},{28,12},{0,16},{4,20},{8,24},{12,28},{17,1},{... | collective-permute-start | bytes 307208 | tf_op jit(solution)/shard_map/ppermute | solution.py:112
  6.4 3.0 %collective-permute-start.5 = (bf16[32,2048]{1,0:T(8,128)(2,1)}, bf16[32,2048]{1,0:T(8,128)(2,1)S(1)}, u32[]{:S(2)}, u32[]{:S(2)}) collective-permute-start(bf16[32,2048]{1,0:T(8,128)(2,1)} %refs_0_.1), channel_id=1, source_target_pairs={{2,0},{3,1},{0,2},{1,3},{6,4},{7,5},{4,6},{5,7},{10,8},{11,9},{8,1... | collective-permute-start | bytes 393224 | tf_op jit(solution)/shard_map/ppermute | solution.py:498
  9.4 1.6 %collective-permute-start.4 = (bf16[32,2048]{1,0:T(8,128)(2,1)}, bf16[32,2048]{1,0:T(8,128)(2,1)S(1)}, u32[]{:S(2)}, u32[]{:S(2)}) collective-permute-start(bf16[32,2048]{1,0:T(8,128)(2,1)} %refs_0_.1), channel_id=1, source_target_pairs={{1,0},{0,1},{3,2},{2,3},{5,4},{4,5},{7,6},{6,7},{9,8},{8,9},{11,10... | collective-permute-start | bytes 393224 | tf_op jit(solution)/shard_map/ppermute | solution.py:498
  11.0 0.6 %collective-permute-start.6 = (bf16[32,2048]{1,0:T(8,128)(2,1)}, bf16[32,2048]{1,0:T(8,128)(2,1)S(1)}, u32[]{:S(2)}, u32[]{:S(2)}) collective-permute-start(bf16[32,2048]{1,0:T(8,128)(2,1)} %refs_0_.1), channel_id=1, source_target_pairs={{3,0},{2,1},{1,2},{0,3},{7,4},{6,5},{5,6},{4,7},{11,8},{10,9},{9,1... | collective-permute-start | bytes 393224 | tf_op jit(solution)/shard_map/ppermute | solution.py:498
  11.9 4.1 %shard_map.136 = (f32[4,2,128,128]{3,2,1,0:T(8,128)S(1)}, f32[4,7,128,128]{3,2,1,0:T(8,128)S(1)}) custom-call(s32[5]{0:T(128)} %off_ref.3, s32[1]{0:T(128)} %bitcast.1.place_ref, s32[1]{0:T(128)} %bitcast.2.mate_ref, bf16[400,128]{1,0:T(8,128)(2,1)S(1)} %get-tuple-element.53.refs_0_.refs_4_, bf16[400,128]{1,0:T(8,128)(2,1)S(1)} %collective-permute-done.refs_1_.refs_5_, ...), custom_call_target="tpu_custom_call" | custom-call | flops 20000000000 | tf_op jit(solution)/shard_map/pallas_call | solution.py:60
  16.1 1.6 %collective-permute-done.5.refs_2_ = bf16[32,2048]{1,0:T(8,128)(2,1)S(1)} collective-permute-done((bf16[32,2048]{1,0:T(8,128)(2,1)}, bf16[32,2048]{1,0:T(8,128)(2,1)S(1)}, u32[]{:S(2)}, u32[]{:S(2)}) %collective-permute-start.5) | collective-permute-done | bytes 131104 | tf_op jit(solution)/shard_map/ppermute | solution.py:498
  17.7 1.4 %collective-permute-done.6.refs_3_ = bf16[32,2048]{1,0:T(8,128)(2,1)S(1)} collective-permute-done((bf16[32,2048]{1,0:T(8,128)(2,1)}, bf16[32,2048]{1,0:T(8,128)(2,1)S(1)}, u32[]{:S(2)}, u32[]{:S(2)}) %collective-permute-start.6) | collective-permute-done | bytes 131104 | tf_op jit(solution)/shard_map/ppermute | solution.py:498
  19.2 0.8 %shard_map.137 = (bf16[768,128]{1,0:T(8,128)(2,1)S(1)}, bf16[768,128]{1,0:T(8,128)(2,1)S(1)}, bf16[768,128]{1,0:T(8,128)(2,1)S(1)}, bf16[768,128]{1,0:T(8,128)(2,1)S(1)}) custom-call(s32[1]{0:T(128)} %bitcast.head_ref, s32[1]{0:T(128)} %bitcast.1.place_ref, bf16[32,2048]{1,0:T(8,128)(2,1)S(1)} %copy-done.1, ...), custom_call_target="tpu_custom_call" | custom-call | flops 30000001024 | tf_op jit(solution)/shard_map/pallas_call | solution.py:60
  20.0 1.3 %shard_map.138 = (f32[4,128,128]{2,1,0:T(8,128)S(1)}, bf16[4,128,128]{2,1,0:T(8,128)(2,1)S(1)}, bf16[4,128,128]{2,1,0:T(8,128)(2,1)S(1)}, bf16[4,128,128]{2,1,0:T(8,128)(2,1)S(1)}, bf16[4,128,128]{2,1,0:T(8,128)(2,1)S(1)}) custom-call(s32[1]{0:T(128)} %bitcast.1.place_ref, s32[1]{0:T(128)} %bitcast.2.mate_ref, ...), custom_call_target="tpu_custom_call" | custom-call | flops 2500000000 | tf_op jit(solution)/shard_map/pallas_call | solution.py:60
  21.3 1.6 %collective-permute-start.7 = (bf16[4,128,128]{2,1,0:T(8,128)(2,1)S(1)}, bf16[4,128,128]{2,1,0:T(8,128)(2,1)S(1)}, u32[]{:S(2)}, u32[]{:S(2)}) collective-permute-start(bf16[4,128,128]{2,1,0:T(8,128)(2,1)S(1)} %get-tuple-element.63), channel_id=1, source_target_pairs={{8,0},{12,4},{0,8},{4,12},{24,16},{28,20},{16,24},{20,28},{9,1},{1... | collective-permute-start | bytes 393224 | tf_op jit(solution)/shard_map/ppermute | solution.py:112
  22.9 1.5 %collective-permute-start.8 = (bf16[4,128,128]{2,1,0:T(8,128)(2,1)S(1)}, bf16[4,128,128]{2,1,0:T(8,128)(2,1)S(1)}, u32[]{:S(2)}, u32[]{:S(2)}) collective-permute-start(bf16[4,128,128]{2,1,0:T(8,128)(2,1)S(1)} %get-tuple-element.64), channel_id=1, source_target_pairs={{16,0},{20,4},{24,8},{28,12},{0,16},{4,20},{8,24},{12,28},{17,1},{... | collective-permute-start | bytes 393224 | tf_op jit(solution)/shard_map/ppermute | solution.py:112
  24.9 1.5 %collective-permute-start.13 = (bf16[768,128]{1,0:T(8,128)(2,1)S(1)}, bf16[768,128]{1,0:T(8,128)(2,1)S(1)}, u32[]{:S(2)}, u32[]{:S(2)}) collective-permute-start(bf16[768,128]{1,0:T(8,128)(2,1)S(1)} %get-tuple-element.76), channel_id=1, source_target_pairs={{8,0},{12,4},{0,8},{4,12},{24,16},{28,20},{16,24},{20,28},{9,1},{1... | collective-permute-start | bytes 589832 | tf_op jit(solution)/shard_map/ppermute | solution.py:112
  26.4 1.5 %collective-permute-start.14 = (bf16[768,128]{1,0:T(8,128)(2,1)S(1)}, bf16[768,128]{1,0:T(8,128)(2,1)S(1)}, u32[]{:S(2)}, u32[]{:S(2)}) collective-permute-start(bf16[768,128]{1,0:T(8,128)(2,1)S(1)} %get-tuple-element.77), channel_id=1, source_target_pairs={{16,0},{20,4},{24,8},{28,12},{0,16},{4,20},{8,24},{12,28},{17,1},{... | collective-permute-start | bytes 589832 | tf_op jit(solution)/shard_map/ppermute | solution.py:112
  27.9 2.4 %collective-permute-start.15 = (bf16[768,128]{1,0:T(8,128)(2,1)S(1)}, bf16[768,128]{1,0:T(8,128)(2,1)S(1)}, u32[]{:S(2)}, u32[]{:S(2)}) collective-permute-start(bf16[768,128]{1,0:T(8,128)(2,1)S(1)} %get-tuple-element.78), channel_id=1, source_target_pairs={{24,0},{28,4},{16,8},{20,12},{8,16},{12,20},{0,24},{4,28},{25,1},{... | collective-permute-start | bytes 589832 | tf_op jit(solution)/shard_map/ppermute | solution.py:112
  30.3 1.5 %collective-permute-done.8.refs_2_.refs_6_ = bf16[4,128,128]{2,1,0:T(8,128)(2,1)S(1)} collective-permute-done((bf16[4,128,128]{2,1,0:T(8,128)(2,1)S(1)}, bf16[4,128,128]{2,1,0:T(8,128)(2,1)S(1)}, u32[]{:S(2)}, u32[]{:S(2)}) %collective-permute-start.8) | collective-permute-done | bytes 131104 | tf_op jit(solution)/shard_map/ppermute | solution.py:112
  32.3 2.4 %collective-permute-start.10 = (bf16[32,2048]{1,0:T(8,128)(2,1)S(1)}, bf16[32,2048]{1,0:T(8,128)(2,1)S(1)}, u32[]{:S(2)}, u32[]{:S(2)}) collective-permute-start(bf16[32,2048]{1,0:T(8,128)(2,1)S(1)} %get-tuple-element.67), channel_id=1, source_target_pairs={{1,0},{0,1},{3,2},{2,3},{5,4},{4,5},{7,6},{6,7},{9,8},{8,9},{11,10... | collective-permute-start | bytes 393224 | tf_op jit(solution)/shard_map/ppermute | solution.py:498
  34.7 2.9 %collective-permute-done.10 = bf16[32,2048]{1,0:T(8,128)(2,1)S(1)} collective-permute-done((bf16[32,2048]{1,0:T(8,128)(2,1)S(1)}, bf16[32,2048]{1,0:T(8,128)(2,1)S(1)}, u32[]{:S(2)}, u32[]{:S(2)}) %collective-permute-start.10) | collective-permute-done | bytes 131104 | tf_op jit(solution)/shard_map/ppermute | solution.py:498
  37.7 1.2 %collective-permute-done.14.refs_2_.refs_10_ = bf16[768,128]{1,0:T(8,128)(2,1)S(1)} collective-permute-done((bf16[768,128]{1,0:T(8,128)(2,1)S(1)}, bf16[768,128]{1,0:T(8,128)(2,1)S(1)}, u32[]{:S(2)}, u32[]{:S(2)}) %collective-permute-start.14) | collective-permute-done | bytes 196640 | tf_op jit(solution)/shard_map/ppermute | solution.py:112
  39.2 4.5 %collective-permute-start.11 = (bf16[32,2048]{1,0:T(8,128)(2,1)S(1)}, bf16[32,2048]{1,0:T(8,128)(2,1)S(1)}, u32[]{:S(2)}, u32[]{:S(2)}) collective-permute-start(bf16[32,2048]{1,0:T(8,128)(2,1)S(1)} %get-tuple-element.68), channel_id=1, source_target_pairs={{2,0},{3,1},{0,2},{1,3},{6,4},{7,5},{4,6},{5,7},{10,8},{11,9},{8,1... | collective-permute-start | bytes 393224 | tf_op jit(solution)/shard_map/ppermute | solution.py:498
  43.7 0.5 collective-permute-start.12
  44.2 4.4 %shard_map.141 = (bf16[400,128]{1,0:T(8,128)(2,1)S(1)}, bf16[400,128]{1,0:T(8,128)(2,1)S(1)}, bf16[400,128]{1,0:T(8,128)(2,1)S(1)}, bf16[400,128]{1,0:T(8,128)(2,1)S(1)}) custom-call(s32[5]{0:T(128)} %off_ref.3, s32[1]{0:T(128)} %bitcast.1.place_ref, s32[1]{0:T(128)} %bitcast.2.mate_ref, f32[4,2,128,128]{3,2,1,0:T(8,128)S(1)} %get-tuple-element.57.refs_0_, ...), custom_call_target="tpu_custom_call" | custom-call | flops 6000000000 | tf_op jit(solution)/shard_map/pallas_call | solution.py:60
  48.6 0.7 %shard_map.142 = (f32[256,512]{1,0:T(8,128)S(1)}, f32[256,512]{1,0:T(8,128)S(1)}) custom-call(s32[1]{0:T(128)} %bitcast.1.place_ref, s32[1]{0:T(128)} %bitcast.2.mate_ref, bf16[768,128]{1,0:T(8,128)(2,1)S(1)} %get-tuple-element.84.refs_0_.refs_8_, bf16[768,128]{1,0:T(8,128)(2,1)S(1)} %collective-permute-done.13.refs_1_.refs_9_, ...), custom_call_target="tpu_custom_call" | custom-call | flops 1000000000 | tf_op jit(solution)/shard_map/pallas_call | solution.py:60
  49.5 0.9 %collective-permute-start.17 = (bf16[400,128]{1,0:T(8,128)(2,1)S(1)}, bf16[400,128]{1,0:T(8,128)(2,1)S(1)}, u32[]{:S(2)}, u32[]{:S(2)}) collective-permute-start(bf16[400,128]{1,0:T(8,128)(2,1)S(1)} %get-tuple-element.81), channel_id=1, source_target_pairs={{8,0},{12,4},{0,8},{4,12},{24,16},{28,20},{16,24},{20,28},{9,1},{1... | collective-permute-start | bytes 307208 | tf_op jit(solution)/shard_map/ppermute | solution.py:112
  50.3 0.8 %collective-permute-start.18 = (bf16[400,128]{1,0:T(8,128)(2,1)S(1)}, bf16[400,128]{1,0:T(8,128)(2,1)S(1)}, u32[]{:S(2)}, u32[]{:S(2)}) collective-permute-start(bf16[400,128]{1,0:T(8,128)(2,1)S(1)} %get-tuple-element.82), channel_id=1, source_target_pairs={{16,0},{20,4},{24,8},{28,12},{0,16},{4,20},{8,24},{12,28},{17,1},{... | collective-permute-start | bytes 307208 | tf_op jit(solution)/shard_map/ppermute | solution.py:112
  51.1 2.5 %collective-permute-done.11 = bf16[32,2048]{1,0:T(8,128)(2,1)S(1)} collective-permute-done((bf16[32,2048]{1,0:T(8,128)(2,1)S(1)}, bf16[32,2048]{1,0:T(8,128)(2,1)S(1)}, u32[]{:S(2)}, u32[]{:S(2)}) %collective-permute-start.11) | collective-permute-done | bytes 131104 | tf_op jit(solution)/shard_map/ppermute | solution.py:498
  53.6 1.0 %collective-permute-start.19 = (bf16[400,128]{1,0:T(8,128)(2,1)S(1)}, bf16[400,128]{1,0:T(8,128)(2,1)S(1)}, u32[]{:S(2)}, u32[]{:S(2)}) collective-permute-start(bf16[400,128]{1,0:T(8,128)(2,1)S(1)} %get-tuple-element.83), channel_id=1, source_target_pairs={{24,0},{28,4},{16,8},{20,12},{8,16},{12,20},{0,24},{4,28},{25,1},{... | collective-permute-start | bytes 307208 | tf_op jit(solution)/shard_map/ppermute | solution.py:112
  54.7 0.8 %convert_add_fusion = f32[32,2048]{1,0:T(8,128)} fusion(bf16[32,2048]{1,0:T(8,128)(2,1)S(1)} %collective-permute-done.12, bf16[32,2048]{1,0:T(8,128)(2,1)S(1)} %collective-permute-done.11, f32[32,2048]{1,0:T(8,128)S(1)} %get-tuple-element.66, bf16[32,2048]{1,0:T(8,128)(2,1)S(1)} %collective-permute-done.10), kind=kLoop, calls=%fused_computation | loop fusion | flops 393216 | bytes 917504 | tf_op jit(solution)/shard_map/add | solution.py:581
  55.4 0.9 %add.21 = f32[256,512]{1,0:T(8,128)} add(f32[256,512]{1,0:T(8,128)S(1)} %get-tuple-element.88, f32[256,512]{1,0:T(8,128)S(1)} %collective-permute-done.20) | non-fusion elementwise | flops 131072 | bytes 1572864 | tf_op jit(solution)/shard_map/add | solution.py:577
  56.3 2.9 %collective-permute-done.19.refs_3_ = bf16[400,128]{1,0:T(8,128)(2,1)S(1)} collective-permute-done((bf16[400,128]{1,0:T(8,128)(2,1)S(1)}, bf16[400,128]{1,0:T(8,128)(2,1)S(1)}, u32[]{:S(2)}, u32[]{:S(2)}) %collective-permute-start.19) | collective-permute-done | bytes 102432 | tf_op jit(solution)/shard_map/ppermute | solution.py:112
  59.2 0.9 %shard_map.143 = (f32[128,256]{1,0:T(8,128)}, f32[128,256]{1,0:T(8,128)}, f32[128,512]{1,0:T(8,128)}, f32[4,128]{1,0:T(4,128)}, f32[4,128]{1,0:T(4,128)}) custom-call(s32[1]{0:T(128)} %bitcast.1.place_ref, bf16[400,128]{1,0:T(8,128)(2,1)S(1)} %get-tuple-element.90.refs_0_, bf16[400,128]{1,0:T(8,128)(2,1)S(1)} %collective-permute-done.17.refs_1_, ...), custom_call_target="tpu_custom_call" | custom-call | flops 1000000000 | tf_op jit(solution)/shard_map/pallas_call | solution.py:60
  (25 shorter events, 1.9 us)
Async XLA Ops:
  1.8 9.2 %collective-permute-start = (bf16[400,128]{1,0:T(8,128)(2,1)S(1)}, bf16[400,128]{1,0:T(8,128)(2,1)S(1)}, u32[]{:S(2)}, u32[]{:S(2)}) collective-permute-start(bf16[400,128]{1,0:T(8,128)(2,1)S(1)} %get-tuple-element.54), channel_id=1, source_target_pairs={{8,0},{12,4},{0,8},{4,12},{24,16},{28,20},{16,24},{20,28},{9,1},{1... | collective-permute-start | bytes 307208 | tf_op jit(solution)/shard_map/ppermute | solution.py:112
  4.8 6.8 %collective-permute-start.1 = (bf16[400,128]{1,0:T(8,128)(2,1)S(1)}, bf16[400,128]{1,0:T(8,128)(2,1)S(1)}, u32[]{:S(2)}, u32[]{:S(2)}) collective-permute-start(bf16[400,128]{1,0:T(8,128)(2,1)S(1)} %get-tuple-element.55), channel_id=1, source_target_pairs={{16,0},{20,4},{24,8},{28,12},{0,16},{4,20},{8,24},{12,28},{17,1},{... | collective-permute-start | bytes 307208 | tf_op jit(solution)/shard_map/ppermute | solution.py:112
  6.3 5.6 %collective-permute-start.2 = (bf16[400,128]{1,0:T(8,128)(2,1)S(1)}, bf16[400,128]{1,0:T(8,128)(2,1)S(1)}, u32[]{:S(2)}, u32[]{:S(2)}) collective-permute-start(bf16[400,128]{1,0:T(8,128)(2,1)S(1)} %get-tuple-element.56), channel_id=1, source_target_pairs={{24,0},{28,4},{16,8},{20,12},{8,16},{12,20},{0,24},{4,28},{25,1},{... | collective-permute-start | bytes 307208 | tf_op jit(solution)/shard_map/ppermute | solution.py:112
  6.4 11.4 %collective-permute-start.5 = (bf16[32,2048]{1,0:T(8,128)(2,1)}, bf16[32,2048]{1,0:T(8,128)(2,1)S(1)}, u32[]{:S(2)}, u32[]{:S(2)}) collective-permute-start(bf16[32,2048]{1,0:T(8,128)(2,1)} %refs_0_.1), channel_id=1, source_target_pairs={{2,0},{3,1},{0,2},{1,3},{6,4},{7,5},{4,6},{5,7},{10,8},{11,9},{8,1... | collective-permute-start | bytes 393224 | tf_op jit(solution)/shard_map/ppermute | solution.py:498
  9.4 8.3 %collective-permute-start.4 = (bf16[32,2048]{1,0:T(8,128)(2,1)}, bf16[32,2048]{1,0:T(8,128)(2,1)S(1)}, u32[]{:S(2)}, u32[]{:S(2)}) collective-permute-start(bf16[32,2048]{1,0:T(8,128)(2,1)} %refs_0_.1), channel_id=1, source_target_pairs={{1,0},{0,1},{3,2},{2,3},{5,4},{4,5},{7,6},{6,7},{9,8},{8,9},{11,10... | collective-permute-start | bytes 393224 | tf_op jit(solution)/shard_map/ppermute | solution.py:498
  11.0 8.2 %collective-permute-start.6 = (bf16[32,2048]{1,0:T(8,128)(2,1)}, bf16[32,2048]{1,0:T(8,128)(2,1)S(1)}, u32[]{:S(2)}, u32[]{:S(2)}) collective-permute-start(bf16[32,2048]{1,0:T(8,128)(2,1)} %refs_0_.1), channel_id=1, source_target_pairs={{3,0},{2,1},{1,2},{0,3},{7,4},{6,5},{5,6},{4,7},{11,8},{10,9},{9,1... | collective-permute-start | bytes 393224 | tf_op jit(solution)/shard_map/ppermute | solution.py:498
  11.9 7.3 %copy-start = (bf16[512,2048]{1,0:T(8,128)(2,1)S(1)}, bf16[512,2048]{1,0:T(8,128)(2,1)}, u32[]{:S(2)}) copy-start(bf16[512,2048]{1,0:T(8,128)(2,1)} %refs_4_.2) | copy-start | bytes 6291460
  11.9 7.3 %copy-start.1 = (bf16[32,2048]{1,0:T(8,128)(2,1)S(1)}, bf16[32,2048]{1,0:T(8,128)(2,1)}, u32[]{:S(2)}) copy-start(bf16[32,2048]{1,0:T(8,128)(2,1)} %refs_0_.1) | copy-start | bytes 393220
  16.0 3.9 %collective-permute-start.3 = (f32[4,2,128,128]{3,2,1,0:T(8,128)S(1)}, f32[4,2,128,128]{3,2,1,0:T(8,128)S(1)}, u32[]{:S(2)}, u32[]{:S(2)}) collective-permute-start(f32[4,2,128,128]{3,2,1,0:T(8,128)S(1)} %get-tuple-element.57.refs_0_), channel_id=1, source_target_pairs={{4,0},{0,4},{12,8},{8,12},{20,16},{16,20},{28,24},{24,28},{5,1},{1... | collective-permute-start | bytes 1572872 | tf_op jit(solution)/shard_map/ppermute | solution.py:118
  21.3 6.6 %collective-permute-start.7 = (bf16[4,128,128]{2,1,0:T(8,128)(2,1)S(1)}, bf16[4,128,128]{2,1,0:T(8,128)(2,1)S(1)}, u32[]{:S(2)}, u32[]{:S(2)}) collective-permute-start(bf16[4,128,128]{2,1,0:T(8,128)(2,1)S(1)} %get-tuple-element.63), channel_id=1, source_target_pairs={{8,0},{12,4},{0,8},{4,12},{24,16},{28,20},{16,24},{20,28},{9,1},{1... | collective-permute-start | bytes 393224 | tf_op jit(solution)/shard_map/ppermute | solution.py:112
  22.9 8.9 %collective-permute-start.8 = (bf16[4,128,128]{2,1,0:T(8,128)(2,1)S(1)}, bf16[4,128,128]{2,1,0:T(8,128)(2,1)S(1)}, u32[]{:S(2)}, u32[]{:S(2)}) collective-permute-start(bf16[4,128,128]{2,1,0:T(8,128)(2,1)S(1)} %get-tuple-element.64), channel_id=1, source_target_pairs={{16,0},{20,4},{24,8},{28,12},{0,16},{4,20},{8,24},{12,28},{17,1},{... | collective-permute-start | bytes 393224 | tf_op jit(solution)/shard_map/ppermute | solution.py:112
  24.4 7.4 %collective-permute-start.9 = (bf16[4,128,128]{2,1,0:T(8,128)(2,1)S(1)}, bf16[4,128,128]{2,1,0:T(8,128)(2,1)S(1)}, u32[]{:S(2)}, u32[]{:S(2)}) collective-permute-start(bf16[4,128,128]{2,1,0:T(8,128)(2,1)S(1)} %get-tuple-element.65), channel_id=1, source_target_pairs={{24,0},{28,4},{16,8},{20,12},{8,16},{12,20},{0,24},{4,28},{25,1},{... | collective-permute-start | bytes 393224 | tf_op jit(solution)/shard_map/ppermute | solution.py:112
  24.9 12.8 %collective-permute-start.13 = (bf16[768,128]{1,0:T(8,128)(2,1)S(1)}, bf16[768,128]{1,0:T(8,128)(2,1)S(1)}, u32[]{:S(2)}, u32[]{:S(2)}) collective-permute-start(bf16[768,128]{1,0:T(8,128)(2,1)S(1)} %get-tuple-element.76), channel_id=1, source_target_pairs={{8,0},{12,4},{0,8},{4,12},{24,16},{28,20},{16,24},{20,28},{9,1},{1... | collective-permute-start | bytes 589832 | tf_op jit(solution)/shard_map/ppermute | solution.py:112
  26.4 12.5 %collective-permute-start.14 = (bf16[768,128]{1,0:T(8,128)(2,1)S(1)}, bf16[768,128]{1,0:T(8,128)(2,1)S(1)}, u32[]{:S(2)}, u32[]{:S(2)}) collective-permute-start(bf16[768,128]{1,0:T(8,128)(2,1)S(1)} %get-tuple-element.77), channel_id=1, source_target_pairs={{16,0},{20,4},{24,8},{28,12},{0,16},{4,20},{8,24},{12,28},{17,1},{... | collective-permute-start | bytes 589832 | tf_op jit(solution)/shard_map/ppermute | solution.py:112
  27.9 11.0 %collective-permute-start.15 = (bf16[768,128]{1,0:T(8,128)(2,1)S(1)}, bf16[768,128]{1,0:T(8,128)(2,1)S(1)}, u32[]{:S(2)}, u32[]{:S(2)}) collective-permute-start(bf16[768,128]{1,0:T(8,128)(2,1)S(1)} %get-tuple-element.78), channel_id=1, source_target_pairs={{24,0},{28,4},{16,8},{20,12},{8,16},{12,20},{0,24},{4,28},{25,1},{... | collective-permute-start | bytes 589832 | tf_op jit(solution)/shard_map/ppermute | solution.py:112
  32.3 5.3 %collective-permute-start.10 = (bf16[32,2048]{1,0:T(8,128)(2,1)S(1)}, bf16[32,2048]{1,0:T(8,128)(2,1)S(1)}, u32[]{:S(2)}, u32[]{:S(2)}) collective-permute-start(bf16[32,2048]{1,0:T(8,128)(2,1)S(1)} %get-tuple-element.67), channel_id=1, source_target_pairs={{1,0},{0,1},{3,2},{2,3},{5,4},{4,5},{7,6},{6,7},{9,8},{8,9},{11,10... | collective-permute-start | bytes 393224 | tf_op jit(solution)/shard_map/ppermute | solution.py:498
  39.1 5.1 %collective-permute-start.16 = (f32[4,128,128]{2,1,0:T(8,128)S(1)}, f32[4,128,128]{2,1,0:T(8,128)S(1)}, u32[]{:S(2)}, u32[]{:S(2)}) collective-permute-start(f32[4,128,128]{2,1,0:T(8,128)S(1)} %shard_map.140.refs_2_), channel_id=1, source_target_pairs={{4,0},{0,4},{12,8},{8,12},{20,16},{16,20},{28,24},{24,28},{5,1},{1... | collective-permute-start | bytes 786440 | tf_op jit(solution)/shard_map/ppermute | solution.py:118
  39.2 14.4 %collective-permute-start.11 = (bf16[32,2048]{1,0:T(8,128)(2,1)S(1)}, bf16[32,2048]{1,0:T(8,128)(2,1)S(1)}, u32[]{:S(2)}, u32[]{:S(2)}) collective-permute-start(bf16[32,2048]{1,0:T(8,128)(2,1)S(1)} %get-tuple-element.68), channel_id=1, source_target_pairs={{2,0},{3,1},{0,2},{1,3},{6,4},{7,5},{4,6},{5,7},{10,8},{11,9},{8,1... | collective-permute-start | bytes 393224 | tf_op jit(solution)/shard_map/ppermute | solution.py:498
  43.7 11.0 %collective-permute-start.12 = (bf16[32,2048]{1,0:T(8,128)(2,1)S(1)}, bf16[32,2048]{1,0:T(8,128)(2,1)S(1)}, u32[]{:S(2)}, u32[]{:S(2)}) collective-permute-start(bf16[32,2048]{1,0:T(8,128)(2,1)S(1)} %get-tuple-element.69), channel_id=1, source_target_pairs={{3,0},{2,1},{1,2},{0,3},{7,4},{6,5},{5,6},{4,7},{11,8},{10,9},{9,1... | collective-permute-start | bytes 393224 | tf_op jit(solution)/shard_map/ppermute | solution.py:498
  49.4 6.1 %collective-permute-start.20 = (f32[256,512]{1,0:T(8,128)S(1)}, f32[256,512]{1,0:T(8,128)S(1)}, u32[]{:S(2)}, u32[]{:S(2)}) collective-permute-start(f32[256,512]{1,0:T(8,128)S(1)} %get-tuple-element.89), channel_id=1, source_target_pairs={{4,0},{0,4},{12,8},{8,12},{20,16},{16,20},{28,24},{24,28},{5,1},{1... | collective-permute-start | bytes 1572872 | tf_op jit(solution)/shard_map/ppermute | solution.py:118
  49.5 6.9 %collective-permute-start.17 = (bf16[400,128]{1,0:T(8,128)(2,1)S(1)}, bf16[400,128]{1,0:T(8,128)(2,1)S(1)}, u32[]{:S(2)}, u32[]{:S(2)}) collective-permute-start(bf16[400,128]{1,0:T(8,128)(2,1)S(1)} %get-tuple-element.81), channel_id=1, source_target_pairs={{8,0},{12,4},{0,8},{4,12},{24,16},{28,20},{16,24},{20,28},{9,1},{1... | collective-permute-start | bytes 307208 | tf_op jit(solution)/shard_map/ppermute | solution.py:112
  50.3 6.0 %collective-permute-start.18 = (bf16[400,128]{1,0:T(8,128)(2,1)S(1)}, bf16[400,128]{1,0:T(8,128)(2,1)S(1)}, u32[]{:S(2)}, u32[]{:S(2)}) collective-permute-start(bf16[400,128]{1,0:T(8,128)(2,1)S(1)} %get-tuple-element.82), channel_id=1, source_target_pairs={{16,0},{20,4},{24,8},{28,12},{0,16},{4,20},{8,24},{12,28},{17,1},{... | collective-permute-start | bytes 307208 | tf_op jit(solution)/shard_map/ppermute | solution.py:112
  53.6 5.6 %collective-permute-start.19 = (bf16[400,128]{1,0:T(8,128)(2,1)S(1)}, bf16[400,128]{1,0:T(8,128)(2,1)S(1)}, u32[]{:S(2)}, u32[]{:S(2)}) collective-permute-start(bf16[400,128]{1,0:T(8,128)(2,1)S(1)} %get-tuple-element.83), channel_id=1, source_target_pairs={{24,0},{28,4},{16,8},{20,12},{8,16},{12,20},{0,24},{4,28},{25,1},{... | collective-permute-start | bytes 307208 | tf_op jit(solution)/shard_map/ppermute | solution.py:112

commit v12 on v10

--- a/solution.py
+++ b/solution.py
@@ -321,7 +321,7 @@
 
 
 def d_out(ref):
-    return ref[:DV], ref[DV : 2 * DV]
+    return ref[:DV], ref[DV:]
 
 
 def backward_kernel(plan, off_ref, place_ref, mate_ref, *refs):
@@ -408,16 +408,23 @@
 
 
 def cotangent_kernel(plan, parts, head_ref, place_ref, *refs):
-    pieces, w_ref, outs, (all_ref, out_ref) = refs[:parts], refs[parts], refs[parts + 1 : -2], refs[-2:]
+    pieces, w_ref, outs, (all_ref, core_ref) = refs[:parts], refs[parts], refs[parts + 1 : -2], refs[-2:]
     gather_rows(head_ref[0], pieces, all_ref)
     high, low = halves(dot(w_ref[...], all_ref[...], 1, 1))
-    share = all_ref.shape[1] // plan.hv
     for m in range(plan.hv):
-        out_ref[m, :DV] = high[m * DV : (m + 1) * DV]
-        out_ref[m, DV : 2 * DV] = low[m * DV : (m + 1) * DV]
+        core_ref[m, :DV] = high[m * DV : (m + 1) * DV]
+        core_ref[m, DV:] = low[m * DV : (m + 1) * DV]
+    hand_out(plan, place_ref[0], core_ref, outs)
+
+
+def turn_kernel(plan, parts, head_ref, place_ref, *refs):
+    pieces, outs, (all_ref, turned_ref) = refs[:parts], refs[parts:-2], refs[-2:]
+    gather_rows(head_ref[0], pieces, all_ref)
+    share = turned_ref.shape[1]
+    for m in range(plan.hv):
         part = all_ref[:, m * share : (m + 1) * share].astype(F32)
-        out_ref[m, 2 * DV :] = jnp.transpose(part).astype(BF16)
-    hand_out(plan, place_ref[0], out_ref, outs)
+        turned_ref[m] = jnp.transpose(part).astype(BF16)
+    hand_out(plan, place_ref[0], turned_ref, outs)
 
 
 def project_kernel(plan, parts, head_ref, place_ref, *refs):
@@ -440,7 +447,7 @@
 
 def weight_kernel(plan, place_ref, mate_ref, *refs):
     hv = plan.hv
-    cot_refs, mixed_refs, outs, all_ref = refs[:hv], refs[hv : 2 * hv], refs[2 * hv : -1], refs[-1]
+    turned, mixed_refs, outs, all_ref = refs[:hv], refs[hv : 2 * hv], refs[2 * hv : -1], refs[-1]
     for d, ref in enumerate(mixed_refs):
         head = plan.ring.source(place_ref[0], d)
         for k in range(hv):
@@ -448,11 +455,11 @@
     share = outs[0].shape[0]
     for d, out_ref in enumerate(outs):
         at = lax.rem(mate_ref[0] + plan.mates - d, plan.mates) * share
-        at = 2 * DV + pl.multiple_of(at, share)
+        at = pl.multiple_of(at, share)
         total = None
         for k in range(hv):
             mixed = all_ref[k].reshape(hv * DV, plan.tok)
-            part = dot(cot_refs[k][pl.ds(at, share), :], mixed, 1, 1)
+            part = dot(turned[k][pl.ds(at, share), :], mixed, 1, 1)
             total = part if total is None else total + part
         out_ref[...] = total
 
@@ -519,15 +526,15 @@
     )(doc_offsets, place, mate, *got)
     links = [link] + [plan.from_mate(link, d) for d in range(1, s)]
 
-    cot = call(
+    d_core = call(
         partial(cotangent_kernel, plan, parts),
-        [arr(BF16, 2 * DV + model // hv, tok)] * hv,
+        [arr(BF16, 2 * DV, tok)] * hv,
         smem=(0, 1),
-        scratch=[vmem(BF16, tok, model), vmem(BF16, hv, 2 * DV + model // hv, tok)],
+        scratch=[vmem(BF16, tok, model), vmem(BF16, hv, 2 * DV, tok)],
         flops=30_000_000_000,
     )(head, place, *rows, after(out_weight, link))
-    kept = after(kept, cot[0])
-    cot = plan.exchange(cot)
+    kept = after(kept, d_core[0])
+    d_core = plan.exchange(d_core)
 
     states, *mixed = call(
         partial(scan_kernel, plan),
@@ -536,10 +543,18 @@
         scratch=[vmem(F32, s, hv, 2, DK, DK), vmem(F32, n, DV, DK)],
         flops=2_500_000_000,
     )(place, mate, *links, kept)
+    turned = call(
+        partial(turn_kernel, plan, parts),
+        [arr(BF16, model // hv, tok)] * hv,
+        smem=(0, 1),
+        scratch=[vmem(BF16, tok, model), vmem(BF16, hv, model // hv, tok)],
+        flops=1_000_000_000,
+    )(head, place, *after(rows, states))
     mixed = plan.exchange(mixed)
+    turned = plan.exchange(turned)
     back = call(
         partial(state_cotangent_kernel, plan), arr(F32, hv, DV, DK), flops=30_000_000_000
-    )(kept, *after(cot, mixed[1]))
+    )(kept, *after(d_core, states))
     backs = [back] + [plan.from_mate(back, d) for d in range(1, s)]
 
     projected = call(
@@ -562,7 +577,7 @@
             vmem(F32, n, DV, DK),
         ],
         flops=6_000_000_000,
-    )(doc_offsets, place, mate, *links, *backs, *got, *cot, kept, after(states, projected[1]))
+    )(doc_offsets, place, mate, *links, *backs, *got, *d_core, kept, after(states, projected[1]))
 
     shares = call(
         partial(weight_kernel, plan),
@@ -570,7 +585,7 @@
         smem=(0, 1),
         scratch=[vmem(BF16, hv, hv, DV, tok)],
         flops=1_000_000_000,
-    )(place, mate, *cot, *mixed)
+    )(place, mate, *turned, *mixed)
     grads = plan.exchange(after(grads, shares[0]))
     weight_grad = shares[0]
     for d in range(1, s):
@@ -579,7 +594,7 @@
     layer_out = layer_parts[0]
     for part in layer_parts[1:]:
         layer_out = layer_out + part.astype(F32)
-    grads = after(grads, layer_out)
+    grads = after(grads, (layer_out, weight_grad))
     grad_q, grad_k, grad_v, grad_rate, grad_decay = call(
         partial(finish_kernel, plan),
         (

time: 58.3 us -> 58.4 us (level)
  waiting for transfers between devices: 12.7 us -> 9.32 us
  starting transfers between devices: 28.8 us -> 32 us
    ppermute x12 -> x15, waiting for transfers between devices: 6.6 us -> 3.8 us  [exchange(): moved.append(lax.ppermute(pieces[d], 'ctx', pairs))]
    ppermute x6, starting transfers between devices: 10.9 us -> 12.8 us  [across_heads(): lax.ppermute(pieces[d], 'head', Ring(parts).pairs(d))]
    ppermute x12 -> x15, starting transfers between devices: 17.6 us -> 19 us  [exchange(): moved.append(lax.ppermute(pieces[d], 'ctx', pairs))]
    pallas_call x9 -> x10, Pallas kernels: 14.2 us -> 14.5 us  [run(): pl.pallas_call(kernel, out_shape=outs, in_specs=[spec(i) for i in range(l...]
  transfers between devices with their start and end apart: 21 -> 24, of which waited for: 9 -> 6; matrix products, arithmetic and copies ran while one was open for 1% -> 3% of each run, Pallas kernels for 23% -> 21%
where the time goes in v12:
time: 58.4 us; the launch traced here: 58.3 us
  starting transfers between devices  32 us (55%)
  Pallas kernels  14.5 us (25%)
  waiting for transfers between devices  9.32 us (16%)
  other arithmetic  1.63 us (3%)
  between operations  0.8 us (1%)
    ppermute x15, starting transfers between devices, exchange(): moved.append(lax.ppermute(pieces[d], 'ctx', pairs))  19 us
    pallas_call x10, Pallas kernels, run(): pl.pallas_call(kernel, out_shape=outs, in_specs=[spec(i) for i in range(l...  14.5 us
    ppermute x6, starting transfers between devices, across_heads(): lax.ppermute(pieces[d], 'head', Ring(parts).pairs(d))  12.8 us
    ppermute x6, waiting for transfers between devices, across_heads(): lax.ppermute(pieces[d], 'head', Ring(parts).pairs(d))  5.51 us
    ppermute x15, waiting for transfers between devices, exchange(): moved.append(lax.ppermute(pieces[d], 'ctx', pairs))  3.8 us
  transfers between devices with their start and end apart: 24, of which 6 were waited for; matrix products, arithmetic and copies ran while one was open for 3% of the time, Pallas kernels for 21%

profile of v12, /device:TPU:0, one launch (start us, length us, event | category | flops | bytes accessed | tf_op | source)
XLA Modules:
  0.0 58.3 jit_solution(6785006686057060672)
XLA Ops:
  0.6 1.2 %shard_map.135 = (bf16[400,128]{1,0:T(8,128)(2,1)S(1)}, bf16[400,128]{1,0:T(8,128)(2,1)S(1)}, bf16[400,128]{1,0:T(8,128)(2,1)S(1)}, bf16[400,128]{1,0:T(8,128)(2,1)S(1)}) custom-call(s32[1]{0:T(128)} %bitcast.1.place_ref, bf16[128,256]{1,0:T(8,128)(2,1)} %q_ref.1, bf16[128,256]{1,0:T(8,128)(2,1)} %k_ref.1, bf16[128,512]{1,0:T(8,128)(2,1)} %v_ref.1, ...), custom_call_target="tpu_custom_call" | custom-call | tf_op jit(solution)/shard_map/pallas_call | solution.py:60
  1.8 3.0 %collective-permute-start = (bf16[400,128]{1,0:T(8,128)(2,1)S(1)}, bf16[400,128]{1,0:T(8,128)(2,1)S(1)}, u32[]{:S(2)}, u32[]{:S(2)}) collective-permute-start(bf16[400,128]{1,0:T(8,128)(2,1)S(1)} %get-tuple-element.61), channel_id=1, source_target_pairs={{8,0},{12,4},{0,8},{4,12},{24,16},{28,20},{16,24},{20,28},{9,1},{1... | collective-permute-start | bytes 307208 | tf_op jit(solution)/shard_map/ppermute | solution.py:112
  4.8 1.5 %collective-permute-start.1 = (bf16[400,128]{1,0:T(8,128)(2,1)S(1)}, bf16[400,128]{1,0:T(8,128)(2,1)S(1)}, u32[]{:S(2)}, u32[]{:S(2)}) collective-permute-start(bf16[400,128]{1,0:T(8,128)(2,1)S(1)} %get-tuple-element.62), channel_id=1, source_target_pairs={{16,0},{20,4},{24,8},{28,12},{0,16},{4,20},{8,24},{12,28},{17,1},{... | collective-permute-start | bytes 307208 | tf_op jit(solution)/shard_map/ppermute | solution.py:112
  6.4 2.0 %collective-permute-start.4 = (bf16[32,2048]{1,0:T(8,128)(2,1)}, bf16[32,2048]{1,0:T(8,128)(2,1)S(1)}, u32[]{:S(2)}, u32[]{:S(2)}) collective-permute-start(bf16[32,2048]{1,0:T(8,128)(2,1)} %refs_0_.2), channel_id=1, source_target_pairs={{1,0},{0,1},{3,2},{2,3},{5,4},{4,5},{7,6},{6,7},{9,8},{8,9},{11,10... | collective-permute-start | bytes 393224 | tf_op jit(solution)/shard_map/ppermute | solution.py:505
  8.4 2.6 %collective-permute-start.5 = (bf16[32,2048]{1,0:T(8,128)(2,1)}, bf16[32,2048]{1,0:T(8,128)(2,1)S(1)}, u32[]{:S(2)}, u32[]{:S(2)}) collective-permute-start(bf16[32,2048]{1,0:T(8,128)(2,1)} %refs_0_.2), channel_id=1, source_target_pairs={{2,0},{3,1},{0,2},{1,3},{6,4},{7,5},{4,6},{5,7},{10,8},{11,9},{8,1... | collective-permute-start | bytes 393224 | tf_op jit(solution)/shard_map/ppermute | solution.py:505
  11.0 0.6 %collective-permute-start.6 = (bf16[32,2048]{1,0:T(8,128)(2,1)}, bf16[32,2048]{1,0:T(8,128)(2,1)S(1)}, u32[]{:S(2)}, u32[]{:S(2)}) collective-permute-start(bf16[32,2048]{1,0:T(8,128)(2,1)} %refs_0_.2), channel_id=1, source_target_pairs={{3,0},{2,1},{1,2},{0,3},{7,4},{6,5},{5,6},{4,7},{11,8},{10,9},{9,1... | collective-permute-start | bytes 393224 | tf_op jit(solution)/shard_map/ppermute | solution.py:505
  11.9 4.1 %shard_map.136 = (f32[4,2,128,128]{3,2,1,0:T(8,128)S(1)}, f32[4,7,128,128]{3,2,1,0:T(8,128)S(1)}) custom-call(s32[5]{0:T(128)} %off_ref.3, s32[1]{0:T(128)} %bitcast.1.place_ref, s32[1]{0:T(128)} %bitcast.2.mate_ref, bf16[400,128]{1,0:T(8,128)(2,1)S(1)} %get-tuple-element.60.refs_0_.refs_4_, bf16[400,128]{1,0:T(8,128)(2,1)S(1)} %collective-permute-done.refs_1_.refs_5_, ...), custom_call_target="tpu_custom_call" | custom-call | flops 20000000000 | tf_op jit(solution)/shard_map/pallas_call | solution.py:60
  16.1 4.6 %collective-permute-done.5.refs_2_ = bf16[32,2048]{1,0:T(8,128)(2,1)S(1)} collective-permute-done((bf16[32,2048]{1,0:T(8,128)(2,1)}, bf16[32,2048]{1,0:T(8,128)(2,1)S(1)}, u32[]{:S(2)}, u32[]{:S(2)}) %collective-permute-start.5) | collective-permute-done | bytes 131104 | tf_op jit(solution)/shard_map/ppermute | solution.py:505
  20.7 0.8 %shard_map.137 = (bf16[256,128]{1,0:T(8,128)(2,1)S(1)}, bf16[256,128]{1,0:T(8,128)(2,1)S(1)}, bf16[256,128]{1,0:T(8,128)(2,1)S(1)}, bf16[256,128]{1,0:T(8,128)(2,1)S(1)}) custom-call(s32[1]{0:T(128)} %bitcast.head_ref, s32[1]{0:T(128)} %bitcast.1.place_ref, bf16[32,2048]{1,0:T(8,128)(2,1)S(1)} %copy-done.1, ...), custom_call_target="tpu_custom_call" | custom-call | flops 30000001024 | tf_op jit(solution)/shard_map/pallas_call | solution.py:60
  21.5 1.6 %collective-permute-start.13 = (bf16[256,128]{1,0:T(8,128)(2,1)S(1)}, bf16[256,128]{1,0:T(8,128)(2,1)S(1)}, u32[]{:S(2)}, u32[]{:S(2)}) collective-permute-start(bf16[256,128]{1,0:T(8,128)(2,1)S(1)} %get-tuple-element.77), channel_id=1, source_target_pairs={{8,0},{12,4},{0,8},{4,12},{24,16},{28,20},{16,24},{20,28},{9,1},{1... | collective-permute-start | bytes 196616 | tf_op jit(solution)/shard_map/ppermute | solution.py:112
  23.1 1.5 %collective-permute-start.14 = (bf16[256,128]{1,0:T(8,128)(2,1)S(1)}, bf16[256,128]{1,0:T(8,128)(2,1)S(1)}, u32[]{:S(2)}, u32[]{:S(2)}) collective-permute-start(bf16[256,128]{1,0:T(8,128)(2,1)S(1)} %get-tuple-element.78), channel_id=1, source_target_pairs={{16,0},{20,4},{24,8},{28,12},{0,16},{4,20},{8,24},{12,28},{17,1},{... | collective-permute-start | bytes 196616 | tf_op jit(solution)/shard_map/ppermute | solution.py:112
  24.6 0.5 collective-permute-start.15
  25.1 1.3 %shard_map.138 = (f32[4,128,128]{2,1,0:T(8,128)S(1)}, bf16[4,128,128]{2,1,0:T(8,128)(2,1)S(1)}, bf16[4,128,128]{2,1,0:T(8,128)(2,1)S(1)}, bf16[4,128,128]{2,1,0:T(8,128)(2,1)S(1)}, bf16[4,128,128]{2,1,0:T(8,128)(2,1)S(1)}) custom-call(s32[1]{0:T(128)} %bitcast.1.place_ref, s32[1]{0:T(128)} %bitcast.2.mate_ref, ...), custom_call_target="tpu_custom_call" | custom-call | flops 2500000000 | tf_op jit(solution)/shard_map/pallas_call | solution.py:60
  26.4 1.6 %collective-permute-start.7 = (bf16[4,128,128]{2,1,0:T(8,128)(2,1)S(1)}, bf16[4,128,128]{2,1,0:T(8,128)(2,1)S(1)}, u32[]{:S(2)}, u32[]{:S(2)}) collective-permute-start(bf16[4,128,128]{2,1,0:T(8,128)(2,1)S(1)} %get-tuple-element.70), channel_id=1, source_target_pairs={{8,0},{12,4},{0,8},{4,12},{24,16},{28,20},{16,24},{20,28},{9,1},{1... | collective-permute-start | bytes 393224 | tf_op jit(solution)/shard_map/ppermute | solution.py:112
  27.9 1.5 %collective-permute-start.8 = (bf16[4,128,128]{2,1,0:T(8,128)(2,1)S(1)}, bf16[4,128,128]{2,1,0:T(8,128)(2,1)S(1)}, u32[]{:S(2)}, u32[]{:S(2)}) collective-permute-start(bf16[4,128,128]{2,1,0:T(8,128)(2,1)S(1)} %get-tuple-element.71), channel_id=1, source_target_pairs={{16,0},{20,4},{24,8},{28,12},{0,16},{4,20},{8,24},{12,28},{17,1},{... | collective-permute-start | bytes 393224 | tf_op jit(solution)/shard_map/ppermute | solution.py:112
  30.7 1.4 %collective-permute-start.17 = (bf16[512,128]{1,0:T(8,128)(2,1)S(1)}, bf16[512,128]{1,0:T(8,128)(2,1)S(1)}, u32[]{:S(2)}, u32[]{:S(2)}) collective-permute-start(bf16[512,128]{1,0:T(8,128)(2,1)S(1)} %get-tuple-element.95), channel_id=1, source_target_pairs={{8,0},{12,4},{0,8},{4,12},{24,16},{28,20},{16,24},{20,28},{9,1},{1... | collective-permute-start | bytes 393224 | tf_op jit(solution)/shard_map/ppermute | solution.py:112
  32.1 1.5 %collective-permute-start.18 = (bf16[512,128]{1,0:T(8,128)(2,1)S(1)}, bf16[512,128]{1,0:T(8,128)(2,1)S(1)}, u32[]{:S(2)}, u32[]{:S(2)}) collective-permute-start(bf16[512,128]{1,0:T(8,128)(2,1)S(1)} %get-tuple-element.96), channel_id=1, source_target_pairs={{16,0},{20,4},{24,8},{28,12},{0,16},{4,20},{8,24},{12,28},{17,1},{... | collective-permute-start | bytes 393224 | tf_op jit(solution)/shard_map/ppermute | solution.py:112
  33.7 0.7 %collective-permute-start.19 = (bf16[512,128]{1,0:T(8,128)(2,1)S(1)}, bf16[512,128]{1,0:T(8,128)(2,1)S(1)}, u32[]{:S(2)}, u32[]{:S(2)}) collective-permute-start(bf16[512,128]{1,0:T(8,128)(2,1)S(1)} %get-tuple-element.97), channel_id=1, source_target_pairs={{24,0},{28,4},{16,8},{20,12},{8,16},{12,20},{0,24},{4,28},{25,1},{... | collective-permute-start | bytes 393224 | tf_op jit(solution)/shard_map/ppermute | solution.py:112
  34.4 1.5 %collective-permute-done.9.refs_3_.refs_7_ = bf16[4,128,128]{2,1,0:T(8,128)(2,1)S(1)} collective-permute-done((bf16[4,128,128]{2,1,0:T(8,128)(2,1)S(1)}, bf16[4,128,128]{2,1,0:T(8,128)(2,1)S(1)}, u32[]{:S(2)}, u32[]{:S(2)}) %collective-permute-start.9) | collective-permute-done | bytes 131104 | tf_op jit(solution)/shard_map/ppermute | solution.py:112
  35.9 0.5 shard_map.139
  36.4 2.2 %collective-permute-start.10 = (bf16[32,2048]{1,0:T(8,128)(2,1)S(1)}, bf16[32,2048]{1,0:T(8,128)(2,1)S(1)}, u32[]{:S(2)}, u32[]{:S(2)}) collective-permute-start(bf16[32,2048]{1,0:T(8,128)(2,1)S(1)} %get-tuple-element.74), channel_id=1, source_target_pairs={{1,0},{0,1},{3,2},{2,3},{5,4},{4,5},{7,6},{6,7},{9,8},{8,9},{11,10... | collective-permute-start | bytes 393224 | tf_op jit(solution)/shard_map/ppermute | solution.py:505
  38.6 2.5 %collective-permute-start.12 = (bf16[32,2048]{1,0:T(8,128)(2,1)S(1)}, bf16[32,2048]{1,0:T(8,128)(2,1)S(1)}, u32[]{:S(2)}, u32[]{:S(2)}) collective-permute-start(bf16[32,2048]{1,0:T(8,128)(2,1)S(1)} %get-tuple-element.76), channel_id=1, source_target_pairs={{3,0},{2,1},{1,2},{0,3},{7,4},{6,5},{5,6},{4,7},{11,8},{10,9},{9,1... | collective-permute-start | bytes 393224 | tf_op jit(solution)/shard_map/ppermute | solution.py:505
  41.0 3.0 %collective-permute-start.11 = (bf16[32,2048]{1,0:T(8,128)(2,1)S(1)}, bf16[32,2048]{1,0:T(8,128)(2,1)S(1)}, u32[]{:S(2)}, u32[]{:S(2)}) collective-permute-start(bf16[32,2048]{1,0:T(8,128)(2,1)S(1)} %get-tuple-element.75), channel_id=1, source_target_pairs={{2,0},{3,1},{0,2},{1,3},{6,4},{7,5},{4,6},{5,7},{10,8},{11,9},{8,1... | collective-permute-start | bytes 393224 | tf_op jit(solution)/shard_map/ppermute | solution.py:505
  44.1 0.7 %shard_map.143 = (f32[256,512]{1,0:T(8,128)S(1)}, f32[256,512]{1,0:T(8,128)S(1)}) custom-call(s32[1]{0:T(128)} %bitcast.1.place_ref, s32[1]{0:T(128)} %bitcast.2.mate_ref, bf16[512,128]{1,0:T(8,128)(2,1)S(1)} %get-tuple-element.94.refs_0_, bf16[512,128]{1,0:T(8,128)(2,1)S(1)} %collective-permute-done.17.refs_1_, ...), custom_call_target="tpu_custom_call" | custom-call | flops 1000000000 | tf_op jit(solution)/shard_map/pallas_call | solution.py:60
  44.9 4.4 %shard_map.141 = (bf16[400,128]{1,0:T(8,128)(2,1)S(1)}, bf16[400,128]{1,0:T(8,128)(2,1)S(1)}, bf16[400,128]{1,0:T(8,128)(2,1)S(1)}, bf16[400,128]{1,0:T(8,128)(2,1)S(1)}) custom-call(s32[5]{0:T(128)} %off_ref.3, s32[1]{0:T(128)} %bitcast.1.place_ref, s32[1]{0:T(128)} %bitcast.2.mate_ref, f32[4,2,128,128]{3,2,1,0:T(8,128)S(1)} %get-tuple-element.64.refs_0_, ...), custom_call_target="tpu_custom_call" | custom-call | flops 6000000000 | tf_op jit(solution)/shard_map/pallas_call | solution.py:60
  49.4 1.5 %collective-permute-start.21 = (bf16[400,128]{1,0:T(8,128)(2,1)S(1)}, bf16[400,128]{1,0:T(8,128)(2,1)S(1)}, u32[]{:S(2)}, u32[]{:S(2)}) collective-permute-start(bf16[400,128]{1,0:T(8,128)(2,1)S(1)} %get-tuple-element.101), channel_id=1, source_target_pairs={{16,0},{20,4},{24,8},{28,12},{0,16},{4,20},{8,24},{12,28},{17,1},{... | collective-permute-start | bytes 307208 | tf_op jit(solution)/shard_map/ppermute | solution.py:112
  50.9 0.9 %collective-permute-done.11 = bf16[32,2048]{1,0:T(8,128)(2,1)S(1)} collective-permute-done((bf16[32,2048]{1,0:T(8,128)(2,1)S(1)}, bf16[32,2048]{1,0:T(8,128)(2,1)S(1)}, u32[]{:S(2)}, u32[]{:S(2)}) %collective-permute-start.11) | collective-permute-done | bytes 131104 | tf_op jit(solution)/shard_map/ppermute | solution.py:505
  51.8 2.1 %collective-permute-start.22 = (bf16[400,128]{1,0:T(8,128)(2,1)S(1)}, bf16[400,128]{1,0:T(8,128)(2,1)S(1)}, u32[]{:S(2)}, u32[]{:S(2)}) collective-permute-start(bf16[400,128]{1,0:T(8,128)(2,1)S(1)} %get-tuple-element.102), channel_id=1, source_target_pairs={{24,0},{28,4},{16,8},{20,12},{8,16},{12,20},{0,24},{4,28},{25,1},{... | collective-permute-start | bytes 307208 | tf_op jit(solution)/shard_map/ppermute | solution.py:112
  53.9 0.8 %convert_add_fusion = f32[32,2048]{1,0:T(8,128)} fusion(bf16[32,2048]{1,0:T(8,128)(2,1)S(1)} %collective-permute-done.12, bf16[32,2048]{1,0:T(8,128)(2,1)S(1)} %collective-permute-done.11, f32[32,2048]{1,0:T(8,128)S(1)} %get-tuple-element.73, bf16[32,2048]{1,0:T(8,128)(2,1)S(1)} %collective-permute-done.10), kind=kLoop, calls=%fused_computation | loop fusion | flops 393216 | bytes 917504 | tf_op jit(solution)/shard_map/add | solution.py:596
  54.7 0.9 %add.21 = f32[256,512]{1,0:T(8,128)} add(f32[256,512]{1,0:T(8,128)S(1)} %get-tuple-element.98, f32[256,512]{1,0:T(8,128)S(1)} %collective-permute-done.23) | non-fusion elementwise | flops 131072 | bytes 1572864 | tf_op jit(solution)/shard_map/add | solution.py:592
  55.6 1.8 %collective-permute-done.22.refs_3_ = bf16[400,128]{1,0:T(8,128)(2,1)S(1)} collective-permute-done((bf16[400,128]{1,0:T(8,128)(2,1)S(1)}, bf16[400,128]{1,0:T(8,128)(2,1)S(1)}, u32[]{:S(2)}, u32[]{:S(2)}) %collective-permute-start.22) | collective-permute-done | bytes 102432 | tf_op jit(solution)/shard_map/ppermute | solution.py:112
  57.4 0.9 %shard_map.144 = (f32[128,256]{1,0:T(8,128)}, f32[128,256]{1,0:T(8,128)}, f32[128,512]{1,0:T(8,128)}, f32[4,128]{1,0:T(4,128)}, f32[4,128]{1,0:T(4,128)}) custom-call(s32[1]{0:T(128)} %bitcast.1.place_ref, bf16[400,128]{1,0:T(8,128)(2,1)S(1)} %get-tuple-element.104.refs_0_, bf16[400,128]{1,0:T(8,128)(2,1)S(1)} %collective-permute-done.20.refs_1_, ...), custom_call_target="tpu_custom_call" | custom-call | flops 1000000000 | tf_op jit(solution)/shard_map/pallas_call | solution.py:60
  (32 shorter events, 1.8 us)
Async XLA Ops:
  1.8 9.2 %collective-permute-start = (bf16[400,128]{1,0:T(8,128)(2,1)S(1)}, bf16[400,128]{1,0:T(8,128)(2,1)S(1)}, u32[]{:S(2)}, u32[]{:S(2)}) collective-permute-start(bf16[400,128]{1,0:T(8,128)(2,1)S(1)} %get-tuple-element.61), channel_id=1, source_target_pairs={{8,0},{12,4},{0,8},{4,12},{24,16},{28,20},{16,24},{20,28},{9,1},{1... | collective-permute-start | bytes 307208 | tf_op jit(solution)/shard_map/ppermute | solution.py:112
  4.8 6.8 %collective-permute-start.1 = (bf16[400,128]{1,0:T(8,128)(2,1)S(1)}, bf16[400,128]{1,0:T(8,128)(2,1)S(1)}, u32[]{:S(2)}, u32[]{:S(2)}) collective-permute-start(bf16[400,128]{1,0:T(8,128)(2,1)S(1)} %get-tuple-element.62), channel_id=1, source_target_pairs={{16,0},{20,4},{24,8},{28,12},{0,16},{4,20},{8,24},{12,28},{17,1},{... | collective-permute-start | bytes 307208 | tf_op jit(solution)/shard_map/ppermute | solution.py:112
  6.3 5.6 %collective-permute-start.2 = (bf16[400,128]{1,0:T(8,128)(2,1)S(1)}, bf16[400,128]{1,0:T(8,128)(2,1)S(1)}, u32[]{:S(2)}, u32[]{:S(2)}) collective-permute-start(bf16[400,128]{1,0:T(8,128)(2,1)S(1)} %get-tuple-element.63), channel_id=1, source_target_pairs={{24,0},{28,4},{16,8},{20,12},{8,16},{12,20},{0,24},{4,28},{25,1},{... | collective-permute-start | bytes 307208 | tf_op jit(solution)/shard_map/ppermute | solution.py:112
  6.4 9.8 %collective-permute-start.4 = (bf16[32,2048]{1,0:T(8,128)(2,1)}, bf16[32,2048]{1,0:T(8,128)(2,1)S(1)}, u32[]{:S(2)}, u32[]{:S(2)}) collective-permute-start(bf16[32,2048]{1,0:T(8,128)(2,1)} %refs_0_.2), channel_id=1, source_target_pairs={{1,0},{0,1},{3,2},{2,3},{5,4},{4,5},{7,6},{6,7},{9,8},{8,9},{11,10... | collective-permute-start | bytes 393224 | tf_op jit(solution)/shard_map/ppermute | solution.py:505
  8.4 12.3 %collective-permute-start.5 = (bf16[32,2048]{1,0:T(8,128)(2,1)}, bf16[32,2048]{1,0:T(8,128)(2,1)S(1)}, u32[]{:S(2)}, u32[]{:S(2)}) collective-permute-start(bf16[32,2048]{1,0:T(8,128)(2,1)} %refs_0_.2), channel_id=1, source_target_pairs={{2,0},{3,1},{0,2},{1,3},{6,4},{7,5},{4,6},{5,7},{10,8},{11,9},{8,1... | collective-permute-start | bytes 393224 | tf_op jit(solution)/shard_map/ppermute | solution.py:505
  11.0 9.7 %collective-permute-start.6 = (bf16[32,2048]{1,0:T(8,128)(2,1)}, bf16[32,2048]{1,0:T(8,128)(2,1)S(1)}, u32[]{:S(2)}, u32[]{:S(2)}) collective-permute-start(bf16[32,2048]{1,0:T(8,128)(2,1)} %refs_0_.2), channel_id=1, source_target_pairs={{3,0},{2,1},{1,2},{0,3},{7,4},{6,5},{5,6},{4,7},{11,8},{10,9},{9,1... | collective-permute-start | bytes 393224 | tf_op jit(solution)/shard_map/ppermute | solution.py:505
  11.9 8.8 %copy-start = (bf16[512,2048]{1,0:T(8,128)(2,1)S(1)}, bf16[512,2048]{1,0:T(8,128)(2,1)}, u32[]{:S(2)}) copy-start(bf16[512,2048]{1,0:T(8,128)(2,1)} %refs_4_.2) | copy-start | bytes 6291460
  11.9 8.8 %copy-start.1 = (bf16[32,2048]{1,0:T(8,128)(2,1)S(1)}, bf16[32,2048]{1,0:T(8,128)(2,1)}, u32[]{:S(2)}) copy-start(bf16[32,2048]{1,0:T(8,128)(2,1)} %refs_0_.2) | copy-start | bytes 393220
  16.0 9.0 %collective-permute-start.3 = (f32[4,2,128,128]{3,2,1,0:T(8,128)S(1)}, f32[4,2,128,128]{3,2,1,0:T(8,128)S(1)}, u32[]{:S(2)}, u32[]{:S(2)}) collective-permute-start(f32[4,2,128,128]{3,2,1,0:T(8,128)S(1)} %get-tuple-element.64.refs_0_), channel_id=1, source_target_pairs={{4,0},{0,4},{12,8},{8,12},{20,16},{16,20},{28,24},{24,28},{5,1},{1... | collective-permute-start | bytes 1572872 | tf_op jit(solution)/shard_map/ppermute | solution.py:118
  21.5 8.0 %collective-permute-start.13 = (bf16[256,128]{1,0:T(8,128)(2,1)S(1)}, bf16[256,128]{1,0:T(8,128)(2,1)S(1)}, u32[]{:S(2)}, u32[]{:S(2)}) collective-permute-start(bf16[256,128]{1,0:T(8,128)(2,1)S(1)} %get-tuple-element.77), channel_id=1, source_target_pairs={{8,0},{12,4},{0,8},{4,12},{24,16},{28,20},{16,24},{20,28},{9,1},{1... | collective-permute-start | bytes 196616 | tf_op jit(solution)/shard_map/ppermute | solution.py:112
  23.1 6.9 %collective-permute-start.14 = (bf16[256,128]{1,0:T(8,128)(2,1)S(1)}, bf16[256,128]{1,0:T(8,128)(2,1)S(1)}, u32[]{:S(2)}, u32[]{:S(2)}) collective-permute-start(bf16[256,128]{1,0:T(8,128)(2,1)S(1)} %get-tuple-element.78), channel_id=1, source_target_pairs={{16,0},{20,4},{24,8},{28,12},{0,16},{4,20},{8,24},{12,28},{17,1},{... | collective-permute-start | bytes 196616 | tf_op jit(solution)/shard_map/ppermute | solution.py:112
  24.6 5.5 %collective-permute-start.15 = (bf16[256,128]{1,0:T(8,128)(2,1)S(1)}, bf16[256,128]{1,0:T(8,128)(2,1)S(1)}, u32[]{:S(2)}, u32[]{:S(2)}) collective-permute-start(bf16[256,128]{1,0:T(8,128)(2,1)S(1)} %get-tuple-element.79), channel_id=1, source_target_pairs={{24,0},{28,4},{16,8},{20,12},{8,16},{12,20},{0,24},{4,28},{25,1},{... | collective-permute-start | bytes 196616 | tf_op jit(solution)/shard_map/ppermute | solution.py:112
  26.4 5.8 %collective-permute-start.7 = (bf16[4,128,128]{2,1,0:T(8,128)(2,1)S(1)}, bf16[4,128,128]{2,1,0:T(8,128)(2,1)S(1)}, u32[]{:S(2)}, u32[]{:S(2)}) collective-permute-start(bf16[4,128,128]{2,1,0:T(8,128)(2,1)S(1)} %get-tuple-element.70), channel_id=1, source_target_pairs={{8,0},{12,4},{0,8},{4,12},{24,16},{28,20},{16,24},{20,28},{9,1},{1... | collective-permute-start | bytes 393224 | tf_op jit(solution)/shard_map/ppermute | solution.py:112
  27.9 5.7 %collective-permute-start.8 = (bf16[4,128,128]{2,1,0:T(8,128)(2,1)S(1)}, bf16[4,128,128]{2,1,0:T(8,128)(2,1)S(1)}, u32[]{:S(2)}, u32[]{:S(2)}) collective-permute-start(bf16[4,128,128]{2,1,0:T(8,128)(2,1)S(1)} %get-tuple-element.71), channel_id=1, source_target_pairs={{16,0},{20,4},{24,8},{28,12},{0,16},{4,20},{8,24},{12,28},{17,1},{... | collective-permute-start | bytes 393224 | tf_op jit(solution)/shard_map/ppermute | solution.py:112
  29.5 6.4 %collective-permute-start.9 = (bf16[4,128,128]{2,1,0:T(8,128)(2,1)S(1)}, bf16[4,128,128]{2,1,0:T(8,128)(2,1)S(1)}, u32[]{:S(2)}, u32[]{:S(2)}) collective-permute-start(bf16[4,128,128]{2,1,0:T(8,128)(2,1)S(1)} %get-tuple-element.72), channel_id=1, source_target_pairs={{24,0},{28,4},{16,8},{20,12},{8,16},{12,20},{0,24},{4,28},{25,1},{... | collective-permute-start | bytes 393224 | tf_op jit(solution)/shard_map/ppermute | solution.py:112
  30.4 14.5 %collective-permute-start.16 = (f32[4,128,128]{2,1,0:T(8,128)S(1)}, f32[4,128,128]{2,1,0:T(8,128)S(1)}, u32[]{:S(2)}, u32[]{:S(2)}) collective-permute-start(f32[4,128,128]{2,1,0:T(8,128)S(1)} %shard_map.140.refs_2_), channel_id=1, source_target_pairs={{4,0},{0,4},{12,8},{8,12},{20,16},{16,20},{28,24},{24,28},{5,1},{1... | collective-permute-start | bytes 786440 | tf_op jit(solution)/shard_map/ppermute | solution.py:118
  30.7 7.9 %collective-permute-start.17 = (bf16[512,128]{1,0:T(8,128)(2,1)S(1)}, bf16[512,128]{1,0:T(8,128)(2,1)S(1)}, u32[]{:S(2)}, u32[]{:S(2)}) collective-permute-start(bf16[512,128]{1,0:T(8,128)(2,1)S(1)} %get-tuple-element.95), channel_id=1, source_target_pairs={{8,0},{12,4},{0,8},{4,12},{24,16},{28,20},{16,24},{20,28},{9,1},{1... | collective-permute-start | bytes 393224 | tf_op jit(solution)/shard_map/ppermute | solution.py:112
  32.1 8.9 %collective-permute-start.18 = (bf16[512,128]{1,0:T(8,128)(2,1)S(1)}, bf16[512,128]{1,0:T(8,128)(2,1)S(1)}, u32[]{:S(2)}, u32[]{:S(2)}) collective-permute-start(bf16[512,128]{1,0:T(8,128)(2,1)S(1)} %get-tuple-element.96), channel_id=1, source_target_pairs={{16,0},{20,4},{24,8},{28,12},{0,16},{4,20},{8,24},{12,28},{17,1},{... | collective-permute-start | bytes 393224 | tf_op jit(solution)/shard_map/ppermute | solution.py:112
  33.7 10.4 %collective-permute-start.19 = (bf16[512,128]{1,0:T(8,128)(2,1)S(1)}, bf16[512,128]{1,0:T(8,128)(2,1)S(1)}, u32[]{:S(2)}, u32[]{:S(2)}) collective-permute-start(bf16[512,128]{1,0:T(8,128)(2,1)S(1)} %get-tuple-element.97), channel_id=1, source_target_pairs={{24,0},{28,4},{16,8},{20,12},{8,16},{12,20},{0,24},{4,28},{25,1},{... | collective-permute-start | bytes 393224 | tf_op jit(solution)/shard_map/ppermute | solution.py:112
  36.4 17.5 %collective-permute-start.10 = (bf16[32,2048]{1,0:T(8,128)(2,1)S(1)}, bf16[32,2048]{1,0:T(8,128)(2,1)S(1)}, u32[]{:S(2)}, u32[]{:S(2)}) collective-permute-start(bf16[32,2048]{1,0:T(8,128)(2,1)S(1)} %get-tuple-element.74), channel_id=1, source_target_pairs={{1,0},{0,1},{3,2},{2,3},{5,4},{4,5},{7,6},{6,7},{9,8},{8,9},{11,10... | collective-permute-start | bytes 393224 | tf_op jit(solution)/shard_map/ppermute | solution.py:505
  38.6 10.8 %collective-permute-start.12 = (bf16[32,2048]{1,0:T(8,128)(2,1)S(1)}, bf16[32,2048]{1,0:T(8,128)(2,1)S(1)}, u32[]{:S(2)}, u32[]{:S(2)}) collective-permute-start(bf16[32,2048]{1,0:T(8,128)(2,1)S(1)} %get-tuple-element.76), channel_id=1, source_target_pairs={{3,0},{2,1},{1,2},{0,3},{7,4},{6,5},{5,6},{4,7},{11,8},{10,9},{9,1... | collective-permute-start | bytes 393224 | tf_op jit(solution)/shard_map/ppermute | solution.py:505
  41.0 10.8 %collective-permute-start.11 = (bf16[32,2048]{1,0:T(8,128)(2,1)S(1)}, bf16[32,2048]{1,0:T(8,128)(2,1)S(1)}, u32[]{:S(2)}, u32[]{:S(2)}) collective-permute-start(bf16[32,2048]{1,0:T(8,128)(2,1)S(1)} %get-tuple-element.75), channel_id=1, source_target_pairs={{2,0},{3,1},{0,2},{1,3},{6,4},{7,5},{4,6},{5,7},{10,8},{11,9},{8,1... | collective-permute-start | bytes 393224 | tf_op jit(solution)/shard_map/ppermute | solution.py:505
  44.8 9.9 %collective-permute-start.23 = (f32[256,512]{1,0:T(8,128)S(1)}, f32[256,512]{1,0:T(8,128)S(1)}, u32[]{:S(2)}, u32[]{:S(2)}) collective-permute-start(f32[256,512]{1,0:T(8,128)S(1)} %get-tuple-element.103), channel_id=1, source_target_pairs={{4,0},{0,4},{12,8},{8,12},{20,16},{16,20},{28,24},{24,28},{5,1},{1... | collective-permute-start | bytes 1572872 | tf_op jit(solution)/shard_map/ppermute | solution.py:118
  49.3 6.2 %collective-permute-start.20 = (bf16[400,128]{1,0:T(8,128)(2,1)S(1)}, bf16[400,128]{1,0:T(8,128)(2,1)S(1)}, u32[]{:S(2)}, u32[]{:S(2)}) collective-permute-start(bf16[400,128]{1,0:T(8,128)(2,1)S(1)} %get-tuple-element.100), channel_id=1, source_target_pairs={{8,0},{12,4},{0,8},{4,12},{24,16},{28,20},{16,24},{20,28},{9,1},{1... | collective-permute-start | bytes 307208 | tf_op jit(solution)/shard_map/ppermute | solution.py:112
  49.4 6.1 %collective-permute-start.21 = (bf16[400,128]{1,0:T(8,128)(2,1)S(1)}, bf16[400,128]{1,0:T(8,128)(2,1)S(1)}, u32[]{:S(2)}, u32[]{:S(2)}) collective-permute-start(bf16[400,128]{1,0:T(8,128)(2,1)S(1)} %get-tuple-element.101), channel_id=1, source_target_pairs={{16,0},{20,4},{24,8},{28,12},{0,16},{4,20},{8,24},{12,28},{17,1},{... | collective-permute-start | bytes 307208 | tf_op jit(solution)/shard_map/ppermute | solution.py:112
  51.8 5.6 %collective-permute-start.22 = (bf16[400,128]{1,0:T(8,128)(2,1)S(1)}, bf16[400,128]{1,0:T(8,128)(2,1)S(1)}, u32[]{:S(2)}, u32[]{:S(2)}) collective-permute-start(bf16[400,128]{1,0:T(8,128)(2,1)S(1)} %get-tuple-element.102), channel_id=1, source_target_pairs={{24,0},{28,4},{16,8},{20,12},{8,16},{12,20},{0,24},{4,28},{25,1},{... | collective-permute-start | bytes 307208 | tf_op jit(solution)/shard_map/ppermute | solution.py:112

commit v13 on v12

--- a/solution.py
+++ b/solution.py
@@ -88,6 +88,9 @@
     def seen(self, d, k):
         return d ^ k if self.paired else (k - d) % self.size
 
+    def far_first(self):
+        return sorted(range(self.size), key=lambda d: d != self.size // 2)
+
     def pairs(self, d):
         return [(self.source(i, d), i) for i in range(self.size)]
 
@@ -104,12 +107,13 @@
     def key_head(self, head):
         return head * self.hk // self.hv
 
-    def exchange(self, pieces):
+    def exchange(self, pieces, in_turn=False):
         s = self.mates
         moved = [pieces[0]]
         for d in range(1, self.hv):
             pairs = [(i * s + b, j * s + b) for i, j in self.ring.pairs(d) for b in range(s)]
-            moved.append(lax.ppermute(pieces[d], "ctx", pairs))
+            piece = after(pieces[d], moved[1]) if in_turn and d > 1 else pieces[d]
+            moved.append(lax.ppermute(piece, "ctx", pairs))
         return moved
 
     def from_mate(self, x, d):
@@ -294,8 +298,8 @@
 
 def scan_kernel(plan, place_ref, mate_ref, *refs):
     s, hv = plan.mates, plan.hv
-    links, kept_ref, state_ref = refs[:s], refs[s], refs[s + 1]
-    outs, (all_ref, states_ref) = refs[s + 2 : -2], refs[-2:]
+    links, kept_ref, d_refs, state_ref = refs[:s], refs[s], refs[s + 1 : s + 1 + hv], refs[s + 1 + hv]
+    outs, (all_ref, states_ref) = refs[s + 2 + hv : -2], refs[-2:]
     place, mate = place_ref[0], mate_ref[0]
     lay_out(plan, place, mate, links, all_ref)
     state = jnp.zeros((DV, DK), F32)
@@ -311,8 +315,9 @@
         core = kept_ref[m, LOCAL] + mm(halves(state), halves(kept_ref[m, READS]), 1, 1)
         cores.append(core.astype(BF16))
     for d in range(hv):
+        outs[d][:2] = d_refs[d][...]
         for k in range(hv):
-            outs[d][k] = cores[plan.ring.seen(d, k)]
+            outs[d][2 + k] = cores[plan.ring.seen(d, k)]
 
 
 def state_cotangent_kernel(plan, kept_ref, *refs):
@@ -321,7 +326,7 @@
 
 
 def d_out(ref):
-    return ref[:DV], ref[DV:]
+    return ref[0], ref[1]
 
 
 def backward_kernel(plan, off_ref, place_ref, mate_ref, *refs):
@@ -402,7 +407,7 @@
 
 def gather_rows(head, pieces, all_ref):
     rows, ring = pieces[0].shape[0], Ring(len(pieces))
-    for d, piece in enumerate(pieces):
+    for d, piece in zip(ring.far_first(), pieces):
         at = ring.source(head, d) * rows
         all_ref[pl.ds(pl.multiple_of(at, rows), rows), :] = piece[...]
 
@@ -412,8 +417,8 @@
     gather_rows(head_ref[0], pieces, all_ref)
     high, low = halves(dot(w_ref[...], all_ref[...], 1, 1))
     for m in range(plan.hv):
-        core_ref[m, :DV] = high[m * DV : (m + 1) * DV]
-        core_ref[m, DV:] = low[m * DV : (m + 1) * DV]
+        core_ref[m, 0] = high[m * DV : (m + 1) * DV]
+        core_ref[m, 1] = low[m * DV : (m + 1) * DV]
     hand_out(plan, place_ref[0], core_ref, outs)
 
 
@@ -435,7 +440,7 @@
         refs[-2:],
     )
     for d, ref in enumerate(mixed_refs):
-        all_ref[plan.ring.source(place_ref[0], d)] = ref[0]
+        all_ref[plan.ring.source(place_ref[0], d)] = ref[2]
     mixed = all_ref[...].reshape(plan.hv * DV, plan.tok)
     total_ref[...] = dot(mixed, w_ref[...], 0, 0)
     rows, ring = outs[0].shape[0], Ring(parts)
@@ -451,7 +456,7 @@
     for d, ref in enumerate(mixed_refs):
         head = plan.ring.source(place_ref[0], d)
         for k in range(hv):
-            all_ref[k, head] = ref[k]
+            all_ref[k, head] = ref[2 + k]
     share = outs[0].shape[0]
     for d, out_ref in enumerate(outs):
         at = lax.rem(mate_ref[0] + plan.mates - d, plan.mates) * share
@@ -502,8 +507,10 @@
     head = lax.axis_index("head").astype(jnp.int32).reshape(1)
 
     def across_heads(pieces):
-        moved = [lax.ppermute(pieces[d], "head", Ring(parts).pairs(d)) for d in range(1, parts)]
-        return [pieces[0]] + moved
+        moved = list(pieces)
+        for d in range(1, parts):
+            moved[d] = lax.ppermute(pieces[d], "head", Ring(parts).pairs(d))
+        return moved
 
     vmem = lambda dtype, *shape: pltpu.VMEM(shape, dtype)
 
@@ -516,6 +523,7 @@
     )(place, queries, key_vectors, value_rows, write_rate, log_decay)
     got = plan.exchange(packed)
     rows = across_heads([grad_out] * parts)
+    rows = [rows[d] for d in Ring(parts).far_first()]
 
     link, kept = call(
         partial(prepare_kernel, plan),
@@ -528,21 +536,19 @@
 
     d_core = call(
         partial(cotangent_kernel, plan, parts),
-        [arr(BF16, 2 * DV, tok)] * hv,
+        [arr(BF16, 2, DV, tok)] * hv,
         smem=(0, 1),
-        scratch=[vmem(BF16, tok, model), vmem(BF16, hv, 2 * DV, tok)],
+        scratch=[vmem(BF16, tok, model), vmem(BF16, hv, 2, DV, tok)],
         flops=30_000_000_000,
     )(head, place, *rows, after(out_weight, link))
-    kept = after(kept, d_core[0])
-    d_core = plan.exchange(d_core)
 
     states, *mixed = call(
         partial(scan_kernel, plan),
-        [arr(F32, hv, DV, DK)] + [arr(BF16, hv, DV, tok)] * hv,
+        [arr(F32, hv, DV, DK)] + [arr(BF16, 2 + hv, DV, tok)] * hv,
         smem=(0, 1),
         scratch=[vmem(F32, s, hv, 2, DK, DK), vmem(F32, n, DV, DK)],
         flops=2_500_000_000,
-    )(place, mate, *links, kept)
+    )(place, mate, *links, kept, *d_core)
     turned = call(
         partial(turn_kernel, plan, parts),
         [arr(BF16, model // hv, tok)] * hv,
@@ -551,10 +557,10 @@
         flops=1_000_000_000,
     )(head, place, *after(rows, states))
     mixed = plan.exchange(mixed)
-    turned = plan.exchange(turned)
+    turned = plan.exchange(turned, in_turn=True)
     back = call(
         partial(state_cotangent_kernel, plan), arr(F32, hv, DV, DK), flops=30_000_000_000
-    )(kept, *after(d_core, states))
+    )(kept, *mixed)
     backs = [back] + [plan.from_mate(back, d) for d in range(1, s)]
 
     projected = call(
@@ -577,7 +583,7 @@
             vmem(F32, n, DV, DK),
         ],
         flops=6_000_000_000,
-    )(doc_offsets, place, mate, *links, *backs, *got, *d_core, kept, after(states, projected[1]))
+    )(doc_offsets, place, mate, *links, *backs, *got, *mixed, kept, after(states, projected[1]))
 
     shares = call(
         partial(weight_kernel, plan),

time: 58.4 us -> 62.4 us (1.068)
  waiting for transfers between devices: 9.32 us -> 14.3 us
  starting transfers between devices: 32 us -> 31 us
    ppermute x21 -> x18, waiting for transfers between devices: 9.31 us -> 14.3 us  [the longest x12 10.9 us: exchange(): moved.append(lax.ppermute(piece, 'ctx', pairs))]
    ppermute x21 -> x18, starting transfers between devices: 31.8 us -> 30.8 us  [the longest x12 15.6 us: exchange(): moved.append(lax.ppermute(piece, 'ctx', pairs))]
  transfers between devices with their start and end apart: 24 -> 21, of which waited for: 6 -> 10; matrix products, arithmetic and copies ran while one was open for 3% -> 3% of each run, Pallas kernels for 21% -> 18%
where the time goes in v13:
time: 62.4 us; the launch traced here: 62.3 us
  starting transfers between devices  31 us (50%)
  Pallas kernels  14.5 us (23%)
  waiting for transfers between devices  14.3 us (23%)
  other arithmetic  1.63 us (3%)
  between operations  0.77 us (1%)
    ppermute x12, starting transfers between devices, exchange(): moved.append(lax.ppermute(piece, 'ctx', pairs))  15.6 us
    ppermute x6, starting transfers between devices, across_heads(): moved[d] = lax.ppermute(pieces[d], 'head', Ring(parts).pairs(d))  15.2 us
    pallas_call x10, Pallas kernels, run(): pl.pallas_call(kernel, out_shape=outs, in_specs=[spec(i) for i in range(l...  14.5 us
    ppermute x12, waiting for transfers between devices, exchange(): moved.append(lax.ppermute(piece, 'ctx', pairs))  10.9 us
    ppermute x6, waiting for transfers between devices, across_heads(): moved[d] = lax.ppermute(pieces[d], 'head', Ring(parts).pairs(d))  3.42 us
  transfers between devices with their start and end apart: 21, of which 10 were waited for; matrix products, arithmetic and copies ran while one was open for 3% of the time, Pallas kernels for 18%

profile of v13, /device:TPU:0, one launch (start us, length us, event | category | flops | bytes accessed | tf_op | source)
XLA Modules:
  0.0 62.3 jit_solution(15374536773710917223)
XLA Ops:
  0.6 1.2 %shard_map.135 = (bf16[400,128]{1,0:T(8,128)(2,1)S(1)}, bf16[400,128]{1,0:T(8,128)(2,1)S(1)}, bf16[400,128]{1,0:T(8,128)(2,1)S(1)}, bf16[400,128]{1,0:T(8,128)(2,1)S(1)}) custom-call(s32[1]{0:T(128)} %bitcast.1.place_ref, bf16[128,256]{1,0:T(8,128)(2,1)} %q_ref.1, bf16[128,256]{1,0:T(8,128)(2,1)} %k_ref.1, bf16[128,512]{1,0:T(8,128)(2,1)} %v_ref.1, ...), custom_call_target="tpu_custom_call" | custom-call | tf_op jit(solution)/shard_map/pallas_call | solution.py:60
  1.8 3.0 %collective-permute-start = (bf16[400,128]{1,0:T(8,128)(2,1)S(1)}, bf16[400,128]{1,0:T(8,128)(2,1)S(1)}, u32[]{:S(2)}, u32[]{:S(2)}) collective-permute-start(bf16[400,128]{1,0:T(8,128)(2,1)S(1)} %get-tuple-element.58), channel_id=1, source_target_pairs={{8,0},{12,4},{0,8},{4,12},{24,16},{28,20},{16,24},{20,28},{9,1},{1... | collective-permute-start | bytes 307208 | tf_op jit(solution)/shard_map/ppermute | solution.py:116
  4.8 1.5 %collective-permute-start.1 = (bf16[400,128]{1,0:T(8,128)(2,1)S(1)}, bf16[400,128]{1,0:T(8,128)(2,1)S(1)}, u32[]{:S(2)}, u32[]{:S(2)}) collective-permute-start(bf16[400,128]{1,0:T(8,128)(2,1)S(1)} %get-tuple-element.59), channel_id=1, source_target_pairs={{16,0},{20,4},{24,8},{28,12},{0,16},{4,20},{8,24},{12,28},{17,1},{... | collective-permute-start | bytes 307208 | tf_op jit(solution)/shard_map/ppermute | solution.py:116
  6.4 3.0 %collective-permute-start.4 = (bf16[32,2048]{1,0:T(8,128)(2,1)}, bf16[32,2048]{1,0:T(8,128)(2,1)S(1)}, u32[]{:S(2)}, u32[]{:S(2)}) collective-permute-start(bf16[32,2048]{1,0:T(8,128)(2,1)} %refs_1_.2), channel_id=1, source_target_pairs={{2,0},{3,1},{0,2},{1,3},{6,4},{7,5},{4,6},{5,7},{10,8},{11,9},{8,1... | collective-permute-start | bytes 393224 | tf_op jit(solution)/shard_map/ppermute | solution.py:512
  9.4 1.6 %collective-permute-start.5 = (bf16[32,2048]{1,0:T(8,128)(2,1)}, bf16[32,2048]{1,0:T(8,128)(2,1)S(1)}, u32[]{:S(2)}, u32[]{:S(2)}) collective-permute-start(bf16[32,2048]{1,0:T(8,128)(2,1)} %refs_1_.2), channel_id=1, source_target_pairs={{1,0},{0,1},{3,2},{2,3},{5,4},{4,5},{7,6},{6,7},{9,8},{8,9},{11,10... | collective-permute-start | bytes 393224 | tf_op jit(solution)/shard_map/ppermute | solution.py:512
  11.0 0.6 collective-permute-start.6
  11.9 4.1 %shard_map.136 = (f32[4,2,128,128]{3,2,1,0:T(8,128)S(1)}, f32[4,7,128,128]{3,2,1,0:T(8,128)S(1)}) custom-call(s32[5]{0:T(128)} %off_ref.3, s32[1]{0:T(128)} %bitcast.1.place_ref, s32[1]{0:T(128)} %bitcast.2.mate_ref, bf16[400,128]{1,0:T(8,128)(2,1)S(1)} %get-tuple-element.57.refs_0_.refs_4_, bf16[400,128]{1,0:T(8,128)(2,1)S(1)} %collective-permute-done.refs_1_.refs_5_, ...), custom_call_target="tpu_custom_call" | custom-call | flops 20000000000 | tf_op jit(solution)/shard_map/pallas_call | solution.py:60
  16.1 1.6 %collective-permute-done.4.refs_0_ = bf16[32,2048]{1,0:T(8,128)(2,1)S(1)} collective-permute-done((bf16[32,2048]{1,0:T(8,128)(2,1)}, bf16[32,2048]{1,0:T(8,128)(2,1)S(1)}, u32[]{:S(2)}, u32[]{:S(2)}) %collective-permute-start.4) | collective-permute-done | bytes 131104 | tf_op jit(solution)/shard_map/ppermute | solution.py:512
  17.7 1.4 %collective-permute-done.6.refs_3_ = bf16[32,2048]{1,0:T(8,128)(2,1)S(1)} collective-permute-done((bf16[32,2048]{1,0:T(8,128)(2,1)}, bf16[32,2048]{1,0:T(8,128)(2,1)S(1)}, u32[]{:S(2)}, u32[]{:S(2)}) %collective-permute-start.6) | collective-permute-done | bytes 131104 | tf_op jit(solution)/shard_map/ppermute | solution.py:512
  19.2 0.8 %shard_map.137 = (bf16[2,128,128]{2,1,0:T(8,128)(2,1)S(1)}, bf16[2,128,128]{2,1,0:T(8,128)(2,1)S(1)}, bf16[2,128,128]{2,1,0:T(8,128)(2,1)S(1)}, bf16[2,128,128]{2,1,0:T(8,128)(2,1)S(1)}) custom-call(s32[1]{0:T(128)} %bitcast.head_ref, s32[1]{0:T(128)} %bitcast.1.place_ref, bf16[32,2048]{1,0:T(8,128)(2,1)S(1)} %collective-permute-done.4.refs_0_, ...), custom_call_target="tpu_custom_call" | custom-call | flops 30000001024 | tf_op jit(solution)/shard_map/pallas_call | solution.py:60
  19.9 1.3 %shard_map.138 = (f32[4,128,128]{2,1,0:T(8,128)S(1)}, bf16[6,128,128]{2,1,0:T(8,128)(2,1)S(1)}, bf16[6,128,128]{2,1,0:T(8,128)(2,1)S(1)}, bf16[6,128,128]{2,1,0:T(8,128)(2,1)S(1)}, bf16[6,128,128]{2,1,0:T(8,128)(2,1)S(1)}) custom-call(s32[1]{0:T(128)} %bitcast.1.place_ref, s32[1]{0:T(128)} %bitcast.2.mate_ref, ...), custom_call_target="tpu_custom_call" | custom-call | flops 2500000000 | tf_op jit(solution)/shard_map/pallas_call | solution.py:60
  21.3 1.6 %collective-permute-start.7 = (bf16[6,128,128]{2,1,0:T(8,128)(2,1)S(1)}, bf16[6,128,128]{2,1,0:T(8,128)(2,1)S(1)}, u32[]{:S(2)}, u32[]{:S(2)}) collective-permute-start(bf16[6,128,128]{2,1,0:T(8,128)(2,1)S(1)} %get-tuple-element.69), channel_id=1, source_target_pairs={{8,0},{12,4},{0,8},{4,12},{24,16},{28,20},{16,24},{20,28},{9,1},{1... | collective-permute-start | bytes 589832 | tf_op jit(solution)/shard_map/ppermute | solution.py:116
  22.8 1.5 %collective-permute-start.8 = (bf16[6,128,128]{2,1,0:T(8,128)(2,1)S(1)}, bf16[6,128,128]{2,1,0:T(8,128)(2,1)S(1)}, u32[]{:S(2)}, u32[]{:S(2)}) collective-permute-start(bf16[6,128,128]{2,1,0:T(8,128)(2,1)S(1)} %get-tuple-element.70), channel_id=1, source_target_pairs={{16,0},{20,4},{24,8},{28,12},{0,16},{4,20},{8,24},{12,28},{17,1},{... | collective-permute-start | bytes 589832 | tf_op jit(solution)/shard_map/ppermute | solution.py:116
  25.1 1.6 %collective-permute-start.14 = (bf16[512,128]{1,0:T(8,128)(2,1)S(1)}, bf16[512,128]{1,0:T(8,128)(2,1)S(1)}, u32[]{:S(2)}, u32[]{:S(2)}) collective-permute-start(bf16[512,128]{1,0:T(8,128)(2,1)S(1)} %get-tuple-element.87), channel_id=1, source_target_pairs={{8,0},{12,4},{0,8},{4,12},{24,16},{28,20},{16,24},{20,28},{9,1},{1... | collective-permute-start | bytes 393224 | tf_op jit(solution)/shard_map/ppermute | solution.py:116
  26.7 2.3 %collective-permute-done.7.refs_1_.refs_9_.refs_5_ = bf16[6,128,128]{2,1,0:T(8,128)(2,1)S(1)} collective-permute-done((bf16[6,128,128]{2,1,0:T(8,128)(2,1)S(1)}, bf16[6,128,128]{2,1,0:T(8,128)(2,1)S(1)}, u32[]{:S(2)}, u32[]{:S(2)}) %collective-permute-start.7) | collective-permute-done | bytes 196640 | tf_op jit(solution)/shard_map/ppermute | solution.py:116
  29.0 1.9 %collective-permute-done.8.refs_2_.refs_10_.refs_6_ = bf16[6,128,128]{2,1,0:T(8,128)(2,1)S(1)} collective-permute-done((bf16[6,128,128]{2,1,0:T(8,128)(2,1)S(1)}, bf16[6,128,128]{2,1,0:T(8,128)(2,1)S(1)}, u32[]{:S(2)}, u32[]{:S(2)}) %collective-permute-start.8) | collective-permute-done | bytes 196640 | tf_op jit(solution)/shard_map/ppermute | solution.py:116
  30.9 2.7 %collective-permute-done.9.refs_3_.refs_11_.refs_7_ = bf16[6,128,128]{2,1,0:T(8,128)(2,1)S(1)} collective-permute-done((bf16[6,128,128]{2,1,0:T(8,128)(2,1)S(1)}, bf16[6,128,128]{2,1,0:T(8,128)(2,1)S(1)}, u32[]{:S(2)}, u32[]{:S(2)}) %collective-permute-start.9) | collective-permute-done | bytes 196640 | tf_op jit(solution)/shard_map/ppermute | solution.py:116
  34.0 1.5 %collective-permute-start.15 = (bf16[512,128]{1,0:T(8,128)(2,1)S(1)}, bf16[512,128]{1,0:T(8,128)(2,1)S(1)}, u32[]{:S(2)}, u32[]{:S(2)}) collective-permute-start(bf16[512,128]{1,0:T(8,128)(2,1)S(1)} %get-tuple-element.89), channel_id=1, source_target_pairs={{16,0},{20,4},{24,8},{28,12},{0,16},{4,20},{8,24},{12,28},{17,1},{... | collective-permute-start | bytes 393224 | tf_op jit(solution)/shard_map/ppermute | solution.py:116
  35.5 1.3 %collective-permute-start.16 = (bf16[512,128]{1,0:T(8,128)(2,1)S(1)}, bf16[512,128]{1,0:T(8,128)(2,1)S(1)}, u32[]{:S(2)}, u32[]{:S(2)}) collective-permute-start(bf16[512,128]{1,0:T(8,128)(2,1)S(1)} %get-tuple-element.91), channel_id=1, source_target_pairs={{24,0},{28,4},{16,8},{20,12},{8,16},{12,20},{0,24},{4,28},{25,1},{... | collective-permute-start | bytes 393224 | tf_op jit(solution)/shard_map/ppermute | solution.py:116
  36.8 0.5 shard_map.139
  37.4 3.2 %collective-permute-start.10 = (bf16[32,2048]{1,0:T(8,128)(2,1)S(1)}, bf16[32,2048]{1,0:T(8,128)(2,1)S(1)}, u32[]{:S(2)}, u32[]{:S(2)}) collective-permute-start(bf16[32,2048]{1,0:T(8,128)(2,1)S(1)} %get-tuple-element.73), channel_id=1, source_target_pairs={{1,0},{0,1},{3,2},{2,3},{5,4},{4,5},{7,6},{6,7},{9,8},{8,9},{11,10... | collective-permute-start | bytes 393224 | tf_op jit(solution)/shard_map/ppermute | solution.py:512
  40.5 3.2 %collective-permute-start.12 = (bf16[32,2048]{1,0:T(8,128)(2,1)S(1)}, bf16[32,2048]{1,0:T(8,128)(2,1)S(1)}, u32[]{:S(2)}, u32[]{:S(2)}) collective-permute-start(bf16[32,2048]{1,0:T(8,128)(2,1)S(1)} %get-tuple-element.75), channel_id=1, source_target_pairs={{3,0},{2,1},{1,2},{0,3},{7,4},{6,5},{5,6},{4,7},{11,8},{10,9},{9,1... | collective-permute-start | bytes 393224 | tf_op jit(solution)/shard_map/ppermute | solution.py:512
  43.8 3.6 %collective-permute-start.11 = (bf16[32,2048]{1,0:T(8,128)(2,1)S(1)}, bf16[32,2048]{1,0:T(8,128)(2,1)S(1)}, u32[]{:S(2)}, u32[]{:S(2)}) collective-permute-start(bf16[32,2048]{1,0:T(8,128)(2,1)S(1)} %get-tuple-element.74), channel_id=1, source_target_pairs={{2,0},{3,1},{0,2},{1,3},{6,4},{7,5},{4,6},{5,7},{10,8},{11,9},{8,1... | collective-permute-start | bytes 393224 | tf_op jit(solution)/shard_map/ppermute | solution.py:512
  47.3 0.7 %shard_map.143 = (f32[256,512]{1,0:T(8,128)S(1)}, f32[256,512]{1,0:T(8,128)S(1)}) custom-call(s32[1]{0:T(128)} %bitcast.1.place_ref, s32[1]{0:T(128)} %bitcast.2.mate_ref, bf16[512,128]{1,0:T(8,128)(2,1)S(1)} %get-tuple-element.86.refs_0_, bf16[512,128]{1,0:T(8,128)(2,1)S(1)} %collective-permute-done.14.refs_1_, ...), custom_call_target="tpu_custom_call" | custom-call | flops 1000000000 | tf_op jit(solution)/shard_map/pallas_call | solution.py:60
  48.2 4.4 %shard_map.141 = (bf16[400,128]{1,0:T(8,128)(2,1)S(1)}, bf16[400,128]{1,0:T(8,128)(2,1)S(1)}, bf16[400,128]{1,0:T(8,128)(2,1)S(1)}, bf16[400,128]{1,0:T(8,128)(2,1)S(1)}) custom-call(s32[5]{0:T(128)} %off_ref.3, s32[1]{0:T(128)} %bitcast.1.place_ref, s32[1]{0:T(128)} %bitcast.2.mate_ref, f32[4,2,128,128]{3,2,1,0:T(8,128)S(1)} %get-tuple-element.61.refs_0_, ...), custom_call_target="tpu_custom_call" | custom-call | flops 6000000000 | tf_op jit(solution)/shard_map/pallas_call | solution.py:60
  52.6 1.6 %collective-permute-start.17 = (bf16[400,128]{1,0:T(8,128)(2,1)S(1)}, bf16[400,128]{1,0:T(8,128)(2,1)S(1)}, u32[]{:S(2)}, u32[]{:S(2)}) collective-permute-start(bf16[400,128]{1,0:T(8,128)(2,1)S(1)} %get-tuple-element.94), channel_id=1, source_target_pairs={{8,0},{12,4},{0,8},{4,12},{24,16},{28,20},{16,24},{20,28},{9,1},{1... | collective-permute-start | bytes 307208 | tf_op jit(solution)/shard_map/ppermute | solution.py:116
  54.2 0.7 %collective-permute-start.18 = (bf16[400,128]{1,0:T(8,128)(2,1)S(1)}, bf16[400,128]{1,0:T(8,128)(2,1)S(1)}, u32[]{:S(2)}, u32[]{:S(2)}) collective-permute-start(bf16[400,128]{1,0:T(8,128)(2,1)S(1)} %get-tuple-element.95), channel_id=1, source_target_pairs={{16,0},{20,4},{24,8},{28,12},{0,16},{4,20},{8,24},{12,28},{17,1},{... | collective-permute-start | bytes 307208 | tf_op jit(solution)/shard_map/ppermute | solution.py:116
  55.3 0.9 %collective-permute-start.19 = (bf16[400,128]{1,0:T(8,128)(2,1)S(1)}, bf16[400,128]{1,0:T(8,128)(2,1)S(1)}, u32[]{:S(2)}, u32[]{:S(2)}) collective-permute-start(bf16[400,128]{1,0:T(8,128)(2,1)S(1)} %get-tuple-element.96), channel_id=1, source_target_pairs={{24,0},{28,4},{16,8},{20,12},{8,16},{12,20},{0,24},{4,28},{25,1},{... | collective-permute-start | bytes 307208 | tf_op jit(solution)/shard_map/ppermute | solution.py:116
  56.2 0.8 %convert_add_fusion = f32[32,2048]{1,0:T(8,128)} fusion(bf16[32,2048]{1,0:T(8,128)(2,1)S(1)} %collective-permute-done.12, bf16[32,2048]{1,0:T(8,128)(2,1)S(1)} %collective-permute-done.11, f32[32,2048]{1,0:T(8,128)S(1)} %get-tuple-element.72, bf16[32,2048]{1,0:T(8,128)(2,1)S(1)} %collective-permute-done.10), kind=kLoop, calls=%fused_computation | loop fusion | flops 393216 | bytes 917504 | tf_op jit(solution)/shard_map/add | solution.py:602
  56.9 0.9 %add.21 = f32[256,512]{1,0:T(8,128)} add(f32[256,512]{1,0:T(8,128)S(1)} %get-tuple-element.92, f32[256,512]{1,0:T(8,128)S(1)} %collective-permute-done.20) | non-fusion elementwise | flops 131072 | bytes 1572864 | tf_op jit(solution)/shard_map/add | solution.py:598
  57.9 3.4 %collective-permute-done.18.refs_2_ = bf16[400,128]{1,0:T(8,128)(2,1)S(1)} collective-permute-done((bf16[400,128]{1,0:T(8,128)(2,1)S(1)}, bf16[400,128]{1,0:T(8,128)(2,1)S(1)}, u32[]{:S(2)}, u32[]{:S(2)}) %collective-permute-start.18) | collective-permute-done | bytes 102432 | tf_op jit(solution)/shard_map/ppermute | solution.py:116
  61.4 0.9 %shard_map.144 = (f32[128,256]{1,0:T(8,128)}, f32[128,256]{1,0:T(8,128)}, f32[128,512]{1,0:T(8,128)}, f32[4,128]{1,0:T(4,128)}, f32[4,128]{1,0:T(4,128)}) custom-call(s32[1]{0:T(128)} %bitcast.1.place_ref, bf16[400,128]{1,0:T(8,128)(2,1)S(1)} %get-tuple-element.98.refs_0_, bf16[400,128]{1,0:T(8,128)(2,1)S(1)} %collective-permute-done.17.refs_1_, ...), custom_call_target="tpu_custom_call" | custom-call | flops 1000000000 | tf_op jit(solution)/shard_map/pallas_call | solution.py:60
  (26 shorter events, 2.2 us)
Async XLA Ops:
  1.8 9.2 %collective-permute-start = (bf16[400,128]{1,0:T(8,128)(2,1)S(1)}, bf16[400,128]{1,0:T(8,128)(2,1)S(1)}, u32[]{:S(2)}, u32[]{:S(2)}) collective-permute-start(bf16[400,128]{1,0:T(8,128)(2,1)S(1)} %get-tuple-element.58), channel_id=1, source_target_pairs={{8,0},{12,4},{0,8},{4,12},{24,16},{28,20},{16,24},{20,28},{9,1},{1... | collective-permute-start | bytes 307208 | tf_op jit(solution)/shard_map/ppermute | solution.py:116
  4.8 6.8 %collective-permute-start.1 = (bf16[400,128]{1,0:T(8,128)(2,1)S(1)}, bf16[400,128]{1,0:T(8,128)(2,1)S(1)}, u32[]{:S(2)}, u32[]{:S(2)}) collective-permute-start(bf16[400,128]{1,0:T(8,128)(2,1)S(1)} %get-tuple-element.59), channel_id=1, source_target_pairs={{16,0},{20,4},{24,8},{28,12},{0,16},{4,20},{8,24},{12,28},{17,1},{... | collective-permute-start | bytes 307208 | tf_op jit(solution)/shard_map/ppermute | solution.py:116
  6.3 5.6 %collective-permute-start.2 = (bf16[400,128]{1,0:T(8,128)(2,1)S(1)}, bf16[400,128]{1,0:T(8,128)(2,1)S(1)}, u32[]{:S(2)}, u32[]{:S(2)}) collective-permute-start(bf16[400,128]{1,0:T(8,128)(2,1)S(1)} %get-tuple-element.60), channel_id=1, source_target_pairs={{24,0},{28,4},{16,8},{20,12},{8,16},{12,20},{0,24},{4,28},{25,1},{... | collective-permute-start | bytes 307208 | tf_op jit(solution)/shard_map/ppermute | solution.py:116
  6.4 11.4 %collective-permute-start.4 = (bf16[32,2048]{1,0:T(8,128)(2,1)}, bf16[32,2048]{1,0:T(8,128)(2,1)S(1)}, u32[]{:S(2)}, u32[]{:S(2)}) collective-permute-start(bf16[32,2048]{1,0:T(8,128)(2,1)} %refs_1_.2), channel_id=1, source_target_pairs={{2,0},{3,1},{0,2},{1,3},{6,4},{7,5},{4,6},{5,7},{10,8},{11,9},{8,1... | collective-permute-start | bytes 393224 | tf_op jit(solution)/shard_map/ppermute | solution.py:512
  9.4 8.3 %collective-permute-start.5 = (bf16[32,2048]{1,0:T(8,128)(2,1)}, bf16[32,2048]{1,0:T(8,128)(2,1)S(1)}, u32[]{:S(2)}, u32[]{:S(2)}) collective-permute-start(bf16[32,2048]{1,0:T(8,128)(2,1)} %refs_1_.2), channel_id=1, source_target_pairs={{1,0},{0,1},{3,2},{2,3},{5,4},{4,5},{7,6},{6,7},{9,8},{8,9},{11,10... | collective-permute-start | bytes 393224 | tf_op jit(solution)/shard_map/ppermute | solution.py:512
  11.0 8.2 %collective-permute-start.6 = (bf16[32,2048]{1,0:T(8,128)(2,1)}, bf16[32,2048]{1,0:T(8,128)(2,1)S(1)}, u32[]{:S(2)}, u32[]{:S(2)}) collective-permute-start(bf16[32,2048]{1,0:T(8,128)(2,1)} %refs_1_.2), channel_id=1, source_target_pairs={{3,0},{2,1},{1,2},{0,3},{7,4},{6,5},{5,6},{4,7},{11,8},{10,9},{9,1... | collective-permute-start | bytes 393224 | tf_op jit(solution)/shard_map/ppermute | solution.py:512
  11.9 7.3 %copy-start = (bf16[512,2048]{1,0:T(8,128)(2,1)S(1)}, bf16[512,2048]{1,0:T(8,128)(2,1)}, u32[]{:S(2)}) copy-start(bf16[512,2048]{1,0:T(8,128)(2,1)} %refs_4_.2) | copy-start | bytes 6291460
  11.9 7.3 %copy-start.1 = (bf16[32,2048]{1,0:T(8,128)(2,1)S(1)}, bf16[32,2048]{1,0:T(8,128)(2,1)}, u32[]{:S(2)}) copy-start(bf16[32,2048]{1,0:T(8,128)(2,1)} %refs_1_.2) | copy-start | bytes 393220
  16.0 3.9 %collective-permute-start.3 = (f32[4,2,128,128]{3,2,1,0:T(8,128)S(1)}, f32[4,2,128,128]{3,2,1,0:T(8,128)S(1)}, u32[]{:S(2)}, u32[]{:S(2)}) collective-permute-start(f32[4,2,128,128]{3,2,1,0:T(8,128)S(1)} %get-tuple-element.61.refs_0_), channel_id=1, source_target_pairs={{4,0},{0,4},{12,8},{8,12},{20,16},{16,20},{28,24},{24,28},{5,1},{1... | collective-permute-start | bytes 1572872 | tf_op jit(solution)/shard_map/ppermute | solution.py:122
  21.3 7.7 %collective-permute-start.7 = (bf16[6,128,128]{2,1,0:T(8,128)(2,1)S(1)}, bf16[6,128,128]{2,1,0:T(8,128)(2,1)S(1)}, u32[]{:S(2)}, u32[]{:S(2)}) collective-permute-start(bf16[6,128,128]{2,1,0:T(8,128)(2,1)S(1)} %get-tuple-element.69), channel_id=1, source_target_pairs={{8,0},{12,4},{0,8},{4,12},{24,16},{28,20},{16,24},{20,28},{9,1},{1... | collective-permute-start | bytes 589832 | tf_op jit(solution)/shard_map/ppermute | solution.py:116
  22.8 8.0 %collective-permute-start.8 = (bf16[6,128,128]{2,1,0:T(8,128)(2,1)S(1)}, bf16[6,128,128]{2,1,0:T(8,128)(2,1)S(1)}, u32[]{:S(2)}, u32[]{:S(2)}) collective-permute-start(bf16[6,128,128]{2,1,0:T(8,128)(2,1)S(1)} %get-tuple-element.70), channel_id=1, source_target_pairs={{16,0},{20,4},{24,8},{28,12},{0,16},{4,20},{8,24},{12,28},{17,1},{... | collective-permute-start | bytes 589832 | tf_op jit(solution)/shard_map/ppermute | solution.py:116
  24.3 9.2 %collective-permute-start.9 = (bf16[6,128,128]{2,1,0:T(8,128)(2,1)S(1)}, bf16[6,128,128]{2,1,0:T(8,128)(2,1)S(1)}, u32[]{:S(2)}, u32[]{:S(2)}) collective-permute-start(bf16[6,128,128]{2,1,0:T(8,128)(2,1)S(1)} %get-tuple-element.71), channel_id=1, source_target_pairs={{24,0},{28,4},{16,8},{20,12},{8,16},{12,20},{0,24},{4,28},{25,1},{... | collective-permute-start | bytes 589832 | tf_op jit(solution)/shard_map/ppermute | solution.py:116
  25.1 8.9 %collective-permute-start.14 = (bf16[512,128]{1,0:T(8,128)(2,1)S(1)}, bf16[512,128]{1,0:T(8,128)(2,1)S(1)}, u32[]{:S(2)}, u32[]{:S(2)}) collective-permute-start(bf16[512,128]{1,0:T(8,128)(2,1)S(1)} %get-tuple-element.87), channel_id=1, source_target_pairs={{8,0},{12,4},{0,8},{4,12},{24,16},{28,20},{16,24},{20,28},{9,1},{1... | collective-permute-start | bytes 393224 | tf_op jit(solution)/shard_map/ppermute | solution.py:116
  33.8 14.3 %collective-permute-start.13 = (f32[4,128,128]{2,1,0:T(8,128)S(1)}, f32[4,128,128]{2,1,0:T(8,128)S(1)}, u32[]{:S(2)}, u32[]{:S(2)}) collective-permute-start(f32[4,128,128]{2,1,0:T(8,128)S(1)} %shard_map.140.refs_2_), channel_id=1, source_target_pairs={{4,0},{0,4},{12,8},{8,12},{20,16},{16,20},{28,24},{24,28},{5,1},{1... | collective-permute-start | bytes 786440 | tf_op jit(solution)/shard_map/ppermute | solution.py:122
  34.0 9.7 %collective-permute-start.15 = (bf16[512,128]{1,0:T(8,128)(2,1)S(1)}, bf16[512,128]{1,0:T(8,128)(2,1)S(1)}, u32[]{:S(2)}, u32[]{:S(2)}) collective-permute-start(bf16[512,128]{1,0:T(8,128)(2,1)S(1)} %get-tuple-element.89), channel_id=1, source_target_pairs={{16,0},{20,4},{24,8},{28,12},{0,16},{4,20},{8,24},{12,28},{17,1},{... | collective-permute-start | bytes 393224 | tf_op jit(solution)/shard_map/ppermute | solution.py:116
  35.5 11.8 %collective-permute-start.16 = (bf16[512,128]{1,0:T(8,128)(2,1)S(1)}, bf16[512,128]{1,0:T(8,128)(2,1)S(1)}, u32[]{:S(2)}, u32[]{:S(2)}) collective-permute-start(bf16[512,128]{1,0:T(8,128)(2,1)S(1)} %get-tuple-element.91), channel_id=1, source_target_pairs={{24,0},{28,4},{16,8},{20,12},{8,16},{12,20},{0,24},{4,28},{25,1},{... | collective-permute-start | bytes 393224 | tf_op jit(solution)/shard_map/ppermute | solution.py:116
  37.4 18.8 %collective-permute-start.10 = (bf16[32,2048]{1,0:T(8,128)(2,1)S(1)}, bf16[32,2048]{1,0:T(8,128)(2,1)S(1)}, u32[]{:S(2)}, u32[]{:S(2)}) collective-permute-start(bf16[32,2048]{1,0:T(8,128)(2,1)S(1)} %get-tuple-element.73), channel_id=1, source_target_pairs={{1,0},{0,1},{3,2},{2,3},{5,4},{4,5},{7,6},{6,7},{9,8},{8,9},{11,10... | collective-permute-start | bytes 393224 | tf_op jit(solution)/shard_map/ppermute | solution.py:512
  40.5 13.7 %collective-permute-start.12 = (bf16[32,2048]{1,0:T(8,128)(2,1)S(1)}, bf16[32,2048]{1,0:T(8,128)(2,1)S(1)}, u32[]{:S(2)}, u32[]{:S(2)}) collective-permute-start(bf16[32,2048]{1,0:T(8,128)(2,1)S(1)} %get-tuple-element.75), channel_id=1, source_target_pairs={{3,0},{2,1},{1,2},{0,3},{7,4},{6,5},{5,6},{4,7},{11,8},{10,9},{9,1... | collective-permute-start | bytes 393224 | tf_op jit(solution)/shard_map/ppermute | solution.py:512
  43.8 11.5 %collective-permute-start.11 = (bf16[32,2048]{1,0:T(8,128)(2,1)S(1)}, bf16[32,2048]{1,0:T(8,128)(2,1)S(1)}, u32[]{:S(2)}, u32[]{:S(2)}) collective-permute-start(bf16[32,2048]{1,0:T(8,128)(2,1)S(1)} %get-tuple-element.74), channel_id=1, source_target_pairs={{2,0},{3,1},{0,2},{1,3},{6,4},{7,5},{4,6},{5,7},{10,8},{11,9},{8,1... | collective-permute-start | bytes 393224 | tf_op jit(solution)/shard_map/ppermute | solution.py:512
  48.1 8.9 %collective-permute-start.20 = (f32[256,512]{1,0:T(8,128)S(1)}, f32[256,512]{1,0:T(8,128)S(1)}, u32[]{:S(2)}, u32[]{:S(2)}) collective-permute-start(f32[256,512]{1,0:T(8,128)S(1)} %get-tuple-element.97), channel_id=1, source_target_pairs={{4,0},{0,4},{12,8},{8,12},{20,16},{16,20},{28,24},{24,28},{5,1},{1... | collective-permute-start | bytes 1572872 | tf_op jit(solution)/shard_map/ppermute | solution.py:122
  52.6 5.3 %collective-permute-start.17 = (bf16[400,128]{1,0:T(8,128)(2,1)S(1)}, bf16[400,128]{1,0:T(8,128)(2,1)S(1)}, u32[]{:S(2)}, u32[]{:S(2)}) collective-permute-start(bf16[400,128]{1,0:T(8,128)(2,1)S(1)} %get-tuple-element.94), channel_id=1, source_target_pairs={{8,0},{12,4},{0,8},{4,12},{24,16},{28,20},{16,24},{20,28},{9,1},{1... | collective-permute-start | bytes 307208 | tf_op jit(solution)/shard_map/ppermute | solution.py:116
  54.2 7.2 %collective-permute-start.18 = (bf16[400,128]{1,0:T(8,128)(2,1)S(1)}, bf16[400,128]{1,0:T(8,128)(2,1)S(1)}, u32[]{:S(2)}, u32[]{:S(2)}) collective-permute-start(bf16[400,128]{1,0:T(8,128)(2,1)S(1)} %get-tuple-element.95), channel_id=1, source_target_pairs={{16,0},{20,4},{24,8},{28,12},{0,16},{4,20},{8,24},{12,28},{17,1},{... | collective-permute-start | bytes 307208 | tf_op jit(solution)/shard_map/ppermute | solution.py:116
  55.3 6.1 %collective-permute-start.19 = (bf16[400,128]{1,0:T(8,128)(2,1)S(1)}, bf16[400,128]{1,0:T(8,128)(2,1)S(1)}, u32[]{:S(2)}, u32[]{:S(2)}) collective-permute-start(bf16[400,128]{1,0:T(8,128)(2,1)S(1)} %get-tuple-element.96), channel_id=1, source_target_pairs={{24,0},{28,4},{16,8},{20,12},{8,16},{12,20},{0,24},{4,28},{25,1},{... | collective-permute-start | bytes 307208 | tf_op jit(solution)/shard_map/ppermute | solution.py:116

commit v14 on v12

--- a/solution.py
+++ b/solution.py
@@ -87,6 +87,9 @@
 
     def seen(self, d, k):
         return d ^ k if self.paired else (k - d) % self.size
+
+    def far_first(self):
+        return sorted(range(self.size), key=lambda d: d != self.size // 2)
 
     def pairs(self, d):
         return [(self.source(i, d), i) for i in range(self.size)]
@@ -402,7 +405,7 @@
 
 def gather_rows(head, pieces, all_ref):
     rows, ring = pieces[0].shape[0], Ring(len(pieces))
-    for d, piece in enumerate(pieces):
+    for d, piece in zip(ring.far_first(), pieces):
         at = ring.source(head, d) * rows
         all_ref[pl.ds(pl.multiple_of(at, rows), rows), :] = piece[...]
 
@@ -516,6 +519,7 @@
     )(place, queries, key_vectors, value_rows, write_rate, log_decay)
     got = plan.exchange(packed)
     rows = across_heads([grad_out] * parts)
+    rows = [rows[d] for d in Ring(parts).far_first()]
 
     link, kept = call(
         partial(prepare_kernel, plan),
@@ -592,7 +596,7 @@
         weight_grad = weight_grad + plan.from_mate(shares[d], d)
 
     layer_out = layer_parts[0]
-    for part in layer_parts[1:]:
+    for part in layer_parts[:0:-1]:
         layer_out = layer_out + part.astype(F32)
     grads = after(grads, (layer_out, weight_grad))
     grad_q, grad_k, grad_v, grad_rate, grad_decay = call(

time: 58.4 us -> 56.8 us (0.973)
  waiting for transfers between devices: 9.32 us -> 7.79 us
    ppermute x6, waiting for transfers between devices: 5.51 us -> 3.11 us  [across_heads(): lax.ppermute(pieces[d], 'head', Ring(parts).pairs(d))]
    ppermute x15, waiting for transfers between devices: 3.8 us -> 4.68 us  [exchange(): moved.append(lax.ppermute(pieces[d], 'ctx', pairs))]
  transfers between devices with their start and end apart: 24 -> 24, of which waited for: 6 -> 8; matrix products, arithmetic and copies ran while one was open for 3% -> 3% of each run, Pallas kernels for 21% -> 22%
where the time goes in v14:
time: 56.8 us; the launch traced here: 56.6 us
  starting transfers between devices  32 us (56%)
  Pallas kernels  14.5 us (26%)
  waiting for transfers between devices  7.79 us (14%)
  other arithmetic  1.63 us (3%)
  between operations  0.77 us (1%)
    ppermute x15, starting transfers between devices, exchange(): moved.append(lax.ppermute(pieces[d], 'ctx', pairs))  19 us
    pallas_call x10, Pallas kernels, run(): pl.pallas_call(kernel, out_shape=outs, in_specs=[spec(i) for i in range(l...  14.5 us
    ppermute x6, starting transfers between devices, across_heads(): lax.ppermute(pieces[d], 'head', Ring(parts).pairs(d))  12.8 us
    ppermute x15, waiting for transfers between devices, exchange(): moved.append(lax.ppermute(pieces[d], 'ctx', pairs))  4.68 us
    ppermute x6, waiting for transfers between devices, across_heads(): lax.ppermute(pieces[d], 'head', Ring(parts).pairs(d))  3.11 us
  transfers between devices with their start and end apart: 24, of which 8 were waited for; matrix products, arithmetic and copies ran while one was open for 3% of the time, Pallas kernels for 22%

profile of v14, /device:TPU:0, one launch (start us, length us, event | category | flops | bytes accessed | tf_op | source)
XLA Modules:
  0.0 56.6 jit_solution(18113046578667549037)
XLA Ops:
  0.6 1.2 %shard_map.135 = (bf16[400,128]{1,0:T(8,128)(2,1)S(1)}, bf16[400,128]{1,0:T(8,128)(2,1)S(1)}, bf16[400,128]{1,0:T(8,128)(2,1)S(1)}, bf16[400,128]{1,0:T(8,128)(2,1)S(1)}) custom-call(s32[1]{0:T(128)} %bitcast.1.place_ref, bf16[128,256]{1,0:T(8,128)(2,1)} %q_ref.1, bf16[128,256]{1,0:T(8,128)(2,1)} %k_ref.1, bf16[128,512]{1,0:T(8,128)(2,1)} %v_ref.1, ...), custom_call_target="tpu_custom_call" | custom-call | tf_op jit(solution)/shard_map/pallas_call | solution.py:60
  1.8 3.0 %collective-permute-start = (bf16[400,128]{1,0:T(8,128)(2,1)S(1)}, bf16[400,128]{1,0:T(8,128)(2,1)S(1)}, u32[]{:S(2)}, u32[]{:S(2)}) collective-permute-start(bf16[400,128]{1,0:T(8,128)(2,1)S(1)} %get-tuple-element.61), channel_id=1, source_target_pairs={{8,0},{12,4},{0,8},{4,12},{24,16},{28,20},{16,24},{20,28},{9,1},{1... | collective-permute-start | bytes 307208 | tf_op jit(solution)/shard_map/ppermute | solution.py:115
  4.8 1.5 %collective-permute-start.1 = (bf16[400,128]{1,0:T(8,128)(2,1)S(1)}, bf16[400,128]{1,0:T(8,128)(2,1)S(1)}, u32[]{:S(2)}, u32[]{:S(2)}) collective-permute-start(bf16[400,128]{1,0:T(8,128)(2,1)S(1)} %get-tuple-element.62), channel_id=1, source_target_pairs={{16,0},{20,4},{24,8},{28,12},{0,16},{4,20},{8,24},{12,28},{17,1},{... | collective-permute-start | bytes 307208 | tf_op jit(solution)/shard_map/ppermute | solution.py:115
  6.4 3.0 %collective-permute-start.4 = (bf16[32,2048]{1,0:T(8,128)(2,1)}, bf16[32,2048]{1,0:T(8,128)(2,1)S(1)}, u32[]{:S(2)}, u32[]{:S(2)}) collective-permute-start(bf16[32,2048]{1,0:T(8,128)(2,1)} %refs_1_.2), channel_id=1, source_target_pairs={{2,0},{3,1},{0,2},{1,3},{6,4},{7,5},{4,6},{5,7},{10,8},{11,9},{8,1... | collective-permute-start | bytes 393224 | tf_op jit(solution)/shard_map/ppermute | solution.py:508
  9.4 1.6 %collective-permute-start.5 = (bf16[32,2048]{1,0:T(8,128)(2,1)}, bf16[32,2048]{1,0:T(8,128)(2,1)S(1)}, u32[]{:S(2)}, u32[]{:S(2)}) collective-permute-start(bf16[32,2048]{1,0:T(8,128)(2,1)} %refs_1_.2), channel_id=1, source_target_pairs={{1,0},{0,1},{3,2},{2,3},{5,4},{4,5},{7,6},{6,7},{9,8},{8,9},{11,10... | collective-permute-start | bytes 393224 | tf_op jit(solution)/shard_map/ppermute | solution.py:508
  11.0 0.6 %collective-permute-start.6 = (bf16[32,2048]{1,0:T(8,128)(2,1)}, bf16[32,2048]{1,0:T(8,128)(2,1)S(1)}, u32[]{:S(2)}, u32[]{:S(2)}) collective-permute-start(bf16[32,2048]{1,0:T(8,128)(2,1)} %refs_1_.2), channel_id=1, source_target_pairs={{3,0},{2,1},{1,2},{0,3},{7,4},{6,5},{5,6},{4,7},{11,8},{10,9},{9,1... | collective-permute-start | bytes 393224 | tf_op jit(solution)/shard_map/ppermute | solution.py:508
  11.9 4.1 %shard_map.136 = (f32[4,2,128,128]{3,2,1,0:T(8,128)S(1)}, f32[4,7,128,128]{3,2,1,0:T(8,128)S(1)}) custom-call(s32[5]{0:T(128)} %off_ref.3, s32[1]{0:T(128)} %bitcast.1.place_ref, s32[1]{0:T(128)} %bitcast.2.mate_ref, bf16[400,128]{1,0:T(8,128)(2,1)S(1)} %get-tuple-element.60.refs_0_.refs_4_, bf16[400,128]{1,0:T(8,128)(2,1)S(1)} %collective-permute-done.refs_1_.refs_5_, ...), custom_call_target="tpu_custom_call" | custom-call | flops 20000000000 | tf_op jit(solution)/shard_map/pallas_call | solution.py:60
  16.1 1.6 %collective-permute-done.4.refs_0_ = bf16[32,2048]{1,0:T(8,128)(2,1)S(1)} collective-permute-done((bf16[32,2048]{1,0:T(8,128)(2,1)}, bf16[32,2048]{1,0:T(8,128)(2,1)S(1)}, u32[]{:S(2)}, u32[]{:S(2)}) %collective-permute-start.4) | collective-permute-done | bytes 131104 | tf_op jit(solution)/shard_map/ppermute | solution.py:508
  17.7 1.4 %collective-permute-done.6.refs_3_ = bf16[32,2048]{1,0:T(8,128)(2,1)S(1)} collective-permute-done((bf16[32,2048]{1,0:T(8,128)(2,1)}, bf16[32,2048]{1,0:T(8,128)(2,1)S(1)}, u32[]{:S(2)}, u32[]{:S(2)}) %collective-permute-start.6) | collective-permute-done | bytes 131104 | tf_op jit(solution)/shard_map/ppermute | solution.py:508
  19.2 0.8 %shard_map.137 = (bf16[256,128]{1,0:T(8,128)(2,1)S(1)}, bf16[256,128]{1,0:T(8,128)(2,1)S(1)}, bf16[256,128]{1,0:T(8,128)(2,1)S(1)}, bf16[256,128]{1,0:T(8,128)(2,1)S(1)}) custom-call(s32[1]{0:T(128)} %bitcast.head_ref, s32[1]{0:T(128)} %bitcast.1.place_ref, bf16[32,2048]{1,0:T(8,128)(2,1)S(1)} %collective-permute-done.4.refs_0_, ...), custom_call_target="tpu_custom_call" | custom-call | flops 30000001024 | tf_op jit(solution)/shard_map/pallas_call | solution.py:60
  19.9 1.6 %collective-permute-start.13 = (bf16[256,128]{1,0:T(8,128)(2,1)S(1)}, bf16[256,128]{1,0:T(8,128)(2,1)S(1)}, u32[]{:S(2)}, u32[]{:S(2)}) collective-permute-start(bf16[256,128]{1,0:T(8,128)(2,1)S(1)} %get-tuple-element.77), channel_id=1, source_target_pairs={{8,0},{12,4},{0,8},{4,12},{24,16},{28,20},{16,24},{20,28},{9,1},{1... | collective-permute-start | bytes 196616 | tf_op jit(solution)/shard_map/ppermute | solution.py:115
  21.5 1.5 %collective-permute-start.14 = (bf16[256,128]{1,0:T(8,128)(2,1)S(1)}, bf16[256,128]{1,0:T(8,128)(2,1)S(1)}, u32[]{:S(2)}, u32[]{:S(2)}) collective-permute-start(bf16[256,128]{1,0:T(8,128)(2,1)S(1)} %get-tuple-element.78), channel_id=1, source_target_pairs={{16,0},{20,4},{24,8},{28,12},{0,16},{4,20},{8,24},{12,28},{17,1},{... | collective-permute-start | bytes 196616 | tf_op jit(solution)/shard_map/ppermute | solution.py:115
  23.0 0.5 collective-permute-start.15
  23.5 1.3 %shard_map.138 = (f32[4,128,128]{2,1,0:T(8,128)S(1)}, bf16[4,128,128]{2,1,0:T(8,128)(2,1)S(1)}, bf16[4,128,128]{2,1,0:T(8,128)(2,1)S(1)}, bf16[4,128,128]{2,1,0:T(8,128)(2,1)S(1)}, bf16[4,128,128]{2,1,0:T(8,128)(2,1)S(1)}) custom-call(s32[1]{0:T(128)} %bitcast.1.place_ref, s32[1]{0:T(128)} %bitcast.2.mate_ref, ...), custom_call_target="tpu_custom_call" | custom-call | flops 2500000000 | tf_op jit(solution)/shard_map/pallas_call | solution.py:60
  24.8 1.6 %collective-permute-start.7 = (bf16[4,128,128]{2,1,0:T(8,128)(2,1)S(1)}, bf16[4,128,128]{2,1,0:T(8,128)(2,1)S(1)}, u32[]{:S(2)}, u32[]{:S(2)}) collective-permute-start(bf16[4,128,128]{2,1,0:T(8,128)(2,1)S(1)} %get-tuple-element.70), channel_id=1, source_target_pairs={{8,0},{12,4},{0,8},{4,12},{24,16},{28,20},{16,24},{20,28},{9,1},{1... | collective-permute-start | bytes 393224 | tf_op jit(solution)/shard_map/ppermute | solution.py:115
  26.4 1.5 %collective-permute-start.8 = (bf16[4,128,128]{2,1,0:T(8,128)(2,1)S(1)}, bf16[4,128,128]{2,1,0:T(8,128)(2,1)S(1)}, u32[]{:S(2)}, u32[]{:S(2)}) collective-permute-start(bf16[4,128,128]{2,1,0:T(8,128)(2,1)S(1)} %get-tuple-element.71), channel_id=1, source_target_pairs={{16,0},{20,4},{24,8},{28,12},{0,16},{4,20},{8,24},{12,28},{17,1},{... | collective-permute-start | bytes 393224 | tf_op jit(solution)/shard_map/ppermute | solution.py:115
  29.1 1.5 %collective-permute-start.17 = (bf16[512,128]{1,0:T(8,128)(2,1)S(1)}, bf16[512,128]{1,0:T(8,128)(2,1)S(1)}, u32[]{:S(2)}, u32[]{:S(2)}) collective-permute-start(bf16[512,128]{1,0:T(8,128)(2,1)S(1)} %get-tuple-element.95), channel_id=1, source_target_pairs={{8,0},{12,4},{0,8},{4,12},{24,16},{28,20},{16,24},{20,28},{9,1},{1... | collective-permute-start | bytes 393224 | tf_op jit(solution)/shard_map/ppermute | solution.py:115
  30.6 1.5 %collective-permute-start.18 = (bf16[512,128]{1,0:T(8,128)(2,1)S(1)}, bf16[512,128]{1,0:T(8,128)(2,1)S(1)}, u32[]{:S(2)}, u32[]{:S(2)}) collective-permute-start(bf16[512,128]{1,0:T(8,128)(2,1)S(1)} %get-tuple-element.96), channel_id=1, source_target_pairs={{16,0},{20,4},{24,8},{28,12},{0,16},{4,20},{8,24},{12,28},{17,1},{... | collective-permute-start | bytes 393224 | tf_op jit(solution)/shard_map/ppermute | solution.py:115
  32.1 0.7 %collective-permute-start.19 = (bf16[512,128]{1,0:T(8,128)(2,1)S(1)}, bf16[512,128]{1,0:T(8,128)(2,1)S(1)}, u32[]{:S(2)}, u32[]{:S(2)}) collective-permute-start(bf16[512,128]{1,0:T(8,128)(2,1)S(1)} %get-tuple-element.97), channel_id=1, source_target_pairs={{24,0},{28,4},{16,8},{20,12},{8,16},{12,20},{0,24},{4,28},{25,1},{... | collective-permute-start | bytes 393224 | tf_op jit(solution)/shard_map/ppermute | solution.py:115
  32.8 1.6 %collective-permute-done.9.refs_3_.refs_7_ = bf16[4,128,128]{2,1,0:T(8,128)(2,1)S(1)} collective-permute-done((bf16[4,128,128]{2,1,0:T(8,128)(2,1)S(1)}, bf16[4,128,128]{2,1,0:T(8,128)(2,1)S(1)}, u32[]{:S(2)}, u32[]{:S(2)}) %collective-permute-start.9) | collective-permute-done | bytes 131104 | tf_op jit(solution)/shard_map/ppermute | solution.py:115
  34.5 0.5 shard_map.139
  35.0 2.5 %collective-permute-start.12 = (bf16[32,2048]{1,0:T(8,128)(2,1)S(1)}, bf16[32,2048]{1,0:T(8,128)(2,1)S(1)}, u32[]{:S(2)}, u32[]{:S(2)}) collective-permute-start(bf16[32,2048]{1,0:T(8,128)(2,1)S(1)} %get-tuple-element.76), channel_id=1, source_target_pairs={{1,0},{0,1},{3,2},{2,3},{5,4},{4,5},{7,6},{6,7},{9,8},{8,9},{11,10... | collective-permute-start | bytes 393224 | tf_op jit(solution)/shard_map/ppermute | solution.py:508
  37.5 2.5 %collective-permute-start.11 = (bf16[32,2048]{1,0:T(8,128)(2,1)S(1)}, bf16[32,2048]{1,0:T(8,128)(2,1)S(1)}, u32[]{:S(2)}, u32[]{:S(2)}) collective-permute-start(bf16[32,2048]{1,0:T(8,128)(2,1)S(1)} %get-tuple-element.75), channel_id=1, source_target_pairs={{2,0},{3,1},{0,2},{1,3},{6,4},{7,5},{4,6},{5,7},{10,8},{11,9},{8,1... | collective-permute-start | bytes 393224 | tf_op jit(solution)/shard_map/ppermute | solution.py:508
  40.1 2.5 %collective-permute-start.10 = (bf16[32,2048]{1,0:T(8,128)(2,1)S(1)}, bf16[32,2048]{1,0:T(8,128)(2,1)S(1)}, u32[]{:S(2)}, u32[]{:S(2)}) collective-permute-start(bf16[32,2048]{1,0:T(8,128)(2,1)S(1)} %get-tuple-element.74), channel_id=1, source_target_pairs={{3,0},{2,1},{1,2},{0,3},{7,4},{6,5},{5,6},{4,7},{11,8},{10,9},{9,1... | collective-permute-start | bytes 393224 | tf_op jit(solution)/shard_map/ppermute | solution.py:508
  42.6 0.7 %shard_map.143 = (f32[256,512]{1,0:T(8,128)S(1)}, f32[256,512]{1,0:T(8,128)S(1)}) custom-call(s32[1]{0:T(128)} %bitcast.1.place_ref, s32[1]{0:T(128)} %bitcast.2.mate_ref, bf16[512,128]{1,0:T(8,128)(2,1)S(1)} %get-tuple-element.94.refs_0_, bf16[512,128]{1,0:T(8,128)(2,1)S(1)} %collective-permute-done.17.refs_1_, ...), custom_call_target="tpu_custom_call" | custom-call | flops 1000000000 | tf_op jit(solution)/shard_map/pallas_call | solution.py:60
  43.4 4.4 %shard_map.141 = (bf16[400,128]{1,0:T(8,128)(2,1)S(1)}, bf16[400,128]{1,0:T(8,128)(2,1)S(1)}, bf16[400,128]{1,0:T(8,128)(2,1)S(1)}, bf16[400,128]{1,0:T(8,128)(2,1)S(1)}) custom-call(s32[5]{0:T(128)} %off_ref.3, s32[1]{0:T(128)} %bitcast.1.place_ref, s32[1]{0:T(128)} %bitcast.2.mate_ref, f32[4,2,128,128]{3,2,1,0:T(8,128)S(1)} %get-tuple-element.64.refs_0_, ...), custom_call_target="tpu_custom_call" | custom-call | flops 6000000000 | tf_op jit(solution)/shard_map/pallas_call | solution.py:60
  48.0 1.4 %collective-permute-start.21 = (bf16[400,128]{1,0:T(8,128)(2,1)S(1)}, bf16[400,128]{1,0:T(8,128)(2,1)S(1)}, u32[]{:S(2)}, u32[]{:S(2)}) collective-permute-start(bf16[400,128]{1,0:T(8,128)(2,1)S(1)} %get-tuple-element.101), channel_id=1, source_target_pairs={{16,0},{20,4},{24,8},{28,12},{0,16},{4,20},{8,24},{12,28},{17,1},{... | collective-permute-start | bytes 307208 | tf_op jit(solution)/shard_map/ppermute | solution.py:115
  49.5 2.0 %collective-permute-start.22 = (bf16[400,128]{1,0:T(8,128)(2,1)S(1)}, bf16[400,128]{1,0:T(8,128)(2,1)S(1)}, u32[]{:S(2)}, u32[]{:S(2)}) collective-permute-start(bf16[400,128]{1,0:T(8,128)(2,1)S(1)} %get-tuple-element.102), channel_id=1, source_target_pairs={{24,0},{28,4},{16,8},{20,12},{8,16},{12,20},{0,24},{4,28},{25,1},{... | collective-permute-start | bytes 307208 | tf_op jit(solution)/shard_map/ppermute | solution.py:115
  51.5 0.8 %convert_add_fusion = f32[32,2048]{1,0:T(8,128)} fusion(bf16[32,2048]{1,0:T(8,128)(2,1)S(1)} %collective-permute-done.12, bf16[32,2048]{1,0:T(8,128)(2,1)S(1)} %collective-permute-done.11, f32[32,2048]{1,0:T(8,128)S(1)} %get-tuple-element.73, bf16[32,2048]{1,0:T(8,128)(2,1)S(1)} %collective-permute-done.10), kind=kLoop, calls=%fused_computation | loop fusion | flops 393216 | bytes 917504 | tf_op jit(solution)/shard_map/add | solution.py:600
  52.3 0.9 %add.21 = f32[256,512]{1,0:T(8,128)} add(f32[256,512]{1,0:T(8,128)S(1)} %get-tuple-element.98, f32[256,512]{1,0:T(8,128)S(1)} %collective-permute-done.23) | non-fusion elementwise | flops 131072 | bytes 1572864 | tf_op jit(solution)/shard_map/add | solution.py:596
  53.6 2.2 %collective-permute-done.22.refs_3_ = bf16[400,128]{1,0:T(8,128)(2,1)S(1)} collective-permute-done((bf16[400,128]{1,0:T(8,128)(2,1)S(1)}, bf16[400,128]{1,0:T(8,128)(2,1)S(1)}, u32[]{:S(2)}, u32[]{:S(2)}) %collective-permute-start.22) | collective-permute-done | bytes 102432 | tf_op jit(solution)/shard_map/ppermute | solution.py:115
  55.8 0.9 %shard_map.144 = (f32[128,256]{1,0:T(8,128)}, f32[128,256]{1,0:T(8,128)}, f32[128,512]{1,0:T(8,128)}, f32[4,128]{1,0:T(4,128)}, f32[4,128]{1,0:T(4,128)}) custom-call(s32[1]{0:T(128)} %bitcast.1.place_ref, bf16[400,128]{1,0:T(8,128)(2,1)S(1)} %get-tuple-element.104.refs_0_, bf16[400,128]{1,0:T(8,128)(2,1)S(1)} %collective-permute-done.20.refs_1_, ...), custom_call_target="tpu_custom_call" | custom-call | flops 1000000000 | tf_op jit(solution)/shard_map/pallas_call | solution.py:60
  (32 shorter events, 2.4 us)
Async XLA Ops:
  1.8 9.2 %collective-permute-start = (bf16[400,128]{1,0:T(8,128)(2,1)S(1)}, bf16[400,128]{1,0:T(8,128)(2,1)S(1)}, u32[]{:S(2)}, u32[]{:S(2)}) collective-permute-start(bf16[400,128]{1,0:T(8,128)(2,1)S(1)} %get-tuple-element.61), channel_id=1, source_target_pairs={{8,0},{12,4},{0,8},{4,12},{24,16},{28,20},{16,24},{20,28},{9,1},{1... | collective-permute-start | bytes 307208 | tf_op jit(solution)/shard_map/ppermute | solution.py:115
  4.8 6.8 %collective-permute-start.1 = (bf16[400,128]{1,0:T(8,128)(2,1)S(1)}, bf16[400,128]{1,0:T(8,128)(2,1)S(1)}, u32[]{:S(2)}, u32[]{:S(2)}) collective-permute-start(bf16[400,128]{1,0:T(8,128)(2,1)S(1)} %get-tuple-element.62), channel_id=1, source_target_pairs={{16,0},{20,4},{24,8},{28,12},{0,16},{4,20},{8,24},{12,28},{17,1},{... | collective-permute-start | bytes 307208 | tf_op jit(solution)/shard_map/ppermute | solution.py:115
  6.3 5.6 %collective-permute-start.2 = (bf16[400,128]{1,0:T(8,128)(2,1)S(1)}, bf16[400,128]{1,0:T(8,128)(2,1)S(1)}, u32[]{:S(2)}, u32[]{:S(2)}) collective-permute-start(bf16[400,128]{1,0:T(8,128)(2,1)S(1)} %get-tuple-element.63), channel_id=1, source_target_pairs={{24,0},{28,4},{16,8},{20,12},{8,16},{12,20},{0,24},{4,28},{25,1},{... | collective-permute-start | bytes 307208 | tf_op jit(solution)/shard_map/ppermute | solution.py:115
  6.4 11.4 %collective-permute-start.4 = (bf16[32,2048]{1,0:T(8,128)(2,1)}, bf16[32,2048]{1,0:T(8,128)(2,1)S(1)}, u32[]{:S(2)}, u32[]{:S(2)}) collective-permute-start(bf16[32,2048]{1,0:T(8,128)(2,1)} %refs_1_.2), channel_id=1, source_target_pairs={{2,0},{3,1},{0,2},{1,3},{6,4},{7,5},{4,6},{5,7},{10,8},{11,9},{8,1... | collective-permute-start | bytes 393224 | tf_op jit(solution)/shard_map/ppermute | solution.py:508
  9.4 8.3 %collective-permute-start.5 = (bf16[32,2048]{1,0:T(8,128)(2,1)}, bf16[32,2048]{1,0:T(8,128)(2,1)S(1)}, u32[]{:S(2)}, u32[]{:S(2)}) collective-permute-start(bf16[32,2048]{1,0:T(8,128)(2,1)} %refs_1_.2), channel_id=1, source_target_pairs={{1,0},{0,1},{3,2},{2,3},{5,4},{4,5},{7,6},{6,7},{9,8},{8,9},{11,10... | collective-permute-start | bytes 393224 | tf_op jit(solution)/shard_map/ppermute | solution.py:508
  11.0 8.2 %collective-permute-start.6 = (bf16[32,2048]{1,0:T(8,128)(2,1)}, bf16[32,2048]{1,0:T(8,128)(2,1)S(1)}, u32[]{:S(2)}, u32[]{:S(2)}) collective-permute-start(bf16[32,2048]{1,0:T(8,128)(2,1)} %refs_1_.2), channel_id=1, source_target_pairs={{3,0},{2,1},{1,2},{0,3},{7,4},{6,5},{5,6},{4,7},{11,8},{10,9},{9,1... | collective-permute-start | bytes 393224 | tf_op jit(solution)/shard_map/ppermute | solution.py:508
  11.9 7.3 %copy-start = (bf16[512,2048]{1,0:T(8,128)(2,1)S(1)}, bf16[512,2048]{1,0:T(8,128)(2,1)}, u32[]{:S(2)}) copy-start(bf16[512,2048]{1,0:T(8,128)(2,1)} %refs_4_.2) | copy-start | bytes 6291460
  11.9 7.3 %copy-start.1 = (bf16[32,2048]{1,0:T(8,128)(2,1)S(1)}, bf16[32,2048]{1,0:T(8,128)(2,1)}, u32[]{:S(2)}) copy-start(bf16[32,2048]{1,0:T(8,128)(2,1)} %refs_1_.2) | copy-start | bytes 393220
  16.0 7.5 %collective-permute-start.3 = (f32[4,2,128,128]{3,2,1,0:T(8,128)S(1)}, f32[4,2,128,128]{3,2,1,0:T(8,128)S(1)}, u32[]{:S(2)}, u32[]{:S(2)}) collective-permute-start(f32[4,2,128,128]{3,2,1,0:T(8,128)S(1)} %get-tuple-element.64.refs_0_), channel_id=1, source_target_pairs={{4,0},{0,4},{12,8},{8,12},{20,16},{16,20},{28,24},{24,28},{5,1},{1... | collective-permute-start | bytes 1572872 | tf_op jit(solution)/shard_map/ppermute | solution.py:121
  19.9 8.0 %collective-permute-start.13 = (bf16[256,128]{1,0:T(8,128)(2,1)S(1)}, bf16[256,128]{1,0:T(8,128)(2,1)S(1)}, u32[]{:S(2)}, u32[]{:S(2)}) collective-permute-start(bf16[256,128]{1,0:T(8,128)(2,1)S(1)} %get-tuple-element.77), channel_id=1, source_target_pairs={{8,0},{12,4},{0,8},{4,12},{24,16},{28,20},{16,24},{20,28},{9,1},{1... | collective-permute-start | bytes 196616 | tf_op jit(solution)/shard_map/ppermute | solution.py:115
  21.5 6.9 %collective-permute-start.14 = (bf16[256,128]{1,0:T(8,128)(2,1)S(1)}, bf16[256,128]{1,0:T(8,128)(2,1)S(1)}, u32[]{:S(2)}, u32[]{:S(2)}) collective-permute-start(bf16[256,128]{1,0:T(8,128)(2,1)S(1)} %get-tuple-element.78), channel_id=1, source_target_pairs={{16,0},{20,4},{24,8},{28,12},{0,16},{4,20},{8,24},{12,28},{17,1},{... | collective-permute-start | bytes 196616 | tf_op jit(solution)/shard_map/ppermute | solution.py:115
  23.0 5.4 %collective-permute-start.15 = (bf16[256,128]{1,0:T(8,128)(2,1)S(1)}, bf16[256,128]{1,0:T(8,128)(2,1)S(1)}, u32[]{:S(2)}, u32[]{:S(2)}) collective-permute-start(bf16[256,128]{1,0:T(8,128)(2,1)S(1)} %get-tuple-element.79), channel_id=1, source_target_pairs={{24,0},{28,4},{16,8},{20,12},{8,16},{12,20},{0,24},{4,28},{25,1},{... | collective-permute-start | bytes 196616 | tf_op jit(solution)/shard_map/ppermute | solution.py:115
  24.8 5.8 %collective-permute-start.7 = (bf16[4,128,128]{2,1,0:T(8,128)(2,1)S(1)}, bf16[4,128,128]{2,1,0:T(8,128)(2,1)S(1)}, u32[]{:S(2)}, u32[]{:S(2)}) collective-permute-start(bf16[4,128,128]{2,1,0:T(8,128)(2,1)S(1)} %get-tuple-element.70), channel_id=1, source_target_pairs={{8,0},{12,4},{0,8},{4,12},{24,16},{28,20},{16,24},{20,28},{9,1},{1... | collective-permute-start | bytes 393224 | tf_op jit(solution)/shard_map/ppermute | solution.py:115
  26.4 5.7 %collective-permute-start.8 = (bf16[4,128,128]{2,1,0:T(8,128)(2,1)S(1)}, bf16[4,128,128]{2,1,0:T(8,128)(2,1)S(1)}, u32[]{:S(2)}, u32[]{:S(2)}) collective-permute-start(bf16[4,128,128]{2,1,0:T(8,128)(2,1)S(1)} %get-tuple-element.71), channel_id=1, source_target_pairs={{16,0},{20,4},{24,8},{28,12},{0,16},{4,20},{8,24},{12,28},{17,1},{... | collective-permute-start | bytes 393224 | tf_op jit(solution)/shard_map/ppermute | solution.py:115
  27.9 6.6 %collective-permute-start.9 = (bf16[4,128,128]{2,1,0:T(8,128)(2,1)S(1)}, bf16[4,128,128]{2,1,0:T(8,128)(2,1)S(1)}, u32[]{:S(2)}, u32[]{:S(2)}) collective-permute-start(bf16[4,128,128]{2,1,0:T(8,128)(2,1)S(1)} %get-tuple-element.72), channel_id=1, source_target_pairs={{24,0},{28,4},{16,8},{20,12},{8,16},{12,20},{0,24},{4,28},{25,1},{... | collective-permute-start | bytes 393224 | tf_op jit(solution)/shard_map/ppermute | solution.py:115
  28.7 14.7 %collective-permute-start.16 = (f32[4,128,128]{2,1,0:T(8,128)S(1)}, f32[4,128,128]{2,1,0:T(8,128)S(1)}, u32[]{:S(2)}, u32[]{:S(2)}) collective-permute-start(f32[4,128,128]{2,1,0:T(8,128)S(1)} %shard_map.140.refs_2_), channel_id=1, source_target_pairs={{4,0},{0,4},{12,8},{8,12},{20,16},{16,20},{28,24},{24,28},{5,1},{1... | collective-permute-start | bytes 786440 | tf_op jit(solution)/shard_map/ppermute | solution.py:121
  29.1 8.5 %collective-permute-start.17 = (bf16[512,128]{1,0:T(8,128)(2,1)S(1)}, bf16[512,128]{1,0:T(8,128)(2,1)S(1)}, u32[]{:S(2)}, u32[]{:S(2)}) collective-permute-start(bf16[512,128]{1,0:T(8,128)(2,1)S(1)} %get-tuple-element.95), channel_id=1, source_target_pairs={{8,0},{12,4},{0,8},{4,12},{24,16},{28,20},{16,24},{20,28},{9,1},{1... | collective-permute-start | bytes 393224 | tf_op jit(solution)/shard_map/ppermute | solution.py:115
  30.6 9.5 %collective-permute-start.18 = (bf16[512,128]{1,0:T(8,128)(2,1)S(1)}, bf16[512,128]{1,0:T(8,128)(2,1)S(1)}, u32[]{:S(2)}, u32[]{:S(2)}) collective-permute-start(bf16[512,128]{1,0:T(8,128)(2,1)S(1)} %get-tuple-element.96), channel_id=1, source_target_pairs={{16,0},{20,4},{24,8},{28,12},{0,16},{4,20},{8,24},{12,28},{17,1},{... | collective-permute-start | bytes 393224 | tf_op jit(solution)/shard_map/ppermute | solution.py:115
  32.1 10.5 %collective-permute-start.19 = (bf16[512,128]{1,0:T(8,128)(2,1)S(1)}, bf16[512,128]{1,0:T(8,128)(2,1)S(1)}, u32[]{:S(2)}, u32[]{:S(2)}) collective-permute-start(bf16[512,128]{1,0:T(8,128)(2,1)S(1)} %get-tuple-element.97), channel_id=1, source_target_pairs={{24,0},{28,4},{16,8},{20,12},{8,16},{12,20},{0,24},{4,28},{25,1},{... | collective-permute-start | bytes 393224 | tf_op jit(solution)/shard_map/ppermute | solution.py:115
  35.0 13.0 %collective-permute-start.12 = (bf16[32,2048]{1,0:T(8,128)(2,1)S(1)}, bf16[32,2048]{1,0:T(8,128)(2,1)S(1)}, u32[]{:S(2)}, u32[]{:S(2)}) collective-permute-start(bf16[32,2048]{1,0:T(8,128)(2,1)S(1)} %get-tuple-element.76), channel_id=1, source_target_pairs={{1,0},{0,1},{3,2},{2,3},{5,4},{4,5},{7,6},{6,7},{9,8},{8,9},{11,10... | collective-permute-start | bytes 393224 | tf_op jit(solution)/shard_map/ppermute | solution.py:508
  37.5 12.0 %collective-permute-start.11 = (bf16[32,2048]{1,0:T(8,128)(2,1)S(1)}, bf16[32,2048]{1,0:T(8,128)(2,1)S(1)}, u32[]{:S(2)}, u32[]{:S(2)}) collective-permute-start(bf16[32,2048]{1,0:T(8,128)(2,1)S(1)} %get-tuple-element.75), channel_id=1, source_target_pairs={{2,0},{3,1},{0,2},{1,3},{6,4},{7,5},{4,6},{5,7},{10,8},{11,9},{8,1... | collective-permute-start | bytes 393224 | tf_op jit(solution)/shard_map/ppermute | solution.py:508
  40.1 11.4 %collective-permute-start.10 = (bf16[32,2048]{1,0:T(8,128)(2,1)S(1)}, bf16[32,2048]{1,0:T(8,128)(2,1)S(1)}, u32[]{:S(2)}, u32[]{:S(2)}) collective-permute-start(bf16[32,2048]{1,0:T(8,128)(2,1)S(1)} %get-tuple-element.74), channel_id=1, source_target_pairs={{3,0},{2,1},{1,2},{0,3},{7,4},{6,5},{5,6},{4,7},{11,8},{10,9},{9,1... | collective-permute-start | bytes 393224 | tf_op jit(solution)/shard_map/ppermute | solution.py:508
  43.3 9.0 %collective-permute-start.23 = (f32[256,512]{1,0:T(8,128)S(1)}, f32[256,512]{1,0:T(8,128)S(1)}, u32[]{:S(2)}, u32[]{:S(2)}) collective-permute-start(f32[256,512]{1,0:T(8,128)S(1)} %get-tuple-element.103), channel_id=1, source_target_pairs={{4,0},{0,4},{12,8},{8,12},{20,16},{16,20},{28,24},{24,28},{5,1},{1... | collective-permute-start | bytes 1572872 | tf_op jit(solution)/shard_map/ppermute | solution.py:121
  47.8 5.7 %collective-permute-start.20 = (bf16[400,128]{1,0:T(8,128)(2,1)S(1)}, bf16[400,128]{1,0:T(8,128)(2,1)S(1)}, u32[]{:S(2)}, u32[]{:S(2)}) collective-permute-start(bf16[400,128]{1,0:T(8,128)(2,1)S(1)} %get-tuple-element.100), channel_id=1, source_target_pairs={{8,0},{12,4},{0,8},{4,12},{24,16},{28,20},{16,24},{20,28},{9,1},{1... | collective-permute-start | bytes 307208 | tf_op jit(solution)/shard_map/ppermute | solution.py:115
  48.0 5.6 %collective-permute-start.21 = (bf16[400,128]{1,0:T(8,128)(2,1)S(1)}, bf16[400,128]{1,0:T(8,128)(2,1)S(1)}, u32[]{:S(2)}, u32[]{:S(2)}) collective-permute-start(bf16[400,128]{1,0:T(8,128)(2,1)S(1)} %get-tuple-element.101), channel_id=1, source_target_pairs={{16,0},{20,4},{24,8},{28,12},{0,16},{4,20},{8,24},{12,28},{17,1},{... | collective-permute-start | bytes 307208 | tf_op jit(solution)/shard_map/ppermute | solution.py:115
  49.5 6.3 %collective-permute-start.22 = (bf16[400,128]{1,0:T(8,128)(2,1)S(1)}, bf16[400,128]{1,0:T(8,128)(2,1)S(1)}, u32[]{:S(2)}, u32[]{:S(2)}) collective-permute-start(bf16[400,128]{1,0:T(8,128)(2,1)S(1)} %get-tuple-element.102), channel_id=1, source_target_pairs={{24,0},{28,4},{16,8},{20,12},{8,16},{12,20},{0,24},{4,28},{25,1},{... | collective-permute-start | bytes 307208 | tf_op jit(solution)/shard_map/ppermute | solution.py:115

commit v15 on v14

--- a/solution.py
+++ b/solution.py
@@ -89,7 +89,7 @@
         return d ^ k if self.paired else (k - d) % self.size
 
     def far_first(self):
-        return sorted(range(self.size), key=lambda d: d != self.size // 2)
+        return sorted(range(self.size), key=lambda d: (d != self.size // 2, -d))
 
     def pairs(self, d):
         return [(self.source(i, d), i) for i in range(self.size)]
@@ -470,7 +470,7 @@
 def finish_kernel(plan, place_ref, *refs):
     pieces, (q_ref, k_ref, v_ref, rate_ref, decay_ref, in_ref) = refs[: plan.hv], refs[plan.hv :]
     tok = plan.tok
-    for d, ref in enumerate(pieces):
+    for d, ref in enumerate(reversed(pieces)):
         in_ref[plan.ring.source(place_ref[0], d)] = ref[...]
     for kh in range(plan.hk):
         mine = [h for h in range(plan.hv) if plan.key_head(h) == kh]
@@ -596,9 +596,9 @@
         weight_grad = weight_grad + plan.from_mate(shares[d], d)
 
     layer_out = layer_parts[0]
-    for part in layer_parts[:0:-1]:
-        layer_out = layer_out + part.astype(F32)
-    grads = after(grads, (layer_out, weight_grad))
+    for d in Ring(parts).far_first()[-2::-1]:
+        layer_out = layer_out + layer_parts[d].astype(F32)
+    grads = after(grads[::-1], (layer_out, weight_grad))
     grad_q, grad_k, grad_v, grad_rate, grad_decay = call(
         partial(finish_kernel, plan),
         (

time: 56.8 us -> 57.9 us (1.019)
  waiting for transfers between devices: 7.79 us -> 8.96 us
    ppermute x15, waiting for transfers between devices: 4.68 us -> 5.81 us  [exchange(): moved.append(lax.ppermute(pieces[d], 'ctx', pairs))]
  transfers between devices with their start and end apart: 24 -> 24, of which waited for: 8 -> 7; matrix products, arithmetic and copies ran while one was open for 3% -> 3% of each run, Pallas kernels for 22% -> 22%
where the time goes in v15:
time: 57.9 us; the launch traced here: 57.7 us
  starting transfers between devices  31.9 us (55%)
  Pallas kernels  14.5 us (25%)
  waiting for transfers between devices  8.96 us (15%)
  other arithmetic  1.63 us (3%)
  between operations  0.77 us (1%)
    ppermute x15, starting transfers between devices, exchange(): moved.append(lax.ppermute(pieces[d], 'ctx', pairs))  18.8 us
    pallas_call x10, Pallas kernels, run(): pl.pallas_call(kernel, out_shape=outs, in_specs=[spec(i) for i in range(l...  14.5 us
    ppermute x6, starting transfers between devices, across_heads(): lax.ppermute(pieces[d], 'head', Ring(parts).pairs(d))  12.9 us
    ppermute x15, waiting for transfers between devices, exchange(): moved.append(lax.ppermute(pieces[d], 'ctx', pairs))  5.81 us
    ppermute x6, waiting for transfers between devices, across_heads(): lax.ppermute(pieces[d], 'head', Ring(parts).pairs(d))  3.14 us
  transfers between devices with their start and end apart: 24, of which 7 were waited for; matrix products, arithmetic and copies ran while one was open for 3% of the time, Pallas kernels for 22%

profile of v15, /device:TPU:0, one launch (start us, length us, event | category | flops | bytes accessed | tf_op | source)
XLA Modules:
  0.0 57.7 jit_solution(4012884238929599314)
XLA Ops:
  0.6 1.2 %shard_map.135 = (bf16[400,128]{1,0:T(8,128)(2,1)S(1)}, bf16[400,128]{1,0:T(8,128)(2,1)S(1)}, bf16[400,128]{1,0:T(8,128)(2,1)S(1)}, bf16[400,128]{1,0:T(8,128)(2,1)S(1)}) custom-call(s32[1]{0:T(128)} %bitcast.1.place_ref, bf16[128,256]{1,0:T(8,128)(2,1)} %q_ref.1, bf16[128,256]{1,0:T(8,128)(2,1)} %k_ref.1, bf16[128,512]{1,0:T(8,128)(2,1)} %v_ref.1, ...), custom_call_target="tpu_custom_call" | custom-call | tf_op jit(solution)/shard_map/pallas_call | solution.py:60
  1.8 3.0 %collective-permute-start = (bf16[400,128]{1,0:T(8,128)(2,1)S(1)}, bf16[400,128]{1,0:T(8,128)(2,1)S(1)}, u32[]{:S(2)}, u32[]{:S(2)}) collective-permute-start(bf16[400,128]{1,0:T(8,128)(2,1)S(1)} %get-tuple-element.61), channel_id=1, source_target_pairs={{8,0},{12,4},{0,8},{4,12},{24,16},{28,20},{16,24},{20,28},{9,1},{1... | collective-permute-start | bytes 307208 | tf_op jit(solution)/shard_map/ppermute | solution.py:115
  4.8 1.5 %collective-permute-start.1 = (bf16[400,128]{1,0:T(8,128)(2,1)S(1)}, bf16[400,128]{1,0:T(8,128)(2,1)S(1)}, u32[]{:S(2)}, u32[]{:S(2)}) collective-permute-start(bf16[400,128]{1,0:T(8,128)(2,1)S(1)} %get-tuple-element.62), channel_id=1, source_target_pairs={{16,0},{20,4},{24,8},{28,12},{0,16},{4,20},{8,24},{12,28},{17,1},{... | collective-permute-start | bytes 307208 | tf_op jit(solution)/shard_map/ppermute | solution.py:115
  6.4 3.0 %collective-permute-start.4 = (bf16[32,2048]{1,0:T(8,128)(2,1)}, bf16[32,2048]{1,0:T(8,128)(2,1)S(1)}, u32[]{:S(2)}, u32[]{:S(2)}) collective-permute-start(bf16[32,2048]{1,0:T(8,128)(2,1)} %refs_3_.2), channel_id=1, source_target_pairs={{2,0},{3,1},{0,2},{1,3},{6,4},{7,5},{4,6},{5,7},{10,8},{11,9},{8,1... | collective-permute-start | bytes 393224 | tf_op jit(solution)/shard_map/ppermute | solution.py:508
  9.4 1.3 %collective-permute-start.5 = (bf16[32,2048]{1,0:T(8,128)(2,1)}, bf16[32,2048]{1,0:T(8,128)(2,1)S(1)}, u32[]{:S(2)}, u32[]{:S(2)}) collective-permute-start(bf16[32,2048]{1,0:T(8,128)(2,1)} %refs_3_.2), channel_id=1, source_target_pairs={{3,0},{2,1},{1,2},{0,3},{7,4},{6,5},{5,6},{4,7},{11,8},{10,9},{9,1... | collective-permute-start | bytes 393224 | tf_op jit(solution)/shard_map/ppermute | solution.py:508
  11.0 0.9 %collective-permute-done.2.refs_3_.refs_7_ = bf16[400,128]{1,0:T(8,128)(2,1)S(1)} collective-permute-done((bf16[400,128]{1,0:T(8,128)(2,1)S(1)}, bf16[400,128]{1,0:T(8,128)(2,1)S(1)}, u32[]{:S(2)}, u32[]{:S(2)}) %collective-permute-start.2) | collective-permute-done | bytes 102432 | tf_op jit(solution)/shard_map/ppermute | solution.py:115
  11.9 4.1 %shard_map.136 = (f32[4,2,128,128]{3,2,1,0:T(8,128)S(1)}, f32[4,7,128,128]{3,2,1,0:T(8,128)S(1)}) custom-call(s32[5]{0:T(128)} %off_ref.3, s32[1]{0:T(128)} %bitcast.1.place_ref, s32[1]{0:T(128)} %bitcast.2.mate_ref, bf16[400,128]{1,0:T(8,128)(2,1)S(1)} %get-tuple-element.60.refs_0_.refs_4_, bf16[400,128]{1,0:T(8,128)(2,1)S(1)} %collective-permute-done.refs_1_.refs_5_, ...), custom_call_target="tpu_custom_call" | custom-call | flops 20000000000 | tf_op jit(solution)/shard_map/pallas_call | solution.py:60
  16.1 3.0 %collective-permute-done.4.refs_0_ = bf16[32,2048]{1,0:T(8,128)(2,1)S(1)} collective-permute-done((bf16[32,2048]{1,0:T(8,128)(2,1)}, bf16[32,2048]{1,0:T(8,128)(2,1)S(1)}, u32[]{:S(2)}, u32[]{:S(2)}) %collective-permute-start.4) | collective-permute-done | bytes 131104 | tf_op jit(solution)/shard_map/ppermute | solution.py:508
  19.3 0.8 %shard_map.137 = (bf16[256,128]{1,0:T(8,128)(2,1)S(1)}, bf16[256,128]{1,0:T(8,128)(2,1)S(1)}, bf16[256,128]{1,0:T(8,128)(2,1)S(1)}, bf16[256,128]{1,0:T(8,128)(2,1)S(1)}) custom-call(s32[1]{0:T(128)} %bitcast.head_ref, s32[1]{0:T(128)} %bitcast.1.place_ref, bf16[32,2048]{1,0:T(8,128)(2,1)S(1)} %collective-permute-done.4.refs_0_, ...), custom_call_target="tpu_custom_call" | custom-call | flops 30000001024 | tf_op jit(solution)/shard_map/pallas_call | solution.py:60
  20.0 1.6 %collective-permute-start.13 = (bf16[256,128]{1,0:T(8,128)(2,1)S(1)}, bf16[256,128]{1,0:T(8,128)(2,1)S(1)}, u32[]{:S(2)}, u32[]{:S(2)}) collective-permute-start(bf16[256,128]{1,0:T(8,128)(2,1)S(1)} %get-tuple-element.77), channel_id=1, source_target_pairs={{8,0},{12,4},{0,8},{4,12},{24,16},{28,20},{16,24},{20,28},{9,1},{1... | collective-permute-start | bytes 196616 | tf_op jit(solution)/shard_map/ppermute | solution.py:115
  21.7 1.5 %collective-permute-start.14 = (bf16[256,128]{1,0:T(8,128)(2,1)S(1)}, bf16[256,128]{1,0:T(8,128)(2,1)S(1)}, u32[]{:S(2)}, u32[]{:S(2)}) collective-permute-start(bf16[256,128]{1,0:T(8,128)(2,1)S(1)} %get-tuple-element.78), channel_id=1, source_target_pairs={{16,0},{20,4},{24,8},{28,12},{0,16},{4,20},{8,24},{12,28},{17,1},{... | collective-permute-start | bytes 196616 | tf_op jit(solution)/shard_map/ppermute | solution.py:115
  23.6 1.3 %shard_map.138 = (f32[4,128,128]{2,1,0:T(8,128)S(1)}, bf16[4,128,128]{2,1,0:T(8,128)(2,1)S(1)}, bf16[4,128,128]{2,1,0:T(8,128)(2,1)S(1)}, bf16[4,128,128]{2,1,0:T(8,128)(2,1)S(1)}, bf16[4,128,128]{2,1,0:T(8,128)(2,1)S(1)}) custom-call(s32[1]{0:T(128)} %bitcast.1.place_ref, s32[1]{0:T(128)} %bitcast.2.mate_ref, ...), custom_call_target="tpu_custom_call" | custom-call | flops 2500000000 | tf_op jit(solution)/shard_map/pallas_call | solution.py:60
  24.9 1.6 %collective-permute-start.7 = (bf16[4,128,128]{2,1,0:T(8,128)(2,1)S(1)}, bf16[4,128,128]{2,1,0:T(8,128)(2,1)S(1)}, u32[]{:S(2)}, u32[]{:S(2)}) collective-permute-start(bf16[4,128,128]{2,1,0:T(8,128)(2,1)S(1)} %get-tuple-element.70), channel_id=1, source_target_pairs={{8,0},{12,4},{0,8},{4,12},{24,16},{28,20},{16,24},{20,28},{9,1},{1... | collective-permute-start | bytes 393224 | tf_op jit(solution)/shard_map/ppermute | solution.py:115
  26.5 1.5 %collective-permute-start.8 = (bf16[4,128,128]{2,1,0:T(8,128)(2,1)S(1)}, bf16[4,128,128]{2,1,0:T(8,128)(2,1)S(1)}, u32[]{:S(2)}, u32[]{:S(2)}) collective-permute-start(bf16[4,128,128]{2,1,0:T(8,128)(2,1)S(1)} %get-tuple-element.71), channel_id=1, source_target_pairs={{16,0},{20,4},{24,8},{28,12},{0,16},{4,20},{8,24},{12,28},{17,1},{... | collective-permute-start | bytes 393224 | tf_op jit(solution)/shard_map/ppermute | solution.py:115
  29.6 1.1 %collective-permute-start.17 = (bf16[512,128]{1,0:T(8,128)(2,1)S(1)}, bf16[512,128]{1,0:T(8,128)(2,1)S(1)}, u32[]{:S(2)}, u32[]{:S(2)}) collective-permute-start(bf16[512,128]{1,0:T(8,128)(2,1)S(1)} %get-tuple-element.95), channel_id=1, source_target_pairs={{8,0},{12,4},{0,8},{4,12},{24,16},{28,20},{16,24},{20,28},{9,1},{1... | collective-permute-start | bytes 393224 | tf_op jit(solution)/shard_map/ppermute | solution.py:115
  30.7 1.5 %collective-permute-start.18 = (bf16[512,128]{1,0:T(8,128)(2,1)S(1)}, bf16[512,128]{1,0:T(8,128)(2,1)S(1)}, u32[]{:S(2)}, u32[]{:S(2)}) collective-permute-start(bf16[512,128]{1,0:T(8,128)(2,1)S(1)} %get-tuple-element.96), channel_id=1, source_target_pairs={{16,0},{20,4},{24,8},{28,12},{0,16},{4,20},{8,24},{12,28},{17,1},{... | collective-permute-start | bytes 393224 | tf_op jit(solution)/shard_map/ppermute | solution.py:115
  32.3 0.9 %collective-permute-start.19 = (bf16[512,128]{1,0:T(8,128)(2,1)S(1)}, bf16[512,128]{1,0:T(8,128)(2,1)S(1)}, u32[]{:S(2)}, u32[]{:S(2)}) collective-permute-start(bf16[512,128]{1,0:T(8,128)(2,1)S(1)} %get-tuple-element.97), channel_id=1, source_target_pairs={{24,0},{28,4},{16,8},{20,12},{8,16},{12,20},{0,24},{4,28},{25,1},{... | collective-permute-start | bytes 393224 | tf_op jit(solution)/shard_map/ppermute | solution.py:115
  33.2 1.2 %collective-permute-done.9.refs_3_.refs_7_ = bf16[4,128,128]{2,1,0:T(8,128)(2,1)S(1)} collective-permute-done((bf16[4,128,128]{2,1,0:T(8,128)(2,1)S(1)}, bf16[4,128,128]{2,1,0:T(8,128)(2,1)S(1)}, u32[]{:S(2)}, u32[]{:S(2)}) %collective-permute-start.9) | collective-permute-done | bytes 131104 | tf_op jit(solution)/shard_map/ppermute | solution.py:115
  34.4 0.5 shard_map.139
  34.9 3.2 %collective-permute-start.10 = (bf16[32,2048]{1,0:T(8,128)(2,1)S(1)}, bf16[32,2048]{1,0:T(8,128)(2,1)S(1)}, u32[]{:S(2)}, u32[]{:S(2)}) collective-permute-start(bf16[32,2048]{1,0:T(8,128)(2,1)S(1)} %get-tuple-element.74), channel_id=1, source_target_pairs={{1,0},{0,1},{3,2},{2,3},{5,4},{4,5},{7,6},{6,7},{9,8},{8,9},{11,10... | collective-permute-start | bytes 393224 | tf_op jit(solution)/shard_map/ppermute | solution.py:508
  38.1 2.0 %collective-permute-start.12 = (bf16[32,2048]{1,0:T(8,128)(2,1)S(1)}, bf16[32,2048]{1,0:T(8,128)(2,1)S(1)}, u32[]{:S(2)}, u32[]{:S(2)}) collective-permute-start(bf16[32,2048]{1,0:T(8,128)(2,1)S(1)} %get-tuple-element.76), channel_id=1, source_target_pairs={{2,0},{3,1},{0,2},{1,3},{6,4},{7,5},{4,6},{5,7},{10,8},{11,9},{8,1... | collective-permute-start | bytes 393224 | tf_op jit(solution)/shard_map/ppermute | solution.py:508
  40.1 3.0 %collective-permute-start.11 = (bf16[32,2048]{1,0:T(8,128)(2,1)S(1)}, bf16[32,2048]{1,0:T(8,128)(2,1)S(1)}, u32[]{:S(2)}, u32[]{:S(2)}) collective-permute-start(bf16[32,2048]{1,0:T(8,128)(2,1)S(1)} %get-tuple-element.75), channel_id=1, source_target_pairs={{3,0},{2,1},{1,2},{0,3},{7,4},{6,5},{5,6},{4,7},{11,8},{10,9},{9,1... | collective-permute-start | bytes 393224 | tf_op jit(solution)/shard_map/ppermute | solution.py:508
  43.2 0.7 %shard_map.143 = (f32[256,512]{1,0:T(8,128)S(1)}, f32[256,512]{1,0:T(8,128)S(1)}) custom-call(s32[1]{0:T(128)} %bitcast.1.place_ref, s32[1]{0:T(128)} %bitcast.2.mate_ref, bf16[512,128]{1,0:T(8,128)(2,1)S(1)} %get-tuple-element.94.refs_0_, bf16[512,128]{1,0:T(8,128)(2,1)S(1)} %collective-permute-done.17.refs_1_, ...), custom_call_target="tpu_custom_call" | custom-call | flops 1000000000 | tf_op jit(solution)/shard_map/pallas_call | solution.py:60
  44.0 4.4 %shard_map.141 = (bf16[400,128]{1,0:T(8,128)(2,1)S(1)}, bf16[400,128]{1,0:T(8,128)(2,1)S(1)}, bf16[400,128]{1,0:T(8,128)(2,1)S(1)}, bf16[400,128]{1,0:T(8,128)(2,1)S(1)}) custom-call(s32[5]{0:T(128)} %off_ref.3, s32[1]{0:T(128)} %bitcast.1.place_ref, s32[1]{0:T(128)} %bitcast.2.mate_ref, f32[4,2,128,128]{3,2,1,0:T(8,128)S(1)} %get-tuple-element.64.refs_0_, ...), custom_call_target="tpu_custom_call" | custom-call | flops 6000000000 | tf_op jit(solution)/shard_map/pallas_call | solution.py:60
  48.5 1.2 %collective-permute-start.20 = (bf16[400,128]{1,0:T(8,128)(2,1)S(1)}, bf16[400,128]{1,0:T(8,128)(2,1)S(1)}, u32[]{:S(2)}, u32[]{:S(2)}) collective-permute-start(bf16[400,128]{1,0:T(8,128)(2,1)S(1)} %get-tuple-element.99), channel_id=1, source_target_pairs={{24,0},{28,4},{16,8},{20,12},{8,16},{12,20},{0,24},{4,28},{25,1},{... | collective-permute-start | bytes 307208 | tf_op jit(solution)/shard_map/ppermute | solution.py:115
  49.7 1.0 %collective-permute-start.21 = (bf16[400,128]{1,0:T(8,128)(2,1)S(1)}, bf16[400,128]{1,0:T(8,128)(2,1)S(1)}, u32[]{:S(2)}, u32[]{:S(2)}) collective-permute-start(bf16[400,128]{1,0:T(8,128)(2,1)S(1)} %get-tuple-element.100), channel_id=1, source_target_pairs={{16,0},{20,4},{24,8},{28,12},{0,16},{4,20},{8,24},{12,28},{17,1},{... | collective-permute-start | bytes 307208 | tf_op jit(solution)/shard_map/ppermute | solution.py:115
  50.7 1.4 %collective-permute-start.22 = (bf16[400,128]{1,0:T(8,128)(2,1)S(1)}, bf16[400,128]{1,0:T(8,128)(2,1)S(1)}, u32[]{:S(2)}, u32[]{:S(2)}) collective-permute-start(bf16[400,128]{1,0:T(8,128)(2,1)S(1)} %get-tuple-element.101), channel_id=1, source_target_pairs={{8,0},{12,4},{0,8},{4,12},{24,16},{28,20},{16,24},{20,28},{9,1},{1... | collective-permute-start | bytes 307208 | tf_op jit(solution)/shard_map/ppermute | solution.py:115
  52.1 0.8 %convert_add_fusion = f32[32,2048]{1,0:T(8,128)} fusion(bf16[32,2048]{1,0:T(8,128)(2,1)S(1)} %collective-permute-done.12, bf16[32,2048]{1,0:T(8,128)(2,1)S(1)} %collective-permute-done.11, f32[32,2048]{1,0:T(8,128)S(1)} %get-tuple-element.73, bf16[32,2048]{1,0:T(8,128)(2,1)S(1)} %collective-permute-done.10), kind=kLoop, calls=%fused_computation | loop fusion | flops 393216 | bytes 917504 | tf_op jit(solution)/shard_map/add | solution.py:600
  52.8 0.9 %add.21 = f32[256,512]{1,0:T(8,128)} add(f32[256,512]{1,0:T(8,128)S(1)} %get-tuple-element.98, f32[256,512]{1,0:T(8,128)S(1)} %collective-permute-done.23) | non-fusion elementwise | flops 131072 | bytes 1572864 | tf_op jit(solution)/shard_map/add | solution.py:596
  53.7 1.4 %collective-permute-done.20.refs_0_ = bf16[400,128]{1,0:T(8,128)(2,1)S(1)} collective-permute-done((bf16[400,128]{1,0:T(8,128)(2,1)S(1)}, bf16[400,128]{1,0:T(8,128)(2,1)S(1)}, u32[]{:S(2)}, u32[]{:S(2)}) %collective-permute-start.20) | collective-permute-done | bytes 102432 | tf_op jit(solution)/shard_map/ppermute | solution.py:115
  55.2 1.7 %collective-permute-done.21.refs_1_ = bf16[400,128]{1,0:T(8,128)(2,1)S(1)} collective-permute-done((bf16[400,128]{1,0:T(8,128)(2,1)S(1)}, bf16[400,128]{1,0:T(8,128)(2,1)S(1)}, u32[]{:S(2)}, u32[]{:S(2)}) %collective-permute-start.21) | collective-permute-done | bytes 102432 | tf_op jit(solution)/shard_map/ppermute | solution.py:115
  56.9 0.9 %shard_map.144 = (f32[128,256]{1,0:T(8,128)}, f32[128,256]{1,0:T(8,128)}, f32[128,512]{1,0:T(8,128)}, f32[4,128]{1,0:T(4,128)}, f32[4,128]{1,0:T(4,128)}) custom-call(s32[1]{0:T(128)} %bitcast.1.place_ref, bf16[400,128]{1,0:T(8,128)(2,1)S(1)} %collective-permute-done.20.refs_0_, bf16[400,128]{1,0:T(8,128)(2,1)S(1)} %collective-permute-done.21.refs_1_, ...), custom_call_target="tpu_custom_call" | custom-call | flops 1000000000 | tf_op jit(solution)/shard_map/pallas_call | solution.py:60
  (32 shorter events, 2.5 us)
Async XLA Ops:
  1.8 8.9 %collective-permute-start = (bf16[400,128]{1,0:T(8,128)(2,1)S(1)}, bf16[400,128]{1,0:T(8,128)(2,1)S(1)}, u32[]{:S(2)}, u32[]{:S(2)}) collective-permute-start(bf16[400,128]{1,0:T(8,128)(2,1)S(1)} %get-tuple-element.61), channel_id=1, source_target_pairs={{8,0},{12,4},{0,8},{4,12},{24,16},{28,20},{16,24},{20,28},{9,1},{1... | collective-permute-start | bytes 307208 | tf_op jit(solution)/shard_map/ppermute | solution.py:115
  4.8 6.2 %collective-permute-start.1 = (bf16[400,128]{1,0:T(8,128)(2,1)S(1)}, bf16[400,128]{1,0:T(8,128)(2,1)S(1)}, u32[]{:S(2)}, u32[]{:S(2)}) collective-permute-start(bf16[400,128]{1,0:T(8,128)(2,1)S(1)} %get-tuple-element.62), channel_id=1, source_target_pairs={{16,0},{20,4},{24,8},{28,12},{0,16},{4,20},{8,24},{12,28},{17,1},{... | collective-permute-start | bytes 307208 | tf_op jit(solution)/shard_map/ppermute | solution.py:115
  6.3 5.6 %collective-permute-start.2 = (bf16[400,128]{1,0:T(8,128)(2,1)S(1)}, bf16[400,128]{1,0:T(8,128)(2,1)S(1)}, u32[]{:S(2)}, u32[]{:S(2)}) collective-permute-start(bf16[400,128]{1,0:T(8,128)(2,1)S(1)} %get-tuple-element.63), channel_id=1, source_target_pairs={{24,0},{28,4},{16,8},{20,12},{8,16},{12,20},{0,24},{4,28},{25,1},{... | collective-permute-start | bytes 307208 | tf_op jit(solution)/shard_map/ppermute | solution.py:115
  6.4 12.8 %collective-permute-start.4 = (bf16[32,2048]{1,0:T(8,128)(2,1)}, bf16[32,2048]{1,0:T(8,128)(2,1)S(1)}, u32[]{:S(2)}, u32[]{:S(2)}) collective-permute-start(bf16[32,2048]{1,0:T(8,128)(2,1)} %refs_3_.2), channel_id=1, source_target_pairs={{2,0},{3,1},{0,2},{1,3},{6,4},{7,5},{4,6},{5,7},{10,8},{11,9},{8,1... | collective-permute-start | bytes 393224 | tf_op jit(solution)/shard_map/ppermute | solution.py:508
  9.4 9.7 %collective-permute-start.5 = (bf16[32,2048]{1,0:T(8,128)(2,1)}, bf16[32,2048]{1,0:T(8,128)(2,1)S(1)}, u32[]{:S(2)}, u32[]{:S(2)}) collective-permute-start(bf16[32,2048]{1,0:T(8,128)(2,1)} %refs_3_.2), channel_id=1, source_target_pairs={{3,0},{2,1},{1,2},{0,3},{7,4},{6,5},{5,6},{4,7},{11,8},{10,9},{9,1... | collective-permute-start | bytes 393224 | tf_op jit(solution)/shard_map/ppermute | solution.py:508
  10.8 8.5 %collective-permute-start.6 = (bf16[32,2048]{1,0:T(8,128)(2,1)}, bf16[32,2048]{1,0:T(8,128)(2,1)S(1)}, u32[]{:S(2)}, u32[]{:S(2)}) collective-permute-start(bf16[32,2048]{1,0:T(8,128)(2,1)} %refs_3_.2), channel_id=1, source_target_pairs={{1,0},{0,1},{3,2},{2,3},{5,4},{4,5},{7,6},{6,7},{9,8},{8,9},{11,10... | collective-permute-start | bytes 393224 | tf_op jit(solution)/shard_map/ppermute | solution.py:508
  11.9 7.4 %copy-start = (bf16[512,2048]{1,0:T(8,128)(2,1)S(1)}, bf16[512,2048]{1,0:T(8,128)(2,1)}, u32[]{:S(2)}) copy-start(bf16[512,2048]{1,0:T(8,128)(2,1)} %refs_4_.2) | copy-start | bytes 6291460
  11.9 7.4 %copy-start.1 = (bf16[32,2048]{1,0:T(8,128)(2,1)S(1)}, bf16[32,2048]{1,0:T(8,128)(2,1)}, u32[]{:S(2)}) copy-start(bf16[32,2048]{1,0:T(8,128)(2,1)} %refs_3_.2) | copy-start | bytes 393220
  16.0 7.6 %collective-permute-start.3 = (f32[4,2,128,128]{3,2,1,0:T(8,128)S(1)}, f32[4,2,128,128]{3,2,1,0:T(8,128)S(1)}, u32[]{:S(2)}, u32[]{:S(2)}) collective-permute-start(f32[4,2,128,128]{3,2,1,0:T(8,128)S(1)} %get-tuple-element.64.refs_0_), channel_id=1, source_target_pairs={{4,0},{0,4},{12,8},{8,12},{20,16},{16,20},{28,24},{24,28},{5,1},{1... | collective-permute-start | bytes 1572872 | tf_op jit(solution)/shard_map/ppermute | solution.py:121
  20.0 8.0 %collective-permute-start.13 = (bf16[256,128]{1,0:T(8,128)(2,1)S(1)}, bf16[256,128]{1,0:T(8,128)(2,1)S(1)}, u32[]{:S(2)}, u32[]{:S(2)}) collective-permute-start(bf16[256,128]{1,0:T(8,128)(2,1)S(1)} %get-tuple-element.77), channel_id=1, source_target_pairs={{8,0},{12,4},{0,8},{4,12},{24,16},{28,20},{16,24},{20,28},{9,1},{1... | collective-permute-start | bytes 196616 | tf_op jit(solution)/shard_map/ppermute | solution.py:115
  21.7 6.8 %collective-permute-start.14 = (bf16[256,128]{1,0:T(8,128)(2,1)S(1)}, bf16[256,128]{1,0:T(8,128)(2,1)S(1)}, u32[]{:S(2)}, u32[]{:S(2)}) collective-permute-start(bf16[256,128]{1,0:T(8,128)(2,1)S(1)} %get-tuple-element.78), channel_id=1, source_target_pairs={{16,0},{20,4},{24,8},{28,12},{0,16},{4,20},{8,24},{12,28},{17,1},{... | collective-permute-start | bytes 196616 | tf_op jit(solution)/shard_map/ppermute | solution.py:115
  23.2 5.8 %collective-permute-start.15 = (bf16[256,128]{1,0:T(8,128)(2,1)S(1)}, bf16[256,128]{1,0:T(8,128)(2,1)S(1)}, u32[]{:S(2)}, u32[]{:S(2)}) collective-permute-start(bf16[256,128]{1,0:T(8,128)(2,1)S(1)} %get-tuple-element.79), channel_id=1, source_target_pairs={{24,0},{28,4},{16,8},{20,12},{8,16},{12,20},{0,24},{4,28},{25,1},{... | collective-permute-start | bytes 196616 | tf_op jit(solution)/shard_map/ppermute | solution.py:115
  24.9 5.8 %collective-permute-start.7 = (bf16[4,128,128]{2,1,0:T(8,128)(2,1)S(1)}, bf16[4,128,128]{2,1,0:T(8,128)(2,1)S(1)}, u32[]{:S(2)}, u32[]{:S(2)}) collective-permute-start(bf16[4,128,128]{2,1,0:T(8,128)(2,1)S(1)} %get-tuple-element.70), channel_id=1, source_target_pairs={{8,0},{12,4},{0,8},{4,12},{24,16},{28,20},{16,24},{20,28},{9,1},{1... | collective-permute-start | bytes 393224 | tf_op jit(solution)/shard_map/ppermute | solution.py:115
  26.5 5.7 %collective-permute-start.8 = (bf16[4,128,128]{2,1,0:T(8,128)(2,1)S(1)}, bf16[4,128,128]{2,1,0:T(8,128)(2,1)S(1)}, u32[]{:S(2)}, u32[]{:S(2)}) collective-permute-start(bf16[4,128,128]{2,1,0:T(8,128)(2,1)S(1)} %get-tuple-element.71), channel_id=1, source_target_pairs={{16,0},{20,4},{24,8},{28,12},{0,16},{4,20},{8,24},{12,28},{17,1},{... | collective-permute-start | bytes 393224 | tf_op jit(solution)/shard_map/ppermute | solution.py:115
  28.1 6.3 %collective-permute-start.9 = (bf16[4,128,128]{2,1,0:T(8,128)(2,1)S(1)}, bf16[4,128,128]{2,1,0:T(8,128)(2,1)S(1)}, u32[]{:S(2)}, u32[]{:S(2)}) collective-permute-start(bf16[4,128,128]{2,1,0:T(8,128)(2,1)S(1)} %get-tuple-element.72), channel_id=1, source_target_pairs={{24,0},{28,4},{16,8},{20,12},{8,16},{12,20},{0,24},{4,28},{25,1},{... | collective-permute-start | bytes 393224 | tf_op jit(solution)/shard_map/ppermute | solution.py:115
  29.2 14.8 %collective-permute-start.16 = (f32[4,128,128]{2,1,0:T(8,128)S(1)}, f32[4,128,128]{2,1,0:T(8,128)S(1)}, u32[]{:S(2)}, u32[]{:S(2)}) collective-permute-start(f32[4,128,128]{2,1,0:T(8,128)S(1)} %shard_map.140.refs_2_), channel_id=1, source_target_pairs={{4,0},{0,4},{12,8},{8,12},{20,16},{16,20},{28,24},{24,28},{5,1},{1... | collective-permute-start | bytes 786440 | tf_op jit(solution)/shard_map/ppermute | solution.py:121
  29.6 8.5 %collective-permute-start.17 = (bf16[512,128]{1,0:T(8,128)(2,1)S(1)}, bf16[512,128]{1,0:T(8,128)(2,1)S(1)}, u32[]{:S(2)}, u32[]{:S(2)}) collective-permute-start(bf16[512,128]{1,0:T(8,128)(2,1)S(1)} %get-tuple-element.95), channel_id=1, source_target_pairs={{8,0},{12,4},{0,8},{4,12},{24,16},{28,20},{16,24},{20,28},{9,1},{1... | collective-permute-start | bytes 393224 | tf_op jit(solution)/shard_map/ppermute | solution.py:115
  30.7 9.4 %collective-permute-start.18 = (bf16[512,128]{1,0:T(8,128)(2,1)S(1)}, bf16[512,128]{1,0:T(8,128)(2,1)S(1)}, u32[]{:S(2)}, u32[]{:S(2)}) collective-permute-start(bf16[512,128]{1,0:T(8,128)(2,1)S(1)} %get-tuple-element.96), channel_id=1, source_target_pairs={{16,0},{20,4},{24,8},{28,12},{0,16},{4,20},{8,24},{12,28},{17,1},{... | collective-permute-start | bytes 393224 | tf_op jit(solution)/shard_map/ppermute | solution.py:115
  32.3 10.9 %collective-permute-start.19 = (bf16[512,128]{1,0:T(8,128)(2,1)S(1)}, bf16[512,128]{1,0:T(8,128)(2,1)S(1)}, u32[]{:S(2)}, u32[]{:S(2)}) collective-permute-start(bf16[512,128]{1,0:T(8,128)(2,1)S(1)} %get-tuple-element.97), channel_id=1, source_target_pairs={{24,0},{28,4},{16,8},{20,12},{8,16},{12,20},{0,24},{4,28},{25,1},{... | collective-permute-start | bytes 393224 | tf_op jit(solution)/shard_map/ppermute | solution.py:115
  34.9 17.1 %collective-permute-start.10 = (bf16[32,2048]{1,0:T(8,128)(2,1)S(1)}, bf16[32,2048]{1,0:T(8,128)(2,1)S(1)}, u32[]{:S(2)}, u32[]{:S(2)}) collective-permute-start(bf16[32,2048]{1,0:T(8,128)(2,1)S(1)} %get-tuple-element.74), channel_id=1, source_target_pairs={{1,0},{0,1},{3,2},{2,3},{5,4},{4,5},{7,6},{6,7},{9,8},{8,9},{11,10... | collective-permute-start | bytes 393224 | tf_op jit(solution)/shard_map/ppermute | solution.py:508
  38.1 11.6 %collective-permute-start.12 = (bf16[32,2048]{1,0:T(8,128)(2,1)S(1)}, bf16[32,2048]{1,0:T(8,128)(2,1)S(1)}, u32[]{:S(2)}, u32[]{:S(2)}) collective-permute-start(bf16[32,2048]{1,0:T(8,128)(2,1)S(1)} %get-tuple-element.76), channel_id=1, source_target_pairs={{2,0},{3,1},{0,2},{1,3},{6,4},{7,5},{4,6},{5,7},{10,8},{11,9},{8,1... | collective-permute-start | bytes 393224 | tf_op jit(solution)/shard_map/ppermute | solution.py:508
  40.1 10.6 %collective-permute-start.11 = (bf16[32,2048]{1,0:T(8,128)(2,1)S(1)}, bf16[32,2048]{1,0:T(8,128)(2,1)S(1)}, u32[]{:S(2)}, u32[]{:S(2)}) collective-permute-start(bf16[32,2048]{1,0:T(8,128)(2,1)S(1)} %get-tuple-element.75), channel_id=1, source_target_pairs={{3,0},{2,1},{1,2},{0,3},{7,4},{6,5},{5,6},{4,7},{11,8},{10,9},{9,1... | collective-permute-start | bytes 393224 | tf_op jit(solution)/shard_map/ppermute | solution.py:508
  43.9 8.9 %collective-permute-start.23 = (f32[256,512]{1,0:T(8,128)S(1)}, f32[256,512]{1,0:T(8,128)S(1)}, u32[]{:S(2)}, u32[]{:S(2)}) collective-permute-start(f32[256,512]{1,0:T(8,128)S(1)} %get-tuple-element.103), channel_id=1, source_target_pairs={{4,0},{0,4},{12,8},{8,12},{20,16},{16,20},{28,24},{24,28},{5,1},{1... | collective-permute-start | bytes 1572872 | tf_op jit(solution)/shard_map/ppermute | solution.py:121
  48.5 6.7 %collective-permute-start.20 = (bf16[400,128]{1,0:T(8,128)(2,1)S(1)}, bf16[400,128]{1,0:T(8,128)(2,1)S(1)}, u32[]{:S(2)}, u32[]{:S(2)}) collective-permute-start(bf16[400,128]{1,0:T(8,128)(2,1)S(1)} %get-tuple-element.99), channel_id=1, source_target_pairs={{24,0},{28,4},{16,8},{20,12},{8,16},{12,20},{0,24},{4,28},{25,1},{... | collective-permute-start | bytes 307208 | tf_op jit(solution)/shard_map/ppermute | solution.py:115
  49.7 7.2 %collective-permute-start.21 = (bf16[400,128]{1,0:T(8,128)(2,1)S(1)}, bf16[400,128]{1,0:T(8,128)(2,1)S(1)}, u32[]{:S(2)}, u32[]{:S(2)}) collective-permute-start(bf16[400,128]{1,0:T(8,128)(2,1)S(1)} %get-tuple-element.100), channel_id=1, source_target_pairs={{16,0},{20,4},{24,8},{28,12},{0,16},{4,20},{8,24},{12,28},{17,1},{... | collective-permute-start | bytes 307208 | tf_op jit(solution)/shard_map/ppermute | solution.py:115
  50.7 6.2 %collective-permute-start.22 = (bf16[400,128]{1,0:T(8,128)(2,1)S(1)}, bf16[400,128]{1,0:T(8,128)(2,1)S(1)}, u32[]{:S(2)}, u32[]{:S(2)}) collective-permute-start(bf16[400,128]{1,0:T(8,128)(2,1)S(1)} %get-tuple-element.101), channel_id=1, source_target_pairs={{8,0},{12,4},{0,8},{4,12},{24,16},{28,20},{16,24},{20,28},{9,1},{1... | collective-permute-start | bytes 307208 | tf_op jit(solution)/shard_map/ppermute | solution.py:115

commit v16 on v14

--- a/solution.py
+++ b/solution.py
@@ -11,7 +11,9 @@
 DK = 128
 DV = 128
 AUX = 16
-INVERSE, SCORES, FROM_STATE, READS, RATIO, WRITES, LOCAL, KEPT = range(8)
+INVERSE, SCORES, FROM_STATE, READS, KEYS, QUERIES, ENDS, SPLIT = range(8)
+RATIO, WRITES, LOCAL, COLUMNS, KEPT = range(5)
+SCALES = 6
 EPS = 1e-06
 F32 = jnp.float32
 BF16 = jnp.bfloat16
@@ -248,7 +250,7 @@
 
 
 def prepare_kernel(plan, off_ref, place_ref, mate_ref, *refs):
-    in_refs, (link_ref, kept_ref) = refs[: plan.hv], refs[plan.hv :]
+    in_refs, (link_ref, split_ref, kept_ref) = refs[: plan.hv], refs[plan.hv :]
     tok = plan.tok
     rows, columns = iotas(tok, tok)
     key_rows, key_columns = iotas(DK, DK)
@@ -256,8 +258,9 @@
     mine = range(plan.hv)
     chunks = chunks_of(plan, place_ref[0], mate_ref[0])
     scales = scalings(plan, off_ref, chunks, [r[plan.aux_at :] for r in in_refs])
-    qn = [unit(in_refs[m][:tok].astype(F32))[0] for m in mine]
-    kn = [unit(in_refs[m][tok : 2 * tok].astype(F32))[0] for m in mine]
+    qu = [unit(in_refs[m][:tok].astype(F32)) for m in mine]
+    ku = [unit(in_refs[m][tok : 2 * tok].astype(F32)) for m in mine]
+    qn, kn = [x[0] for x in qu], [x[0] for x in ku]
     kp = [halves(x) for x in kn]
     qp = [halves(x) for x in qn]
     dots = [mm(cat([q, k], 0), k, 1, 1) for q, k in zip(qp, kp)]
@@ -279,14 +282,23 @@
     for m in mine:
         link_ref[m, 0] = scales[m][5] * identity - mm(wp[m], ke[m], 0, 0)
         link_ref[m, 1] = mm(up[m], ke[m])
+    lanes = lax.broadcasted_iota(jnp.int32, (tok, DK), 1)
     for m in mine:
-        kept_ref[m, INVERSE] = inv[m]
-        kept_ref[m, SCORES] = scores[m]
-        kept_ref[m, FROM_STATE] = w[m]
-        kept_ref[m, READS] = scales[m][3] * qn[m] - mm(ap[m], wp[m])
-        kept_ref[m, RATIO] = scales[m][2]
+        _, b_col, ratio, start_col, end_col, whole = scales[m]
+        reads = start_col * qn[m] - mm(ap[m], wp[m])
+        for i, pair in enumerate((halves(inv[m]), ap[m], wp[m], halves(reads), kp[m], qp[m], ke[m])):
+            split_ref[m, i, 0], split_ref[m, i, 1] = pair
+        kept_ref[m, RATIO] = ratio
         kept_ref[m, WRITES] = u[m]
         kept_ref[m, LOCAL] = mm(up[m], ap[m], 1, 1)
+        columns_of = jnp.zeros((tok, DK), F32)
+        for i, x in enumerate((b_col, start_col, end_col, qu[m][1], ku[m][1], whole)):
+            columns_of = jnp.where(lanes == i, x, columns_of)
+        kept_ref[m, COLUMNS] = columns_of
+
+
+def get(split_ref, m, i):
+    return split_ref[m, i, 0], split_ref[m, i, 1]
 
 
 def lay_out(plan, place, mate, refs, all_ref):
@@ -297,8 +309,8 @@
 
 def scan_kernel(plan, place_ref, mate_ref, *refs):
     s, hv = plan.mates, plan.hv
-    links, kept_ref, state_ref = refs[:s], refs[s], refs[s + 1]
-    outs, (all_ref, states_ref) = refs[s + 2 : -2], refs[-2:]
+    links, split_ref, kept_ref, state_ref = refs[:s], refs[s], refs[s + 1], refs[s + 2]
+    outs, (all_ref, states_ref) = refs[s + 3 : -2], refs[-2:]
     place, mate = place_ref[0], mate_ref[0]
     lay_out(plan, place, mate, links, all_ref)
     state = jnp.zeros((DV, DK), F32)
@@ -311,27 +323,28 @@
     for m, c in enumerate(chunks_of(plan, place, mate)):
         state = states_ref[c]
         state_ref[m] = state
-        core = kept_ref[m, LOCAL] + mm(halves(state), halves(kept_ref[m, READS]), 1, 1)
+        core = kept_ref[m, LOCAL] + mm(halves(state), get(split_ref, m, READS), 1, 1)
         cores.append(core.astype(BF16))
     for d in range(hv):
         for k in range(hv):
             outs[d][k] = cores[plan.ring.seen(d, k)]
 
 
-def state_cotangent_kernel(plan, kept_ref, *refs):
+def state_cotangent_kernel(plan, split_ref, *refs):
     for m in range(plan.hv):
-        refs[-1][m] = mm(d_out(refs[m]), halves(kept_ref[m, READS]))
+        refs[-1][m] = mm(d_out(refs[m]), get(split_ref, m, READS))
 
 
 def d_out(ref):
     return ref[:DV], ref[DV:]
 
 
-def backward_kernel(plan, off_ref, place_ref, mate_ref, *refs):
+def backward_kernel(plan, place_ref, mate_ref, *refs):
     s, n, tok, hv = plan.mates, plan.n, plan.tok, plan.hv
     links, backs, refs = refs[:s], refs[s : 2 * s], refs[2 * s :]
-    in_refs, d_refs, kept_ref, state_ref = refs[:hv], refs[hv : 2 * hv], refs[2 * hv], refs[2 * hv + 1]
-    outs, (links_ref, backs_ref, cots_ref) = refs[2 * hv + 2 : -3], refs[-3:]
+    in_refs, d_refs = refs[:hv], refs[hv : 2 * hv]
+    split_ref, kept_ref, state_ref = refs[2 * hv : 2 * hv + 3]
+    outs, (links_ref, backs_ref, cots_ref) = refs[2 * hv + 3 : -3], refs[-3:]
     outs = [outs[plan.ring.seen(m, 0)] for m in range(hv)]
     place, mate = place_ref[0], mate_ref[0]
     lay_out(plan, place, mate, links, links_ref)
@@ -348,21 +361,25 @@
     upto = (rows >= columns).astype(BF16)
     mine = range(hv)
     chunks = chunks_of(plan, place, mate)
-    scales = scalings(plan, off_ref, chunks, [r[plan.aux_at :] for r in in_refs])
-    qu = [unit(in_refs[m][:tok].astype(F32)) for m in mine]
-    ku = [unit(in_refs[m][tok : 2 * tok].astype(F32)) for m in mine]
-    qp = [halves(x[0]) for x in qu]
-    kp = [halves(x[0]) for x in ku]
+    scales = []
+    for m in mine:
+        held = kept_ref[m, COLUMNS]
+        columns_of = [held[:, i : i + 1] for i in range(SCALES)]
+        rate = jnp.sum(in_refs[m][plan.aux_at :][0:3].astype(F32), axis=0, keepdims=True)
+        scales.append([rate] + columns_of[:-1] + [columns_of[-1][:1]])
+    qp = [get(split_ref, m, QUERIES) for m in mine]
+    kp = [get(split_ref, m, KEYS) for m in mine]
+    ke = [get(split_ref, m, ENDS) for m in mine]
+    whole_of = lambda pair: pair[0].astype(F32) + pair[1].astype(F32)
     do = [d_out(r) for r in d_refs]
     s0 = [state_ref[m] for m in mine]
     ds = [cots_ref[c] for c in chunks]
     s0p = [halves(x) for x in s0]
     dsp = [halves(x) for x in ds]
-    pseudo = [kept_ref[m, WRITES] - mm(s0p[m], halves(kept_ref[m, FROM_STATE]), 1, 1) for m in mine]
+    pseudo = [kept_ref[m, WRITES] - mm(s0p[m], get(split_ref, m, FROM_STATE), 1, 1) for m in mine]
     pp = [halves(x) for x in pseudo]
-    ke = [halves(s[4] * k[0]) for s, k in zip(scales, ku)]
-    dp = [mm(do[m], halves(kept_ref[m, SCORES])) + mm(dsp[m], ke[m], 1, 1) for m in mine]
-    dr = [mm(halves(dp[m]), halves(kept_ref[m, INVERSE])) for m in mine]
+    dp = [mm(do[m], get(split_ref, m, SCORES)) + mm(dsp[m], ke[m], 1, 1) for m in mine]
+    dr = [mm(halves(dp[m]), get(split_ref, m, INVERSE)) for m in mine]
     drp = [halves(x) for x in dr]
     big = [mm(cat([o, r], 1), cat([p, s], 1), 0, 0) for o, r, p, s in zip(do, drp, pp, s0p)]
     pds = [mm(p, d, 0, 0) for p, d in zip(pp, dsp)]
@@ -377,8 +394,8 @@
     ]
     sums = []
     for m in mine:
-        _, b_col, _, start_col, end_col, whole = scales[m]
-        (qn, q_scale), (kn, k_scale) = qu[m], ku[m]
+        _, b_col, start_col, end_col, q_scale, k_scale, whole = scales[m]
+        qn, kn = whole_of(qp[m]), whole_of(kp[m])
         out = outs[m]
         dqn = by_row[m][:tok] + start_col * big[m][:tok, tok:]
         erase = by_row[m][tok:] - start_col * big[m][tok:, tok:]
@@ -521,9 +538,13 @@
     rows = across_heads([grad_out] * parts)
     rows = [rows[d] for d in Ring(parts).far_first()]
 
-    link, kept = call(
+    link, split, kept = call(
         partial(prepare_kernel, plan),
-        (arr(F32, hv, 2, DK, DK), arr(F32, hv, KEPT, tok, DK)),
+        (
+            arr(F32, hv, 2, DK, DK),
+            arr(BF16, hv, SPLIT, 2, tok, DK),
+            arr(F32, hv, KEPT, tok, DK),
+        ),
         smem=(0, 1, 2),
         fetch=(0,),
         flops=20_000_000_000,
@@ -546,7 +567,7 @@
         smem=(0, 1),
         scratch=[vmem(F32, s, hv, 2, DK, DK), vmem(F32, n, DV, DK)],
         flops=2_500_000_000,
-    )(place, mate, *links, kept)
+    )(place, mate, *links, split, kept)
     turned = call(
         partial(turn_kernel, plan, parts),
         [arr(BF16, model // hv, tok)] * hv,
@@ -558,7 +579,7 @@
     turned = plan.exchange(turned)
     back = call(
         partial(state_cotangent_kernel, plan), arr(F32, hv, DV, DK), flops=30_000_000_000
-    )(kept, *after(d_core, states))
+    )(split, *after(d_core, states))
     backs = [back] + [plan.from_mate(back, d) for d in range(1, s)]
 
     projected = call(
@@ -573,15 +594,14 @@
     grads = call(
         partial(backward_kernel, plan),
         [arr(BF16, plan.rows, DK)] * hv,
-        smem=(0, 1, 2),
-        fetch=(0,),
+        smem=(0, 1),
         scratch=[
             vmem(F32, s, hv, 2, DK, DK),
             vmem(F32, s, hv, DV, DK),
             vmem(F32, n, DV, DK),
         ],
         flops=6_000_000_000,
-    )(doc_offsets, place, mate, *links, *backs, *got, *d_core, kept, after(states, projected[1]))
+    )(place, mate, *links, *backs, *got, *d_core, split, kept, after(states, projected[1]))
 
     shares = call(
         partial(weight_kernel, plan),

time: 56.8 us -> 56.1 us (0.988)
  Pallas kernels: 14.5 us -> 13.4 us
    ppermute x6, waiting for transfers between devices: 3.11 us -> 4.21 us  [across_heads(): lax.ppermute(pieces[d], 'head', Ring(parts).pairs(d))]
    pallas_call x10, Pallas kernels: 14.5 us -> 13.4 us  [run(): pl.pallas_call(kernel, out_shape=outs, in_specs=[spec(i) for i in range(l...]
    ppermute x15, waiting for transfers between devices: 4.68 us -> 3.87 us  [exchange(): moved.append(lax.ppermute(pieces[d], 'ctx', pairs))]
  transfers between devices with their start and end apart: 24 -> 24, of which waited for: 8 -> 6; matrix products, arithmetic and copies ran while one was open for 3% -> 3% of each run, Pallas kernels for 22% -> 20%
where the time goes in v16:
time: 56.1 us; the launch traced here: 55.9 us
  starting transfers between devices  32 us (57%)
  Pallas kernels  13.4 us (24%)
  waiting for transfers between devices  8.09 us (14%)
  other arithmetic  1.64 us (3%)
  between operations  0.77 us (1%)
    ppermute x15, starting transfers between devices, exchange(): moved.append(lax.ppermute(pieces[d], 'ctx', pairs))  19 us
    pallas_call x10, Pallas kernels, run(): pl.pallas_call(kernel, out_shape=outs, in_specs=[spec(i) for i in range(l...  13.4 us
    ppermute x6, starting transfers between devices, across_heads(): lax.ppermute(pieces[d], 'head', Ring(parts).pairs(d))  12.8 us
    ppermute x6, waiting for transfers between devices, across_heads(): lax.ppermute(pieces[d], 'head', Ring(parts).pairs(d))  4.21 us
    ppermute x15, waiting for transfers between devices, exchange(): moved.append(lax.ppermute(pieces[d], 'ctx', pairs))  3.87 us
  transfers between devices with their start and end apart: 24, of which 6 were waited for; matrix products, arithmetic and copies ran while one was open for 3% of the time, Pallas kernels for 20%

profile of v16, /device:TPU:0, one launch (start us, length us, event | category | flops | bytes accessed | tf_op | source)
XLA Modules:
  0.0 55.9 jit_solution(10534825719902433123)
XLA Ops:
  0.6 1.2 %shard_map.135 = (bf16[400,128]{1,0:T(8,128)(2,1)S(1)}, bf16[400,128]{1,0:T(8,128)(2,1)S(1)}, bf16[400,128]{1,0:T(8,128)(2,1)S(1)}, bf16[400,128]{1,0:T(8,128)(2,1)S(1)}) custom-call(s32[1]{0:T(128)} %bitcast.1.place_ref, bf16[128,256]{1,0:T(8,128)(2,1)} %q_ref.1, bf16[128,256]{1,0:T(8,128)(2,1)} %k_ref.1, bf16[128,512]{1,0:T(8,128)(2,1)} %v_ref.1, ...), custom_call_target="tpu_custom_call" | custom-call | tf_op jit(solution)/shard_map/pallas_call | solution.py:62
  1.8 3.0 %collective-permute-start = (bf16[400,128]{1,0:T(8,128)(2,1)S(1)}, bf16[400,128]{1,0:T(8,128)(2,1)S(1)}, u32[]{:S(2)}, u32[]{:S(2)}) collective-permute-start(bf16[400,128]{1,0:T(8,128)(2,1)S(1)} %get-tuple-element.62), channel_id=1, source_target_pairs={{8,0},{12,4},{0,8},{4,12},{24,16},{28,20},{16,24},{20,28},{9,1},{1... | collective-permute-start | bytes 307208 | tf_op jit(solution)/shard_map/ppermute | solution.py:117
  4.8 1.5 %collective-permute-start.1 = (bf16[400,128]{1,0:T(8,128)(2,1)S(1)}, bf16[400,128]{1,0:T(8,128)(2,1)S(1)}, u32[]{:S(2)}, u32[]{:S(2)}) collective-permute-start(bf16[400,128]{1,0:T(8,128)(2,1)S(1)} %get-tuple-element.63), channel_id=1, source_target_pairs={{16,0},{20,4},{24,8},{28,12},{0,16},{4,20},{8,24},{12,28},{17,1},{... | collective-permute-start | bytes 307208 | tf_op jit(solution)/shard_map/ppermute | solution.py:117
  6.4 3.0 %collective-permute-start.4 = (bf16[32,2048]{1,0:T(8,128)(2,1)}, bf16[32,2048]{1,0:T(8,128)(2,1)S(1)}, u32[]{:S(2)}, u32[]{:S(2)}) collective-permute-start(bf16[32,2048]{1,0:T(8,128)(2,1)} %refs_1_.2), channel_id=1, source_target_pairs={{2,0},{3,1},{0,2},{1,3},{6,4},{7,5},{4,6},{5,7},{10,8},{11,9},{8,1... | collective-permute-start | bytes 393224 | tf_op jit(solution)/shard_map/ppermute | solution.py:525
  9.4 1.6 %collective-permute-start.5 = (bf16[32,2048]{1,0:T(8,128)(2,1)}, bf16[32,2048]{1,0:T(8,128)(2,1)S(1)}, u32[]{:S(2)}, u32[]{:S(2)}) collective-permute-start(bf16[32,2048]{1,0:T(8,128)(2,1)} %refs_1_.2), channel_id=1, source_target_pairs={{1,0},{0,1},{3,2},{2,3},{5,4},{4,5},{7,6},{6,7},{9,8},{8,9},{11,10... | collective-permute-start | bytes 393224 | tf_op jit(solution)/shard_map/ppermute | solution.py:525
  11.0 0.6 %collective-permute-start.6 = (bf16[32,2048]{1,0:T(8,128)(2,1)}, bf16[32,2048]{1,0:T(8,128)(2,1)S(1)}, u32[]{:S(2)}, u32[]{:S(2)}) collective-permute-start(bf16[32,2048]{1,0:T(8,128)(2,1)} %refs_1_.2), channel_id=1, source_target_pairs={{3,0},{2,1},{1,2},{0,3},{7,4},{6,5},{5,6},{4,7},{11,8},{10,9},{9,1... | collective-permute-start | bytes 393224 | tf_op jit(solution)/shard_map/ppermute | solution.py:525
  11.9 4.2 %shard_map.136 = (f32[4,2,128,128]{3,2,1,0:T(8,128)S(1)}, bf16[4,7,2,128,128]{4,3,2,1,0:T(8,128)(2,1)S(1)}, f32[4,4,128,128]{3,2,1,0:T(8,128)S(1)}) custom-call(s32[5]{0:T(128)} %off_ref.1, s32[1]{0:T(128)} %bitcast.1.place_ref, s32[1]{0:T(128)} %bitcast.2.mate_ref, bf16[400,128]{1,0:T(8,128)(2,1)S(1)} %get-tuple-element.61.refs_0_.refs_4_, ...), custom_call_target="tpu_custom_call" | custom-call | flops 20000000000 | tf_op jit(solution)/shard_map/pallas_call | solution.py:62
  16.2 1.5 %collective-permute-done.4.refs_0_ = bf16[32,2048]{1,0:T(8,128)(2,1)S(1)} collective-permute-done((bf16[32,2048]{1,0:T(8,128)(2,1)}, bf16[32,2048]{1,0:T(8,128)(2,1)S(1)}, u32[]{:S(2)}, u32[]{:S(2)}) %collective-permute-start.4) | collective-permute-done | bytes 131104 | tf_op jit(solution)/shard_map/ppermute | solution.py:525
  17.7 1.4 %collective-permute-done.6.refs_3_ = bf16[32,2048]{1,0:T(8,128)(2,1)S(1)} collective-permute-done((bf16[32,2048]{1,0:T(8,128)(2,1)}, bf16[32,2048]{1,0:T(8,128)(2,1)S(1)}, u32[]{:S(2)}, u32[]{:S(2)}) %collective-permute-start.6) | collective-permute-done | bytes 131104 | tf_op jit(solution)/shard_map/ppermute | solution.py:525
  19.2 0.8 %shard_map.137 = (bf16[256,128]{1,0:T(8,128)(2,1)S(1)}, bf16[256,128]{1,0:T(8,128)(2,1)S(1)}, bf16[256,128]{1,0:T(8,128)(2,1)S(1)}, bf16[256,128]{1,0:T(8,128)(2,1)S(1)}) custom-call(s32[1]{0:T(128)} %bitcast.head_ref, s32[1]{0:T(128)} %bitcast.1.place_ref, bf16[32,2048]{1,0:T(8,128)(2,1)S(1)} %collective-permute-done.4.refs_0_, ...), custom_call_target="tpu_custom_call" | custom-call | flops 30000001024 | tf_op jit(solution)/shard_map/pallas_call | solution.py:62
  19.9 1.6 %collective-permute-start.13 = (bf16[256,128]{1,0:T(8,128)(2,1)S(1)}, bf16[256,128]{1,0:T(8,128)(2,1)S(1)}, u32[]{:S(2)}, u32[]{:S(2)}) collective-permute-start(bf16[256,128]{1,0:T(8,128)(2,1)S(1)} %get-tuple-element.79), channel_id=1, source_target_pairs={{8,0},{12,4},{0,8},{4,12},{24,16},{28,20},{16,24},{20,28},{9,1},{1... | collective-permute-start | bytes 196616 | tf_op jit(solution)/shard_map/ppermute | solution.py:117
  21.5 1.5 %collective-permute-start.14 = (bf16[256,128]{1,0:T(8,128)(2,1)S(1)}, bf16[256,128]{1,0:T(8,128)(2,1)S(1)}, u32[]{:S(2)}, u32[]{:S(2)}) collective-permute-start(bf16[256,128]{1,0:T(8,128)(2,1)S(1)} %get-tuple-element.80), channel_id=1, source_target_pairs={{16,0},{20,4},{24,8},{28,12},{0,16},{4,20},{8,24},{12,28},{17,1},{... | collective-permute-start | bytes 196616 | tf_op jit(solution)/shard_map/ppermute | solution.py:117
  23.5 1.3 %shard_map.138 = (f32[4,128,128]{2,1,0:T(8,128)S(1)}, bf16[4,128,128]{2,1,0:T(8,128)(2,1)S(1)}, bf16[4,128,128]{2,1,0:T(8,128)(2,1)S(1)}, bf16[4,128,128]{2,1,0:T(8,128)(2,1)S(1)}, bf16[4,128,128]{2,1,0:T(8,128)(2,1)S(1)}) custom-call(s32[1]{0:T(128)} %bitcast.1.place_ref, s32[1]{0:T(128)} %bitcast.2.mate_ref, ...), custom_call_target="tpu_custom_call" | custom-call | flops 2500000000 | tf_op jit(solution)/shard_map/pallas_call | solution.py:62
  24.8 1.6 %collective-permute-start.7 = (bf16[4,128,128]{2,1,0:T(8,128)(2,1)S(1)}, bf16[4,128,128]{2,1,0:T(8,128)(2,1)S(1)}, u32[]{:S(2)}, u32[]{:S(2)}) collective-permute-start(bf16[4,128,128]{2,1,0:T(8,128)(2,1)S(1)} %get-tuple-element.72), channel_id=1, source_target_pairs={{8,0},{12,4},{0,8},{4,12},{24,16},{28,20},{16,24},{20,28},{9,1},{1... | collective-permute-start | bytes 393224 | tf_op jit(solution)/shard_map/ppermute | solution.py:117
  26.4 1.5 %collective-permute-start.8 = (bf16[4,128,128]{2,1,0:T(8,128)(2,1)S(1)}, bf16[4,128,128]{2,1,0:T(8,128)(2,1)S(1)}, u32[]{:S(2)}, u32[]{:S(2)}) collective-permute-start(bf16[4,128,128]{2,1,0:T(8,128)(2,1)S(1)} %get-tuple-element.73), channel_id=1, source_target_pairs={{16,0},{20,4},{24,8},{28,12},{0,16},{4,20},{8,24},{12,28},{17,1},{... | collective-permute-start | bytes 393224 | tf_op jit(solution)/shard_map/ppermute | solution.py:117
  29.0 1.6 %collective-permute-start.17 = (bf16[512,128]{1,0:T(8,128)(2,1)S(1)}, bf16[512,128]{1,0:T(8,128)(2,1)S(1)}, u32[]{:S(2)}, u32[]{:S(2)}) collective-permute-start(bf16[512,128]{1,0:T(8,128)(2,1)S(1)} %get-tuple-element.97), channel_id=1, source_target_pairs={{8,0},{12,4},{0,8},{4,12},{24,16},{28,20},{16,24},{20,28},{9,1},{1... | collective-permute-start | bytes 393224 | tf_op jit(solution)/shard_map/ppermute | solution.py:117
  30.6 1.5 %collective-permute-start.18 = (bf16[512,128]{1,0:T(8,128)(2,1)S(1)}, bf16[512,128]{1,0:T(8,128)(2,1)S(1)}, u32[]{:S(2)}, u32[]{:S(2)}) collective-permute-start(bf16[512,128]{1,0:T(8,128)(2,1)S(1)} %get-tuple-element.98), channel_id=1, source_target_pairs={{16,0},{20,4},{24,8},{28,12},{0,16},{4,20},{8,24},{12,28},{17,1},{... | collective-permute-start | bytes 393224 | tf_op jit(solution)/shard_map/ppermute | solution.py:117
  32.1 0.7 %collective-permute-start.19 = (bf16[512,128]{1,0:T(8,128)(2,1)S(1)}, bf16[512,128]{1,0:T(8,128)(2,1)S(1)}, u32[]{:S(2)}, u32[]{:S(2)}) collective-permute-start(bf16[512,128]{1,0:T(8,128)(2,1)S(1)} %get-tuple-element.99), channel_id=1, source_target_pairs={{24,0},{28,4},{16,8},{20,12},{8,16},{12,20},{0,24},{4,28},{25,1},{... | collective-permute-start | bytes 393224 | tf_op jit(solution)/shard_map/ppermute | solution.py:117
  32.8 1.6 %collective-permute-done.9.refs_3_.refs_7_ = bf16[4,128,128]{2,1,0:T(8,128)(2,1)S(1)} collective-permute-done((bf16[4,128,128]{2,1,0:T(8,128)(2,1)S(1)}, bf16[4,128,128]{2,1,0:T(8,128)(2,1)S(1)}, u32[]{:S(2)}, u32[]{:S(2)}) %collective-permute-start.9) | collective-permute-done | bytes 131104 | tf_op jit(solution)/shard_map/ppermute | solution.py:117
  34.4 0.5 shard_map.139
  35.0 2.5 %collective-permute-start.12 = (bf16[32,2048]{1,0:T(8,128)(2,1)S(1)}, bf16[32,2048]{1,0:T(8,128)(2,1)S(1)}, u32[]{:S(2)}, u32[]{:S(2)}) collective-permute-start(bf16[32,2048]{1,0:T(8,128)(2,1)S(1)} %get-tuple-element.78), channel_id=1, source_target_pairs={{1,0},{0,1},{3,2},{2,3},{5,4},{4,5},{7,6},{6,7},{9,8},{8,9},{11,10... | collective-permute-start | bytes 393224 | tf_op jit(solution)/shard_map/ppermute | solution.py:525
  37.5 2.5 %collective-permute-start.11 = (bf16[32,2048]{1,0:T(8,128)(2,1)S(1)}, bf16[32,2048]{1,0:T(8,128)(2,1)S(1)}, u32[]{:S(2)}, u32[]{:S(2)}) collective-permute-start(bf16[32,2048]{1,0:T(8,128)(2,1)S(1)} %get-tuple-element.77), channel_id=1, source_target_pairs={{2,0},{3,1},{0,2},{1,3},{6,4},{7,5},{4,6},{5,7},{10,8},{11,9},{8,1... | collective-permute-start | bytes 393224 | tf_op jit(solution)/shard_map/ppermute | solution.py:525
  40.1 2.5 %collective-permute-start.10 = (bf16[32,2048]{1,0:T(8,128)(2,1)S(1)}, bf16[32,2048]{1,0:T(8,128)(2,1)S(1)}, u32[]{:S(2)}, u32[]{:S(2)}) collective-permute-start(bf16[32,2048]{1,0:T(8,128)(2,1)S(1)} %get-tuple-element.76), channel_id=1, source_target_pairs={{3,0},{2,1},{1,2},{0,3},{7,4},{6,5},{5,6},{4,7},{11,8},{10,9},{9,1... | collective-permute-start | bytes 393224 | tf_op jit(solution)/shard_map/ppermute | solution.py:525
  42.5 0.7 %shard_map.143 = (f32[256,512]{1,0:T(8,128)S(1)}, f32[256,512]{1,0:T(8,128)S(1)}) custom-call(s32[1]{0:T(128)} %bitcast.1.place_ref, s32[1]{0:T(128)} %bitcast.2.mate_ref, bf16[512,128]{1,0:T(8,128)(2,1)S(1)} %get-tuple-element.96.refs_0_, bf16[512,128]{1,0:T(8,128)(2,1)S(1)} %collective-permute-done.17.refs_1_, ...), custom_call_target="tpu_custom_call" | custom-call | flops 1000000000 | tf_op jit(solution)/shard_map/pallas_call | solution.py:62
  43.4 3.2 %shard_map.141 = (bf16[400,128]{1,0:T(8,128)(2,1)S(1)}, bf16[400,128]{1,0:T(8,128)(2,1)S(1)}, bf16[400,128]{1,0:T(8,128)(2,1)S(1)}, bf16[400,128]{1,0:T(8,128)(2,1)S(1)}) custom-call(s32[1]{0:T(128)} %bitcast.1.place_ref, s32[1]{0:T(128)} %bitcast.2.mate_ref, f32[4,2,128,128]{3,2,1,0:T(8,128)S(1)} %get-tuple-element.65.refs_0_, ...), custom_call_target="tpu_custom_call" | custom-call | flops 6000000000 | tf_op jit(solution)/shard_map/pallas_call | solution.py:62
  46.8 1.4 %collective-permute-start.21 = (bf16[400,128]{1,0:T(8,128)(2,1)S(1)}, bf16[400,128]{1,0:T(8,128)(2,1)S(1)}, u32[]{:S(2)}, u32[]{:S(2)}) collective-permute-start(bf16[400,128]{1,0:T(8,128)(2,1)S(1)} %get-tuple-element.103), channel_id=1, source_target_pairs={{16,0},{20,4},{24,8},{28,12},{0,16},{4,20},{8,24},{12,28},{17,1},{... | collective-permute-start | bytes 307208 | tf_op jit(solution)/shard_map/ppermute | solution.py:117
  48.2 1.3 %collective-permute-done.11 = bf16[32,2048]{1,0:T(8,128)(2,1)S(1)} collective-permute-done((bf16[32,2048]{1,0:T(8,128)(2,1)S(1)}, bf16[32,2048]{1,0:T(8,128)(2,1)S(1)}, u32[]{:S(2)}, u32[]{:S(2)}) %collective-permute-start.11) | collective-permute-done | bytes 131104 | tf_op jit(solution)/shard_map/ppermute | solution.py:525
  49.5 2.0 %collective-permute-start.22 = (bf16[400,128]{1,0:T(8,128)(2,1)S(1)}, bf16[400,128]{1,0:T(8,128)(2,1)S(1)}, u32[]{:S(2)}, u32[]{:S(2)}) collective-permute-start(bf16[400,128]{1,0:T(8,128)(2,1)S(1)} %get-tuple-element.104), channel_id=1, source_target_pairs={{24,0},{28,4},{16,8},{20,12},{8,16},{12,20},{0,24},{4,28},{25,1},{... | collective-permute-start | bytes 307208 | tf_op jit(solution)/shard_map/ppermute | solution.py:117
  51.5 0.8 %convert_add_fusion = f32[32,2048]{1,0:T(8,128)} fusion(bf16[32,2048]{1,0:T(8,128)(2,1)S(1)} %collective-permute-done.12, bf16[32,2048]{1,0:T(8,128)(2,1)S(1)} %collective-permute-done.11, f32[32,2048]{1,0:T(8,128)S(1)} %get-tuple-element.75, bf16[32,2048]{1,0:T(8,128)(2,1)S(1)} %collective-permute-done.10), kind=kLoop, calls=%fused_computation | loop fusion | flops 393216 | bytes 917504 | tf_op jit(solution)/shard_map/add | solution.py:620
  52.3 0.9 %add.21 = f32[256,512]{1,0:T(8,128)} add(f32[256,512]{1,0:T(8,128)S(1)} %get-tuple-element.100, f32[256,512]{1,0:T(8,128)S(1)} %collective-permute-done.23) | non-fusion elementwise | flops 131072 | bytes 1572864 | tf_op jit(solution)/shard_map/add | solution.py:616
  53.1 1.9 %collective-permute-done.22.refs_3_ = bf16[400,128]{1,0:T(8,128)(2,1)S(1)} collective-permute-done((bf16[400,128]{1,0:T(8,128)(2,1)S(1)}, bf16[400,128]{1,0:T(8,128)(2,1)S(1)}, u32[]{:S(2)}, u32[]{:S(2)}) %collective-permute-start.22) | collective-permute-done | bytes 102432 | tf_op jit(solution)/shard_map/ppermute | solution.py:117
  55.0 0.9 %shard_map.144 = (f32[128,256]{1,0:T(8,128)}, f32[128,256]{1,0:T(8,128)}, f32[128,512]{1,0:T(8,128)}, f32[4,128]{1,0:T(4,128)}, f32[4,128]{1,0:T(4,128)}) custom-call(s32[1]{0:T(128)} %bitcast.1.place_ref, bf16[400,128]{1,0:T(8,128)(2,1)S(1)} %get-tuple-element.106.refs_0_, bf16[400,128]{1,0:T(8,128)(2,1)S(1)} %collective-permute-done.20.refs_1_, ...), custom_call_target="tpu_custom_call" | custom-call | flops 1000000000 | tf_op jit(solution)/shard_map/pallas_call | solution.py:62
  (32 shorter events, 2.3 us)
Async XLA Ops:
  1.8 9.2 %collective-permute-start = (bf16[400,128]{1,0:T(8,128)(2,1)S(1)}, bf16[400,128]{1,0:T(8,128)(2,1)S(1)}, u32[]{:S(2)}, u32[]{:S(2)}) collective-permute-start(bf16[400,128]{1,0:T(8,128)(2,1)S(1)} %get-tuple-element.62), channel_id=1, source_target_pairs={{8,0},{12,4},{0,8},{4,12},{24,16},{28,20},{16,24},{20,28},{9,1},{1... | collective-permute-start | bytes 307208 | tf_op jit(solution)/shard_map/ppermute | solution.py:117
  4.8 6.8 %collective-permute-start.1 = (bf16[400,128]{1,0:T(8,128)(2,1)S(1)}, bf16[400,128]{1,0:T(8,128)(2,1)S(1)}, u32[]{:S(2)}, u32[]{:S(2)}) collective-permute-start(bf16[400,128]{1,0:T(8,128)(2,1)S(1)} %get-tuple-element.63), channel_id=1, source_target_pairs={{16,0},{20,4},{24,8},{28,12},{0,16},{4,20},{8,24},{12,28},{17,1},{... | collective-permute-start | bytes 307208 | tf_op jit(solution)/shard_map/ppermute | solution.py:117
  6.3 5.6 %collective-permute-start.2 = (bf16[400,128]{1,0:T(8,128)(2,1)S(1)}, bf16[400,128]{1,0:T(8,128)(2,1)S(1)}, u32[]{:S(2)}, u32[]{:S(2)}) collective-permute-start(bf16[400,128]{1,0:T(8,128)(2,1)S(1)} %get-tuple-element.64), channel_id=1, source_target_pairs={{24,0},{28,4},{16,8},{20,12},{8,16},{12,20},{0,24},{4,28},{25,1},{... | collective-permute-start | bytes 307208 | tf_op jit(solution)/shard_map/ppermute | solution.py:117
  6.4 11.4 %collective-permute-start.4 = (bf16[32,2048]{1,0:T(8,128)(2,1)}, bf16[32,2048]{1,0:T(8,128)(2,1)S(1)}, u32[]{:S(2)}, u32[]{:S(2)}) collective-permute-start(bf16[32,2048]{1,0:T(8,128)(2,1)} %refs_1_.2), channel_id=1, source_target_pairs={{2,0},{3,1},{0,2},{1,3},{6,4},{7,5},{4,6},{5,7},{10,8},{11,9},{8,1... | collective-permute-start | bytes 393224 | tf_op jit(solution)/shard_map/ppermute | solution.py:525
  9.4 8.3 %collective-permute-start.5 = (bf16[32,2048]{1,0:T(8,128)(2,1)}, bf16[32,2048]{1,0:T(8,128)(2,1)S(1)}, u32[]{:S(2)}, u32[]{:S(2)}) collective-permute-start(bf16[32,2048]{1,0:T(8,128)(2,1)} %refs_1_.2), channel_id=1, source_target_pairs={{1,0},{0,1},{3,2},{2,3},{5,4},{4,5},{7,6},{6,7},{9,8},{8,9},{11,10... | collective-permute-start | bytes 393224 | tf_op jit(solution)/shard_map/ppermute | solution.py:525
  11.0 8.2 %collective-permute-start.6 = (bf16[32,2048]{1,0:T(8,128)(2,1)}, bf16[32,2048]{1,0:T(8,128)(2,1)S(1)}, u32[]{:S(2)}, u32[]{:S(2)}) collective-permute-start(bf16[32,2048]{1,0:T(8,128)(2,1)} %refs_1_.2), channel_id=1, source_target_pairs={{3,0},{2,1},{1,2},{0,3},{7,4},{6,5},{5,6},{4,7},{11,8},{10,9},{9,1... | collective-permute-start | bytes 393224 | tf_op jit(solution)/shard_map/ppermute | solution.py:525
  11.9 7.3 %copy-start = (bf16[512,2048]{1,0:T(8,128)(2,1)S(1)}, bf16[512,2048]{1,0:T(8,128)(2,1)}, u32[]{:S(2)}) copy-start(bf16[512,2048]{1,0:T(8,128)(2,1)} %refs_4_.2) | copy-start | bytes 6291460
  11.9 7.3 %copy-start.1 = (bf16[32,2048]{1,0:T(8,128)(2,1)S(1)}, bf16[32,2048]{1,0:T(8,128)(2,1)}, u32[]{:S(2)}) copy-start(bf16[32,2048]{1,0:T(8,128)(2,1)} %refs_1_.2) | copy-start | bytes 393220
  16.1 7.3 %collective-permute-start.3 = (f32[4,2,128,128]{3,2,1,0:T(8,128)S(1)}, f32[4,2,128,128]{3,2,1,0:T(8,128)S(1)}, u32[]{:S(2)}, u32[]{:S(2)}) collective-permute-start(f32[4,2,128,128]{3,2,1,0:T(8,128)S(1)} %get-tuple-element.65.refs_0_), channel_id=1, source_target_pairs={{4,0},{0,4},{12,8},{8,12},{20,16},{16,20},{28,24},{24,28},{5,1},{1... | collective-permute-start | bytes 1572872 | tf_op jit(solution)/shard_map/ppermute | solution.py:123
  19.9 7.9 %collective-permute-start.13 = (bf16[256,128]{1,0:T(8,128)(2,1)S(1)}, bf16[256,128]{1,0:T(8,128)(2,1)S(1)}, u32[]{:S(2)}, u32[]{:S(2)}) collective-permute-start(bf16[256,128]{1,0:T(8,128)(2,1)S(1)} %get-tuple-element.79), channel_id=1, source_target_pairs={{8,0},{12,4},{0,8},{4,12},{24,16},{28,20},{16,24},{20,28},{9,1},{1... | collective-permute-start | bytes 196616 | tf_op jit(solution)/shard_map/ppermute | solution.py:117
  21.5 6.9 %collective-permute-start.14 = (bf16[256,128]{1,0:T(8,128)(2,1)S(1)}, bf16[256,128]{1,0:T(8,128)(2,1)S(1)}, u32[]{:S(2)}, u32[]{:S(2)}) collective-permute-start(bf16[256,128]{1,0:T(8,128)(2,1)S(1)} %get-tuple-element.80), channel_id=1, source_target_pairs={{16,0},{20,4},{24,8},{28,12},{0,16},{4,20},{8,24},{12,28},{17,1},{... | collective-permute-start | bytes 196616 | tf_op jit(solution)/shard_map/ppermute | solution.py:117
  23.0 5.3 %collective-permute-start.15 = (bf16[256,128]{1,0:T(8,128)(2,1)S(1)}, bf16[256,128]{1,0:T(8,128)(2,1)S(1)}, u32[]{:S(2)}, u32[]{:S(2)}) collective-permute-start(bf16[256,128]{1,0:T(8,128)(2,1)S(1)} %get-tuple-element.81), channel_id=1, source_target_pairs={{24,0},{28,4},{16,8},{20,12},{8,16},{12,20},{0,24},{4,28},{25,1},{... | collective-permute-start | bytes 196616 | tf_op jit(solution)/shard_map/ppermute | solution.py:117
  24.8 5.8 %collective-permute-start.7 = (bf16[4,128,128]{2,1,0:T(8,128)(2,1)S(1)}, bf16[4,128,128]{2,1,0:T(8,128)(2,1)S(1)}, u32[]{:S(2)}, u32[]{:S(2)}) collective-permute-start(bf16[4,128,128]{2,1,0:T(8,128)(2,1)S(1)} %get-tuple-element.72), channel_id=1, source_target_pairs={{8,0},{12,4},{0,8},{4,12},{24,16},{28,20},{16,24},{20,28},{9,1},{1... | collective-permute-start | bytes 393224 | tf_op jit(solution)/shard_map/ppermute | solution.py:117
  26.4 5.7 %collective-permute-start.8 = (bf16[4,128,128]{2,1,0:T(8,128)(2,1)S(1)}, bf16[4,128,128]{2,1,0:T(8,128)(2,1)S(1)}, u32[]{:S(2)}, u32[]{:S(2)}) collective-permute-start(bf16[4,128,128]{2,1,0:T(8,128)(2,1)S(1)} %get-tuple-element.73), channel_id=1, source_target_pairs={{16,0},{20,4},{24,8},{28,12},{0,16},{4,20},{8,24},{12,28},{17,1},{... | collective-permute-start | bytes 393224 | tf_op jit(solution)/shard_map/ppermute | solution.py:117
  27.9 6.6 %collective-permute-start.9 = (bf16[4,128,128]{2,1,0:T(8,128)(2,1)S(1)}, bf16[4,128,128]{2,1,0:T(8,128)(2,1)S(1)}, u32[]{:S(2)}, u32[]{:S(2)}) collective-permute-start(bf16[4,128,128]{2,1,0:T(8,128)(2,1)S(1)} %get-tuple-element.74), channel_id=1, source_target_pairs={{24,0},{28,4},{16,8},{20,12},{8,16},{12,20},{0,24},{4,28},{25,1},{... | collective-permute-start | bytes 393224 | tf_op jit(solution)/shard_map/ppermute | solution.py:117
  28.6 14.7 %collective-permute-start.16 = (f32[4,128,128]{2,1,0:T(8,128)S(1)}, f32[4,128,128]{2,1,0:T(8,128)S(1)}, u32[]{:S(2)}, u32[]{:S(2)}) collective-permute-start(f32[4,128,128]{2,1,0:T(8,128)S(1)} %shard_map.140.refs_2_), channel_id=1, source_target_pairs={{4,0},{0,4},{12,8},{8,12},{20,16},{16,20},{28,24},{24,28},{5,1},{1... | collective-permute-start | bytes 786440 | tf_op jit(solution)/shard_map/ppermute | solution.py:123
  29.0 8.5 %collective-permute-start.17 = (bf16[512,128]{1,0:T(8,128)(2,1)S(1)}, bf16[512,128]{1,0:T(8,128)(2,1)S(1)}, u32[]{:S(2)}, u32[]{:S(2)}) collective-permute-start(bf16[512,128]{1,0:T(8,128)(2,1)S(1)} %get-tuple-element.97), channel_id=1, source_target_pairs={{8,0},{12,4},{0,8},{4,12},{24,16},{28,20},{16,24},{20,28},{9,1},{1... | collective-permute-start | bytes 393224 | tf_op jit(solution)/shard_map/ppermute | solution.py:117
  30.6 9.5 %collective-permute-start.18 = (bf16[512,128]{1,0:T(8,128)(2,1)S(1)}, bf16[512,128]{1,0:T(8,128)(2,1)S(1)}, u32[]{:S(2)}, u32[]{:S(2)}) collective-permute-start(bf16[512,128]{1,0:T(8,128)(2,1)S(1)} %get-tuple-element.98), channel_id=1, source_target_pairs={{16,0},{20,4},{24,8},{28,12},{0,16},{4,20},{8,24},{12,28},{17,1},{... | collective-permute-start | bytes 393224 | tf_op jit(solution)/shard_map/ppermute | solution.py:117
  32.1 10.5 %collective-permute-start.19 = (bf16[512,128]{1,0:T(8,128)(2,1)S(1)}, bf16[512,128]{1,0:T(8,128)(2,1)S(1)}, u32[]{:S(2)}, u32[]{:S(2)}) collective-permute-start(bf16[512,128]{1,0:T(8,128)(2,1)S(1)} %get-tuple-element.99), channel_id=1, source_target_pairs={{24,0},{28,4},{16,8},{20,12},{8,16},{12,20},{0,24},{4,28},{25,1},{... | collective-permute-start | bytes 393224 | tf_op jit(solution)/shard_map/ppermute | solution.py:117
  35.0 11.8 %collective-permute-start.12 = (bf16[32,2048]{1,0:T(8,128)(2,1)S(1)}, bf16[32,2048]{1,0:T(8,128)(2,1)S(1)}, u32[]{:S(2)}, u32[]{:S(2)}) collective-permute-start(bf16[32,2048]{1,0:T(8,128)(2,1)S(1)} %get-tuple-element.78), channel_id=1, source_target_pairs={{1,0},{0,1},{3,2},{2,3},{5,4},{4,5},{7,6},{6,7},{9,8},{8,9},{11,10... | collective-permute-start | bytes 393224 | tf_op jit(solution)/shard_map/ppermute | solution.py:525
  37.5 11.9 %collective-permute-start.11 = (bf16[32,2048]{1,0:T(8,128)(2,1)S(1)}, bf16[32,2048]{1,0:T(8,128)(2,1)S(1)}, u32[]{:S(2)}, u32[]{:S(2)}) collective-permute-start(bf16[32,2048]{1,0:T(8,128)(2,1)S(1)} %get-tuple-element.77), channel_id=1, source_target_pairs={{2,0},{3,1},{0,2},{1,3},{6,4},{7,5},{4,6},{5,7},{10,8},{11,9},{8,1... | collective-permute-start | bytes 393224 | tf_op jit(solution)/shard_map/ppermute | solution.py:525
  40.1 11.4 %collective-permute-start.10 = (bf16[32,2048]{1,0:T(8,128)(2,1)S(1)}, bf16[32,2048]{1,0:T(8,128)(2,1)S(1)}, u32[]{:S(2)}, u32[]{:S(2)}) collective-permute-start(bf16[32,2048]{1,0:T(8,128)(2,1)S(1)} %get-tuple-element.76), channel_id=1, source_target_pairs={{3,0},{2,1},{1,2},{0,3},{7,4},{6,5},{5,6},{4,7},{11,8},{10,9},{9,1... | collective-permute-start | bytes 393224 | tf_op jit(solution)/shard_map/ppermute | solution.py:525
  43.3 9.0 %collective-permute-start.23 = (f32[256,512]{1,0:T(8,128)S(1)}, f32[256,512]{1,0:T(8,128)S(1)}, u32[]{:S(2)}, u32[]{:S(2)}) collective-permute-start(f32[256,512]{1,0:T(8,128)S(1)} %get-tuple-element.105), channel_id=1, source_target_pairs={{4,0},{0,4},{12,8},{8,12},{20,16},{16,20},{28,24},{24,28},{5,1},{1... | collective-permute-start | bytes 1572872 | tf_op jit(solution)/shard_map/ppermute | solution.py:123
  46.6 6.5 %collective-permute-start.20 = (bf16[400,128]{1,0:T(8,128)(2,1)S(1)}, bf16[400,128]{1,0:T(8,128)(2,1)S(1)}, u32[]{:S(2)}, u32[]{:S(2)}) collective-permute-start(bf16[400,128]{1,0:T(8,128)(2,1)S(1)} %get-tuple-element.102), channel_id=1, source_target_pairs={{8,0},{12,4},{0,8},{4,12},{24,16},{28,20},{16,24},{20,28},{9,1},{1... | collective-permute-start | bytes 307208 | tf_op jit(solution)/shard_map/ppermute | solution.py:117
  46.8 6.3 %collective-permute-start.21 = (bf16[400,128]{1,0:T(8,128)(2,1)S(1)}, bf16[400,128]{1,0:T(8,128)(2,1)S(1)}, u32[]{:S(2)}, u32[]{:S(2)}) collective-permute-start(bf16[400,128]{1,0:T(8,128)(2,1)S(1)} %get-tuple-element.103), channel_id=1, source_target_pairs={{16,0},{20,4},{24,8},{28,12},{0,16},{4,20},{8,24},{12,28},{17,1},{... | collective-permute-start | bytes 307208 | tf_op jit(solution)/shard_map/ppermute | solution.py:117
  49.5 5.6 %collective-permute-start.22 = (bf16[400,128]{1,0:T(8,128)(2,1)S(1)}, bf16[400,128]{1,0:T(8,128)(2,1)S(1)}, u32[]{:S(2)}, u32[]{:S(2)}) collective-permute-start(bf16[400,128]{1,0:T(8,128)(2,1)S(1)} %get-tuple-element.104), channel_id=1, source_target_pairs={{24,0},{28,4},{16,8},{20,12},{8,16},{12,20},{0,24},{4,28},{25,1},{... | collective-permute-start | bytes 307208 | tf_op jit(solution)/shard_map/ppermute | solution.py:117

commit v17 on v16

--- a/solution.py
+++ b/solution.py
@@ -547,7 +547,7 @@
         ),
         smem=(0, 1, 2),
         fetch=(0,),
-        flops=20_000_000_000,
+        flops=0,
     )(doc_offsets, place, mate, *got)
     links = [link] + [plan.from_mate(link, d) for d in range(1, s)]
 

time: 56.1 us -> 59.3 us (1.057)
  waiting for transfers between devices: 8.09 us -> 11.9 us
  starting transfers between devices: 32 us -> 28.9 us
  local copies, waits for them, and re-layouts: 0.01 us -> 2.5 us
    ppermute x15, waiting for transfers between devices: 3.87 us -> 11.1 us  [exchange(): moved.append(lax.ppermute(pieces[d], 'ctx', pairs))]
    ppermute x6, waiting for transfers between devices: 4.21 us -> 0.8 us  [across_heads(): lax.ppermute(pieces[d], 'head', Ring(parts).pairs(d))]
    unnamed x4 -> x6, local copies, waits for them, and re-layouts: 0.01 us -> 2.5 us
    ppermute x15, starting transfers between devices: 19 us -> 17 us  [exchange(): moved.append(lax.ppermute(pieces[d], 'ctx', pairs))]
    ppermute x6, starting transfers between devices: 12.8 us -> 11.7 us  [across_heads(): lax.ppermute(pieces[d], 'head', Ring(parts).pairs(d))]
  transfers between devices with their start and end apart: 24 -> 24, of which waited for: 6 -> 8; matrix products, arithmetic and copies ran while one was open for 3% -> 3% of each run, Pallas kernels for 20% -> 19%
where the time goes in v17:
time: 59.3 us; the launch traced here: 59.1 us
  starting transfers between devices  28.9 us (49%)
  Pallas kernels  13.3 us (22%)
  waiting for transfers between devices  11.9 us (20%)
  local copies, waits for them, and re-layouts  2.5 us (4%)
  other arithmetic  1.63 us (3%)
  between operations  0.83 us (1%)
    ppermute x15, starting transfers between devices, exchange(): moved.append(lax.ppermute(pieces[d], 'ctx', pairs))  17 us
    pallas_call x10, Pallas kernels, run(): pl.pallas_call(kernel, out_shape=outs, in_specs=[spec(i) for i in range(l...  13.3 us
    ppermute x6, starting transfers between devices, across_heads(): lax.ppermute(pieces[d], 'head', Ring(parts).pairs(d))  11.7 us
    ppermute x15, waiting for transfers between devices, exchange(): moved.append(lax.ppermute(pieces[d], 'ctx', pairs))  11.1 us
    unnamed x6, local copies, waits for them, and re-layouts  2.5 us
  transfers between devices with their start and end apart: 24, of which 8 were waited for; matrix products, arithmetic and copies ran while one was open for 3% of the time, Pallas kernels for 19%

profile of v17, /device:TPU:0, one launch (start us, length us, event | category | flops | bytes accessed | tf_op | source)
XLA Modules:
  0.0 59.1 jit_solution(12859255825457089184)
XLA Ops:
  0.6 1.2 %shard_map.135 = (bf16[400,128]{1,0:T(8,128)(2,1)S(1)}, bf16[400,128]{1,0:T(8,128)(2,1)S(1)}, bf16[400,128]{1,0:T(8,128)(2,1)S(1)}, bf16[400,128]{1,0:T(8,128)(2,1)S(1)}) custom-call(s32[1]{0:T(128)} %bitcast.1.place_ref, bf16[128,256]{1,0:T(8,128)(2,1)} %q_ref.1, bf16[128,256]{1,0:T(8,128)(2,1)} %k_ref.1, bf16[128,512]{1,0:T(8,128)(2,1)} %v_ref.1, ...), custom_call_target="tpu_custom_call" | custom-call | tf_op jit(solution)/shard_map/pallas_call | solution.py:62
  1.8 3.0 %collective-permute-start = (bf16[400,128]{1,0:T(8,128)(2,1)S(1)}, bf16[400,128]{1,0:T(8,128)(2,1)S(1)}, u32[]{:S(2)}, u32[]{:S(2)}) collective-permute-start(bf16[400,128]{1,0:T(8,128)(2,1)S(1)} %get-tuple-element.62), channel_id=1, source_target_pairs={{8,0},{12,4},{0,8},{4,12},{24,16},{28,20},{16,24},{20,28},{9,1},{1... | collective-permute-start | bytes 307208 | tf_op jit(solution)/shard_map/ppermute | solution.py:117
  4.8 2.6 %collective-permute-start.4 = (bf16[32,2048]{1,0:T(8,128)(2,1)}, bf16[32,2048]{1,0:T(8,128)(2,1)S(1)}, u32[]{:S(2)}, u32[]{:S(2)}) collective-permute-start(bf16[32,2048]{1,0:T(8,128)(2,1)} %refs_1_.2), channel_id=1, source_target_pairs={{2,0},{3,1},{0,2},{1,3},{6,4},{7,5},{4,6},{5,7},{10,8},{11,9},{8,1... | collective-permute-start | bytes 393224 | tf_op jit(solution)/shard_map/ppermute | solution.py:525
  7.4 1.6 %collective-permute-start.5 = (bf16[32,2048]{1,0:T(8,128)(2,1)}, bf16[32,2048]{1,0:T(8,128)(2,1)S(1)}, u32[]{:S(2)}, u32[]{:S(2)}) collective-permute-start(bf16[32,2048]{1,0:T(8,128)(2,1)} %refs_1_.2), channel_id=1, source_target_pairs={{1,0},{0,1},{3,2},{2,3},{5,4},{4,5},{7,6},{6,7},{9,8},{8,9},{11,10... | collective-permute-start | bytes 393224 | tf_op jit(solution)/shard_map/ppermute | solution.py:525
  9.2 1.5 %collective-permute-start.1 = (bf16[400,128]{1,0:T(8,128)(2,1)S(1)}, bf16[400,128]{1,0:T(8,128)(2,1)S(1)}, u32[]{:S(2)}, u32[]{:S(2)}) collective-permute-start(bf16[400,128]{1,0:T(8,128)(2,1)S(1)} %get-tuple-element.63), channel_id=1, source_target_pairs={{16,0},{20,4},{24,8},{28,12},{0,16},{4,20},{8,24},{12,28},{17,1},{... | collective-permute-start | bytes 307208 | tf_op jit(solution)/shard_map/ppermute | solution.py:117
  11.0 3.9 %collective-permute-done.1.refs_2_.refs_6_ = bf16[400,128]{1,0:T(8,128)(2,1)S(1)} collective-permute-done((bf16[400,128]{1,0:T(8,128)(2,1)S(1)}, bf16[400,128]{1,0:T(8,128)(2,1)S(1)}, u32[]{:S(2)}, u32[]{:S(2)}) %collective-permute-start.1) | collective-permute-done | bytes 102432 | tf_op jit(solution)/shard_map/ppermute | solution.py:117
  14.9 1.4 %collective-permute-done.2.refs_3_.refs_7_ = bf16[400,128]{1,0:T(8,128)(2,1)S(1)} collective-permute-done((bf16[400,128]{1,0:T(8,128)(2,1)S(1)}, bf16[400,128]{1,0:T(8,128)(2,1)S(1)}, u32[]{:S(2)}, u32[]{:S(2)}) %collective-permute-start.2) | collective-permute-done | bytes 102432 | tf_op jit(solution)/shard_map/ppermute | solution.py:117
  16.3 4.1 %shard_map.136 = (f32[4,2,128,128]{3,2,1,0:T(8,128)S(1)}, bf16[4,7,2,128,128]{4,3,2,1,0:T(8,128)(2,1)S(1)}, f32[4,4,128,128]{3,2,1,0:T(8,128)S(1)}) custom-call(s32[5]{0:T(128)} %off_ref.1, s32[1]{0:T(128)} %bitcast.1.place_ref, s32[1]{0:T(128)} %bitcast.2.mate_ref, bf16[400,128]{1,0:T(8,128)(2,1)S(1)} %get-tuple-element.61.refs_0_.refs_4_, ...), custom_call_target="tpu_custom_call" | custom-call | tf_op jit(solution)/shard_map/pallas_call | solution.py:62
  20.5 1.6 %copy-done = bf16[512,2048]{1,0:T(8,128)(2,1)S(1)} copy-done((bf16[512,2048]{1,0:T(8,128)(2,1)S(1)}, bf16[512,2048]{1,0:T(8,128)(2,1)}, u32[]{:S(2)}) %copy-start) | copy-done | bytes 2097176
  22.1 0.9 %copy-done.2 = bf16[32,2048]{1,0:T(8,128)(2,1)S(1)} copy-done((bf16[32,2048]{1,0:T(8,128)(2,1)S(1)}, bf16[32,2048]{1,0:T(8,128)(2,1)}, u32[]{:S(2)}) %copy-start.2) | copy-done | bytes 131096
  23.0 0.8 %shard_map.137 = (bf16[256,128]{1,0:T(8,128)(2,1)S(1)}, bf16[256,128]{1,0:T(8,128)(2,1)S(1)}, bf16[256,128]{1,0:T(8,128)(2,1)S(1)}, bf16[256,128]{1,0:T(8,128)(2,1)S(1)}) custom-call(s32[1]{0:T(128)} %bitcast.head_ref, s32[1]{0:T(128)} %bitcast.1.place_ref, bf16[32,2048]{1,0:T(8,128)(2,1)S(1)} %collective-permute-done.4.refs_0_, ...), custom_call_target="tpu_custom_call" | custom-call | flops 30000001024 | tf_op jit(solution)/shard_map/pallas_call | solution.py:62
  23.8 0.6 %collective-permute-start.13 = (bf16[256,128]{1,0:T(8,128)(2,1)S(1)}, bf16[256,128]{1,0:T(8,128)(2,1)S(1)}, u32[]{:S(2)}, u32[]{:S(2)}) collective-permute-start(bf16[256,128]{1,0:T(8,128)(2,1)S(1)} %get-tuple-element.79), channel_id=1, source_target_pairs={{8,0},{12,4},{0,8},{4,12},{24,16},{28,20},{16,24},{20,28},{9,1},{1... | collective-permute-start | bytes 196616 | tf_op jit(solution)/shard_map/ppermute | solution.py:117
  24.7 2.7 %collective-permute-start.15 = (bf16[256,128]{1,0:T(8,128)(2,1)S(1)}, bf16[256,128]{1,0:T(8,128)(2,1)S(1)}, u32[]{:S(2)}, u32[]{:S(2)}) collective-permute-start(bf16[256,128]{1,0:T(8,128)(2,1)S(1)} %get-tuple-element.81), channel_id=1, source_target_pairs={{24,0},{28,4},{16,8},{20,12},{8,16},{12,20},{0,24},{4,28},{25,1},{... | collective-permute-start | bytes 196616 | tf_op jit(solution)/shard_map/ppermute | solution.py:117
  27.4 1.3 %shard_map.138 = (f32[4,128,128]{2,1,0:T(8,128)S(1)}, bf16[4,128,128]{2,1,0:T(8,128)(2,1)S(1)}, bf16[4,128,128]{2,1,0:T(8,128)(2,1)S(1)}, bf16[4,128,128]{2,1,0:T(8,128)(2,1)S(1)}, bf16[4,128,128]{2,1,0:T(8,128)(2,1)S(1)}) custom-call(s32[1]{0:T(128)} %bitcast.1.place_ref, s32[1]{0:T(128)} %bitcast.2.mate_ref, ...), custom_call_target="tpu_custom_call" | custom-call | flops 2500000000 | tf_op jit(solution)/shard_map/pallas_call | solution.py:62
  28.7 0.6 %collective-permute-start.7 = (bf16[4,128,128]{2,1,0:T(8,128)(2,1)S(1)}, bf16[4,128,128]{2,1,0:T(8,128)(2,1)S(1)}, u32[]{:S(2)}, u32[]{:S(2)}) collective-permute-start(bf16[4,128,128]{2,1,0:T(8,128)(2,1)S(1)} %get-tuple-element.72), channel_id=1, source_target_pairs={{8,0},{12,4},{0,8},{4,12},{24,16},{28,20},{16,24},{20,28},{9,1},{1... | collective-permute-start | bytes 393224 | tf_op jit(solution)/shard_map/ppermute | solution.py:117
  29.6 2.7 %collective-permute-start.9 = (bf16[4,128,128]{2,1,0:T(8,128)(2,1)S(1)}, bf16[4,128,128]{2,1,0:T(8,128)(2,1)S(1)}, u32[]{:S(2)}, u32[]{:S(2)}) collective-permute-start(bf16[4,128,128]{2,1,0:T(8,128)(2,1)S(1)} %get-tuple-element.74), channel_id=1, source_target_pairs={{24,0},{28,4},{16,8},{20,12},{8,16},{12,20},{0,24},{4,28},{25,1},{... | collective-permute-start | bytes 393224 | tf_op jit(solution)/shard_map/ppermute | solution.py:117
  32.9 0.6 %collective-permute-start.17 = (bf16[512,128]{1,0:T(8,128)(2,1)S(1)}, bf16[512,128]{1,0:T(8,128)(2,1)S(1)}, u32[]{:S(2)}, u32[]{:S(2)}) collective-permute-start(bf16[512,128]{1,0:T(8,128)(2,1)S(1)} %get-tuple-element.97), channel_id=1, source_target_pairs={{8,0},{12,4},{0,8},{4,12},{24,16},{28,20},{16,24},{20,28},{9,1},{1... | collective-permute-start | bytes 393224 | tf_op jit(solution)/shard_map/ppermute | solution.py:117
  33.5 1.7 %collective-permute-done.7.refs_1_.refs_5_ = bf16[4,128,128]{2,1,0:T(8,128)(2,1)S(1)} collective-permute-done((bf16[4,128,128]{2,1,0:T(8,128)(2,1)S(1)}, bf16[4,128,128]{2,1,0:T(8,128)(2,1)S(1)}, u32[]{:S(2)}, u32[]{:S(2)}) %collective-permute-start.7) | collective-permute-done | bytes 131104 | tf_op jit(solution)/shard_map/ppermute | solution.py:117
  35.6 1.2 %collective-permute-done.8.refs_2_.refs_6_ = bf16[4,128,128]{2,1,0:T(8,128)(2,1)S(1)} collective-permute-done((bf16[4,128,128]{2,1,0:T(8,128)(2,1)S(1)}, bf16[4,128,128]{2,1,0:T(8,128)(2,1)S(1)}, u32[]{:S(2)}, u32[]{:S(2)}) %collective-permute-start.8) | collective-permute-done | bytes 131104 | tf_op jit(solution)/shard_map/ppermute | solution.py:117
  36.8 1.3 %collective-permute-start.19 = (bf16[512,128]{1,0:T(8,128)(2,1)S(1)}, bf16[512,128]{1,0:T(8,128)(2,1)S(1)}, u32[]{:S(2)}, u32[]{:S(2)}) collective-permute-start(bf16[512,128]{1,0:T(8,128)(2,1)S(1)} %get-tuple-element.99), channel_id=1, source_target_pairs={{24,0},{28,4},{16,8},{20,12},{8,16},{12,20},{0,24},{4,28},{25,1},{... | collective-permute-start | bytes 393224 | tf_op jit(solution)/shard_map/ppermute | solution.py:117
  38.7 0.7 %collective-permute-start.12 = (bf16[32,2048]{1,0:T(8,128)(2,1)S(1)}, bf16[32,2048]{1,0:T(8,128)(2,1)S(1)}, u32[]{:S(2)}, u32[]{:S(2)}) collective-permute-start(bf16[32,2048]{1,0:T(8,128)(2,1)S(1)} %get-tuple-element.78), channel_id=1, source_target_pairs={{1,0},{0,1},{3,2},{2,3},{5,4},{4,5},{7,6},{6,7},{9,8},{8,9},{11,10... | collective-permute-start | bytes 393224 | tf_op jit(solution)/shard_map/ppermute | solution.py:525
  39.9 3.1 %collective-permute-start.11 = (bf16[32,2048]{1,0:T(8,128)(2,1)S(1)}, bf16[32,2048]{1,0:T(8,128)(2,1)S(1)}, u32[]{:S(2)}, u32[]{:S(2)}) collective-permute-start(bf16[32,2048]{1,0:T(8,128)(2,1)S(1)} %get-tuple-element.77), channel_id=1, source_target_pairs={{2,0},{3,1},{0,2},{1,3},{6,4},{7,5},{4,6},{5,7},{10,8},{11,9},{8,1... | collective-permute-start | bytes 393224 | tf_op jit(solution)/shard_map/ppermute | solution.py:525
  43.0 3.5 %collective-permute-start.10 = (bf16[32,2048]{1,0:T(8,128)(2,1)S(1)}, bf16[32,2048]{1,0:T(8,128)(2,1)S(1)}, u32[]{:S(2)}, u32[]{:S(2)}) collective-permute-start(bf16[32,2048]{1,0:T(8,128)(2,1)S(1)} %get-tuple-element.76), channel_id=1, source_target_pairs={{3,0},{2,1},{1,2},{0,3},{7,4},{6,5},{5,6},{4,7},{11,8},{10,9},{9,1... | collective-permute-start | bytes 393224 | tf_op jit(solution)/shard_map/ppermute | solution.py:525
  46.5 0.7 %shard_map.143 = (f32[256,512]{1,0:T(8,128)S(1)}, f32[256,512]{1,0:T(8,128)S(1)}) custom-call(s32[1]{0:T(128)} %bitcast.1.place_ref, s32[1]{0:T(128)} %bitcast.2.mate_ref, bf16[512,128]{1,0:T(8,128)(2,1)S(1)} %get-tuple-element.96.refs_0_, bf16[512,128]{1,0:T(8,128)(2,1)S(1)} %collective-permute-done.17.refs_1_, ...), custom_call_target="tpu_custom_call" | custom-call | flops 1000000000 | tf_op jit(solution)/shard_map/pallas_call | solution.py:62
  47.3 3.2 %shard_map.141 = (bf16[400,128]{1,0:T(8,128)(2,1)S(1)}, bf16[400,128]{1,0:T(8,128)(2,1)S(1)}, bf16[400,128]{1,0:T(8,128)(2,1)S(1)}, bf16[400,128]{1,0:T(8,128)(2,1)S(1)}) custom-call(s32[1]{0:T(128)} %bitcast.1.place_ref, s32[1]{0:T(128)} %bitcast.2.mate_ref, f32[4,2,128,128]{3,2,1,0:T(8,128)S(1)} %get-tuple-element.65.refs_0_, ...), custom_call_target="tpu_custom_call" | custom-call | flops 6000000000 | tf_op jit(solution)/shard_map/pallas_call | solution.py:62
  50.7 0.6 collective-permute-start.21
  51.2 0.8 %collective-permute-done.11 = bf16[32,2048]{1,0:T(8,128)(2,1)S(1)} collective-permute-done((bf16[32,2048]{1,0:T(8,128)(2,1)S(1)}, bf16[32,2048]{1,0:T(8,128)(2,1)S(1)}, u32[]{:S(2)}, u32[]{:S(2)}) %collective-permute-start.11) | collective-permute-done | bytes 131104 | tf_op jit(solution)/shard_map/ppermute | solution.py:525
  52.0 2.1 %collective-permute-start.22 = (bf16[400,128]{1,0:T(8,128)(2,1)S(1)}, bf16[400,128]{1,0:T(8,128)(2,1)S(1)}, u32[]{:S(2)}, u32[]{:S(2)}) collective-permute-start(bf16[400,128]{1,0:T(8,128)(2,1)S(1)} %get-tuple-element.104), channel_id=1, source_target_pairs={{24,0},{28,4},{16,8},{20,12},{8,16},{12,20},{0,24},{4,28},{25,1},{... | collective-permute-start | bytes 307208 | tf_op jit(solution)/shard_map/ppermute | solution.py:117
  54.1 0.8 %convert_add_fusion = f32[32,2048]{1,0:T(8,128)} fusion(bf16[32,2048]{1,0:T(8,128)(2,1)S(1)} %collective-permute-done.12, bf16[32,2048]{1,0:T(8,128)(2,1)S(1)} %collective-permute-done.11, f32[32,2048]{1,0:T(8,128)S(1)} %get-tuple-element.75, bf16[32,2048]{1,0:T(8,128)(2,1)S(1)} %collective-permute-done.10), kind=kLoop, calls=%fused_computation | loop fusion | flops 393216 | bytes 917504 | tf_op jit(solution)/shard_map/add | solution.py:620
  54.9 0.9 %add.21 = f32[256,512]{1,0:T(8,128)} add(f32[256,512]{1,0:T(8,128)S(1)} %get-tuple-element.100, f32[256,512]{1,0:T(8,128)S(1)} %collective-permute-done.23) | non-fusion elementwise | flops 131072 | bytes 1572864 | tf_op jit(solution)/shard_map/add | solution.py:616
  56.3 1.9 %collective-permute-done.21.refs_2_ = bf16[400,128]{1,0:T(8,128)(2,1)S(1)} collective-permute-done((bf16[400,128]{1,0:T(8,128)(2,1)S(1)}, bf16[400,128]{1,0:T(8,128)(2,1)S(1)}, u32[]{:S(2)}, u32[]{:S(2)}) %collective-permute-start.21) | collective-permute-done | bytes 102432 | tf_op jit(solution)/shard_map/ppermute | solution.py:117
  58.2 0.9 %shard_map.144 = (f32[128,256]{1,0:T(8,128)}, f32[128,256]{1,0:T(8,128)}, f32[128,512]{1,0:T(8,128)}, f32[4,128]{1,0:T(4,128)}, f32[4,128]{1,0:T(4,128)}) custom-call(s32[1]{0:T(128)} %bitcast.1.place_ref, bf16[400,128]{1,0:T(8,128)(2,1)S(1)} %get-tuple-element.106.refs_0_, bf16[400,128]{1,0:T(8,128)(2,1)S(1)} %collective-permute-done.20.refs_1_, ...), custom_call_target="tpu_custom_call" | custom-call | flops 1000000000 | tf_op jit(solution)/shard_map/pallas_call | solution.py:62
  (34 shorter events, 4.0 us)
Async XLA Ops:
  1.8 8.9 %collective-permute-start = (bf16[400,128]{1,0:T(8,128)(2,1)S(1)}, bf16[400,128]{1,0:T(8,128)(2,1)S(1)}, u32[]{:S(2)}, u32[]{:S(2)}) collective-permute-start(bf16[400,128]{1,0:T(8,128)(2,1)S(1)} %get-tuple-element.62), channel_id=1, source_target_pairs={{8,0},{12,4},{0,8},{4,12},{24,16},{28,20},{16,24},{20,28},{9,1},{1... | collective-permute-start | bytes 307208 | tf_op jit(solution)/shard_map/ppermute | solution.py:117
  4.8 15.7 %collective-permute-start.4 = (bf16[32,2048]{1,0:T(8,128)(2,1)}, bf16[32,2048]{1,0:T(8,128)(2,1)S(1)}, u32[]{:S(2)}, u32[]{:S(2)}) collective-permute-start(bf16[32,2048]{1,0:T(8,128)(2,1)} %refs_1_.2), channel_id=1, source_target_pairs={{2,0},{3,1},{0,2},{1,3},{6,4},{7,5},{4,6},{5,7},{10,8},{11,9},{8,1... | collective-permute-start | bytes 393224 | tf_op jit(solution)/shard_map/ppermute | solution.py:525
  7.4 13.1 %collective-permute-start.5 = (bf16[32,2048]{1,0:T(8,128)(2,1)}, bf16[32,2048]{1,0:T(8,128)(2,1)S(1)}, u32[]{:S(2)}, u32[]{:S(2)}) collective-permute-start(bf16[32,2048]{1,0:T(8,128)(2,1)} %refs_1_.2), channel_id=1, source_target_pairs={{1,0},{0,1},{3,2},{2,3},{5,4},{4,5},{7,6},{6,7},{9,8},{8,9},{11,10... | collective-permute-start | bytes 393224 | tf_op jit(solution)/shard_map/ppermute | solution.py:525
  9.0 11.5 %collective-permute-start.6 = (bf16[32,2048]{1,0:T(8,128)(2,1)}, bf16[32,2048]{1,0:T(8,128)(2,1)S(1)}, u32[]{:S(2)}, u32[]{:S(2)}) collective-permute-start(bf16[32,2048]{1,0:T(8,128)(2,1)} %refs_1_.2), channel_id=1, source_target_pairs={{3,0},{2,1},{1,2},{0,3},{7,4},{6,5},{5,6},{4,7},{11,8},{10,9},{9,1... | collective-permute-start | bytes 393224 | tf_op jit(solution)/shard_map/ppermute | solution.py:525
  9.2 5.7 %collective-permute-start.1 = (bf16[400,128]{1,0:T(8,128)(2,1)S(1)}, bf16[400,128]{1,0:T(8,128)(2,1)S(1)}, u32[]{:S(2)}, u32[]{:S(2)}) collective-permute-start(bf16[400,128]{1,0:T(8,128)(2,1)S(1)} %get-tuple-element.63), channel_id=1, source_target_pairs={{16,0},{20,4},{24,8},{28,12},{0,16},{4,20},{8,24},{12,28},{17,1},{... | collective-permute-start | bytes 307208 | tf_op jit(solution)/shard_map/ppermute | solution.py:117
  10.7 5.6 %collective-permute-start.2 = (bf16[400,128]{1,0:T(8,128)(2,1)S(1)}, bf16[400,128]{1,0:T(8,128)(2,1)S(1)}, u32[]{:S(2)}, u32[]{:S(2)}) collective-permute-start(bf16[400,128]{1,0:T(8,128)(2,1)S(1)} %get-tuple-element.64), channel_id=1, source_target_pairs={{24,0},{28,4},{16,8},{20,12},{8,16},{12,20},{0,24},{4,28},{25,1},{... | collective-permute-start | bytes 307208 | tf_op jit(solution)/shard_map/ppermute | solution.py:117
  20.4 6.9 %collective-permute-start.3 = (f32[4,2,128,128]{3,2,1,0:T(8,128)S(1)}, f32[4,2,128,128]{3,2,1,0:T(8,128)S(1)}, u32[]{:S(2)}, u32[]{:S(2)}) collective-permute-start(f32[4,2,128,128]{3,2,1,0:T(8,128)S(1)} %get-tuple-element.65.refs_0_), channel_id=1, source_target_pairs={{4,0},{0,4},{12,8},{8,12},{20,16},{16,20},{28,24},{24,28},{5,1},{1... | collective-permute-start | bytes 1572872 | tf_op jit(solution)/shard_map/ppermute | solution.py:123
  20.5 1.6 %copy-start = (bf16[512,2048]{1,0:T(8,128)(2,1)S(1)}, bf16[512,2048]{1,0:T(8,128)(2,1)}, u32[]{:S(2)}) copy-start(bf16[512,2048]{1,0:T(8,128)(2,1)} %refs_4_.2) | copy-start | bytes 6291460
  22.1 0.9 %copy-start.2 = (bf16[32,2048]{1,0:T(8,128)(2,1)S(1)}, bf16[32,2048]{1,0:T(8,128)(2,1)}, u32[]{:S(2)}) copy-start(bf16[32,2048]{1,0:T(8,128)(2,1)} %refs_1_.2) | copy-start | bytes 393220
  23.8 5.8 %collective-permute-start.13 = (bf16[256,128]{1,0:T(8,128)(2,1)S(1)}, bf16[256,128]{1,0:T(8,128)(2,1)S(1)}, u32[]{:S(2)}, u32[]{:S(2)}) collective-permute-start(bf16[256,128]{1,0:T(8,128)(2,1)S(1)} %get-tuple-element.79), channel_id=1, source_target_pairs={{8,0},{12,4},{0,8},{4,12},{24,16},{28,20},{16,24},{20,28},{9,1},{1... | collective-permute-start | bytes 196616 | tf_op jit(solution)/shard_map/ppermute | solution.py:117
  24.4 7.8 %collective-permute-start.14 = (bf16[256,128]{1,0:T(8,128)(2,1)S(1)}, bf16[256,128]{1,0:T(8,128)(2,1)S(1)}, u32[]{:S(2)}, u32[]{:S(2)}) collective-permute-start(bf16[256,128]{1,0:T(8,128)(2,1)S(1)} %get-tuple-element.80), channel_id=1, source_target_pairs={{16,0},{20,4},{24,8},{28,12},{0,16},{4,20},{8,24},{12,28},{17,1},{... | collective-permute-start | bytes 196616 | tf_op jit(solution)/shard_map/ppermute | solution.py:117
  24.7 7.5 %collective-permute-start.15 = (bf16[256,128]{1,0:T(8,128)(2,1)S(1)}, bf16[256,128]{1,0:T(8,128)(2,1)S(1)}, u32[]{:S(2)}, u32[]{:S(2)}) collective-permute-start(bf16[256,128]{1,0:T(8,128)(2,1)S(1)} %get-tuple-element.81), channel_id=1, source_target_pairs={{24,0},{28,4},{16,8},{20,12},{8,16},{12,20},{0,24},{4,28},{25,1},{... | collective-permute-start | bytes 196616 | tf_op jit(solution)/shard_map/ppermute | solution.py:117
  28.7 6.5 %collective-permute-start.7 = (bf16[4,128,128]{2,1,0:T(8,128)(2,1)S(1)}, bf16[4,128,128]{2,1,0:T(8,128)(2,1)S(1)}, u32[]{:S(2)}, u32[]{:S(2)}) collective-permute-start(bf16[4,128,128]{2,1,0:T(8,128)(2,1)S(1)} %get-tuple-element.72), channel_id=1, source_target_pairs={{8,0},{12,4},{0,8},{4,12},{24,16},{28,20},{16,24},{20,28},{9,1},{1... | collective-permute-start | bytes 393224 | tf_op jit(solution)/shard_map/ppermute | solution.py:117
  29.3 7.6 %collective-permute-start.8 = (bf16[4,128,128]{2,1,0:T(8,128)(2,1)S(1)}, bf16[4,128,128]{2,1,0:T(8,128)(2,1)S(1)}, u32[]{:S(2)}, u32[]{:S(2)}) collective-permute-start(bf16[4,128,128]{2,1,0:T(8,128)(2,1)S(1)} %get-tuple-element.73), channel_id=1, source_target_pairs={{16,0},{20,4},{24,8},{28,12},{0,16},{4,20},{8,24},{12,28},{17,1},{... | collective-permute-start | bytes 393224 | tf_op jit(solution)/shard_map/ppermute | solution.py:117
  29.6 8.5 %collective-permute-start.9 = (bf16[4,128,128]{2,1,0:T(8,128)(2,1)S(1)}, bf16[4,128,128]{2,1,0:T(8,128)(2,1)S(1)}, u32[]{:S(2)}, u32[]{:S(2)}) collective-permute-start(bf16[4,128,128]{2,1,0:T(8,128)(2,1)S(1)} %get-tuple-element.74), channel_id=1, source_target_pairs={{24,0},{28,4},{16,8},{20,12},{8,16},{12,20},{0,24},{4,28},{25,1},{... | collective-permute-start | bytes 393224 | tf_op jit(solution)/shard_map/ppermute | solution.py:117
  32.5 5.6 %copy-start.1 = (bf16[512,2048]{1,0:T(8,128)(2,1)S(1)}, bf16[512,2048]{1,0:T(8,128)(2,1)}, u32[]{:S(2)}) copy-start(bf16[512,2048]{1,0:T(8,128)(2,1)} %refs_4_.2) | copy-start | bytes 6291460
  32.5 14.8 %collective-permute-start.16 = (f32[4,128,128]{2,1,0:T(8,128)S(1)}, f32[4,128,128]{2,1,0:T(8,128)S(1)}, u32[]{:S(2)}, u32[]{:S(2)}) collective-permute-start(f32[4,128,128]{2,1,0:T(8,128)S(1)} %shard_map.140.refs_2_), channel_id=1, source_target_pairs={{4,0},{0,4},{12,8},{8,12},{20,16},{16,20},{28,24},{24,28},{5,1},{1... | collective-permute-start | bytes 786440 | tf_op jit(solution)/shard_map/ppermute | solution.py:123
  32.9 7.0 %collective-permute-start.17 = (bf16[512,128]{1,0:T(8,128)(2,1)S(1)}, bf16[512,128]{1,0:T(8,128)(2,1)S(1)}, u32[]{:S(2)}, u32[]{:S(2)}) collective-permute-start(bf16[512,128]{1,0:T(8,128)(2,1)S(1)} %get-tuple-element.97), channel_id=1, source_target_pairs={{8,0},{12,4},{0,8},{4,12},{24,16},{28,20},{16,24},{20,28},{9,1},{1... | collective-permute-start | bytes 393224 | tf_op jit(solution)/shard_map/ppermute | solution.py:117
  35.1 7.8 %collective-permute-start.18 = (bf16[512,128]{1,0:T(8,128)(2,1)S(1)}, bf16[512,128]{1,0:T(8,128)(2,1)S(1)}, u32[]{:S(2)}, u32[]{:S(2)}) collective-permute-start(bf16[512,128]{1,0:T(8,128)(2,1)S(1)} %get-tuple-element.98), channel_id=1, source_target_pairs={{16,0},{20,4},{24,8},{28,12},{0,16},{4,20},{8,24},{12,28},{17,1},{... | collective-permute-start | bytes 393224 | tf_op jit(solution)/shard_map/ppermute | solution.py:117
  36.8 9.7 %collective-permute-start.19 = (bf16[512,128]{1,0:T(8,128)(2,1)S(1)}, bf16[512,128]{1,0:T(8,128)(2,1)S(1)}, u32[]{:S(2)}, u32[]{:S(2)}) collective-permute-start(bf16[512,128]{1,0:T(8,128)(2,1)S(1)} %get-tuple-element.99), channel_id=1, source_target_pairs={{24,0},{28,4},{16,8},{20,12},{8,16},{12,20},{0,24},{4,28},{25,1},{... | collective-permute-start | bytes 393224 | tf_op jit(solution)/shard_map/ppermute | solution.py:117
  38.7 12.0 %collective-permute-start.12 = (bf16[32,2048]{1,0:T(8,128)(2,1)S(1)}, bf16[32,2048]{1,0:T(8,128)(2,1)S(1)}, u32[]{:S(2)}, u32[]{:S(2)}) collective-permute-start(bf16[32,2048]{1,0:T(8,128)(2,1)S(1)} %get-tuple-element.78), channel_id=1, source_target_pairs={{1,0},{0,1},{3,2},{2,3},{5,4},{4,5},{7,6},{6,7},{9,8},{8,9},{11,10... | collective-permute-start | bytes 393224 | tf_op jit(solution)/shard_map/ppermute | solution.py:525
  39.9 12.2 %collective-permute-start.11 = (bf16[32,2048]{1,0:T(8,128)(2,1)S(1)}, bf16[32,2048]{1,0:T(8,128)(2,1)S(1)}, u32[]{:S(2)}, u32[]{:S(2)}) collective-permute-start(bf16[32,2048]{1,0:T(8,128)(2,1)S(1)} %get-tuple-element.77), channel_id=1, source_target_pairs={{2,0},{3,1},{0,2},{1,3},{6,4},{7,5},{4,6},{5,7},{10,8},{11,9},{8,1... | collective-permute-start | bytes 393224 | tf_op jit(solution)/shard_map/ppermute | solution.py:525
  43.0 11.2 %collective-permute-start.10 = (bf16[32,2048]{1,0:T(8,128)(2,1)S(1)}, bf16[32,2048]{1,0:T(8,128)(2,1)S(1)}, u32[]{:S(2)}, u32[]{:S(2)}) collective-permute-start(bf16[32,2048]{1,0:T(8,128)(2,1)S(1)} %get-tuple-element.76), channel_id=1, source_target_pairs={{3,0},{2,1},{1,2},{0,3},{7,4},{6,5},{5,6},{4,7},{11,8},{10,9},{9,1... | collective-permute-start | bytes 393224 | tf_op jit(solution)/shard_map/ppermute | solution.py:525
  47.2 7.7 %collective-permute-start.23 = (f32[256,512]{1,0:T(8,128)S(1)}, f32[256,512]{1,0:T(8,128)S(1)}, u32[]{:S(2)}, u32[]{:S(2)}) collective-permute-start(f32[256,512]{1,0:T(8,128)S(1)} %get-tuple-element.105), channel_id=1, source_target_pairs={{4,0},{0,4},{12,8},{8,12},{20,16},{16,20},{28,24},{24,28},{5,1},{1... | collective-permute-start | bytes 1572872 | tf_op jit(solution)/shard_map/ppermute | solution.py:123
  50.6 5.7 %collective-permute-start.20 = (bf16[400,128]{1,0:T(8,128)(2,1)S(1)}, bf16[400,128]{1,0:T(8,128)(2,1)S(1)}, u32[]{:S(2)}, u32[]{:S(2)}) collective-permute-start(bf16[400,128]{1,0:T(8,128)(2,1)S(1)} %get-tuple-element.102), channel_id=1, source_target_pairs={{8,0},{12,4},{0,8},{4,12},{24,16},{28,20},{16,24},{20,28},{9,1},{1... | collective-permute-start | bytes 307208 | tf_op jit(solution)/shard_map/ppermute | solution.py:117
  50.7 7.5 %collective-permute-start.21 = (bf16[400,128]{1,0:T(8,128)(2,1)S(1)}, bf16[400,128]{1,0:T(8,128)(2,1)S(1)}, u32[]{:S(2)}, u32[]{:S(2)}) collective-permute-start(bf16[400,128]{1,0:T(8,128)(2,1)S(1)} %get-tuple-element.103), channel_id=1, source_target_pairs={{16,0},{20,4},{24,8},{28,12},{0,16},{4,20},{8,24},{12,28},{17,1},{... | collective-permute-start | bytes 307208 | tf_op jit(solution)/shard_map/ppermute | solution.py:117
  52.0 6.2 %collective-permute-start.22 = (bf16[400,128]{1,0:T(8,128)(2,1)S(1)}, bf16[400,128]{1,0:T(8,128)(2,1)S(1)}, u32[]{:S(2)}, u32[]{:S(2)}) collective-permute-start(bf16[400,128]{1,0:T(8,128)(2,1)S(1)} %get-tuple-element.104), channel_id=1, source_target_pairs={{24,0},{28,4},{16,8},{20,12},{8,16},{12,20},{0,24},{4,28},{25,1},{... | collective-permute-start | bytes 307208 | tf_op jit(solution)/shard_map/ppermute | solution.py:117

commit v18 on v16

--- a/solution.py
+++ b/solution.py
@@ -487,7 +487,7 @@
 def finish_kernel(plan, place_ref, *refs):
     pieces, (q_ref, k_ref, v_ref, rate_ref, decay_ref, in_ref) = refs[: plan.hv], refs[plan.hv :]
     tok = plan.tok
-    for d, ref in enumerate(pieces):
+    for d, ref in enumerate(reversed(pieces)):
         in_ref[plan.ring.source(place_ref[0], d)] = ref[...]
     for kh in range(plan.hk):
         mine = [h for h in range(plan.hv) if plan.key_head(h) == kh]
@@ -618,7 +618,7 @@
     layer_out = layer_parts[0]
     for part in layer_parts[:0:-1]:
         layer_out = layer_out + part.astype(F32)
-    grads = after(grads, (layer_out, weight_grad))
+    grads = after(grads[::-1], (layer_out, weight_grad))
     grad_q, grad_k, grad_v, grad_rate, grad_decay = call(
         partial(finish_kernel, plan),
         (

time: 56.1 us -> 55.9 us (level)
  transfers between devices with their start and end apart: 24 -> 24, of which waited for: 6 -> 7; matrix products, arithmetic and copies ran while one was open for 3% -> 3% of each run, Pallas kernels for 20% -> 20%
where the time goes in v18:
time: 55.9 us; the launch traced here: 55.7 us
  starting transfers between devices  31.5 us (56%)
  Pallas kernels  13.4 us (24%)
  waiting for transfers between devices  8.41 us (15%)
  other arithmetic  1.64 us (3%)
  between operations  0.77 us (1%)
    ppermute x15, starting transfers between devices, exchange(): moved.append(lax.ppermute(pieces[d], 'ctx', pairs))  18.5 us
    pallas_call x10, Pallas kernels, run(): pl.pallas_call(kernel, out_shape=outs, in_specs=[spec(i) for i in range(l...  13.4 us
    ppermute x6, starting transfers between devices, across_heads(): lax.ppermute(pieces[d], 'head', Ring(parts).pairs(d))  12.8 us
    ppermute x15, waiting for transfers between devices, exchange(): moved.append(lax.ppermute(pieces[d], 'ctx', pairs))  4.27 us
    ppermute x6, waiting for transfers between devices, across_heads(): lax.ppermute(pieces[d], 'head', Ring(parts).pairs(d))  4.14 us
  transfers between devices with their start and end apart: 24, of which 7 were waited for; matrix products, arithmetic and copies ran while one was open for 3% of the time, Pallas kernels for 20%

profile of v18, /device:TPU:0, one launch (start us, length us, event | category | flops | bytes accessed | tf_op | source)
XLA Modules:
  0.0 55.7 jit_solution(14855512049267391370)
XLA Ops:
  0.6 1.2 %shard_map.135 = (bf16[400,128]{1,0:T(8,128)(2,1)S(1)}, bf16[400,128]{1,0:T(8,128)(2,1)S(1)}, bf16[400,128]{1,0:T(8,128)(2,1)S(1)}, bf16[400,128]{1,0:T(8,128)(2,1)S(1)}) custom-call(s32[1]{0:T(128)} %bitcast.1.place_ref, bf16[128,256]{1,0:T(8,128)(2,1)} %q_ref.1, bf16[128,256]{1,0:T(8,128)(2,1)} %k_ref.1, bf16[128,512]{1,0:T(8,128)(2,1)} %v_ref.1, ...), custom_call_target="tpu_custom_call" | custom-call | tf_op jit(solution)/shard_map/pallas_call | solution.py:62
  1.8 3.0 %collective-permute-start = (bf16[400,128]{1,0:T(8,128)(2,1)S(1)}, bf16[400,128]{1,0:T(8,128)(2,1)S(1)}, u32[]{:S(2)}, u32[]{:S(2)}) collective-permute-start(bf16[400,128]{1,0:T(8,128)(2,1)S(1)} %get-tuple-element.62), channel_id=1, source_target_pairs={{8,0},{12,4},{0,8},{4,12},{24,16},{28,20},{16,24},{20,28},{9,1},{1... | collective-permute-start | bytes 307208 | tf_op jit(solution)/shard_map/ppermute | solution.py:117
  4.8 1.5 %collective-permute-start.1 = (bf16[400,128]{1,0:T(8,128)(2,1)S(1)}, bf16[400,128]{1,0:T(8,128)(2,1)S(1)}, u32[]{:S(2)}, u32[]{:S(2)}) collective-permute-start(bf16[400,128]{1,0:T(8,128)(2,1)S(1)} %get-tuple-element.63), channel_id=1, source_target_pairs={{16,0},{20,4},{24,8},{28,12},{0,16},{4,20},{8,24},{12,28},{17,1},{... | collective-permute-start | bytes 307208 | tf_op jit(solution)/shard_map/ppermute | solution.py:117
  6.4 3.0 %collective-permute-start.4 = (bf16[32,2048]{1,0:T(8,128)(2,1)}, bf16[32,2048]{1,0:T(8,128)(2,1)S(1)}, u32[]{:S(2)}, u32[]{:S(2)}) collective-permute-start(bf16[32,2048]{1,0:T(8,128)(2,1)} %refs_1_.2), channel_id=1, source_target_pairs={{2,0},{3,1},{0,2},{1,3},{6,4},{7,5},{4,6},{5,7},{10,8},{11,9},{8,1... | collective-permute-start | bytes 393224 | tf_op jit(solution)/shard_map/ppermute | solution.py:525
  9.4 1.6 %collective-permute-start.5 = (bf16[32,2048]{1,0:T(8,128)(2,1)}, bf16[32,2048]{1,0:T(8,128)(2,1)S(1)}, u32[]{:S(2)}, u32[]{:S(2)}) collective-permute-start(bf16[32,2048]{1,0:T(8,128)(2,1)} %refs_1_.2), channel_id=1, source_target_pairs={{1,0},{0,1},{3,2},{2,3},{5,4},{4,5},{7,6},{6,7},{9,8},{8,9},{11,10... | collective-permute-start | bytes 393224 | tf_op jit(solution)/shard_map/ppermute | solution.py:525
  11.9 4.2 %shard_map.136 = (f32[4,2,128,128]{3,2,1,0:T(8,128)S(1)}, bf16[4,7,2,128,128]{4,3,2,1,0:T(8,128)(2,1)S(1)}, f32[4,4,128,128]{3,2,1,0:T(8,128)S(1)}) custom-call(s32[5]{0:T(128)} %off_ref.1, s32[1]{0:T(128)} %bitcast.1.place_ref, s32[1]{0:T(128)} %bitcast.2.mate_ref, bf16[400,128]{1,0:T(8,128)(2,1)S(1)} %get-tuple-element.61.refs_0_.refs_4_, ...), custom_call_target="tpu_custom_call" | custom-call | flops 20000000000 | tf_op jit(solution)/shard_map/pallas_call | solution.py:62
  16.2 1.5 %collective-permute-done.4.refs_0_ = bf16[32,2048]{1,0:T(8,128)(2,1)S(1)} collective-permute-done((bf16[32,2048]{1,0:T(8,128)(2,1)}, bf16[32,2048]{1,0:T(8,128)(2,1)S(1)}, u32[]{:S(2)}, u32[]{:S(2)}) %collective-permute-start.4) | collective-permute-done | bytes 131104 | tf_op jit(solution)/shard_map/ppermute | solution.py:525
  17.7 1.4 %collective-permute-done.6.refs_3_ = bf16[32,2048]{1,0:T(8,128)(2,1)S(1)} collective-permute-done((bf16[32,2048]{1,0:T(8,128)(2,1)}, bf16[32,2048]{1,0:T(8,128)(2,1)S(1)}, u32[]{:S(2)}, u32[]{:S(2)}) %collective-permute-start.6) | collective-permute-done | bytes 131104 | tf_op jit(solution)/shard_map/ppermute | solution.py:525
  19.2 0.8 %shard_map.137 = (bf16[256,128]{1,0:T(8,128)(2,1)S(1)}, bf16[256,128]{1,0:T(8,128)(2,1)S(1)}, bf16[256,128]{1,0:T(8,128)(2,1)S(1)}, bf16[256,128]{1,0:T(8,128)(2,1)S(1)}) custom-call(s32[1]{0:T(128)} %bitcast.head_ref, s32[1]{0:T(128)} %bitcast.1.place_ref, bf16[32,2048]{1,0:T(8,128)(2,1)S(1)} %collective-permute-done.4.refs_0_, ...), custom_call_target="tpu_custom_call" | custom-call | flops 30000001024 | tf_op jit(solution)/shard_map/pallas_call | solution.py:62
  19.9 1.6 %collective-permute-start.13 = (bf16[256,128]{1,0:T(8,128)(2,1)S(1)}, bf16[256,128]{1,0:T(8,128)(2,1)S(1)}, u32[]{:S(2)}, u32[]{:S(2)}) collective-permute-start(bf16[256,128]{1,0:T(8,128)(2,1)S(1)} %get-tuple-element.79), channel_id=1, source_target_pairs={{8,0},{12,4},{0,8},{4,12},{24,16},{28,20},{16,24},{20,28},{9,1},{1... | collective-permute-start | bytes 196616 | tf_op jit(solution)/shard_map/ppermute | solution.py:117
  21.5 1.5 %collective-permute-start.14 = (bf16[256,128]{1,0:T(8,128)(2,1)S(1)}, bf16[256,128]{1,0:T(8,128)(2,1)S(1)}, u32[]{:S(2)}, u32[]{:S(2)}) collective-permute-start(bf16[256,128]{1,0:T(8,128)(2,1)S(1)} %get-tuple-element.80), channel_id=1, source_target_pairs={{16,0},{20,4},{24,8},{28,12},{0,16},{4,20},{8,24},{12,28},{17,1},{... | collective-permute-start | bytes 196616 | tf_op jit(solution)/shard_map/ppermute | solution.py:117
  23.5 1.3 %shard_map.138 = (f32[4,128,128]{2,1,0:T(8,128)S(1)}, bf16[4,128,128]{2,1,0:T(8,128)(2,1)S(1)}, bf16[4,128,128]{2,1,0:T(8,128)(2,1)S(1)}, bf16[4,128,128]{2,1,0:T(8,128)(2,1)S(1)}, bf16[4,128,128]{2,1,0:T(8,128)(2,1)S(1)}) custom-call(s32[1]{0:T(128)} %bitcast.1.place_ref, s32[1]{0:T(128)} %bitcast.2.mate_ref, ...), custom_call_target="tpu_custom_call" | custom-call | flops 2500000000 | tf_op jit(solution)/shard_map/pallas_call | solution.py:62
  24.8 1.6 %collective-permute-start.7 = (bf16[4,128,128]{2,1,0:T(8,128)(2,1)S(1)}, bf16[4,128,128]{2,1,0:T(8,128)(2,1)S(1)}, u32[]{:S(2)}, u32[]{:S(2)}) collective-permute-start(bf16[4,128,128]{2,1,0:T(8,128)(2,1)S(1)} %get-tuple-element.72), channel_id=1, source_target_pairs={{8,0},{12,4},{0,8},{4,12},{24,16},{28,20},{16,24},{20,28},{9,1},{1... | collective-permute-start | bytes 393224 | tf_op jit(solution)/shard_map/ppermute | solution.py:117
  26.4 1.5 %collective-permute-start.8 = (bf16[4,128,128]{2,1,0:T(8,128)(2,1)S(1)}, bf16[4,128,128]{2,1,0:T(8,128)(2,1)S(1)}, u32[]{:S(2)}, u32[]{:S(2)}) collective-permute-start(bf16[4,128,128]{2,1,0:T(8,128)(2,1)S(1)} %get-tuple-element.73), channel_id=1, source_target_pairs={{16,0},{20,4},{24,8},{28,12},{0,16},{4,20},{8,24},{12,28},{17,1},{... | collective-permute-start | bytes 393224 | tf_op jit(solution)/shard_map/ppermute | solution.py:117
  29.0 1.6 %collective-permute-start.17 = (bf16[512,128]{1,0:T(8,128)(2,1)S(1)}, bf16[512,128]{1,0:T(8,128)(2,1)S(1)}, u32[]{:S(2)}, u32[]{:S(2)}) collective-permute-start(bf16[512,128]{1,0:T(8,128)(2,1)S(1)} %get-tuple-element.97), channel_id=1, source_target_pairs={{8,0},{12,4},{0,8},{4,12},{24,16},{28,20},{16,24},{20,28},{9,1},{1... | collective-permute-start | bytes 393224 | tf_op jit(solution)/shard_map/ppermute | solution.py:117
  30.6 1.5 %collective-permute-start.18 = (bf16[512,128]{1,0:T(8,128)(2,1)S(1)}, bf16[512,128]{1,0:T(8,128)(2,1)S(1)}, u32[]{:S(2)}, u32[]{:S(2)}) collective-permute-start(bf16[512,128]{1,0:T(8,128)(2,1)S(1)} %get-tuple-element.98), channel_id=1, source_target_pairs={{16,0},{20,4},{24,8},{28,12},{0,16},{4,20},{8,24},{12,28},{17,1},{... | collective-permute-start | bytes 393224 | tf_op jit(solution)/shard_map/ppermute | solution.py:117
  32.1 0.7 %collective-permute-start.19 = (bf16[512,128]{1,0:T(8,128)(2,1)S(1)}, bf16[512,128]{1,0:T(8,128)(2,1)S(1)}, u32[]{:S(2)}, u32[]{:S(2)}) collective-permute-start(bf16[512,128]{1,0:T(8,128)(2,1)S(1)} %get-tuple-element.99), channel_id=1, source_target_pairs={{24,0},{28,4},{16,8},{20,12},{8,16},{12,20},{0,24},{4,28},{25,1},{... | collective-permute-start | bytes 393224 | tf_op jit(solution)/shard_map/ppermute | solution.py:117
  32.8 1.6 %collective-permute-done.9.refs_3_.refs_7_ = bf16[4,128,128]{2,1,0:T(8,128)(2,1)S(1)} collective-permute-done((bf16[4,128,128]{2,1,0:T(8,128)(2,1)S(1)}, bf16[4,128,128]{2,1,0:T(8,128)(2,1)S(1)}, u32[]{:S(2)}, u32[]{:S(2)}) %collective-permute-start.9) | collective-permute-done | bytes 131104 | tf_op jit(solution)/shard_map/ppermute | solution.py:117
  35.0 2.5 %collective-permute-start.12 = (bf16[32,2048]{1,0:T(8,128)(2,1)S(1)}, bf16[32,2048]{1,0:T(8,128)(2,1)S(1)}, u32[]{:S(2)}, u32[]{:S(2)}) collective-permute-start(bf16[32,2048]{1,0:T(8,128)(2,1)S(1)} %get-tuple-element.78), channel_id=1, source_target_pairs={{1,0},{0,1},{3,2},{2,3},{5,4},{4,5},{7,6},{6,7},{9,8},{8,9},{11,10... | collective-permute-start | bytes 393224 | tf_op jit(solution)/shard_map/ppermute | solution.py:525
  37.5 2.5 %collective-permute-start.11 = (bf16[32,2048]{1,0:T(8,128)(2,1)S(1)}, bf16[32,2048]{1,0:T(8,128)(2,1)S(1)}, u32[]{:S(2)}, u32[]{:S(2)}) collective-permute-start(bf16[32,2048]{1,0:T(8,128)(2,1)S(1)} %get-tuple-element.77), channel_id=1, source_target_pairs={{2,0},{3,1},{0,2},{1,3},{6,4},{7,5},{4,6},{5,7},{10,8},{11,9},{8,1... | collective-permute-start | bytes 393224 | tf_op jit(solution)/shard_map/ppermute | solution.py:525
  40.1 2.5 %collective-permute-start.10 = (bf16[32,2048]{1,0:T(8,128)(2,1)S(1)}, bf16[32,2048]{1,0:T(8,128)(2,1)S(1)}, u32[]{:S(2)}, u32[]{:S(2)}) collective-permute-start(bf16[32,2048]{1,0:T(8,128)(2,1)S(1)} %get-tuple-element.76), channel_id=1, source_target_pairs={{3,0},{2,1},{1,2},{0,3},{7,4},{6,5},{5,6},{4,7},{11,8},{10,9},{9,1... | collective-permute-start | bytes 393224 | tf_op jit(solution)/shard_map/ppermute | solution.py:525
  42.5 0.7 %shard_map.143 = (f32[256,512]{1,0:T(8,128)S(1)}, f32[256,512]{1,0:T(8,128)S(1)}) custom-call(s32[1]{0:T(128)} %bitcast.1.place_ref, s32[1]{0:T(128)} %bitcast.2.mate_ref, bf16[512,128]{1,0:T(8,128)(2,1)S(1)} %get-tuple-element.96.refs_0_, bf16[512,128]{1,0:T(8,128)(2,1)S(1)} %collective-permute-done.17.refs_1_, ...), custom_call_target="tpu_custom_call" | custom-call | flops 1000000000 | tf_op jit(solution)/shard_map/pallas_call | solution.py:62
  43.4 3.2 %shard_map.141 = (bf16[400,128]{1,0:T(8,128)(2,1)S(1)}, bf16[400,128]{1,0:T(8,128)(2,1)S(1)}, bf16[400,128]{1,0:T(8,128)(2,1)S(1)}, bf16[400,128]{1,0:T(8,128)(2,1)S(1)}) custom-call(s32[1]{0:T(128)} %bitcast.1.place_ref, s32[1]{0:T(128)} %bitcast.2.mate_ref, f32[4,2,128,128]{3,2,1,0:T(8,128)S(1)} %get-tuple-element.65.refs_0_, ...), custom_call_target="tpu_custom_call" | custom-call | flops 6000000000 | tf_op jit(solution)/shard_map/pallas_call | solution.py:62
  46.6 1.0 %collective-permute-start.20 = (bf16[400,128]{1,0:T(8,128)(2,1)S(1)}, bf16[400,128]{1,0:T(8,128)(2,1)S(1)}, u32[]{:S(2)}, u32[]{:S(2)}) collective-permute-start(bf16[400,128]{1,0:T(8,128)(2,1)S(1)} %get-tuple-element.101), channel_id=1, source_target_pairs={{24,0},{28,4},{16,8},{20,12},{8,16},{12,20},{0,24},{4,28},{25,1},{... | collective-permute-start | bytes 307208 | tf_op jit(solution)/shard_map/ppermute | solution.py:117
  47.6 0.6 %collective-permute-start.21 = (bf16[400,128]{1,0:T(8,128)(2,1)S(1)}, bf16[400,128]{1,0:T(8,128)(2,1)S(1)}, u32[]{:S(2)}, u32[]{:S(2)}) collective-permute-start(bf16[400,128]{1,0:T(8,128)(2,1)S(1)} %get-tuple-element.102), channel_id=1, source_target_pairs={{16,0},{20,4},{24,8},{28,12},{0,16},{4,20},{8,24},{12,28},{17,1},{... | collective-permute-start | bytes 307208 | tf_op jit(solution)/shard_map/ppermute | solution.py:117
  48.3 1.2 %collective-permute-done.11 = bf16[32,2048]{1,0:T(8,128)(2,1)S(1)} collective-permute-done((bf16[32,2048]{1,0:T(8,128)(2,1)S(1)}, bf16[32,2048]{1,0:T(8,128)(2,1)S(1)}, u32[]{:S(2)}, u32[]{:S(2)}) %collective-permute-start.11) | collective-permute-done | bytes 131104 | tf_op jit(solution)/shard_map/ppermute | solution.py:525
  49.5 1.4 %collective-permute-start.22 = (bf16[400,128]{1,0:T(8,128)(2,1)S(1)}, bf16[400,128]{1,0:T(8,128)(2,1)S(1)}, u32[]{:S(2)}, u32[]{:S(2)}) collective-permute-start(bf16[400,128]{1,0:T(8,128)(2,1)S(1)} %get-tuple-element.103), channel_id=1, source_target_pairs={{8,0},{12,4},{0,8},{4,12},{24,16},{28,20},{16,24},{20,28},{9,1},{1... | collective-permute-start | bytes 307208 | tf_op jit(solution)/shard_map/ppermute | solution.py:117
  50.9 0.8 %convert_add_fusion = f32[32,2048]{1,0:T(8,128)} fusion(bf16[32,2048]{1,0:T(8,128)(2,1)S(1)} %collective-permute-done.12, bf16[32,2048]{1,0:T(8,128)(2,1)S(1)} %collective-permute-done.11, f32[32,2048]{1,0:T(8,128)S(1)} %get-tuple-element.75, bf16[32,2048]{1,0:T(8,128)(2,1)S(1)} %collective-permute-done.10), kind=kLoop, calls=%fused_computation | loop fusion | flops 393216 | bytes 917504 | tf_op jit(solution)/shard_map/add | solution.py:620
  51.6 0.9 %add.21 = f32[256,512]{1,0:T(8,128)} add(f32[256,512]{1,0:T(8,128)S(1)} %get-tuple-element.100, f32[256,512]{1,0:T(8,128)S(1)} %collective-permute-done.23) | non-fusion elementwise | flops 131072 | bytes 1572864 | tf_op jit(solution)/shard_map/add | solution.py:616
  52.5 0.8 %collective-permute-done.20.refs_0_ = bf16[400,128]{1,0:T(8,128)(2,1)S(1)} collective-permute-done((bf16[400,128]{1,0:T(8,128)(2,1)S(1)}, bf16[400,128]{1,0:T(8,128)(2,1)S(1)}, u32[]{:S(2)}, u32[]{:S(2)}) %collective-permute-start.20) | collective-permute-done | bytes 102432 | tf_op jit(solution)/shard_map/ppermute | solution.py:117
  53.3 1.5 %collective-permute-done.21.refs_1_ = bf16[400,128]{1,0:T(8,128)(2,1)S(1)} collective-permute-done((bf16[400,128]{1,0:T(8,128)(2,1)S(1)}, bf16[400,128]{1,0:T(8,128)(2,1)S(1)}, u32[]{:S(2)}, u32[]{:S(2)}) %collective-permute-start.21) | collective-permute-done | bytes 102432 | tf_op jit(solution)/shard_map/ppermute | solution.py:117
  54.8 0.9 %shard_map.144 = (f32[128,256]{1,0:T(8,128)}, f32[128,256]{1,0:T(8,128)}, f32[128,512]{1,0:T(8,128)}, f32[4,128]{1,0:T(4,128)}, f32[4,128]{1,0:T(4,128)}) custom-call(s32[1]{0:T(128)} %bitcast.1.place_ref, bf16[400,128]{1,0:T(8,128)(2,1)S(1)} %collective-permute-done.20.refs_0_, bf16[400,128]{1,0:T(8,128)(2,1)S(1)} %collective-permute-done.21.refs_1_, ...), custom_call_target="tpu_custom_call" | custom-call | flops 1000000000 | tf_op jit(solution)/shard_map/pallas_call | solution.py:62
  (32 shorter events, 3.2 us)
Async XLA Ops:
  1.8 9.2 %collective-permute-start = (bf16[400,128]{1,0:T(8,128)(2,1)S(1)}, bf16[400,128]{1,0:T(8,128)(2,1)S(1)}, u32[]{:S(2)}, u32[]{:S(2)}) collective-permute-start(bf16[400,128]{1,0:T(8,128)(2,1)S(1)} %get-tuple-element.62), channel_id=1, source_target_pairs={{8,0},{12,4},{0,8},{4,12},{24,16},{28,20},{16,24},{20,28},{9,1},{1... | collective-permute-start | bytes 307208 | tf_op jit(solution)/shard_map/ppermute | solution.py:117
  4.8 6.8 %collective-permute-start.1 = (bf16[400,128]{1,0:T(8,128)(2,1)S(1)}, bf16[400,128]{1,0:T(8,128)(2,1)S(1)}, u32[]{:S(2)}, u32[]{:S(2)}) collective-permute-start(bf16[400,128]{1,0:T(8,128)(2,1)S(1)} %get-tuple-element.63), channel_id=1, source_target_pairs={{16,0},{20,4},{24,8},{28,12},{0,16},{4,20},{8,24},{12,28},{17,1},{... | collective-permute-start | bytes 307208 | tf_op jit(solution)/shard_map/ppermute | solution.py:117
  6.3 5.6 %collective-permute-start.2 = (bf16[400,128]{1,0:T(8,128)(2,1)S(1)}, bf16[400,128]{1,0:T(8,128)(2,1)S(1)}, u32[]{:S(2)}, u32[]{:S(2)}) collective-permute-start(bf16[400,128]{1,0:T(8,128)(2,1)S(1)} %get-tuple-element.64), channel_id=1, source_target_pairs={{24,0},{28,4},{16,8},{20,12},{8,16},{12,20},{0,24},{4,28},{25,1},{... | collective-permute-start | bytes 307208 | tf_op jit(solution)/shard_map/ppermute | solution.py:117
  6.4 11.4 %collective-permute-start.4 = (bf16[32,2048]{1,0:T(8,128)(2,1)}, bf16[32,2048]{1,0:T(8,128)(2,1)S(1)}, u32[]{:S(2)}, u32[]{:S(2)}) collective-permute-start(bf16[32,2048]{1,0:T(8,128)(2,1)} %refs_1_.2), channel_id=1, source_target_pairs={{2,0},{3,1},{0,2},{1,3},{6,4},{7,5},{4,6},{5,7},{10,8},{11,9},{8,1... | collective-permute-start | bytes 393224 | tf_op jit(solution)/shard_map/ppermute | solution.py:525
  9.4 8.3 %collective-permute-start.5 = (bf16[32,2048]{1,0:T(8,128)(2,1)}, bf16[32,2048]{1,0:T(8,128)(2,1)S(1)}, u32[]{:S(2)}, u32[]{:S(2)}) collective-permute-start(bf16[32,2048]{1,0:T(8,128)(2,1)} %refs_1_.2), channel_id=1, source_target_pairs={{1,0},{0,1},{3,2},{2,3},{5,4},{4,5},{7,6},{6,7},{9,8},{8,9},{11,10... | collective-permute-start | bytes 393224 | tf_op jit(solution)/shard_map/ppermute | solution.py:525
  11.0 8.2 %collective-permute-start.6 = (bf16[32,2048]{1,0:T(8,128)(2,1)}, bf16[32,2048]{1,0:T(8,128)(2,1)S(1)}, u32[]{:S(2)}, u32[]{:S(2)}) collective-permute-start(bf16[32,2048]{1,0:T(8,128)(2,1)} %refs_1_.2), channel_id=1, source_target_pairs={{3,0},{2,1},{1,2},{0,3},{7,4},{6,5},{5,6},{4,7},{11,8},{10,9},{9,1... | collective-permute-start | bytes 393224 | tf_op jit(solution)/shard_map/ppermute | solution.py:525
  11.9 7.3 %copy-start = (bf16[512,2048]{1,0:T(8,128)(2,1)S(1)}, bf16[512,2048]{1,0:T(8,128)(2,1)}, u32[]{:S(2)}) copy-start(bf16[512,2048]{1,0:T(8,128)(2,1)} %refs_4_.2) | copy-start | bytes 6291460
  11.9 7.3 %copy-start.1 = (bf16[32,2048]{1,0:T(8,128)(2,1)S(1)}, bf16[32,2048]{1,0:T(8,128)(2,1)}, u32[]{:S(2)}) copy-start(bf16[32,2048]{1,0:T(8,128)(2,1)} %refs_1_.2) | copy-start | bytes 393220
  16.1 7.3 %collective-permute-start.3 = (f32[4,2,128,128]{3,2,1,0:T(8,128)S(1)}, f32[4,2,128,128]{3,2,1,0:T(8,128)S(1)}, u32[]{:S(2)}, u32[]{:S(2)}) collective-permute-start(f32[4,2,128,128]{3,2,1,0:T(8,128)S(1)} %get-tuple-element.65.refs_0_), channel_id=1, source_target_pairs={{4,0},{0,4},{12,8},{8,12},{20,16},{16,20},{28,24},{24,28},{5,1},{1... | collective-permute-start | bytes 1572872 | tf_op jit(solution)/shard_map/ppermute | solution.py:123
  19.9 7.9 %collective-permute-start.13 = (bf16[256,128]{1,0:T(8,128)(2,1)S(1)}, bf16[256,128]{1,0:T(8,128)(2,1)S(1)}, u32[]{:S(2)}, u32[]{:S(2)}) collective-permute-start(bf16[256,128]{1,0:T(8,128)(2,1)S(1)} %get-tuple-element.79), channel_id=1, source_target_pairs={{8,0},{12,4},{0,8},{4,12},{24,16},{28,20},{16,24},{20,28},{9,1},{1... | collective-permute-start | bytes 196616 | tf_op jit(solution)/shard_map/ppermute | solution.py:117
  21.5 6.9 %collective-permute-start.14 = (bf16[256,128]{1,0:T(8,128)(2,1)S(1)}, bf16[256,128]{1,0:T(8,128)(2,1)S(1)}, u32[]{:S(2)}, u32[]{:S(2)}) collective-permute-start(bf16[256,128]{1,0:T(8,128)(2,1)S(1)} %get-tuple-element.80), channel_id=1, source_target_pairs={{16,0},{20,4},{24,8},{28,12},{0,16},{4,20},{8,24},{12,28},{17,1},{... | collective-permute-start | bytes 196616 | tf_op jit(solution)/shard_map/ppermute | solution.py:117
  23.0 5.3 %collective-permute-start.15 = (bf16[256,128]{1,0:T(8,128)(2,1)S(1)}, bf16[256,128]{1,0:T(8,128)(2,1)S(1)}, u32[]{:S(2)}, u32[]{:S(2)}) collective-permute-start(bf16[256,128]{1,0:T(8,128)(2,1)S(1)} %get-tuple-element.81), channel_id=1, source_target_pairs={{24,0},{28,4},{16,8},{20,12},{8,16},{12,20},{0,24},{4,28},{25,1},{... | collective-permute-start | bytes 196616 | tf_op jit(solution)/shard_map/ppermute | solution.py:117
  24.8 5.8 %collective-permute-start.7 = (bf16[4,128,128]{2,1,0:T(8,128)(2,1)S(1)}, bf16[4,128,128]{2,1,0:T(8,128)(2,1)S(1)}, u32[]{:S(2)}, u32[]{:S(2)}) collective-permute-start(bf16[4,128,128]{2,1,0:T(8,128)(2,1)S(1)} %get-tuple-element.72), channel_id=1, source_target_pairs={{8,0},{12,4},{0,8},{4,12},{24,16},{28,20},{16,24},{20,28},{9,1},{1... | collective-permute-start | bytes 393224 | tf_op jit(solution)/shard_map/ppermute | solution.py:117
  26.4 5.7 %collective-permute-start.8 = (bf16[4,128,128]{2,1,0:T(8,128)(2,1)S(1)}, bf16[4,128,128]{2,1,0:T(8,128)(2,1)S(1)}, u32[]{:S(2)}, u32[]{:S(2)}) collective-permute-start(bf16[4,128,128]{2,1,0:T(8,128)(2,1)S(1)} %get-tuple-element.73), channel_id=1, source_target_pairs={{16,0},{20,4},{24,8},{28,12},{0,16},{4,20},{8,24},{12,28},{17,1},{... | collective-permute-start | bytes 393224 | tf_op jit(solution)/shard_map/ppermute | solution.py:117
  27.9 6.6 %collective-permute-start.9 = (bf16[4,128,128]{2,1,0:T(8,128)(2,1)S(1)}, bf16[4,128,128]{2,1,0:T(8,128)(2,1)S(1)}, u32[]{:S(2)}, u32[]{:S(2)}) collective-permute-start(bf16[4,128,128]{2,1,0:T(8,128)(2,1)S(1)} %get-tuple-element.74), channel_id=1, source_target_pairs={{24,0},{28,4},{16,8},{20,12},{8,16},{12,20},{0,24},{4,28},{25,1},{... | collective-permute-start | bytes 393224 | tf_op jit(solution)/shard_map/ppermute | solution.py:117
  28.6 14.7 %collective-permute-start.16 = (f32[4,128,128]{2,1,0:T(8,128)S(1)}, f32[4,128,128]{2,1,0:T(8,128)S(1)}, u32[]{:S(2)}, u32[]{:S(2)}) collective-permute-start(f32[4,128,128]{2,1,0:T(8,128)S(1)} %shard_map.140.refs_2_), channel_id=1, source_target_pairs={{4,0},{0,4},{12,8},{8,12},{20,16},{16,20},{28,24},{24,28},{5,1},{1... | collective-permute-start | bytes 786440 | tf_op jit(solution)/shard_map/ppermute | solution.py:123
  29.0 8.5 %collective-permute-start.17 = (bf16[512,128]{1,0:T(8,128)(2,1)S(1)}, bf16[512,128]{1,0:T(8,128)(2,1)S(1)}, u32[]{:S(2)}, u32[]{:S(2)}) collective-permute-start(bf16[512,128]{1,0:T(8,128)(2,1)S(1)} %get-tuple-element.97), channel_id=1, source_target_pairs={{8,0},{12,4},{0,8},{4,12},{24,16},{28,20},{16,24},{20,28},{9,1},{1... | collective-permute-start | bytes 393224 | tf_op jit(solution)/shard_map/ppermute | solution.py:117
  30.6 9.5 %collective-permute-start.18 = (bf16[512,128]{1,0:T(8,128)(2,1)S(1)}, bf16[512,128]{1,0:T(8,128)(2,1)S(1)}, u32[]{:S(2)}, u32[]{:S(2)}) collective-permute-start(bf16[512,128]{1,0:T(8,128)(2,1)S(1)} %get-tuple-element.98), channel_id=1, source_target_pairs={{16,0},{20,4},{24,8},{28,12},{0,16},{4,20},{8,24},{12,28},{17,1},{... | collective-permute-start | bytes 393224 | tf_op jit(solution)/shard_map/ppermute | solution.py:117
  32.1 10.5 %collective-permute-start.19 = (bf16[512,128]{1,0:T(8,128)(2,1)S(1)}, bf16[512,128]{1,0:T(8,128)(2,1)S(1)}, u32[]{:S(2)}, u32[]{:S(2)}) collective-permute-start(bf16[512,128]{1,0:T(8,128)(2,1)S(1)} %get-tuple-element.99), channel_id=1, source_target_pairs={{24,0},{28,4},{16,8},{20,12},{8,16},{12,20},{0,24},{4,28},{25,1},{... | collective-permute-start | bytes 393224 | tf_op jit(solution)/shard_map/ppermute | solution.py:117
  35.0 12.6 %collective-permute-start.12 = (bf16[32,2048]{1,0:T(8,128)(2,1)S(1)}, bf16[32,2048]{1,0:T(8,128)(2,1)S(1)}, u32[]{:S(2)}, u32[]{:S(2)}) collective-permute-start(bf16[32,2048]{1,0:T(8,128)(2,1)S(1)} %get-tuple-element.78), channel_id=1, source_target_pairs={{1,0},{0,1},{3,2},{2,3},{5,4},{4,5},{7,6},{6,7},{9,8},{8,9},{11,10... | collective-permute-start | bytes 393224 | tf_op jit(solution)/shard_map/ppermute | solution.py:525
  37.5 11.9 %collective-permute-start.11 = (bf16[32,2048]{1,0:T(8,128)(2,1)S(1)}, bf16[32,2048]{1,0:T(8,128)(2,1)S(1)}, u32[]{:S(2)}, u32[]{:S(2)}) collective-permute-start(bf16[32,2048]{1,0:T(8,128)(2,1)S(1)} %get-tuple-element.77), channel_id=1, source_target_pairs={{2,0},{3,1},{0,2},{1,3},{6,4},{7,5},{4,6},{5,7},{10,8},{11,9},{8,1... | collective-permute-start | bytes 393224 | tf_op jit(solution)/shard_map/ppermute | solution.py:525
  40.1 10.8 %collective-permute-start.10 = (bf16[32,2048]{1,0:T(8,128)(2,1)S(1)}, bf16[32,2048]{1,0:T(8,128)(2,1)S(1)}, u32[]{:S(2)}, u32[]{:S(2)}) collective-permute-start(bf16[32,2048]{1,0:T(8,128)(2,1)S(1)} %get-tuple-element.76), channel_id=1, source_target_pairs={{3,0},{2,1},{1,2},{0,3},{7,4},{6,5},{5,6},{4,7},{11,8},{10,9},{9,1... | collective-permute-start | bytes 393224 | tf_op jit(solution)/shard_map/ppermute | solution.py:525
  43.3 8.4 %collective-permute-start.23 = (f32[256,512]{1,0:T(8,128)S(1)}, f32[256,512]{1,0:T(8,128)S(1)}, u32[]{:S(2)}, u32[]{:S(2)}) collective-permute-start(f32[256,512]{1,0:T(8,128)S(1)} %get-tuple-element.105), channel_id=1, source_target_pairs={{4,0},{0,4},{12,8},{8,12},{20,16},{16,20},{28,24},{24,28},{5,1},{1... | collective-permute-start | bytes 1572872 | tf_op jit(solution)/shard_map/ppermute | solution.py:123
  46.6 6.7 %collective-permute-start.20 = (bf16[400,128]{1,0:T(8,128)(2,1)S(1)}, bf16[400,128]{1,0:T(8,128)(2,1)S(1)}, u32[]{:S(2)}, u32[]{:S(2)}) collective-permute-start(bf16[400,128]{1,0:T(8,128)(2,1)S(1)} %get-tuple-element.101), channel_id=1, source_target_pairs={{24,0},{28,4},{16,8},{20,12},{8,16},{12,20},{0,24},{4,28},{25,1},{... | collective-permute-start | bytes 307208 | tf_op jit(solution)/shard_map/ppermute | solution.py:117
  47.6 7.2 %collective-permute-start.21 = (bf16[400,128]{1,0:T(8,128)(2,1)S(1)}, bf16[400,128]{1,0:T(8,128)(2,1)S(1)}, u32[]{:S(2)}, u32[]{:S(2)}) collective-permute-start(bf16[400,128]{1,0:T(8,128)(2,1)S(1)} %get-tuple-element.102), channel_id=1, source_target_pairs={{16,0},{20,4},{24,8},{28,12},{0,16},{4,20},{8,24},{12,28},{17,1},{... | collective-permute-start | bytes 307208 | tf_op jit(solution)/shard_map/ppermute | solution.py:117
  49.5 5.3 %collective-permute-start.22 = (bf16[400,128]{1,0:T(8,128)(2,1)S(1)}, bf16[400,128]{1,0:T(8,128)(2,1)S(1)}, u32[]{:S(2)}, u32[]{:S(2)}) collective-permute-start(bf16[400,128]{1,0:T(8,128)(2,1)S(1)} %get-tuple-element.103), channel_id=1, source_target_pairs={{8,0},{12,4},{0,8},{4,12},{24,16},{28,20},{16,24},{20,28},{9,1},{1... | collective-permute-start | bytes 307208 | tf_op jit(solution)/shard_map/ppermute | solution.py:117
